TPU v7x, 32 devices: a whole 2x2x4 slice. The times are simulated.
32 devices in a mesh: plane: 4 (over z), slab: 8 (over y, x, core).
Axes of the slice: x: 2, y: 2, z: 4, core: 2. Of those that a mesh axis runs over, the one named last changes fastest.
Arguments:
- potential: float32 [20, 48, 4096], P('plane', None, 'slab'), may hold values from -1.5 to 1.5
- mixing: float32 [20], P('plane'), may hold values from 1.05 to 1.6
- lens_weight: float32 [20], P('plane'), may hold values from 0.02 to 0.08
- observed: float32 [20, 3, 48, 4096], P('plane', None, 'slab'), may hold values from -6 to 6
- noise_weight: float32 [20, 48, 4096], P('plane', 'slab'), may hold values from 0.3 to 3
Outputs:
- deflection: float32 [20, 2, 48, 4096], P('plane', None, 'slab')
- shear: float32 [20, 3, 48, 4096], P('plane', None, 'slab')
- potential_grad: float32 [20, 48, 4096], P('plane', None, 'slab')
All inputs are finite; a program needn't handle non-finite values.
Results may differ from a plain program's by a relative error of at most 0.00013.
Values sent between devices are 32-bit elements; how exact they have to be, the bound alone decides.
No kernel may reach another device: no remote copies, remote signals or barrier semaphores. Data moves between devices by JAX's collectives and lax.ppermute only.
A program may use at most 256 MiB of HBM per device.

v0:
```python
import jax
import jax.numpy as jnp
from jax import lax
from jax.sharding import PartitionSpec as P


def with_halo(x, sides, width):
    for axis, dim in sides:
        size, length = (lax.axis_size(axis), x.shape[dim])
        up = [(i, (i + 1) % size) for i in range(size)]
        down = [(j, i) for i, j in up]
        last = lax.slice_in_dim(x, length - width, length, axis=dim)
        initial = lax.slice_in_dim(x, 0, width, axis=dim)
        before = lax.ppermute(last, axis, up)
        after = lax.ppermute(initial, axis, down)
        x = jnp.concatenate([before, x, after], axis=dim)
    return x


def from_behind(block, axis, distance):
    devices = range(lax.axis_size(axis))
    route = [(i - distance, i) for i in devices if i - distance in devices]
    return lax.ppermute(block, axis, route)


def wrap_pad(array, dim):
    extent = array.shape[dim]
    leading = lax.slice_in_dim(array, 0, 1, axis=dim)
    trailing = lax.slice_in_dim(array, extent - 1, extent, axis=dim)
    return jnp.concatenate([trailing, array, leading], axis=dim)


def five_fields(padded):
    center = padded[..., 1:-1, 1:-1]
    row_next = padded[..., 2:, 1:-1]
    row_prev = padded[..., :-2, 1:-1]
    col_next = padded[..., 1:-1, 2:]
    col_prev = padded[..., 1:-1, :-2]
    mixed = 0.25 * (
        padded[..., 2:, 2:] - padded[..., 2:, :-2] - padded[..., :-2, 2:] + padded[..., :-2, :-2]
    )
    return jnp.stack(
        [
            0.5 * (row_next - row_prev),
            0.5 * (col_next - col_prev),
            row_next - 2.0 * center + row_prev,
            col_next - 2.0 * center + col_prev,
            mixed,
        ],
        axis=-3,
    )


def adjoint_fields(padded):
    rows_part = (
        padded[..., 0, 2:, 1:-1] - 2.0 * padded[..., 0, 1:-1, 1:-1] + padded[..., 0, :-2, 1:-1]
    )
    cols_part = (
        padded[..., 1, 1:-1, 2:] - 2.0 * padded[..., 1, 1:-1, 1:-1] + padded[..., 1, 1:-1, :-2]
    )
    mixed_part = 0.25 * (
        padded[..., 2, 2:, 2:]
        - padded[..., 2, 2:, :-2]
        - padded[..., 2, :-2, 2:]
        + padded[..., 2, :-2, :-2]
    )
    return rows_part + cols_part + mixed_part


def plane_forward(a_now, a_before, defl_now, defl_before, fields, mix, weight):
    diag_first = mix - weight * fields[2]
    diag_second = mix - weight * fields[3]
    off_diag = -weight * fields[4]
    keep = 1.0 - mix
    new_a = jnp.stack(
        [
            diag_first * a_now[0] + off_diag * a_now[2] + keep * a_before[0],
            diag_first * a_now[1] + off_diag * a_now[3] + keep * a_before[1],
            off_diag * a_now[0] + diag_second * a_now[2] + keep * a_before[2],
            off_diag * a_now[1] + diag_second * a_now[3] + keep * a_before[3],
        ]
    )
    new_defl = mix * defl_now + keep * defl_before - weight * fields[0:2]
    return (new_a, new_defl)


def shear_of(distort):
    return jnp.stack(
        [
            1.0 - 0.5 * (distort[0] + distort[3]),
            0.5 * (distort[3] - distort[0]),
            -0.5 * (distort[1] + distort[2]),
        ]
    )


def source_adjoint(residual):
    return jnp.stack(
        [
            -0.5 * (residual[..., 0, :, :] + residual[..., 1, :, :]),
            -0.5 * residual[..., 2, :, :],
            -0.5 * residual[..., 2, :, :],
            -0.5 * (residual[..., 0, :, :] - residual[..., 1, :, :]),
        ],
        axis=-3,
    )


def plane_adjoint(p_full, q_state, a_now, fields, mix, weight):
    diag_first = mix - weight * fields[2]
    diag_second = mix - weight * fields[3]
    off_diag = -weight * fields[4]
    keep = 1.0 - mix
    new_p = (
        jnp.stack(
            [
                diag_first * p_full[0] + off_diag * p_full[2],
                diag_first * p_full[1] + off_diag * p_full[3],
                off_diag * p_full[0] + diag_second * p_full[2],
                off_diag * p_full[1] + diag_second * p_full[3],
            ]
        )
        + q_state
    )
    new_q = keep * p_full
    cot = jnp.stack(
        [
            -weight * (p_full[0] * a_now[0] + p_full[1] * a_now[1]),
            -weight * (p_full[2] * a_now[2] + p_full[3] * a_now[3]),
            -weight
            * (
                p_full[0] * a_now[2]
                + p_full[1] * a_now[3]
                + p_full[2] * a_now[0]
                + p_full[3] * a_now[1]
            ),
        ]
    )
    return (new_p, new_q, cot)


def forward_pass(incoming, fields, mixing, lens_weight):
    a_now = incoming[0:4]
    a_before = incoming[4:8]
    defl_now = incoming[8:10]
    defl_before = incoming[10:12]
    stored = []
    deflections = []
    shears = []
    for plane_index in range(fields.shape[0]):
        stored.append(a_now)
        new_a, new_defl = plane_forward(
            a_now,
            a_before,
            defl_now,
            defl_before,
            fields[plane_index],
            mixing[plane_index],
            lens_weight[plane_index],
        )
        a_before, a_now = (a_now, new_a)
        defl_before, defl_now = (defl_now, new_defl)
        deflections.append(new_defl)
        shears.append(shear_of(new_a))
    outgoing = jnp.concatenate([a_now, a_before, defl_now, defl_before], axis=0)
    return (outgoing, jnp.stack(stored), jnp.stack(deflections), jnp.stack(shears))


def adjoint_pass(incoming, sources, stored, fields, mixing, lens_weight):
    p_state = incoming[0:4]
    q_state = incoming[4:8]
    cotangents = [None] * fields.shape[0]
    for plane_index in reversed(range(fields.shape[0])):
        p_full = p_state + sources[plane_index]
        p_state, q_state, cotangents[plane_index] = plane_adjoint(
            p_full,
            q_state,
            stored[plane_index],
            fields[plane_index],
            mixing[plane_index],
            lens_weight[plane_index],
        )
    return (jnp.concatenate([p_state, q_state], axis=0), jnp.stack(cotangents))


def start_of(map_shape):
    ones_map = jnp.ones(map_shape, jnp.float32)
    zeros_map = jnp.zeros(map_shape, jnp.float32)
    identity_a = jnp.stack([ones_map, zeros_map, zeros_map, ones_map])
    return jnp.concatenate(
        [identity_a, identity_a, jnp.zeros((4,) + map_shape, jnp.float32)], axis=0
    )


def on_device(potential, mixing, lens_weight, observed, noise_weight):
    widened = with_halo(potential, (("slab", 2),), 1)
    fields = lax.all_to_all(
        five_fields(wrap_pad(widened, 1)), "slab", split_axis=2, concat_axis=3, tiled=True
    )
    map_shape = fields.shape[2:]
    start_state = start_of(map_shape)
    is_first = lax.axis_index("plane") == 0

    def relay_turn(turn_index, incoming):
        outgoing = forward_pass(incoming, fields, mixing, lens_weight)[0]
        received = from_behind(outgoing, "plane", 1)
        return jnp.where(is_first, start_state, received)

    incoming = lax.fori_loop(0, lax.axis_size("plane") - 1, relay_turn, start_state)
    leftover, stored, deflection, shear = forward_pass(incoming, fields, mixing, lens_weight)
    residual = noise_weight[:, None] * (shear - observed)
    sources = source_adjoint(residual)
    zero_state = jnp.zeros((8,) + map_shape, jnp.float32)
    is_last = lax.axis_index("plane") == lax.axis_size("plane") - 1

    def back_turn(turn_index, incoming_back):
        outgoing = adjoint_pass(incoming_back, sources, stored, fields, mixing, lens_weight)[0]
        received = from_behind(outgoing, "plane", -1)
        return jnp.where(is_last, zero_state, received)

    incoming_back = lax.fori_loop(0, lax.axis_size("plane") - 1, back_turn, zero_state)
    leftover_back, cot = adjoint_pass(incoming_back, sources, stored, fields, mixing, lens_weight)
    column_block = lax.all_to_all(cot, "slab", split_axis=3, concat_axis=2, tiled=True)
    widened_back = with_halo(column_block, (("slab", 3),), 1)
    potential_grad = adjoint_fields(wrap_pad(widened_back, 2))
    return (deflection, shear, potential_grad)


def solution(mesh):
    placed = (
        P("plane", None, "slab"),
        P("plane"),
        P("plane"),
        P("plane", None, "slab", None),
        P("plane", "slab", None),
    )
    return jax.shard_map(
        on_device,
        mesh=mesh,
        in_specs=placed,
        out_specs=(
            P("plane", None, "slab", None),
            P("plane", None, "slab", None),
            P("plane", None, "slab"),
        ),
        check_vma=False,
    )
```

profile of v0, /device:TPU:0, one launch (start us, length us, event | category | flops | bytes accessed | tf_op | source)
XLA Modules:
  0.0 684.2 jit_solution(17564305452485828587)
XLA Ops:
  5.5 4.3 collective-permute-done.3
  19.9 4.7 all-to-all-start
  33.7 37.3 %all-to-all-done = f32[5,5,48,512]{3,0,1,2:T(8,128)} async-done(((f32[5,5,48,512]{3,0,1,2:T(8,128)}), f32[5,5,48,512]{3,0,1,2:T(8,128)}, u32[]{:S(2)}, u32[]{:S(2)}) %all-to-all-start) | async-done | bytes 2457632 | tf_op jit(solution)/shard_map/all_to_all | solution.py:197
  75.9 4.1 slice_multiply_fusion.13
  83.1 7.1 %fusion.111 = (f32[1,1,6,8,512]{4,3,2,1,0:T(8,128)}, f32[1,1,6,8,512]{4,3,2,1,0:T(8,128)}, f32[1,1,6,8,512]{4,3,2,1,0:T(8,128)}, f32[1,1,6,8,512]{4,3,2,1,0:T(8,...) fusion(f32[5,5,6,8,512]{4,3,2,1,0:T(8,128)} %bitcast.660, ...), kind=kLoop, calls=%fused_computation.328 | loop fusion | flops 393216 | bytes 1769512 | tf_op jit(solution)/shard_map/sub | solution.py:72
  90.2 4.7 fusion.112
  94.9 218.3 %while.23 = (s32[]{:T(128)}, f32[12,6,4096]{2,1,0:T(8,128)}, pred[]{:T(512)}, f32[5]{0:T(128)S(1)}, f32[5]{0:T(128)S(1)}, /*index=5*/f32[5,5,6,4096]{3,2,1,0:T(8...) while((s32[]{:T(128)}, f32[12,6,4096]{2,1,0:T(8,128)}, ...), condition=%wide.region_1.2_spmd, body=%wide.region_0.1_spmd.sunk | while | flops 5283841 | bytes 24397784 | solution.py:209
  98.1 5.0 fusion.155
  103.1 3.9 fusion.157
  107.0 4.6 fusion.156
  111.7 4.6 fusion.158
  122.8 7.3 %fusion.161 = (f32[12,6,4096]{2,1,0:T(8,128)}, f32[2,6,4096]{2,1,0:T(8,128)S(1)}) fusion(f32[12,6,4096]{2,1,0:T(8,128)} %constant_dynamic-update-slice_fusion.13, f32[5,5,6,4096]{3,2,1,0:T(8,128)S(1)} %get-tuple-element.1007, f32[]{:T(128)} %bitcast.628, f32[]{:T(128)} %get-tuple-element.1017, f32[]{:T(128)} %bitcast.629, f32[]{:T(128)} %bitcast.624, ...), kind=kLoop, calls=%fused_computation.2.clone.1 | loop fusion | flops 1228800 | bytes 1842688 | tf_op jit(solution)/shard_map/while
  130.8 4.7 collective-permute-start
  135.4 29.8 %collective-permute-done = f32[12,6,4096]{2,1,0:T(8,128)} collective-permute-done((f32[12,6,4096]{2,1,0:T(8,128)}, f32[12,6,4096]{2,1,0:T(8,128)}, u32[]{:S(2)}, u32[]{:S(2)}) %collective-permute-start) | collective-permute-done | bytes 1179680 | tf_op jit(solution)/shard_map/while/body/eval_jaxpr/ppermute | solution.py:23
  171.2 5.0 fusion.155
  176.2 3.9 fusion.157
  180.1 4.6 fusion.156
  184.8 4.6 fusion.158
  195.9 7.3 %fusion.161 = (f32[12,6,4096]{2,1,0:T(8,128)}, f32[2,6,4096]{2,1,0:T(8,128)S(1)}) fusion(f32[12,6,4096]{2,1,0:T(8,128)} %constant_dynamic-update-slice_fusion.13, f32[5,5,6,4096]{3,2,1,0:T(8,128)S(1)} %get-tuple-element.1007, f32[]{:T(128)} %bitcast.628, f32[]{:T(128)} %get-tuple-element.1017, f32[]{:T(128)} %bitcast.629, f32[]{:T(128)} %bitcast.624, ...), kind=kLoop, calls=%fused_computation.2.clone.1 | loop fusion | flops 1228800 | bytes 1842688 | tf_op jit(solution)/shard_map/while
  203.9 5.6 collective-permute-start
  209.4 28.9 %collective-permute-done = f32[12,6,4096]{2,1,0:T(8,128)} collective-permute-done((f32[12,6,4096]{2,1,0:T(8,128)}, f32[12,6,4096]{2,1,0:T(8,128)}, u32[]{:S(2)}, u32[]{:S(2)}) %collective-permute-start) | collective-permute-done | bytes 1179680 | tf_op jit(solution)/shard_map/while/body/eval_jaxpr/ppermute | solution.py:23
  244.3 5.0 fusion.155
  249.3 3.9 fusion.157
  253.2 4.6 fusion.156
  257.8 4.6 fusion.158
  269.0 7.3 %fusion.161 = (f32[12,6,4096]{2,1,0:T(8,128)}, f32[2,6,4096]{2,1,0:T(8,128)S(1)}) fusion(f32[12,6,4096]{2,1,0:T(8,128)} %constant_dynamic-update-slice_fusion.13, f32[5,5,6,4096]{3,2,1,0:T(8,128)S(1)} %get-tuple-element.1007, f32[]{:T(128)} %bitcast.628, f32[]{:T(128)} %get-tuple-element.1017, f32[]{:T(128)} %bitcast.629, f32[]{:T(128)} %bitcast.624, ...), kind=kLoop, calls=%fused_computation.2.clone.1 | loop fusion | flops 1228800 | bytes 1842688 | tf_op jit(solution)/shard_map/while
  277.0 5.6 collective-permute-start
  282.5 28.0 %collective-permute-done = f32[12,6,4096]{2,1,0:T(8,128)} collective-permute-done((f32[12,6,4096]{2,1,0:T(8,128)}, f32[12,6,4096]{2,1,0:T(8,128)}, u32[]{:S(2)}, u32[]{:S(2)}) %collective-permute-start) | collective-permute-done | bytes 1179680 | tf_op jit(solution)/shard_map/while/body/eval_jaxpr/ppermute | solution.py:23
  333.0 4.9 multiply_subtract_fusion.20
  346.5 108.3 %while.24 = (s32[]{:T(128)}, f32[8,6,4096]{2,0,1:T(8,128)S(1)}, pred[]{:T(512)}, f32[5]{0:T(128)S(1)}, f32[5]{0:T(128)S(1)}, /*index=5*/f32[5,5,6,4096]{3,0,2,1:...) while((s32[]{:T(128)}, f32[8,6,4096]{2,0,1:T(8,128)S(1)}, ...), condition=%wide.region_3.4_spmd.clone, body=%wide.region_2.3_spmd.clone.sunk | while | flops 5627907 | bytes 22315392 | solution.py:221
  347.3 3.6 fusion.163
  355.4 3.6 fusion.167
  359.4 3.6 fusion.169
  368.8 14.9 %collective-permute-done.1 = f32[8,6,4096]{2,0,1:T(8,128)S(1)} collective-permute-done((f32[8,6,4096]{2,0,1:T(8,128)S(1)}, f32[8,6,4096]{2,0,1:T(8,128)S(1)}, u32[]{:S(2)}, u32[]{:S(2)}) %collective-permute-start.1) | collective-permute-done | bytes 786464 | tf_op jit(solution)/shard_map/while/body/eval_jaxpr/ppermute | solution.py:23
  384.6 3.6 fusion.163
  392.6 3.6 fusion.167
  396.7 3.6 fusion.169
  406.1 13.5 %collective-permute-done.1 = f32[8,6,4096]{2,0,1:T(8,128)S(1)} collective-permute-done((f32[8,6,4096]{2,0,1:T(8,128)S(1)}, f32[8,6,4096]{2,0,1:T(8,128)S(1)}, u32[]{:S(2)}, u32[]{:S(2)}) %collective-permute-start.1) | collective-permute-done | bytes 786464 | tf_op jit(solution)/shard_map/while/body/eval_jaxpr/ppermute | solution.py:23
  420.5 3.6 fusion.163
  428.5 3.6 fusion.167
  441.9 12.6 %collective-permute-done.1 = f32[8,6,4096]{2,0,1:T(8,128)S(1)} collective-permute-done((f32[8,6,4096]{2,0,1:T(8,128)S(1)}, f32[8,6,4096]{2,0,1:T(8,128)S(1)}, u32[]{:S(2)}, u32[]{:S(2)}) %collective-permute-start.1) | collective-permute-done | bytes 786464 | tf_op jit(solution)/shard_map/while/body/eval_jaxpr/ppermute | solution.py:23
  476.1 25.2 %copy.301 = f32[5,3,6,4096]{2,1,0,3:T(4,128)} copy(f32[5,3,6,4096]{3,1,2,0:T(4,128)S(1)} %fusion.100) | data formatting | bytes 2949120 | tf_op jit(solution)/shard_map/stack | solution.py:183
  501.3 53.3 %reshape.1331 = f32[8,1,46080]{2,1,0:T(1,128)} reshape(f32[4096,5,3,6]{3,2,1,0:T(4,128)} %bitcast.656) | data formatting | bytes 2949120
  554.6 21.8 %all-to-all-start.1 = ((f32[8,1,46080]{2,1,0:T(1,128)}), f32[8,1,46080]{2,1,0:T(1,128)S(1)}, u32[]{:S(2)}, u32[]{:S(2)}) async-start(f32[8,1,46080]{2,1,0:T(1,128)} %reshape.1331), calls=%async_computation.1 | async-start | bytes 2949120 | tf_op jit(solution)/shard_map/all_to_all | solution.py:223
  583.0 13.0 %all-to-all-done.1 = f32[8,1,46080]{2,1,0:T(1,128)S(1)} async-done(((f32[8,1,46080]{2,1,0:T(1,128)}), f32[8,1,46080]{2,1,0:T(1,128)S(1)}, u32[]{:S(2)}, u32[]{:S(2)}) %all-to-all-start.1) | async-done | bytes 1474592 | tf_op jit(solution)/shard_map/all_to_all | solution.py:223
  596.6 4.1 reduce
  600.7 42.4 %reshape.1332 = f32[4096,5,3,6]{3,2,1,0:T(4,128)} reshape(f32[8,46080]{1,0:T(8,128)S(1)} %reduce) | data formatting | bytes 2949120
  643.1 28.3 %copy.302 = f32[5,3,6,8,512]{4,2,3,1,0:T(8,128)S(1)} copy(f32[5,3,6,8,512]{2,1,0,4,3:T(4,128)} %bitcast.657) | data formatting | bytes 2949120 | tf_op jit(solution)/shard_map/all_to_all | solution.py:223
  (353 shorter events, 171.3 us)
Async XLA Ops:
  2.1 7.8 %collective-permute-start.3 = (f32[5,48,1]{2,0,1:T(8,128)S(1)}, f32[5,48,1]{2,0,1:T(8,128)S(1)}, u32[]{:S(2)}, u32[]{:S(2)}) collective-permute-start(f32[5,48,1]{2,0,1:T(8,128)S(1)} %get-tuple-element.575), channel_id=1, source_target_pairs={{1,0},{2,1},{3,2},{4,3},{5,4},{6,5},{7,6},{0,7},{9,8},{10,9},{11,1... | collective-permute-start | bytes 2888 | tf_op jit(solution)/shard_map/ppermute | solution.py:15
  5.5 6.3 collective-permute-start.2
  19.9 51.0 %all-to-all-start = ((f32[5,5,48,512]{3,0,1,2:T(8,128)}), f32[5,5,48,512]{3,0,1,2:T(8,128)}, u32[]{:S(2)}, u32[]{:S(2)}) async-start(f32[5,5,48,512]{3,0,1,2:T(8,128)} %fusion.74), calls=%async_computation | async-start | bytes 7864320 | tf_op jit(solution)/shard_map/all_to_all | solution.py:197
  24.8 49.7 %copy-start.1 = (f32[12,6,4096]{2,1,0:T(8,128)}, f32[12,6,4096]{2,1,0:T(8,128)S(1)}, u32[]{:S(2)}) copy-start(f32[12,6,4096]{2,1,0:T(8,128)S(1)} %broadcast_dynamic-update-slice_fusion) | copy-start | bytes 3538948
  94.9 8.2 %copy-start = (f32[12,6,4096]{2,1,0:T(8,128)S(1)}, f32[12,6,4096]{2,1,0:T(8,128)}, u32[]{:S(2)}) copy-start(f32[12,6,4096]{2,1,0:T(8,128)} %get-tuple-element.985) | copy-start | bytes 3538948 | tf_op jit(solution)/shard_map/while
  130.8 34.5 %collective-permute-start = (f32[12,6,4096]{2,1,0:T(8,128)}, f32[12,6,4096]{2,1,0:T(8,128)}, u32[]{:S(2)}, u32[]{:S(2)}) collective-permute-start(f32[12,6,4096]{2,1,0:T(8,128)} %constant_dynamic-update-slice_fusion.14), channel_id=1, source_target_pairs={{0,8},{8,16},{16,24},{1,9},{9,17},{17,25},{2,10},{10,18},{18,26},{... | collective-permute-start | bytes 3538952 | tf_op jit(solution)/shard_map/while/body/eval_jaxpr/ppermute | solution.py:23
  168.0 8.2 %copy-start = (f32[12,6,4096]{2,1,0:T(8,128)S(1)}, f32[12,6,4096]{2,1,0:T(8,128)}, u32[]{:S(2)}) copy-start(f32[12,6,4096]{2,1,0:T(8,128)} %get-tuple-element.985) | copy-start | bytes 3538948 | tf_op jit(solution)/shard_map/while
  203.9 34.4 %collective-permute-start = (f32[12,6,4096]{2,1,0:T(8,128)}, f32[12,6,4096]{2,1,0:T(8,128)}, u32[]{:S(2)}, u32[]{:S(2)}) collective-permute-start(f32[12,6,4096]{2,1,0:T(8,128)} %constant_dynamic-update-slice_fusion.14), channel_id=1, source_target_pairs={{0,8},{8,16},{16,24},{1,9},{9,17},{17,25},{2,10},{10,18},{18,26},{... | collective-permute-start | bytes 3538952 | tf_op jit(solution)/shard_map/while/body/eval_jaxpr/ppermute | solution.py:23
  241.1 8.2 %copy-start = (f32[12,6,4096]{2,1,0:T(8,128)S(1)}, f32[12,6,4096]{2,1,0:T(8,128)}, u32[]{:S(2)}) copy-start(f32[12,6,4096]{2,1,0:T(8,128)} %get-tuple-element.985) | copy-start | bytes 3538948 | tf_op jit(solution)/shard_map/while
  277.0 33.5 %collective-permute-start = (f32[12,6,4096]{2,1,0:T(8,128)}, f32[12,6,4096]{2,1,0:T(8,128)}, u32[]{:S(2)}, u32[]{:S(2)}) collective-permute-start(f32[12,6,4096]{2,1,0:T(8,128)} %constant_dynamic-update-slice_fusion.14), channel_id=1, source_target_pairs={{0,8},{8,16},{16,24},{1,9},{9,17},{17,25},{2,10},{10,18},{18,26},{... | collective-permute-start | bytes 3538952 | tf_op jit(solution)/shard_map/while/body/eval_jaxpr/ppermute | solution.py:23
  321.8 10.6 %copy-start.78 = (f32[1,1,6,8,512]{4,3,2,1,0:T(8,128)S(1)}, f32[1,1,6,8,512]{4,3,2,1,0:T(8,128)}, u32[]{:S(2)}) copy-start(f32[1,1,6,8,512]{4,3,2,1,0:T(8,128)} %get-tuple-element.553) | copy-start | bytes 294916
  321.8 10.7 %copy-start.77 = (f32[1,1,6,8,512]{4,3,2,1,0:T(8,128)S(1)}, f32[1,1,6,8,512]{4,3,2,1,0:T(8,128)}, u32[]{:S(2)}) copy-start(f32[1,1,6,8,512]{4,3,2,1,0:T(8,128)} %get-tuple-element.551) | copy-start | bytes 294916
  321.8 10.9 %copy-start.76 = (f32[1,1,6,8,512]{4,3,2,1,0:T(8,128)S(1)}, f32[1,1,6,8,512]{4,3,2,1,0:T(8,128)}, u32[]{:S(2)}) copy-start(f32[1,1,6,8,512]{4,3,2,1,0:T(8,128)} %get-tuple-element.554) | copy-start | bytes 294916
  321.8 11.0 %copy-start.75 = (f32[1,1,6,8,512]{4,3,2,1,0:T(8,128)S(1)}, f32[1,1,6,8,512]{4,3,2,1,0:T(8,128)}, u32[]{:S(2)}) copy-start(f32[1,1,6,8,512]{4,3,2,1,0:T(8,128)} %get-tuple-element.549) | copy-start | bytes 294916
  321.8 11.1 %copy-start.74 = (f32[1,1,6,8,512]{4,3,2,1,0:T(8,128)S(1)}, f32[1,1,6,8,512]{4,3,2,1,0:T(8,128)}, u32[]{:S(2)}) copy-start(f32[1,1,6,8,512]{4,3,2,1,0:T(8,128)} %get-tuple-element.540) | copy-start | bytes 294916
  321.8 11.2 %copy-start.72 = (f32[1,6,4096]{2,1,0:T(8,128)S(1)}, f32[1,6,4096]{2,1,0:T(8,128)}, u32[]{:S(2)}) copy-start(f32[1,6,4096]{2,1,0:T(8,128)} %get-tuple-element.568) | copy-start | bytes 294916
  321.8 11.2 %copy-start.73 = (f32[1,6,4096]{2,1,0:T(8,128)S(1)}, f32[1,6,4096]{2,1,0:T(8,128)}, u32[]{:S(2)}) copy-start(f32[1,6,4096]{2,1,0:T(8,128)} %get-tuple-element.569) | copy-start | bytes 294916
  322.9 16.8 %copy-start.11 = (f32[1,6,4096]{2,0,1:T(1,128)}, f32[1,6,4096]{2,0,1:T(1,128)S(1)}, u32[]{:S(2)}) copy-start(f32[1,6,4096]{2,0,1:T(1,128)S(1)} %mul.3815) | copy-start | bytes 294916
  323.9 15.7 %copy-start.12 = (f32[1,6,4096]{2,0,1:T(1,128)}, f32[1,6,4096]{2,0,1:T(1,128)S(1)}, u32[]{:S(2)}) copy-start(f32[1,6,4096]{2,0,1:T(1,128)S(1)} %sub.972) | copy-start | bytes 294916
  325.0 14.7 %copy-start.13 = (f32[1,6,4096]{2,0,1:T(1,128)}, f32[1,6,4096]{2,0,1:T(1,128)S(1)}, u32[]{:S(2)}) copy-start(f32[1,6,4096]{2,0,1:T(1,128)S(1)} %sub.974) | copy-start | bytes 294916
  326.0 11.9 %copy-start.28 = (f32[1,6,4096]{2,0,1:T(1,128)}, f32[1,6,4096]{2,0,1:T(1,128)S(1)}, u32[]{:S(2)}) copy-start(f32[1,6,4096]{2,0,1:T(1,128)S(1)} %mul.3793) | copy-start | bytes 294916
  327.1 10.9 %copy-start.30 = (f32[1,6,4096]{2,0,1:T(1,128)}, f32[1,6,4096]{2,0,1:T(1,128)S(1)}, u32[]{:S(2)}) copy-start(f32[1,6,4096]{2,0,1:T(1,128)S(1)} %sub.965) | copy-start | bytes 294916
  328.1 9.8 %copy-start.32 = (f32[1,6,4096]{2,0,1:T(1,128)}, f32[1,6,4096]{2,0,1:T(1,128)S(1)}, u32[]{:S(2)}) copy-start(f32[1,6,4096]{2,0,1:T(1,128)S(1)} %sub.967) | copy-start | bytes 294916
  329.2 8.8 %copy-start.22 = (f32[1,6,4096]{2,0,1:T(1,128)}, f32[1,6,4096]{2,0,1:T(1,128)S(1)}, u32[]{:S(2)}) copy-start(f32[1,6,4096]{2,0,1:T(1,128)S(1)} %mul.3771) | copy-start | bytes 294916
  330.2 7.7 %copy-start.24 = (f32[1,6,4096]{2,0,1:T(1,128)}, f32[1,6,4096]{2,0,1:T(1,128)S(1)}, u32[]{:S(2)}) copy-start(f32[1,6,4096]{2,0,1:T(1,128)S(1)} %sub.958) | copy-start | bytes 294916
  331.3 6.7 copy-start.26
  332.3 5.7 copy-start.16
  332.5 5.5 copy-start.18
  332.6 5.4 copy-start.20
  367.5 16.2 %collective-permute-start.1 = (f32[8,6,4096]{2,0,1:T(8,128)S(1)}, f32[8,6,4096]{2,0,1:T(8,128)S(1)}, u32[]{:S(2)}, u32[]{:S(2)}) collective-permute-start(f32[8,6,4096]{2,0,1:T(8,128)S(1)} %pad_maximum_fusion.19), channel_id=1, source_target_pairs={{8,0},{16,8},{24,16},{9,1},{17,9},{25,17},{10,2},{18,10},{26,18},{... | collective-permute-start | bytes 2359304 | tf_op jit(solution)/shard_map/while/body/eval_jaxpr/ppermute | solution.py:23
  404.8 14.8 %collective-permute-start.1 = (f32[8,6,4096]{2,0,1:T(8,128)S(1)}, f32[8,6,4096]{2,0,1:T(8,128)S(1)}, u32[]{:S(2)}, u32[]{:S(2)}) collective-permute-start(f32[8,6,4096]{2,0,1:T(8,128)S(1)} %pad_maximum_fusion.19), channel_id=1, source_target_pairs={{8,0},{16,8},{24,16},{9,1},{17,9},{25,17},{10,2},{18,10},{26,18},{... | collective-permute-start | bytes 2359304 | tf_op jit(solution)/shard_map/while/body/eval_jaxpr/ppermute | solution.py:23
  440.6 13.9 %collective-permute-start.1 = (f32[8,6,4096]{2,0,1:T(8,128)S(1)}, f32[8,6,4096]{2,0,1:T(8,128)S(1)}, u32[]{:S(2)}, u32[]{:S(2)}) collective-permute-start(f32[8,6,4096]{2,0,1:T(8,128)S(1)} %pad_maximum_fusion.19), channel_id=1, source_target_pairs={{8,0},{16,8},{24,16},{9,1},{17,9},{25,17},{10,2},{18,10},{26,18},{... | collective-permute-start | bytes 2359304 | tf_op jit(solution)/shard_map/while/body/eval_jaxpr/ppermute | solution.py:23
  459.1 5.9 copy-start.35
  459.1 5.9 copy-start.37
  459.1 5.9 copy-start.39
  459.1 5.9 copy-start.41
  460.3 6.3 copy-start.70
  463.4 6.2 copy-start.69
  470.1 5.0 copy-start.82
  470.1 5.0 copy-start.83
  470.1 5.0 copy-start.84
  554.6 26.0 %copy-start.67 = (f32[1,2,6,8,512]{4,3,2,1,0:T(8,128)S(1)}, f32[1,2,6,8,512]{4,3,2,1,0:T(8,128)}, u32[]{:S(2)}) copy-start(f32[1,2,6,8,512]{4,3,2,1,0:T(8,128)} %get-tuple-element.556) | copy-start | bytes 589828
  554.6 41.4 %all-to-all-start.1 = ((f32[8,1,46080]{2,1,0:T(1,128)}), f32[8,1,46080]{2,1,0:T(1,128)S(1)}, u32[]{:S(2)}, u32[]{:S(2)}) async-start(f32[8,1,46080]{2,1,0:T(1,128)} %reshape.1331), calls=%async_computation.1 | async-start | bytes 2949120 | tf_op jit(solution)/shard_map/all_to_all | solution.py:223
  579.2 16.9 %copy-start.6 = (f32[2,6,4096]{2,0,1:T(2,128)}, f32[2,6,4096]{2,0,1:T(2,128)S(1)}, u32[]{:S(2)}) copy-start(f32[2,6,4096]{2,0,1:T(2,128)S(1)} %get-tuple-element.485) | copy-start | bytes 589828
  580.6 15.4 %copy-start.9 = (f32[2,6,4096]{2,0,1:T(2,128)}, f32[2,6,4096]{2,0,1:T(2,128)S(1)}, u32[]{:S(2)}) copy-start(f32[2,6,4096]{2,0,1:T(2,128)S(1)} %get-tuple-element.483) | copy-start | bytes 589828
  580.8 15.2 %copy-start.10 = (f32[2,6,4096]{2,0,1:T(2,128)}, f32[2,6,4096]{2,0,1:T(2,128)S(1)}, u32[]{:S(2)}) copy-start(f32[2,6,4096]{2,0,1:T(2,128)S(1)} %mul.3714) | copy-start | bytes 589828
  671.8 9.0 %collective-permute-start.5 = (f32[5,3,48,1]{3,2,1,0:T(8,128)S(1)}, f32[5,3,48,1]{3,2,1,0:T(8,128)S(1)}, u32[]{:S(2)}, u32[]{:S(2)}) collective-permute-start(f32[5,3,48,1]{3,2,1,0:T(8,128)S(1)} %get-tuple-element.571), channel_id=1, source_target_pairs={{1,0},{2,1},{3,2},{4,3},{5,4},{6,5},{7,6},{0,7},{9,8},{10,9},{11,1... | collective-permute-start | bytes 8648 | tf_op jit(solution)/shard_map/ppermute | solution.py:15
  671.9 10.0 %collective-permute-start.4 = (f32[5,3,48,1]{3,2,1,0:T(8,128)S(1)}, f32[5,3,48,1]{3,2,1,0:T(8,128)S(1)}, u32[]{:S(2)}, u32[]{:S(2)}) collective-permute-start(f32[5,3,48,1]{3,2,1,0:T(8,128)S(1)} %get-tuple-element.570), channel_id=1, source_target_pairs={{0,1},{1,2},{2,3},{3,4},{4,5},{5,6},{6,7},{7,0},{8,9},{9,10},{10,1... | collective-permute-start | bytes 8648 | tf_op jit(solution)/shard_map/ppermute | solution.py:14
  (57 other events, 163.7 us)
where the time goes:
time: 692 us; the launch traced here: 684 us
  other arithmetic  238 us (34%)
  local copies, waits for them, and re-layouts  198 us (29%)
  waiting for transfers between devices  188 us (27%)
  starting transfers between devices  50.1 us (7%)
  between operations  8.87 us (1%)
    ppermute x6, waiting for transfers between devices, from_behind(): return lax.ppermute(block, axis, route)  128 us
    unnamed x192, local copies, waits for them, and re-layouts  106 us
    while x18, other arithmetic  61.2 us
    add x19, other arithmetic, plane_adjoint(): diag_first * p_full[0] + off_diag * p_full[2]  56.7 us
    all_to_all x1, waiting for transfers between devices, on_device(): lax.all_to_all(five_fields(wrap_pad(widened, 1)), 'slab', split_axis=2, c...  37.3 us
    all_to_all x3, local copies, waits for them, and re-layouts, on_device(): lax.all_to_all(cot, 'slab', split_axis=3, concat_axis=2, tiled=True)  29 us
    another operation x1, local copies, waits for them, and re-layouts, adjoint_pass(): return (jnp.concatenate([p_state, q_state], axis=0), jnp.stack(cotangents))  25.2 us
    all_to_all x1, starting transfers between devices, on_device(): lax.all_to_all(cot, 'slab', split_axis=3, concat_axis=2, tiled=True)  21.8 us
  transfers between devices with their start and end apart: 12, of which 12 were waited for; matrix products, arithmetic and copies ran while one was open for 2% of the time, Pallas kernels for 0%

commit v1 on v0

v1 whole, which is shorter than its diff:
```python
import functools

import jax
import jax.numpy as jnp
from jax import lax
from jax.experimental import pallas as pl
from jax.experimental.pallas import tpu as pltpu
from jax.sharding import PartitionSpec as P

R = 6
SUB = 8
EDGE = 128
F32 = jnp.float32
VMEM_LIMIT = 32 * 1024 * 1024


def pack_kernel(weight_ref, p_ref, out_ref):
    planes, rows, _ = p_ref.shape
    for k in range(planes):
        w = weight_ref[k]
        for s in range(out_ref.shape[0]):
            before = (R * s - 1) % rows
            after = (R * (s + 1)) % rows
            out_ref[s, k] = w * jnp.concatenate(
                [
                    p_ref[k, R * s : R * (s + 1), :],
                    p_ref[k, after : after + 1, :],
                    p_ref[k, before : before + 1, :],
                ],
                axis=0,
            )


def row_up(x):
    return pltpu.roll(x, SUB - 1, 0)


def row_down(x):
    return pltpu.roll(x, 1, 0)


def col_prev(x):
    return pltpu.roll(x, 1, 1)[:, EDGE:-EDGE]


def col_next(x):
    return pltpu.roll(x, x.shape[1] - 1, 1)[:, EDGE:-EDGE]


def transposed_step(m0, m1, off, p, q, keep):
    new_p = [
        m0 * p[0] + off * p[2] + q[0],
        m0 * p[1] + off * p[3] + q[1],
        off * p[0] + m1 * p[2] + q[2],
        off * p[1] + m1 * p[3] + q[3],
    ]
    return (new_p, [keep * x for x in p])


def pack_state(out_ref, fields):
    for j in range(R):
        out_ref[0, j] = jnp.concatenate(
            [fields[j], fields[6][j : j + 1], fields[7][j : j + 1]], axis=0
        )


def unpack_state(in_ref):
    tiles = [in_ref[0, j] for j in range(R)]
    fields = [t[0:R] for t in tiles]
    fields.append(jnp.concatenate([t[6:7] for t in tiles], axis=0))
    fields.append(jnp.concatenate([t[7:8] for t in tiles], axis=0))
    return fields


def forward_kernel(groups, planes, mix_ref, *refs):
    sources = refs[: 3 * groups]
    obs_ref, noise_ref = refs[3 * groups : 3 * groups + 2]
    defl_ref, shear_ref, m_ref, a_ref, src_ref, b_ref = refs[3 * groups + 2 :]
    width = obs_ref.shape[-1]
    one = jnp.ones((SUB, width), F32)
    zero = jnp.zeros((SUB, width), F32)
    a = [one, zero, zero, one]
    a_before = a
    psi = jnp.zeros((SUB, width + 2 * EDGE), F32)
    psi_before = psi
    for group in range(groups):
        mid_ref, left_ref, right_ref = sources[3 * group : 3 * group + 3]
        own = group == groups - 1
        for k in range(planes):
            mix = mix_ref[group * planes + k]
            keep = 1.0 - mix
            mid = mid_ref[0, k]
            ext = jnp.concatenate([left_ref[0, k], mid, right_ref[0, k]], axis=1)
            up = row_up(ext)
            down = row_down(ext)
            across = up - down
            twice = 2.0 * mid
            m0 = mix - ((up + down)[:, EDGE:-EDGE] - twice)
            m1 = mix - (col_next(ext) + col_prev(ext) - twice)
            off = 0.25 * (col_prev(across) - col_next(across))
            if own:
                m_ref[0, 3 * k] = m0
                m_ref[0, 3 * k + 1] = m1
                m_ref[0, 3 * k + 2] = off
                for j in range(4):
                    a_ref[0, 4 * k + j] = a[j]
            new_a = [
                m0 * a[0] + off * a[2] + keep * a_before[0],
                m0 * a[1] + off * a[3] + keep * a_before[1],
                off * a[0] + m1 * a[2] + keep * a_before[2],
                off * a[1] + m1 * a[3] + keep * a_before[3],
            ]
            a_before, a = (a, new_a)
            psi, psi_before = (mix * psi + keep * psi_before - ext, psi)
            if own:
                slope_rows = 0.5 * (row_up(psi) - row_down(psi))[:, EDGE:-EDGE]
                slope_cols = 0.5 * (col_next(psi) - col_prev(psi))
                defl_ref[k, 0] = slope_rows[0:R]
                defl_ref[k, 1] = slope_cols[0:R]
                shear = [
                    1.0 - 0.5 * (a[0] + a[3])[0:R],
                    0.5 * (a[3] - a[0])[0:R],
                    -0.5 * (a[1] + a[2])[0:R],
                ]
                noise = -0.5 * noise_ref[k]
                r = []
                for j in range(3):
                    shear_ref[k, j] = shear[j]
                    r.append(noise * (shear[j] - obs_ref[k, j]))
                src_ref[0, 3 * k, 0:R] = r[0] + r[1]
                src_ref[0, 3 * k + 1, 0:R] = r[2]
                src_ref[0, 3 * k + 2, 0:R] = r[0] - r[1]
    none = jnp.zeros((R, width), F32)
    p = [none] * 4
    q = [none] * 4
    for k in reversed(range(planes)):
        keep = 1.0 - mix_ref[(groups - 1) * planes + k]
        s0, s1, s3 = (src_ref[0, 3 * k + j, 0:R] for j in range(3))
        p = [p[0] + s0, p[1] + s1, p[2] + s1, p[3] + s3]
        m0, m1, off = (m_ref[0, 3 * k + j, 0:R] for j in range(3))
        p, q = transposed_step(m0, m1, off, p, q, keep)
    pack_state(b_ref, p + q)


def carry_kernel(planes, mix_ref, in_ref, b_ref, m_ref, out_ref):
    fields = unpack_state(in_ref)
    p, q = (fields[0:4], fields[4:8])
    for k in reversed(range(planes)):
        m0, m1, off = (m_ref[0, 3 * k + j, 0:R] for j in range(3))
        p, q = transposed_step(m0, m1, off, p, q, 1.0 - mix_ref[k])
    pack_state(out_ref, p + q)
    out_ref[...] += b_ref[...]


def gradient_kernel(planes, mix_ref, weight_ref, in_ref, src_ref, m_ref, a_ref, out_ref, cot_ref):
    step = pl.program_id(0)
    blocks = pl.num_programs(0)
    width = in_ref.shape[-1]
    fields = unpack_state(in_ref)
    p, q = (fields[0:4], fields[4:8])
    blank = jnp.zeros((SUB - R, width), F32)
    for k in reversed(range(planes)):
        s0, s1, s3 = (src_ref[0, 3 * k + j, 0:R] for j in range(3))
        p = [p[0] + s0, p[1] + s1, p[2] + s1, p[3] + s3]
        a = [a_ref[0, 4 * k + j, 0:R] for j in range(4)]
        w = -weight_ref[k]
        cots = [
            w * (p[0] * a[0] + p[1] * a[1]),
            w * (p[2] * a[2] + p[3] * a[3]),
            (0.25 * w) * (p[0] * a[2] + p[1] * a[3] + p[2] * a[0] + p[3] * a[1]),
        ]
        for j in range(3):
            cot_ref[step, 3 * k + j] = jnp.concatenate([cots[j], blank], axis=0)
        m0, m1, off = (m_ref[0, 3 * k + j, 0:R] for j in range(3))
        p, q = transposed_step(m0, m1, off, p, q, 1.0 - mix_ref[k])

    @pl.when(step == blocks - 1)
    def _():
        def block(c, carry):
            before = lax.rem(c + blocks - 1, blocks)
            after = lax.rem(c + 1, blocks)

            def ext(field):
                return jnp.concatenate(
                    [
                        cot_ref[before, field, :, width - EDGE :],
                        cot_ref[c, field],
                        cot_ref[after, field, :, 0:EDGE],
                    ],
                    axis=1,
                )

            for k in range(planes):
                cot_rows = cot_ref[c, 3 * k]
                cot_cols = ext(3 * k + 1)
                cot_mixed = ext(3 * k + 2)
                across = row_up(cot_mixed) - row_down(cot_mixed)
                rows_part = row_up(cot_rows) + row_down(cot_rows) - 2.0 * cot_rows
                cols_part = (
                    col_next(cot_cols) + col_prev(cot_cols) - 2.0 * cot_cols[:, EDGE:-EDGE]
                )
                out_ref[c, k] = rows_part + cols_part + (col_next(across) - col_prev(across))
            return carry

        lax.fori_loop(0, blocks, block, 0)


def combine_kernel(in_ref, out_ref):
    slabs, planes, _, width = in_ref.shape
    blank = jnp.zeros((R - 2, width), F32)
    for k in range(planes):
        for s in range(slabs):
            halo = jnp.concatenate(
                [in_ref[(s - 1) % slabs, k, 6:7], blank, in_ref[(s + 1) % slabs, k, 7:8]], axis=0
            )
            out_ref[k, R * s : R * (s + 1), :] = in_ref[s, k, 0:R] + halo


def shape(*dims):
    return jax.ShapeDtypeStruct(dims, F32)


def params():
    return pltpu.CompilerParams(vmem_limit_bytes=VMEM_LIMIT)


def block_of(*dims):
    return pl.BlockSpec((1,) + dims, lambda c: (c,) + (0,) * len(dims))


SCALARS = pl.BlockSpec(memory_space=pltpu.SMEM)
WHOLE = pl.BlockSpec(memory_space=pltpu.VMEM)


def on_device(potential, mixing, lens_weight, observed, noise_weight):
    groups = lax.axis_size("plane")
    slabs = lax.axis_size("slab")
    planes, rows, width = potential.shape
    assert rows == R * slabs and width % EDGE == 0
    columns = width * slabs
    tiles = width // EDGE
    group = lax.axis_index("plane")

    packed = pl.pallas_call(
        pack_kernel,
        out_shape=shape(slabs, planes, SUB, width),
        in_specs=[SCALARS, WHOLE],
        out_specs=WHOLE,
        compiler_params=params(),
        name="pack",
    )(lens_weight, potential)
    mix_all = lax.all_gather(mixing, "plane", axis=0, tiled=True)
    mix_line = lax.dynamic_slice(
        jnp.concatenate([jnp.ones(((groups - 1) * planes,), F32), mix_all]),
        (group * planes,),
        (groups * planes,),
    )
    strips = [lax.all_to_all(packed, "slab", split_axis=0, concat_axis=0, tiled=True)]
    up_route = [(i, i + 1) for i in range(groups - 1)]
    down_route = [(i + 1, i) for i in range(groups - 1)]
    for hop in range(groups - 1):
        strips.insert(0, lax.ppermute(strips[0], "plane", up_route))

    mid = block_of(planes, SUB, width)
    left = pl.BlockSpec(
        (1, planes, SUB, EDGE), lambda c: (lax.rem(c + slabs - 1, slabs), 0, 0, tiles - 1)
    )
    right = pl.BlockSpec((1, planes, SUB, EDGE), lambda c: (lax.rem(c + 1, slabs), 0, 0, 0))
    three_rows = pl.BlockSpec((planes, 3, R, width), lambda c: (0, 0, 0, c))
    two_rows = pl.BlockSpec((planes, 2, R, width), lambda c: (0, 0, 0, c))
    one_row = pl.BlockSpec((planes, R, width), lambda c: (0, 0, c))
    state = block_of(R, SUB, width)
    triple = block_of(3 * planes, SUB, width)
    quad = block_of(4 * planes, SUB, width)
    deflection, shear, matrices, states, sources, b = pl.pallas_call(
        functools.partial(forward_kernel, groups, planes),
        grid=(slabs,),
        out_shape=(
            shape(planes, 2, R, columns),
            shape(planes, 3, R, columns),
            shape(slabs, 3 * planes, SUB, width),
            shape(slabs, 4 * planes, SUB, width),
            shape(slabs, 3 * planes, SUB, width),
            shape(slabs, R, SUB, width),
        ),
        in_specs=[SCALARS] + [mid, left, right] * groups + [three_rows, one_row],
        out_specs=(two_rows, three_rows, triple, quad, triple, state),
        compiler_params=params(),
        name="forward",
    )(mix_line, *[x for strip in strips for x in (strip,) * 3], observed, noise_weight)

    incoming = lax.ppermute(b, "plane", down_route)
    for hop in range(groups - 2):
        outgoing = pl.pallas_call(
            functools.partial(carry_kernel, planes),
            grid=(slabs,),
            out_shape=shape(slabs, R, SUB, width),
            in_specs=[SCALARS, state, state, triple],
            out_specs=state,
            compiler_params=params(),
            name="carry",
        )(mixing, incoming, b, matrices)
        incoming = lax.ppermute(outgoing, "plane", down_route)

    partial = pl.pallas_call(
        functools.partial(gradient_kernel, planes),
        grid=(slabs,),
        out_shape=shape(slabs, planes, SUB, width),
        in_specs=[SCALARS, SCALARS, state, triple, triple, quad],
        out_specs=pl.BlockSpec((slabs, planes, SUB, width), lambda c: (0, 0, 0, 0)),
        scratch_shapes=[pltpu.VMEM((slabs, 3 * planes, SUB, width), F32)],
        compiler_params=params(),
        name="gradient",
    )(mixing, lens_weight, incoming, sources, matrices, states)
    returned = lax.all_to_all(partial, "slab", split_axis=0, concat_axis=0, tiled=True)
    potential_grad = pl.pallas_call(
        combine_kernel,
        out_shape=shape(planes, rows, width),
        in_specs=[WHOLE],
        out_specs=WHOLE,
        compiler_params=params(),
        name="combine",
    )(returned)
    return (deflection, shear, potential_grad)


def solution(mesh):
    placed = (
        P("plane", None, "slab"),
        P("plane"),
        P("plane"),
        P("plane", None, "slab", None),
        P("plane", "slab", None),
    )
    return jax.shard_map(
        on_device,
        mesh=mesh,
        in_specs=placed,
        out_specs=(
            P("plane", None, "slab", None),
            P("plane", None, "slab", None),
            P("plane", None, "slab"),
        ),
        check_vma=False,
    )
```

time: 692 us -> 158 us (0.23); the launches traced: 684 us -> 157 us
  other arithmetic: 238 us -> 0 us
  local copies, waits for them, and re-layouts: 198 us -> 5.93 us
  waiting for transfers between devices: 188 us -> 81.1 us
  blocking collectives: 0 us -> 32.8 us
  starting transfers between devices: 50.1 us -> 19.9 us
  Pallas kernels: 0 us -> 16.3 us
  between operations: 8.87 us -> 1.45 us
    add x49 -> x0, other arithmetic: 102 us -> none  [the longest x19 56.7 us: plane_adjoint(): diag_first * p_full[0] + off_diag * p_full[2]]
    unnamed x192 -> x22, local copies, waits for them, and re-layouts: 106 us -> 5.85 us
    ppermute x10 -> x6, waiting for transfers between devices: 138 us -> 71.7 us  [the longest x2 29.2 us: on_device(): incoming = lax.ppermute(outgoing, 'plane', down_route)]
    while x18 -> x0, other arithmetic: 61.2 us -> none
    all_to_all x2 -> x1, waiting for transfers between devices: 50.2 us -> 9.37 us  [on_device(): lax.all_to_all(partial, 'slab', split_axis=0, concat_axis=0, tiled=True)]
    all_to_all x5 -> x0, local copies, waits for them, and re-layouts: 35.6 us -> none  [the longest x3 29 us: on_device(): lax.all_to_all(cot, 'slab', split_axis=3, concat_axis=2, tiled=True)]
    another operation x1 -> x0, local copies, waits for them, and re-layouts: 25.2 us -> none  [adjoint_pass(): return (jnp.concatenate([p_state, q_state], axis=0), jnp.stack(cotangents))]
    all_to_all x2 -> x1, starting transfers between devices: 26.5 us -> 3.67 us  [on_device(): lax.all_to_all(partial, 'slab', split_axis=0, concat_axis=0, tiled=True)]
  transfers between devices with their start and end apart: 12 -> 7, of which waited for: 12 -> 6; matrix products, arithmetic and copies ran while one was open for 2% -> 2% of each run, Pallas kernels for 0% -> 0%
where the time goes in v1:
time: 158 us; the launch traced here: 157 us
  waiting for transfers between devices  81.1 us (51%)
  blocking collectives  32.8 us (21%)
  starting transfers between devices  19.9 us (13%)
  Pallas kernels  16.3 us (10%)
  local copies, waits for them, and re-layouts  5.93 us (4%)
    ppermute x2, waiting for transfers between devices, on_device(): incoming = lax.ppermute(outgoing, 'plane', down_route)  29.2 us
    ppermute x3, waiting for transfers between devices, on_device(): strips.insert(0, lax.ppermute(strips[0], 'plane', up_route))  26.6 us
    unnamed x1, blocking collectives  16.7 us
    all_to_all x1, blocking collectives, on_device(): lax.all_to_all(packed, 'slab', split_axis=0, concat_axis=0, tiled=True)  16.1 us
    ppermute x1, waiting for transfers between devices, on_device(): incoming = lax.ppermute(b, 'plane', down_route)  16 us
    ppermute x3, starting transfers between devices, on_device(): strips.insert(0, lax.ppermute(strips[0], 'plane', up_route))  12.3 us
    all_to_all x1, waiting for transfers between devices, on_device(): lax.all_to_all(partial, 'slab', split_axis=0, concat_axis=0, tiled=True)  9.37 us
    pallas_call x1, Pallas kernels, on_device(): pl.pallas_call(functools.partial(forward_kernel, groups, planes), grid=(s...  7.83 us
  transfers between devices with their start and end apart: 7, of which 6 were waited for; matrix products, arithmetic and copies ran while one was open for 2% of the time, Pallas kernels for 0%

profile of v1, /device:TPU:0, one launch (start us, length us, event | category | flops | bytes accessed | tf_op | source)
XLA Modules:
  0.0 157.5 jit_solution(15801449528893109696)
XLA Ops:
  0.6 0.0 copy-start.8
  0.6 0.0 copy-start.3
  0.7 0.0 copy-start.4
  0.7 1.1 copy-done.4
  1.8 0.0 copy-start.6
  1.8 0.7 copy-done.6
  2.4 0.0 copy-start.5
  2.4 0.7 pack.1
  3.1 16.1 %all_to_all.10.refs_9_.refs_10_.refs_11_ = f32[8,5,8,512]{3,2,1,0:T(8,128)S(1)} all-to-all(f32[8,5,8,512]{3,2,1,0:T(8,128)S(1)} %pack.1), channel_id=1, replica_groups=mesh['plane'=4,'slab'=8] {'slab'}, dimensions={0} | all-to-all | bytes 1310720 | tf_op jit(solution)/shard_map/all_to_all | solution.py:258
  19.2 3.5 %collective-permute-start = (f32[8,5,8,512]{3,2,1,0:T(8,128)S(1)}, f32[8,5,8,512]{3,2,1,0:T(8,128)S(1)}, u32[]{:S(2)}, u32[]{:S(2)}) collective-permute-start(f32[8,5,8,512]{3,2,1,0:T(8,128)S(1)} %all_to_all.10.refs_9_.refs_10_.refs_11_), channel_id=1, source_target_pairs={{0,8},{8,16},{16,24},{1,9},{9,17},{17,25},{2,10},{10,18},{18,26},{... | collective-permute-start | bytes 1966088 | tf_op jit(solution)/shard_map/ppermute | solution.py:262
  22.7 13.7 %collective-permute-done.refs_6_.refs_7_.refs_8_ = f32[8,5,8,512]{3,2,1,0:T(8,128)S(1)} collective-permute-done((f32[8,5,8,512]{3,2,1,0:T(8,128)S(1)}, f32[8,5,8,512]{3,2,1,0:T(8,128)S(1)}, u32[]{:S(2)}, u32[]{:S(2)}) %collective-permute-start) | collective-permute-done | bytes 655392 | tf_op jit(solution)/shard_map/ppermute | solution.py:262
  36.5 4.4 %collective-permute-start.1 = (f32[8,5,8,512]{3,2,1,0:T(8,128)S(1)}, f32[8,5,8,512]{3,2,1,0:T(8,128)S(1)}, u32[]{:S(2)}, u32[]{:S(2)}) collective-permute-start(f32[8,5,8,512]{3,2,1,0:T(8,128)S(1)} %collective-permute-done.refs_6_.refs_7_.refs_8_), channel_id=1, source_target_pairs={{0,8},{8,16},{16,24},{1,9},{9,17},{17,25},{2,10},{10,18},{18,26},{... | collective-permute-start | bytes 1966088 | tf_op jit(solution)/shard_map/ppermute | solution.py:262
  40.9 12.8 %collective-permute-done.1.refs_3_.refs_4_.refs_5_ = f32[8,5,8,512]{3,2,1,0:T(8,128)S(1)} collective-permute-done((f32[8,5,8,512]{3,2,1,0:T(8,128)S(1)}, f32[8,5,8,512]{3,2,1,0:T(8,128)S(1)}, u32[]{:S(2)}, u32[]{:S(2)}) %collective-permute-start.1) | collective-permute-done | bytes 655392 | tf_op jit(solution)/shard_map/ppermute | solution.py:262
  53.7 4.4 %collective-permute-start.2 = (f32[8,5,8,512]{3,2,1,0:T(8,128)S(1)}, f32[8,5,8,512]{3,2,1,0:T(8,128)S(1)}, u32[]{:S(2)}, u32[]{:S(2)}) collective-permute-start(f32[8,5,8,512]{3,2,1,0:T(8,128)S(1)} %collective-permute-done.1.refs_3_.refs_4_.refs_5_), channel_id=1, source_target_pairs={{0,8},{8,16},{16,24},{1,9},{9,17},{17,25},{2,10},{10,18},{18,26},{... | collective-permute-start | bytes 1966088 | tf_op jit(solution)/shard_map/ppermute | solution.py:262
  58.2 0.0 copy-done.8
  58.2 0.6 dynamic-slice
  59.4 0.0 copy-done.5
  59.4 0.2 dynamic-update-slice
  59.7 16.7 %all-reduce.1 = f32[20]{0:T(128)S(1)} all-reduce(f32[20]{0:T(128)S(1)} %dynamic-update-slice), channel_id=1, replica_groups=mesh['plane'=4,'slab'=8] {'plane'}, use_global_device_ids=true, to_apply=%add.1 | all-reduce | flops 20 | bytes 160
  76.4 0.1 pad_dynamic-slice_fusion.mix_ref
  76.5 0.0 collective-permute-done.2.refs_0_.refs_1_.refs_2_
  76.5 0.0 copy-done.3
  76.5 0.0 copy-start
  76.5 1.5 copy-done
  78.0 7.8 %forward.1 = (f32[5,2,6,4096]{3,2,1,0:T(8,128)S(1)}, f32[5,3,6,4096]{3,2,1,0:T(8,128)}, f32[8,15,8,512]{3,2,1,0:T(8,128)S(1)}, f32[8,20,8,512]{3,2,1,0:T(8,128)S...) custom-call(f32[20]{0:T(128)S(1)} %pad_dynamic-slice_fusion.mix_ref, ...), custom_call_target="tpu_custom_call" | custom-call | tf_op jit(solution)/shard_map/forward/pallas_call | solution.py:275
  85.9 0.0 copy-start.1
  85.9 1.3 collective-permute-start.3
  87.1 16.0 %collective-permute-done.3.in_ref = f32[8,6,8,512]{3,2,1,0:T(8,128)S(1)} collective-permute-done((f32[8,6,8,512]{3,2,1,0:T(8,128)S(1)}, f32[8,6,8,512]{3,2,1,0:T(8,128)S(1)}, u32[]{:S(2)}, u32[]{:S(2)}) %collective-permute-start.3) | collective-permute-done | bytes 786464 | tf_op jit(solution)/shard_map/ppermute | solution.py:292
  103.1 1.4 carry.2
  104.5 0.0 copy-done.1
  104.5 0.0 copy-start.7
  104.6 1.3 collective-permute-start.4
  105.9 15.1 %collective-permute-done.4.in_ref = f32[8,6,8,512]{3,2,1,0:T(8,128)S(1)} collective-permute-done((f32[8,6,8,512]{3,2,1,0:T(8,128)S(1)}, f32[8,6,8,512]{3,2,1,0:T(8,128)S(1)}, u32[]{:S(2)}, u32[]{:S(2)}) %collective-permute-start.4) | collective-permute-done | bytes 786464 | tf_op jit(solution)/shard_map/ppermute | solution.py:303
  120.9 1.4 carry.3
  122.3 1.3 collective-permute-start.5
  123.6 14.1 %collective-permute-done.5.in_ref = f32[8,6,8,512]{3,2,1,0:T(8,128)S(1)} collective-permute-done((f32[8,6,8,512]{3,2,1,0:T(8,128)S(1)}, f32[8,6,8,512]{3,2,1,0:T(8,128)S(1)}, u32[]{:S(2)}, u32[]{:S(2)}) %collective-permute-start.5) | collective-permute-done | bytes 786464 | tf_op jit(solution)/shard_map/ppermute | solution.py:303
  137.8 0.0 copy-done.7
  137.8 4.0 %gradient.1 = f32[8,5,8,512]{3,2,1,0:T(8,128)} custom-call(f32[5]{0:T(128)S(1)} %copy-done.5, f32[5]{0:T(128)S(1)} %copy-done.7, f32[8,6,8,512]{3,2,1,0:T(8,128)S(1)} %collective-permute-done.5.in_ref, f32[8,15,8,512]{3,2,1,0:T(8,128)S(1)} %get-tuple-element.13.src_ref, f32[8,15,8,512]{3,2,1,0:T(8,128)S(1)} %get-tuple-element.12.m_ref, ...), custom_call_target="tpu_custom_call" | custom-call | tf_op jit(solution)/shard_map/gradient/pallas_call | solution.py:305
  141.8 0.0 copy-start.2
  141.8 3.7 %all-to-all-start.1 = ((f32[8,5,8,512]{3,2,1,0:T(8,128)}), f32[8,5,8,512]{3,2,1,0:T(8,128)S(1)}, u32[]{:S(2)}, u32[]{:S(2)}) async-start(f32[8,5,8,512]{3,2,1,0:T(8,128)} %gradient.1), calls=%async_computation.1 | async-start | bytes 1310720 | tf_op jit(solution)/shard_map/all_to_all | solution.py:315
  145.4 0.0 copy-done.2
  145.5 1.7 %copy.8 = f32[5,2,6,4096]{3,1,2,0:T(2,128)} copy(f32[5,2,6,4096]{3,2,1,0:T(8,128)S(1)} %copy-done.2) | data formatting | bytes 1966080
  147.2 9.4 %all-to-all-done.1.in_ref = f32[8,5,8,512]{3,2,1,0:T(8,128)S(1)} async-done(((f32[8,5,8,512]{3,2,1,0:T(8,128)}), f32[8,5,8,512]{3,2,1,0:T(8,128)S(1)}, u32[]{:S(2)}, u32[]{:S(2)}) %all-to-all-start.1) | async-done | bytes 655392 | tf_op jit(solution)/shard_map/all_to_all | solution.py:315
  156.5 0.9 combine.1
  (1 shorter events, 0.0 us)
Async XLA Ops:
  0.6 57.5 %copy-start.8 = (u32[32]{0:T(128)S(1)}, u32[32]{0:T(128)}, u32[]{:S(2)}) copy-start(u32[32]{0:T(128)} %constant.22) | copy-start | bytes 388
  0.6 75.8 %copy-start.3 = (f32[5,6,4096]{2,1,0:T(8,128)S(1)}, f32[5,6,4096]{2,1,0:T(8,128)}, u32[]{:S(2)}) copy-start(f32[5,6,4096]{2,1,0:T(8,128)} %refs_13_.1) | copy-start | bytes 1474564
  0.7 1.1 copy-start.4
  1.8 0.7 copy-start.6
  2.4 57.0 %copy-start.5 = (f32[5]{0:T(128)S(1)}, f32[5]{0:T(128)}, u32[]{:S(2)}) copy-start(f32[5]{0:T(128)} %mix_ref.5) | copy-start | bytes 64
  19.2 17.3 %collective-permute-start = (f32[8,5,8,512]{3,2,1,0:T(8,128)S(1)}, f32[8,5,8,512]{3,2,1,0:T(8,128)S(1)}, u32[]{:S(2)}, u32[]{:S(2)}) collective-permute-start(f32[8,5,8,512]{3,2,1,0:T(8,128)S(1)} %all_to_all.10.refs_9_.refs_10_.refs_11_), channel_id=1, source_target_pairs={{0,8},{8,16},{16,24},{1,9},{9,17},{17,25},{2,10},{10,18},{18,26},{... | collective-permute-start | bytes 1966088 | tf_op jit(solution)/shard_map/ppermute | solution.py:262
  36.5 17.3 %collective-permute-start.1 = (f32[8,5,8,512]{3,2,1,0:T(8,128)S(1)}, f32[8,5,8,512]{3,2,1,0:T(8,128)S(1)}, u32[]{:S(2)}, u32[]{:S(2)}) collective-permute-start(f32[8,5,8,512]{3,2,1,0:T(8,128)S(1)} %collective-permute-done.refs_6_.refs_7_.refs_8_), channel_id=1, source_target_pairs={{0,8},{8,16},{16,24},{1,9},{9,17},{17,25},{2,10},{10,18},{18,26},{... | collective-permute-start | bytes 1966088 | tf_op jit(solution)/shard_map/ppermute | solution.py:262
  53.7 22.7 %collective-permute-start.2 = (f32[8,5,8,512]{3,2,1,0:T(8,128)S(1)}, f32[8,5,8,512]{3,2,1,0:T(8,128)S(1)}, u32[]{:S(2)}, u32[]{:S(2)}) collective-permute-start(f32[8,5,8,512]{3,2,1,0:T(8,128)S(1)} %collective-permute-done.1.refs_3_.refs_4_.refs_5_), channel_id=1, source_target_pairs={{0,8},{8,16},{16,24},{1,9},{9,17},{17,25},{2,10},{10,18},{18,26},{... | collective-permute-start | bytes 1966088 | tf_op jit(solution)/shard_map/ppermute | solution.py:262
  76.5 1.5 copy-start
  85.9 18.7 %copy-start.1 = (f32[5,2,6,4096]{3,2,1,0:T(8,128)}, f32[5,2,6,4096]{3,2,1,0:T(8,128)S(1)}, u32[]{:S(2)}) copy-start(f32[5,2,6,4096]{3,2,1,0:T(8,128)S(1)} %get-tuple-element.15) | copy-start | bytes 2949124
  85.9 17.3 %collective-permute-start.3 = (f32[8,6,8,512]{3,2,1,0:T(8,128)S(1)}, f32[8,6,8,512]{3,2,1,0:T(8,128)S(1)}, u32[]{:S(2)}, u32[]{:S(2)}) collective-permute-start(f32[8,6,8,512]{3,2,1,0:T(8,128)S(1)} %get-tuple-element.11.b_ref), channel_id=1, source_target_pairs={{8,0},{16,8},{24,16},{9,1},{17,9},{25,17},{10,2},{18,10},{26,18},{... | collective-permute-start | bytes 2359304 | tf_op jit(solution)/shard_map/ppermute | solution.py:292
  104.5 33.2 %copy-start.7 = (f32[5]{0:T(128)S(1)}, f32[5]{0:T(128)}, u32[]{:S(2)}) copy-start(f32[5]{0:T(128)} %weight_ref.3) | copy-start | bytes 64
  104.6 16.4 %collective-permute-start.4 = (f32[8,6,8,512]{3,2,1,0:T(8,128)S(1)}, f32[8,6,8,512]{3,2,1,0:T(8,128)S(1)}, u32[]{:S(2)}, u32[]{:S(2)}) collective-permute-start(f32[8,6,8,512]{3,2,1,0:T(8,128)S(1)} %carry.2), channel_id=1, source_target_pairs={{8,0},{16,8},{24,16},{9,1},{17,9},{25,17},{10,2},{18,10},{26,18},{... | collective-permute-start | bytes 2359304 | tf_op jit(solution)/shard_map/ppermute | solution.py:303
  122.3 15.4 %collective-permute-start.5 = (f32[8,6,8,512]{3,2,1,0:T(8,128)S(1)}, f32[8,6,8,512]{3,2,1,0:T(8,128)S(1)}, u32[]{:S(2)}, u32[]{:S(2)}) collective-permute-start(f32[8,6,8,512]{3,2,1,0:T(8,128)S(1)} %carry.3), channel_id=1, source_target_pairs={{8,0},{16,8},{24,16},{9,1},{17,9},{25,17},{10,2},{18,10},{26,18},{... | collective-permute-start | bytes 2359304 | tf_op jit(solution)/shard_map/ppermute | solution.py:303
  141.8 3.7 %copy-start.2 = (f32[5,2,6,4096]{3,2,1,0:T(8,128)S(1)}, f32[5,2,6,4096]{3,2,1,0:T(8,128)}, u32[]{:S(2)}) copy-start(f32[5,2,6,4096]{3,2,1,0:T(8,128)} %copy-done.1) | copy-start | bytes 2949124
  141.8 14.8 %all-to-all-start.1 = ((f32[8,5,8,512]{3,2,1,0:T(8,128)}), f32[8,5,8,512]{3,2,1,0:T(8,128)S(1)}, u32[]{:S(2)}, u32[]{:S(2)}) async-start(f32[8,5,8,512]{3,2,1,0:T(8,128)} %gradient.1), calls=%async_computation.1 | async-start | bytes 1310720 | tf_op jit(solution)/shard_map/all_to_all | solution.py:315

commit v2 on v1

v2 whole, which is shorter than its diff:
```python
import functools

import jax
import jax.numpy as jnp
from jax import lax
from jax.experimental import pallas as pl
from jax.experimental.pallas import tpu as pltpu
from jax.sharding import PartitionSpec as P

R = 6
SUB = 8
EDGE = 128
F32 = jnp.float32
VMEM_LIMIT = 32 * 1024 * 1024
CHUNKS = 4
SPAN = 4
MIX_LANE = 64


def pack_kernel(weight_ref, p_ref, out_ref):
    planes, rows, width = p_ref.shape
    for k in range(planes):
        w = weight_ref[k]
        for s in range(out_ref.shape[0]):
            before = (R * s - 1) % rows
            after = (R * (s + 1)) % rows
            strip = w * jnp.concatenate(
                [
                    p_ref[k, R * s : R * (s + 1), :],
                    p_ref[k, after : after + 1, :],
                    p_ref[k, before : before + 1, :],
                ],
                axis=0,
            )
            for t in range(width // EDGE):
                out_ref[s, t, k] = strip[:, EDGE * t : EDGE * (t + 1)]


def split_kernel(mix_ref, in_ref, *outs):
    tiles, planes = in_ref.shape[0:2]
    length = tiles // len(outs)
    lane = lax.broadcasted_iota(jnp.int32, (SUB, EDGE), 1)
    for c, out_ref in enumerate(outs):
        out_ref[0:length] = in_ref[length * c : length * (c + 1)]
    for k in range(planes):
        edge = jnp.where(lane == MIX_LANE, mix_ref[k] - 1.0, 0.0)
        for c in range(len(outs)):
            after = in_ref[(length * (c + 1)) % tiles, k]
            before = in_ref[(length * c - 1) % tiles, k]
            edge = jnp.where(lane == 2 * c, pltpu.roll(after, 2 * c, 1), edge)
            edge = jnp.where(lane == (2 * c - 1) % EDGE, pltpu.roll(before, 2 * c, 1), edge)
        outs[0][length, k] = edge


def row_up(x):
    return pltpu.roll(x, SUB - 1, 0)


def row_down(x):
    return pltpu.roll(x, 1, 0)


def col_prev(x):
    return pltpu.roll(x, 1, 1)[:, EDGE:-EDGE]


def col_next(x):
    return pltpu.roll(x, x.shape[1] - 1, 1)[:, EDGE:-EDGE]


def transposed_step(m0, m1, off, p, q, keep):
    new_p = [
        m0 * p[0] + off * p[2] + q[0],
        m0 * p[1] + off * p[3] + q[1],
        off * p[0] + m1 * p[2] + q[2],
        off * p[1] + m1 * p[3] + q[3],
    ]
    return (new_p, [keep * x for x in p])


def pack_state(out_ref, fields):
    for j in range(R):
        out_ref[0, j] = jnp.concatenate(
            [fields[j], fields[6][j : j + 1], fields[7][j : j + 1]], axis=0
        )


def unpack_state(in_ref):
    tiles = [in_ref[0, j] for j in range(R)]
    fields = [t[0:R] for t in tiles]
    fields.append(jnp.concatenate([t[6:7] for t in tiles], axis=0))
    fields.append(jnp.concatenate([t[7:8] for t in tiles], axis=0))
    return fields


def forward_kernel(groups, planes, chunk, length, *refs):
    strips = refs[: 2 * groups]
    obs_ref, noise_ref = refs[2 * groups : 2 * groups + 2]
    defl_ref, shear_ref, m_ref, a_ref, src_ref, b_ref = refs[-6:]
    step = pl.program_id(0)
    width = obs_ref.shape[-1]
    span = width // EDGE
    first = step * span
    at_start = first == 0
    at_end = first + span == length
    one = jnp.ones((SUB, width), F32)
    zero = jnp.zeros((SUB, width), F32)
    a = [one, zero, zero, one]
    a_before = a
    psi = jnp.zeros((SUB, width + 2 * EDGE), F32)
    psi_before = psi
    keeps = []
    for group in range(groups):
        strip_ref, edge_ref = strips[2 * group : 2 * group + 2]
        own = group == groups - 1
        for k in range(planes):
            edge = edge_ref[edge_ref.shape[0] - 1, k]
            excess = edge[:, MIX_LANE : MIX_LANE + 1]
            mix = 1.0 + excess
            beside = pltpu.roll(edge, (EDGE - 2 * chunk) % EDGE, 1)
            left = jnp.where(at_start, beside, strip_ref[jnp.maximum(first - 1, 0), k])
            right = jnp.where(at_end, beside, strip_ref[jnp.minimum(first + span, length - 1), k])
            tiles = [strip_ref[first + t, k] for t in range(span)]
            mid = jnp.concatenate(tiles, axis=1)
            ext = jnp.concatenate([left] + tiles + [right], axis=1)
            up = row_up(ext)
            down = row_down(ext)
            across = up - down
            twice = 2.0 * mid
            m0 = mix - ((up + down)[:, EDGE:-EDGE] - twice)
            m1 = mix - (col_next(ext) + col_prev(ext) - twice)
            off = 0.25 * (col_prev(across) - col_next(across))
            if own:
                m_ref[0, 3 * k] = m0
                m_ref[0, 3 * k + 1] = m1
                m_ref[0, 3 * k + 2] = off
                keeps.append(-excess[0:R])
                for j in range(4):
                    a_ref[0, 4 * k + j] = a[j]
            new_a = [
                m0 * a[0] + off * a[2] - excess * a_before[0],
                m0 * a[1] + off * a[3] - excess * a_before[1],
                off * a[0] + m1 * a[2] - excess * a_before[2],
                off * a[1] + m1 * a[3] - excess * a_before[3],
            ]
            a_before, a = (a, new_a)
            psi, psi_before = (mix * psi - excess * psi_before - ext, psi)
            if own:
                slope_rows = 0.5 * (row_up(psi) - row_down(psi))[:, EDGE:-EDGE]
                slope_cols = 0.5 * (col_next(psi) - col_prev(psi))
                defl_ref[k, 0] = slope_rows[0:R]
                defl_ref[k, 1] = slope_cols[0:R]
                shear = [
                    1.0 - 0.5 * (a[0] + a[3])[0:R],
                    0.5 * (a[3] - a[0])[0:R],
                    -0.5 * (a[1] + a[2])[0:R],
                ]
                noise = -0.5 * noise_ref[k]
                r = []
                for j in range(3):
                    shear_ref[k, j] = shear[j]
                    r.append(noise * (shear[j] - obs_ref[k, j]))
                src_ref[0, 3 * k, 0:R] = r[0] + r[1]
                src_ref[0, 3 * k + 1, 0:R] = r[2]
                src_ref[0, 3 * k + 2, 0:R] = r[0] - r[1]
    none = jnp.zeros((R, width), F32)
    p = [none] * 4
    q = [none] * 4
    for k in reversed(range(planes)):
        s0, s1, s3 = (src_ref[0, 3 * k + j, 0:R] for j in range(3))
        p = [p[0] + s0, p[1] + s1, p[2] + s1, p[3] + s3]
        m0, m1, off = (m_ref[0, 3 * k + j, 0:R] for j in range(3))
        p, q = transposed_step(m0, m1, off, p, q, keeps[k])
    pack_state(b_ref, p + q)


def carry_kernel(planes, mix_ref, in_ref, b_ref, m_ref, out_ref):
    fields = unpack_state(in_ref)
    p, q = (fields[0:4], fields[4:8])
    for k in reversed(range(planes)):
        m0, m1, off = (m_ref[0, 3 * k + j, 0:R] for j in range(3))
        p, q = transposed_step(m0, m1, off, p, q, 1.0 - mix_ref[k])
    pack_state(out_ref, p + q)
    out_ref[...] += b_ref[...]


def cotangent_kernel(planes, mix_ref, weight_ref, in_ref, src_ref, m_ref, a_ref, cot_ref):
    width = in_ref.shape[-1]
    fields = unpack_state(in_ref)
    p, q = (fields[0:4], fields[4:8])
    blank = jnp.zeros((SUB - R, width), F32)
    for k in reversed(range(planes)):
        s0, s1, s3 = (src_ref[0, 3 * k + j, 0:R] for j in range(3))
        p = [p[0] + s0, p[1] + s1, p[2] + s1, p[3] + s3]
        a = [a_ref[0, 4 * k + j, 0:R] for j in range(4)]
        w = -weight_ref[k]
        cots = [
            w * (p[0] * a[0] + p[1] * a[1]),
            w * (p[2] * a[2] + p[3] * a[3]),
            (0.25 * w) * (p[0] * a[2] + p[1] * a[3] + p[2] * a[0] + p[3] * a[1]),
        ]
        for j in range(3):
            cot_ref[0, 3 * k + j] = jnp.concatenate([cots[j], blank], axis=0)
        m0, m1, off = (m_ref[0, 3 * k + j, 0:R] for j in range(3))
        p, q = transposed_step(m0, m1, off, p, q, 1.0 - mix_ref[k])


def stencil_kernel(planes, *refs):
    cots, out_ref = (refs[:-1], refs[-1])
    out = out_ref.shape[-1]
    steps, width = (cots[0].shape[0], cots[0].shape[-1])
    blocks = len(cots) * steps

    def cot(block, field):
        return cots[block // steps].at[block % steps, field]

    for c in range(blocks):
        before = (c - 1) % blocks
        after = (c + 1) % blocks

        def ext(field):
            return jnp.concatenate(
                [
                    cot(before, field)[:, width - EDGE :],
                    cot(c, field)[...],
                    cot(after, field)[:, 0:EDGE],
                ],
                axis=1,
            )

        for k in range(planes):
            cot_rows = cot(c, 3 * k)[...]
            cot_cols = ext(3 * k + 1)
            cot_mixed = ext(3 * k + 2)
            across = row_up(cot_mixed) - row_down(cot_mixed)
            rows_part = row_up(cot_rows) + row_down(cot_rows) - 2.0 * cot_rows
            cols_part = col_next(cot_cols) + col_prev(cot_cols) - 2.0 * cot_cols[:, EDGE:-EDGE]
            grad = rows_part + cols_part + (col_next(across) - col_prev(across))
            for part in range(max(1, width // out)):
                place = c * width + part * out
                size = min(out, width)
                start = place % out
                out_ref[place // out, k, :, start : start + size] = grad[
                    :, part * out : part * out + size
                ]


def combine_kernel(in_ref, out_ref):
    slabs, planes, _, width = in_ref.shape
    blank = jnp.zeros((R - 2, width), F32)
    for k in range(planes):
        for s in range(slabs):
            halo = jnp.concatenate(
                [in_ref[(s - 1) % slabs, k, 6:7], blank, in_ref[(s + 1) % slabs, k, 7:8]], axis=0
            )
            out_ref[k, R * s : R * (s + 1), :] = in_ref[s, k, 0:R] + halo


def shape(*dims):
    return jax.ShapeDtypeStruct(dims, F32)


def params():
    return pltpu.CompilerParams(vmem_limit_bytes=VMEM_LIMIT)


def block_of(*dims):
    return pl.BlockSpec((1,) + dims, lambda c: (c,) + (0,) * len(dims))


SCALARS = pl.BlockSpec(memory_space=pltpu.SMEM)
WHOLE = pl.BlockSpec(memory_space=pltpu.VMEM)


def on_device(potential, mixing, lens_weight, observed, noise_weight):
    groups = lax.axis_size("plane")
    slabs = lax.axis_size("slab")
    planes, rows, width = potential.shape
    assert rows == R * slabs and width % EDGE == 0
    columns = width * slabs
    tiles = width // EDGE
    length = tiles * slabs // CHUNKS
    span = SPAN * EDGE
    steps = length // SPAN
    up_route = [(i, i + 1) for i in range(groups - 1)]
    down_route = [(i + 1, i) for i in range(groups - 1)]

    packed = pl.pallas_call(
        pack_kernel,
        out_shape=shape(slabs, tiles, planes, SUB, EDGE),
        in_specs=[SCALARS, WHOLE],
        out_specs=WHOLE,
        compiler_params=params(),
        name="pack",
    )(lens_weight, potential)
    own = lax.all_to_all(packed, "slab", split_axis=0, concat_axis=0, tiled=True)
    own = own.reshape(slabs * tiles, planes, SUB, EDGE)
    pieces = pl.pallas_call(
        split_kernel,
        out_shape=tuple(
            shape(length + (c == 0), planes, SUB, EDGE) for c in range(CHUNKS)
        ),
        in_specs=[SCALARS, WHOLE],
        out_specs=(WHOLE,) * CHUNKS,
        compiler_params=params(),
        name="split",
    )(mixing, own)
    strips = [[piece] for piece in pieces]
    for turn in range(CHUNKS + groups - 2):
        for c in range(CHUNKS):
            if 0 <= turn - c < groups - 1:
                strips[c].insert(0, lax.ppermute(strips[c][0], "plane", up_route))

    state = block_of(R, SUB, span)
    triple = block_of(3 * planes, SUB, span)
    quad = block_of(4 * planes, SUB, span)
    kept = pl.BlockSpec(memory_space=pl.ANY)

    def columns_of(c, *dims):
        return pl.BlockSpec(dims + (span,), lambda i: (0,) * len(dims) + (c * steps + i,))

    deflection, shear = (None, None)
    work = []
    for c in range(CHUNKS):
        operands = [x for pair in zip(strips[c], strips[0]) for x in pair]
        operands += [observed, noise_weight]
        specs = [WHOLE] * (2 * groups) + [columns_of(c, planes, 3, R), columns_of(c, planes, R)]
        aliases = {}
        if c > 0:
            aliases = {len(operands): 0, len(operands) + 1: 1}
            operands += [deflection, shear]
            specs += [kept, kept]
        deflection, shear, *held = pl.pallas_call(
            functools.partial(forward_kernel, groups, planes, c, length),
            grid=(steps,),
            out_shape=(
                shape(planes, 2, R, columns),
                shape(planes, 3, R, columns),
                shape(steps, 3 * planes, SUB, span),
                shape(steps, 4 * planes, SUB, span),
                shape(steps, 3 * planes, SUB, span),
                shape(steps, R, SUB, span),
            ),
            in_specs=specs,
            out_specs=(
                columns_of(c, planes, 2, R),
                columns_of(c, planes, 3, R),
                triple,
                quad,
                triple,
                state,
            ),
            input_output_aliases=aliases,
            compiler_params=params(),
            name="forward",
        )(*operands)
        work.append(held)

    cots = []
    for matrices, states, sources, b in work:
        incoming = lax.ppermute(b, "plane", down_route)
        for hop in range(groups - 2):
            outgoing = pl.pallas_call(
                functools.partial(carry_kernel, planes),
                grid=(steps,),
                out_shape=shape(steps, R, SUB, span),
                in_specs=[SCALARS, state, state, triple],
                out_specs=state,
                compiler_params=params(),
                name="carry",
            )(mixing, incoming, b, matrices)
            incoming = lax.ppermute(outgoing, "plane", down_route)
        cots.append(
            pl.pallas_call(
                functools.partial(cotangent_kernel, planes),
                grid=(steps,),
                out_shape=shape(steps, 3 * planes, SUB, span),
                in_specs=[SCALARS, SCALARS, state, triple, triple, quad],
                out_specs=triple,
                compiler_params=params(),
                name="cotangent",
            )(mixing, lens_weight, incoming, sources, matrices, states)
        )

    partial = pl.pallas_call(
        functools.partial(stencil_kernel, planes),
        out_shape=shape(slabs, planes, SUB, width),
        in_specs=[WHOLE] * CHUNKS,
        out_specs=WHOLE,
        compiler_params=params(),
        name="stencil",
    )(*cots)
    returned = lax.all_to_all(partial, "slab", split_axis=0, concat_axis=0, tiled=True)
    potential_grad = pl.pallas_call(
        combine_kernel,
        out_shape=shape(planes, rows, width),
        in_specs=[WHOLE],
        out_specs=WHOLE,
        compiler_params=params(),
        name="combine",
    )(returned)
    return (deflection, shear, potential_grad)


def solution(mesh):
    placed = (
        P("plane", None, "slab"),
        P("plane"),
        P("plane"),
        P("plane", None, "slab", None),
        P("plane", "slab", None),
    )
    return jax.shard_map(
        on_device,
        mesh=mesh,
        in_specs=placed,
        out_specs=(
            P("plane", None, "slab", None),
            P("plane", None, "slab", None),
            P("plane", None, "slab"),
        ),
        check_vma=False,
    )
```

time: 158 us -> 141 us (0.89)
  waiting for transfers between devices: 81.1 us -> 32 us
  starting transfers between devices: 19.9 us -> 56.7 us
  blocking collectives: 32.8 us -> 16.1 us
  Pallas kernels: 16.3 us -> 30 us
  local copies, waits for them, and re-layouts: 5.93 us -> 4.12 us
    ppermute x3 -> x12, waiting for transfers between devices: 26.6 us -> 0.03 us  [on_device(): strips[c].insert(0, lax.ppermute(strips[c][0], 'plane', up_route))]
    ppermute x3 -> x12, starting transfers between devices: 12.3 us -> 37.8 us  [on_device(): strips[c].insert(0, lax.ppermute(strips[c][0], 'plane', up_route))]
    unnamed x1 -> x0, blocking collectives: 16.7 us -> none
    pallas_call x5 -> x19, Pallas kernels: 15.3 us -> 29.1 us  [the longest x4 16.6 us: on_device(): pl.pallas_call(functools.partial(forward_kernel, groups, planes, c, lengt...]
    ppermute x1 -> x4, waiting for transfers between devices: 16 us -> 3.98 us  [on_device(): incoming = lax.ppermute(b, 'plane', down_route)]
    ppermute x2 -> x8, waiting for transfers between devices: 29.2 us -> 18.6 us  [on_device(): incoming = lax.ppermute(outgoing, 'plane', down_route)]
    ppermute x2 -> x8, starting transfers between devices: 2.58 us -> 10.3 us  [on_device(): incoming = lax.ppermute(outgoing, 'plane', down_route)]
    ppermute x1 -> x4, starting transfers between devices: 1.28 us -> 5.12 us  [on_device(): incoming = lax.ppermute(b, 'plane', down_route)]
  transfers between devices with their start and end apart: 7 -> 25, of which waited for: 6 -> 10; matrix products, arithmetic and copies ran while one was open for 2% -> 1% of each run, Pallas kernels for 0% -> 18%
where the time goes in v2:
time: 141 us; the launch traced here: 140 us
  starting transfers between devices  56.7 us (40%)
  waiting for transfers between devices  32 us (23%)
  Pallas kernels  30 us (21%)
  blocking collectives  16.1 us (11%)
  local copies, waits for them, and re-layouts  4.12 us (3%)
    ppermute x12, starting transfers between devices, on_device(): strips[c].insert(0, lax.ppermute(strips[c][0], 'plane', up_route))  37.8 us
    ppermute x8, waiting for transfers between devices, on_device(): incoming = lax.ppermute(outgoing, 'plane', down_route)  18.6 us
    pallas_call x4, Pallas kernels, on_device(): pl.pallas_call(functools.partial(forward_kernel, groups, planes, c, lengt...  16.6 us
    all_to_all x1, blocking collectives, on_device(): lax.all_to_all(packed, 'slab', split_axis=0, concat_axis=0, tiled=True)  16.1 us
    ppermute x8, starting transfers between devices, on_device(): incoming = lax.ppermute(outgoing, 'plane', down_route)  10.3 us
    all_to_all x1, waiting for transfers between devices, on_device(): lax.all_to_all(partial, 'slab', split_axis=0, concat_axis=0, tiled=True)  9.38 us
    pallas_call x8, Pallas kernels, on_device(): pl.pallas_call(functools.partial(carry_kernel, planes), grid=(steps,), ou...  6.09 us
    ppermute x4, starting transfers between devices, on_device(): incoming = lax.ppermute(b, 'plane', down_route)  5.12 us
  transfers between devices with their start and end apart: 25, of which 10 were waited for; matrix products, arithmetic and copies ran while one was open for 1% of the time, Pallas kernels for 18%

profile of v2, /device:TPU:0, one launch (start us, length us, event | category | flops | bytes accessed | tf_op | source)
XLA Modules:
  0.0 140.1 jit_solution(1227100978103648581)
XLA Ops:
  0.7 1.1 copy-done.2
  3.1 16.1 %all_to_all.10 = f32[8,4,5,8,128]{4,3,2,1,0:T(8,128)S(1)} all-to-all(f32[8,4,5,8,128]{4,3,2,1,0:T(8,128)S(1)} %pack.1), channel_id=1, replica_groups=mesh['plane'=4,'slab'=8] {'slab'}, dimensions={0} | all-to-all | bytes 1310720 | tf_op jit(solution)/shard_map/all_to_all | solution.py:296
  20.5 3.5 %collective-permute-start.3 = (f32[9,5,8,128]{3,2,1,0:T(8,128)S(1)}, f32[9,5,8,128]{3,2,1,0:T(8,128)S(1)}, u32[]{:S(2)}, u32[]{:S(2)}) collective-permute-start(f32[9,5,8,128]{3,2,1,0:T(8,128)S(1)} %get-tuple-element.32.refs_6_.refs_7_), channel_id=1, source_target_pairs={{0,8},{8,16},{16,24},{1,9},{9,17},{17,25},{2,10},{10,18},{18,26},{... | collective-permute-start | bytes 552968 | tf_op jit(solution)/shard_map/ppermute | solution.py:312
  24.0 3.5 %collective-permute-start.9 = (f32[8,5,8,128]{3,2,1,0:T(8,128)S(1)}, f32[8,5,8,128]{3,2,1,0:T(8,128)S(1)}, u32[]{:S(2)}, u32[]{:S(2)}) collective-permute-start(f32[8,5,8,128]{3,2,1,0:T(8,128)S(1)} %get-tuple-element.34.refs_6_), channel_id=1, source_target_pairs={{0,8},{8,16},{16,24},{1,9},{9,17},{17,25},{2,10},{10,18},{18,26},{... | collective-permute-start | bytes 491528 | tf_op jit(solution)/shard_map/ppermute | solution.py:312
  27.5 3.5 %collective-permute-start.6 = (f32[8,5,8,128]{3,2,1,0:T(8,128)S(1)}, f32[8,5,8,128]{3,2,1,0:T(8,128)S(1)}, u32[]{:S(2)}, u32[]{:S(2)}) collective-permute-start(f32[8,5,8,128]{3,2,1,0:T(8,128)S(1)} %get-tuple-element.33.refs_6_), channel_id=1, source_target_pairs={{0,8},{8,16},{16,24},{1,9},{9,17},{17,25},{2,10},{10,18},{18,26},{... | collective-permute-start | bytes 491528 | tf_op jit(solution)/shard_map/ppermute | solution.py:312
  31.0 1.9 %collective-permute-start = (f32[8,5,8,128]{3,2,1,0:T(8,128)S(1)}, f32[8,5,8,128]{3,2,1,0:T(8,128)S(1)}, u32[]{:S(2)}, u32[]{:S(2)}) collective-permute-start(f32[8,5,8,128]{3,2,1,0:T(8,128)S(1)} %get-tuple-element.31.refs_6_), channel_id=1, source_target_pairs={{0,8},{8,16},{16,24},{1,9},{9,17},{17,25},{2,10},{10,18},{18,26},{... | collective-permute-start | bytes 491528 | tf_op jit(solution)/shard_map/ppermute | solution.py:312
  32.9 1.9 %collective-permute-start.4 = (f32[9,5,8,128]{3,2,1,0:T(8,128)S(1)}, f32[9,5,8,128]{3,2,1,0:T(8,128)S(1)}, u32[]{:S(2)}, u32[]{:S(2)}) collective-permute-start(f32[9,5,8,128]{3,2,1,0:T(8,128)S(1)} %collective-permute-done.3.refs_4_.refs_5_), channel_id=1, source_target_pairs={{0,8},{8,16},{16,24},{1,9},{9,17},{17,25},{2,10},{10,18},{18,26},{... | collective-permute-start | bytes 552968 | tf_op jit(solution)/shard_map/ppermute | solution.py:312
  34.9 1.9 %collective-permute-start.10 = (f32[8,5,8,128]{3,2,1,0:T(8,128)S(1)}, f32[8,5,8,128]{3,2,1,0:T(8,128)S(1)}, u32[]{:S(2)}, u32[]{:S(2)}) collective-permute-start(f32[8,5,8,128]{3,2,1,0:T(8,128)S(1)} %collective-permute-done.9.refs_4_), channel_id=1, source_target_pairs={{0,8},{8,16},{16,24},{1,9},{9,17},{17,25},{2,10},{10,18},{18,26},{... | collective-permute-start | bytes 491528 | tf_op jit(solution)/shard_map/ppermute | solution.py:312
  36.8 3.6 %collective-permute-start.7 = (f32[8,5,8,128]{3,2,1,0:T(8,128)S(1)}, f32[8,5,8,128]{3,2,1,0:T(8,128)S(1)}, u32[]{:S(2)}, u32[]{:S(2)}) collective-permute-start(f32[8,5,8,128]{3,2,1,0:T(8,128)S(1)} %collective-permute-done.6.refs_4_), channel_id=1, source_target_pairs={{0,8},{8,16},{16,24},{1,9},{9,17},{17,25},{2,10},{10,18},{18,26},{... | collective-permute-start | bytes 491528 | tf_op jit(solution)/shard_map/ppermute | solution.py:312
  40.4 3.5 %collective-permute-start.1 = (f32[8,5,8,128]{3,2,1,0:T(8,128)S(1)}, f32[8,5,8,128]{3,2,1,0:T(8,128)S(1)}, u32[]{:S(2)}, u32[]{:S(2)}) collective-permute-start(f32[8,5,8,128]{3,2,1,0:T(8,128)S(1)} %collective-permute-done.refs_4_), channel_id=1, source_target_pairs={{0,8},{8,16},{16,24},{1,9},{9,17},{17,25},{2,10},{10,18},{18,26},{... | collective-permute-start | bytes 491528 | tf_op jit(solution)/shard_map/ppermute | solution.py:312
  44.0 3.5 %collective-permute-start.5 = (f32[9,5,8,128]{3,2,1,0:T(8,128)S(1)}, f32[9,5,8,128]{3,2,1,0:T(8,128)S(1)}, u32[]{:S(2)}, u32[]{:S(2)}) collective-permute-start(f32[9,5,8,128]{3,2,1,0:T(8,128)S(1)} %collective-permute-done.4.refs_2_.refs_3_), channel_id=1, source_target_pairs={{0,8},{8,16},{16,24},{1,9},{9,17},{17,25},{2,10},{10,18},{18,26},{... | collective-permute-start | bytes 552968 | tf_op jit(solution)/shard_map/ppermute | solution.py:312
  47.5 3.5 %collective-permute-start.11 = (f32[8,5,8,128]{3,2,1,0:T(8,128)S(1)}, f32[8,5,8,128]{3,2,1,0:T(8,128)S(1)}, u32[]{:S(2)}, u32[]{:S(2)}) collective-permute-start(f32[8,5,8,128]{3,2,1,0:T(8,128)S(1)} %collective-permute-done.10.refs_2_), channel_id=1, source_target_pairs={{0,8},{8,16},{16,24},{1,9},{9,17},{17,25},{2,10},{10,18},{18,26},{... | collective-permute-start | bytes 491528 | tf_op jit(solution)/shard_map/ppermute | solution.py:312
  51.0 3.9 %collective-permute-start.8 = (f32[8,5,8,128]{3,2,1,0:T(8,128)S(1)}, f32[8,5,8,128]{3,2,1,0:T(8,128)S(1)}, u32[]{:S(2)}, u32[]{:S(2)}) collective-permute-start(f32[8,5,8,128]{3,2,1,0:T(8,128)S(1)} %collective-permute-done.7.refs_2_), channel_id=1, source_target_pairs={{0,8},{8,16},{16,24},{1,9},{9,17},{17,25},{2,10},{10,18},{18,26},{... | collective-permute-start | bytes 491528 | tf_op jit(solution)/shard_map/ppermute | solution.py:312
  54.9 3.5 %collective-permute-start.2 = (f32[8,5,8,128]{3,2,1,0:T(8,128)S(1)}, f32[8,5,8,128]{3,2,1,0:T(8,128)S(1)}, u32[]{:S(2)}, u32[]{:S(2)}) collective-permute-start(f32[8,5,8,128]{3,2,1,0:T(8,128)S(1)} %collective-permute-done.1.refs_2_), channel_id=1, source_target_pairs={{0,8},{8,16},{16,24},{1,9},{9,17},{17,25},{2,10},{10,18},{18,26},{... | collective-permute-start | bytes 491528 | tf_op jit(solution)/shard_map/ppermute | solution.py:312
  58.5 2.7 %forward.4 = (f32[5,2,6,4096]{3,2,1,0:T(8,128)S(1)}, f32[5,3,6,4096]{3,2,1,0:T(8,128)}, f32[2,15,8,512]{3,2,1,0:T(8,128)S(1)}, f32[2,20,8,512]{3,2,1,0:T(8,128)S...) custom-call(f32[9,5,8,128]{3,2,1,0:T(8,128)S(1)} %collective-permute-done.5.refs_0_.refs_1_, ...), custom_call_target="tpu_custom_call" | custom-call | tf_op jit(solution)/shard_map/forward/pallas_call | solution.py:333
  61.1 1.3 collective-permute-start.12
  62.4 4.6 %forward.5 = (f32[5,2,6,4096]{3,2,1,0:T(8,128)S(1)}, f32[5,3,6,4096]{3,2,1,0:T(8,128)}, f32[2,15,8,512]{3,2,1,0:T(8,128)S(1)}, f32[2,20,8,512]{3,2,1,0:T(8,128)S...) custom-call(f32[8,5,8,128]{3,2,1,0:T(8,128)S(1)} %collective-permute, ...), custom_call_target="tpu_custom_call", output_to_operand_aliasing={{0}: (10, {}), {1}: (11, {})} | custom-call | tf_op jit(solution)/shard_map/forward/pallas_call | solution.py:333
  67.1 1.3 collective-permute-start.15
  68.4 4.6 %forward.6 = (f32[5,2,6,4096]{3,2,1,0:T(8,128)S(1)}, f32[5,3,6,4096]{3,2,1,0:T(8,128)}, f32[2,15,8,512]{3,2,1,0:T(8,128)S(1)}, f32[2,20,8,512]{3,2,1,0:T(8,128)S...) custom-call(f32[8,5,8,128]{3,2,1,0:T(8,128)S(1)} %collective-permute, ...), custom_call_target="tpu_custom_call", output_to_operand_aliasing={{0}: (10, {}), {1}: (11, {})} | custom-call | tf_op jit(solution)/shard_map/forward/pallas_call | solution.py:333
  73.0 1.3 collective-permute-start.18
  74.3 4.6 %forward.7 = (f32[5,2,6,4096]{3,2,1,0:T(8,128)S(1)}, f32[5,3,6,4096]{3,2,1,0:T(8,128)}, f32[2,15,8,512]{3,2,1,0:T(8,128)S(1)}, f32[2,20,8,512]{3,2,1,0:T(8,128)S...) custom-call(f32[8,5,8,128]{3,2,1,0:T(8,128)S(1)} %collective-permute, ...), custom_call_target="tpu_custom_call", output_to_operand_aliasing={{0}: (10, {}), {1}: (11, {})} | custom-call | tf_op jit(solution)/shard_map/forward/pallas_call | solution.py:333
  78.9 1.3 collective-permute-start.21
  81.0 1.3 collective-permute-start.13
  83.1 1.3 collective-permute-start.16
  85.2 1.3 collective-permute-start.19
  86.5 4.0 %collective-permute-done.21.in_ref = f32[2,6,8,512]{3,2,1,0:T(8,128)S(1)} collective-permute-done((f32[2,6,8,512]{3,2,1,0:T(8,128)S(1)}, f32[2,6,8,512]{3,2,1,0:T(8,128)S(1)}, u32[]{:S(2)}, u32[]{:S(2)}) %collective-permute-start.21) | collective-permute-done | bytes 196640 | tf_op jit(solution)/shard_map/ppermute | solution.py:361
  91.3 1.3 collective-permute-start.22
  92.6 2.1 %collective-permute-done.13.in_ref = f32[2,6,8,512]{3,2,1,0:T(8,128)S(1)} collective-permute-done((f32[2,6,8,512]{3,2,1,0:T(8,128)S(1)}, f32[2,6,8,512]{3,2,1,0:T(8,128)S(1)}, u32[]{:S(2)}, u32[]{:S(2)}) %collective-permute-start.13) | collective-permute-done | bytes 196640 | tf_op jit(solution)/shard_map/ppermute | solution.py:372
  95.5 1.3 collective-permute-start.14
  96.8 2.1 %collective-permute-done.16.in_ref = f32[2,6,8,512]{3,2,1,0:T(8,128)S(1)} collective-permute-done((f32[2,6,8,512]{3,2,1,0:T(8,128)S(1)}, f32[2,6,8,512]{3,2,1,0:T(8,128)S(1)}, u32[]{:S(2)}, u32[]{:S(2)}) %collective-permute-start.16) | collective-permute-done | bytes 196640 | tf_op jit(solution)/shard_map/ppermute | solution.py:372
  99.7 1.3 collective-permute-start.17
  101.0 2.1 %collective-permute-done.19.in_ref = f32[2,6,8,512]{3,2,1,0:T(8,128)S(1)} collective-permute-done((f32[2,6,8,512]{3,2,1,0:T(8,128)S(1)}, f32[2,6,8,512]{3,2,1,0:T(8,128)S(1)}, u32[]{:S(2)}, u32[]{:S(2)}) %collective-permute-start.19) | collective-permute-done | bytes 196640 | tf_op jit(solution)/shard_map/ppermute | solution.py:372
  103.9 1.3 collective-permute-start.20
  105.2 2.1 %collective-permute-done.22.in_ref = f32[2,6,8,512]{3,2,1,0:T(8,128)S(1)} collective-permute-done((f32[2,6,8,512]{3,2,1,0:T(8,128)S(1)}, f32[2,6,8,512]{3,2,1,0:T(8,128)S(1)}, u32[]{:S(2)}, u32[]{:S(2)}) %collective-permute-start.22) | collective-permute-done | bytes 196640 | tf_op jit(solution)/shard_map/ppermute | solution.py:372
  108.1 1.3 collective-permute-start.23
  109.4 2.1 %collective-permute-done.14.in_ref = f32[2,6,8,512]{3,2,1,0:T(8,128)S(1)} collective-permute-done((f32[2,6,8,512]{3,2,1,0:T(8,128)S(1)}, f32[2,6,8,512]{3,2,1,0:T(8,128)S(1)}, u32[]{:S(2)}, u32[]{:S(2)}) %collective-permute-start.14) | collective-permute-done | bytes 196640 | tf_op jit(solution)/shard_map/ppermute | solution.py:372
  111.5 0.8 cotangent.4.refs_0_
  112.4 3.4 %collective-permute-done.17.in_ref = f32[2,6,8,512]{3,2,1,0:T(8,128)S(1)} collective-permute-done((f32[2,6,8,512]{3,2,1,0:T(8,128)S(1)}, f32[2,6,8,512]{3,2,1,0:T(8,128)S(1)}, u32[]{:S(2)}, u32[]{:S(2)}) %collective-permute-start.17) | collective-permute-done | bytes 196640 | tf_op jit(solution)/shard_map/ppermute | solution.py:372
  115.8 0.8 cotangent.5.refs_1_
  116.6 3.2 %collective-permute-done.20.in_ref = f32[2,6,8,512]{3,2,1,0:T(8,128)S(1)} collective-permute-done((f32[2,6,8,512]{3,2,1,0:T(8,128)S(1)}, f32[2,6,8,512]{3,2,1,0:T(8,128)S(1)}, u32[]{:S(2)}, u32[]{:S(2)}) %collective-permute-start.20) | collective-permute-done | bytes 196640 | tf_op jit(solution)/shard_map/ppermute | solution.py:372
  119.8 0.8 cotangent.6.refs_2_
  120.6 1.3 collective-permute-done.23.in_ref
  121.9 0.8 cotangent.7.refs_3_
  122.7 1.8 %stencil.1 = f32[8,5,8,512]{3,2,1,0:T(8,128)} custom-call(f32[2,15,8,512]{3,2,1,0:T(8,128)S(1)} %cotangent.4.refs_0_, f32[2,15,8,512]{3,2,1,0:T(8,128)S(1)} %cotangent.5.refs_1_, f32[2,15,8,512]{3,2,1,0:T(8,128)S(1)} %cotangent.6.refs_2_, f32[2,15,8,512]{3,2,1,0:T(8,128)S(1)} %cotangent.7.refs_3_), custom_call_target="tpu_custom_call" | custom-call | tf_op jit(solution)/shard_map/stencil/pallas_call | solution.py:385
  124.5 3.5 %all-to-all-start.1 = ((f32[8,5,8,512]{3,2,1,0:T(8,128)}), f32[8,5,8,512]{3,2,1,0:T(8,128)S(1)}, u32[]{:S(2)}, u32[]{:S(2)}) async-start(f32[8,5,8,512]{3,2,1,0:T(8,128)} %stencil.1), calls=%async_computation.1 | async-start | bytes 1310720 | tf_op jit(solution)/shard_map/all_to_all | solution.py:393
  128.1 1.7 %copy.14 = f32[5,2,6,4096]{3,1,2,0:T(2,128)} copy(f32[5,2,6,4096]{3,2,1,0:T(8,128)S(1)} %get-tuple-element.59) | data formatting | bytes 1966080
  129.8 9.4 %all-to-all-done.1.in_ref = f32[8,5,8,512]{3,2,1,0:T(8,128)S(1)} async-done(((f32[8,5,8,512]{3,2,1,0:T(8,128)}), f32[8,5,8,512]{3,2,1,0:T(8,128)S(1)}, u32[]{:S(2)}, u32[]{:S(2)}) %all-to-all-start.1) | async-done | bytes 655392 | tf_op jit(solution)/shard_map/all_to_all | solution.py:393
  139.1 0.9 combine.1
  (38 shorter events, 8.8 us)
Async XLA Ops:
  0.6 57.8 %copy-start.1 = (f32[5,6,4096]{2,1,0:T(8,128)S(1)}, f32[5,6,4096]{2,1,0:T(8,128)}, u32[]{:S(2)}) copy-start(f32[5,6,4096]{2,1,0:T(8,128)} %refs_9_.7) | copy-start | bytes 1474564
  0.6 1.1 copy-start.2
  1.7 0.7 copy-start.5
  2.4 56.1 %copy-start = (f32[5,3,6,4096]{3,2,1,0:T(8,128)S(1)}, f32[5,3,6,4096]{3,2,1,0:T(8,128)}, u32[]{:S(2)}) copy-start(f32[5,3,6,4096]{3,2,1,0:T(8,128)} %refs_8_.7) | copy-start | bytes 4423684
  19.2 0.7 copy-start.3
  20.5 12.4 %collective-permute-start.3 = (f32[9,5,8,128]{3,2,1,0:T(8,128)S(1)}, f32[9,5,8,128]{3,2,1,0:T(8,128)S(1)}, u32[]{:S(2)}, u32[]{:S(2)}) collective-permute-start(f32[9,5,8,128]{3,2,1,0:T(8,128)S(1)} %get-tuple-element.32.refs_6_.refs_7_), channel_id=1, source_target_pairs={{0,8},{8,16},{16,24},{1,9},{9,17},{17,25},{2,10},{10,18},{18,26},{... | collective-permute-start | bytes 552968 | tf_op jit(solution)/shard_map/ppermute | solution.py:312
  24.0 10.9 %collective-permute-start.9 = (f32[8,5,8,128]{3,2,1,0:T(8,128)S(1)}, f32[8,5,8,128]{3,2,1,0:T(8,128)S(1)}, u32[]{:S(2)}, u32[]{:S(2)}) collective-permute-start(f32[8,5,8,128]{3,2,1,0:T(8,128)S(1)} %get-tuple-element.34.refs_6_), channel_id=1, source_target_pairs={{0,8},{8,16},{16,24},{1,9},{9,17},{17,25},{2,10},{10,18},{18,26},{... | collective-permute-start | bytes 491528 | tf_op jit(solution)/shard_map/ppermute | solution.py:312
  27.5 9.3 %collective-permute-start.6 = (f32[8,5,8,128]{3,2,1,0:T(8,128)S(1)}, f32[8,5,8,128]{3,2,1,0:T(8,128)S(1)}, u32[]{:S(2)}, u32[]{:S(2)}) collective-permute-start(f32[8,5,8,128]{3,2,1,0:T(8,128)S(1)} %get-tuple-element.33.refs_6_), channel_id=1, source_target_pairs={{0,8},{8,16},{16,24},{1,9},{9,17},{17,25},{2,10},{10,18},{18,26},{... | collective-permute-start | bytes 491528 | tf_op jit(solution)/shard_map/ppermute | solution.py:312
  31.0 9.5 %collective-permute-start = (f32[8,5,8,128]{3,2,1,0:T(8,128)S(1)}, f32[8,5,8,128]{3,2,1,0:T(8,128)S(1)}, u32[]{:S(2)}, u32[]{:S(2)}) collective-permute-start(f32[8,5,8,128]{3,2,1,0:T(8,128)S(1)} %get-tuple-element.31.refs_6_), channel_id=1, source_target_pairs={{0,8},{8,16},{16,24},{1,9},{9,17},{17,25},{2,10},{10,18},{18,26},{... | collective-permute-start | bytes 491528 | tf_op jit(solution)/shard_map/ppermute | solution.py:312
  32.9 11.0 %collective-permute-start.4 = (f32[9,5,8,128]{3,2,1,0:T(8,128)S(1)}, f32[9,5,8,128]{3,2,1,0:T(8,128)S(1)}, u32[]{:S(2)}, u32[]{:S(2)}) collective-permute-start(f32[9,5,8,128]{3,2,1,0:T(8,128)S(1)} %collective-permute-done.3.refs_4_.refs_5_), channel_id=1, source_target_pairs={{0,8},{8,16},{16,24},{1,9},{9,17},{17,25},{2,10},{10,18},{18,26},{... | collective-permute-start | bytes 552968 | tf_op jit(solution)/shard_map/ppermute | solution.py:312
  34.9 12.6 %collective-permute-start.10 = (f32[8,5,8,128]{3,2,1,0:T(8,128)S(1)}, f32[8,5,8,128]{3,2,1,0:T(8,128)S(1)}, u32[]{:S(2)}, u32[]{:S(2)}) collective-permute-start(f32[8,5,8,128]{3,2,1,0:T(8,128)S(1)} %collective-permute-done.9.refs_4_), channel_id=1, source_target_pairs={{0,8},{8,16},{16,24},{1,9},{9,17},{17,25},{2,10},{10,18},{18,26},{... | collective-permute-start | bytes 491528 | tf_op jit(solution)/shard_map/ppermute | solution.py:312
  36.8 14.2 %collective-permute-start.7 = (f32[8,5,8,128]{3,2,1,0:T(8,128)S(1)}, f32[8,5,8,128]{3,2,1,0:T(8,128)S(1)}, u32[]{:S(2)}, u32[]{:S(2)}) collective-permute-start(f32[8,5,8,128]{3,2,1,0:T(8,128)S(1)} %collective-permute-done.6.refs_4_), channel_id=1, source_target_pairs={{0,8},{8,16},{16,24},{1,9},{9,17},{17,25},{2,10},{10,18},{18,26},{... | collective-permute-start | bytes 491528 | tf_op jit(solution)/shard_map/ppermute | solution.py:312
  40.4 14.5 %collective-permute-start.1 = (f32[8,5,8,128]{3,2,1,0:T(8,128)S(1)}, f32[8,5,8,128]{3,2,1,0:T(8,128)S(1)}, u32[]{:S(2)}, u32[]{:S(2)}) collective-permute-start(f32[8,5,8,128]{3,2,1,0:T(8,128)S(1)} %collective-permute-done.refs_4_), channel_id=1, source_target_pairs={{0,8},{8,16},{16,24},{1,9},{9,17},{17,25},{2,10},{10,18},{18,26},{... | collective-permute-start | bytes 491528 | tf_op jit(solution)/shard_map/ppermute | solution.py:312
  44.0 14.5 %collective-permute-start.5 = (f32[9,5,8,128]{3,2,1,0:T(8,128)S(1)}, f32[9,5,8,128]{3,2,1,0:T(8,128)S(1)}, u32[]{:S(2)}, u32[]{:S(2)}) collective-permute-start(f32[9,5,8,128]{3,2,1,0:T(8,128)S(1)} %collective-permute-done.4.refs_2_.refs_3_), channel_id=1, source_target_pairs={{0,8},{8,16},{16,24},{1,9},{9,17},{17,25},{2,10},{10,18},{18,26},{... | collective-permute-start | bytes 552968 | tf_op jit(solution)/shard_map/ppermute | solution.py:312
  47.5 14.9 %collective-permute-start.11 = (f32[8,5,8,128]{3,2,1,0:T(8,128)S(1)}, f32[8,5,8,128]{3,2,1,0:T(8,128)S(1)}, u32[]{:S(2)}, u32[]{:S(2)}) collective-permute-start(f32[8,5,8,128]{3,2,1,0:T(8,128)S(1)} %collective-permute-done.10.refs_2_), channel_id=1, source_target_pairs={{0,8},{8,16},{16,24},{1,9},{9,17},{17,25},{2,10},{10,18},{18,26},{... | collective-permute-start | bytes 491528 | tf_op jit(solution)/shard_map/ppermute | solution.py:312
  51.0 17.4 %collective-permute-start.8 = (f32[8,5,8,128]{3,2,1,0:T(8,128)S(1)}, f32[8,5,8,128]{3,2,1,0:T(8,128)S(1)}, u32[]{:S(2)}, u32[]{:S(2)}) collective-permute-start(f32[8,5,8,128]{3,2,1,0:T(8,128)S(1)} %collective-permute-done.7.refs_2_), channel_id=1, source_target_pairs={{0,8},{8,16},{16,24},{1,9},{9,17},{17,25},{2,10},{10,18},{18,26},{... | collective-permute-start | bytes 491528 | tf_op jit(solution)/shard_map/ppermute | solution.py:312
  54.9 19.4 %collective-permute-start.2 = (f32[8,5,8,128]{3,2,1,0:T(8,128)S(1)}, f32[8,5,8,128]{3,2,1,0:T(8,128)S(1)}, u32[]{:S(2)}, u32[]{:S(2)}) collective-permute-start(f32[8,5,8,128]{3,2,1,0:T(8,128)S(1)} %collective-permute-done.1.refs_2_), channel_id=1, source_target_pairs={{0,8},{8,16},{16,24},{1,9},{9,17},{17,25},{2,10},{10,18},{18,26},{... | collective-permute-start | bytes 491528 | tf_op jit(solution)/shard_map/ppermute | solution.py:312
  61.1 19.1 %collective-permute-start.12 = (f32[2,6,8,512]{3,2,1,0:T(8,128)S(1)}, f32[2,6,8,512]{3,2,1,0:T(8,128)S(1)}, u32[]{:S(2)}, u32[]{:S(2)}) collective-permute-start(f32[2,6,8,512]{3,2,1,0:T(8,128)S(1)} %get-tuple-element.43.b_ref), channel_id=1, source_target_pairs={{8,0},{16,8},{24,16},{9,1},{17,9},{25,17},{10,2},{18,10},{26,18},{... | collective-permute-start | bytes 589832 | tf_op jit(solution)/shard_map/ppermute | solution.py:361
  67.1 15.2 %collective-permute-start.15 = (f32[2,6,8,512]{3,2,1,0:T(8,128)S(1)}, f32[2,6,8,512]{3,2,1,0:T(8,128)S(1)}, u32[]{:S(2)}, u32[]{:S(2)}) collective-permute-start(f32[2,6,8,512]{3,2,1,0:T(8,128)S(1)} %get-tuple-element.47.b_ref), channel_id=1, source_target_pairs={{8,0},{16,8},{24,16},{9,1},{17,9},{25,17},{10,2},{18,10},{26,18},{... | collective-permute-start | bytes 589832 | tf_op jit(solution)/shard_map/ppermute | solution.py:361
  73.0 11.4 %collective-permute-start.18 = (f32[2,6,8,512]{3,2,1,0:T(8,128)S(1)}, f32[2,6,8,512]{3,2,1,0:T(8,128)S(1)}, u32[]{:S(2)}, u32[]{:S(2)}) collective-permute-start(f32[2,6,8,512]{3,2,1,0:T(8,128)S(1)} %get-tuple-element.51.b_ref), channel_id=1, source_target_pairs={{8,0},{16,8},{24,16},{9,1},{17,9},{25,17},{10,2},{18,10},{26,18},{... | collective-permute-start | bytes 589832 | tf_op jit(solution)/shard_map/ppermute | solution.py:361
  74.3 5.9 %copy-start.4 = (f32[5]{0:T(128)S(1)}, f32[5]{0:T(128)}, u32[]{:S(2)}) copy-start(f32[5]{0:T(128)} %mix_ref.25) | copy-start | bytes 64
  78.9 11.5 %collective-permute-start.21 = (f32[2,6,8,512]{3,2,1,0:T(8,128)S(1)}, f32[2,6,8,512]{3,2,1,0:T(8,128)S(1)}, u32[]{:S(2)}, u32[]{:S(2)}) collective-permute-start(f32[2,6,8,512]{3,2,1,0:T(8,128)S(1)} %get-tuple-element.55.b_ref), channel_id=1, source_target_pairs={{8,0},{16,8},{24,16},{9,1},{17,9},{25,17},{10,2},{18,10},{26,18},{... | collective-permute-start | bytes 589832 | tf_op jit(solution)/shard_map/ppermute | solution.py:361
  81.0 13.7 %collective-permute-start.13 = (f32[2,6,8,512]{3,2,1,0:T(8,128)S(1)}, f32[2,6,8,512]{3,2,1,0:T(8,128)S(1)}, u32[]{:S(2)}, u32[]{:S(2)}) collective-permute-start(f32[2,6,8,512]{3,2,1,0:T(8,128)S(1)} %carry.8), channel_id=1, source_target_pairs={{8,0},{16,8},{24,16},{9,1},{17,9},{25,17},{10,2},{18,10},{26,18},{... | collective-permute-start | bytes 589832 | tf_op jit(solution)/shard_map/ppermute | solution.py:372
  83.1 15.8 %collective-permute-start.16 = (f32[2,6,8,512]{3,2,1,0:T(8,128)S(1)}, f32[2,6,8,512]{3,2,1,0:T(8,128)S(1)}, u32[]{:S(2)}, u32[]{:S(2)}) collective-permute-start(f32[2,6,8,512]{3,2,1,0:T(8,128)S(1)} %carry.10), channel_id=1, source_target_pairs={{8,0},{16,8},{24,16},{9,1},{17,9},{25,17},{10,2},{18,10},{26,18},{... | collective-permute-start | bytes 589832 | tf_op jit(solution)/shard_map/ppermute | solution.py:372
  85.2 17.9 %collective-permute-start.19 = (f32[2,6,8,512]{3,2,1,0:T(8,128)S(1)}, f32[2,6,8,512]{3,2,1,0:T(8,128)S(1)}, u32[]{:S(2)}, u32[]{:S(2)}) collective-permute-start(f32[2,6,8,512]{3,2,1,0:T(8,128)S(1)} %carry.12), channel_id=1, source_target_pairs={{8,0},{16,8},{24,16},{9,1},{17,9},{25,17},{10,2},{18,10},{26,18},{... | collective-permute-start | bytes 589832 | tf_op jit(solution)/shard_map/ppermute | solution.py:372
  91.2 20.3 %copy-start.6 = (f32[5]{0:T(128)S(1)}, f32[5]{0:T(128)}, u32[]{:S(2)}) copy-start(f32[5]{0:T(128)} %weight_ref.9) | copy-start | bytes 64
  91.3 16.1 %collective-permute-start.22 = (f32[2,6,8,512]{3,2,1,0:T(8,128)S(1)}, f32[2,6,8,512]{3,2,1,0:T(8,128)S(1)}, u32[]{:S(2)}, u32[]{:S(2)}) collective-permute-start(f32[2,6,8,512]{3,2,1,0:T(8,128)S(1)} %carry.14), channel_id=1, source_target_pairs={{8,0},{16,8},{24,16},{9,1},{17,9},{25,17},{10,2},{18,10},{26,18},{... | collective-permute-start | bytes 589832 | tf_op jit(solution)/shard_map/ppermute | solution.py:372
  95.5 16.1 %collective-permute-start.14 = (f32[2,6,8,512]{3,2,1,0:T(8,128)S(1)}, f32[2,6,8,512]{3,2,1,0:T(8,128)S(1)}, u32[]{:S(2)}, u32[]{:S(2)}) collective-permute-start(f32[2,6,8,512]{3,2,1,0:T(8,128)S(1)} %carry.9), channel_id=1, source_target_pairs={{8,0},{16,8},{24,16},{9,1},{17,9},{25,17},{10,2},{18,10},{26,18},{... | collective-permute-start | bytes 589832 | tf_op jit(solution)/shard_map/ppermute | solution.py:372
  99.7 16.1 %collective-permute-start.17 = (f32[2,6,8,512]{3,2,1,0:T(8,128)S(1)}, f32[2,6,8,512]{3,2,1,0:T(8,128)S(1)}, u32[]{:S(2)}, u32[]{:S(2)}) collective-permute-start(f32[2,6,8,512]{3,2,1,0:T(8,128)S(1)} %carry.11), channel_id=1, source_target_pairs={{8,0},{16,8},{24,16},{9,1},{17,9},{25,17},{10,2},{18,10},{26,18},{... | collective-permute-start | bytes 589832 | tf_op jit(solution)/shard_map/ppermute | solution.py:372
  103.9 15.9 %collective-permute-start.20 = (f32[2,6,8,512]{3,2,1,0:T(8,128)S(1)}, f32[2,6,8,512]{3,2,1,0:T(8,128)S(1)}, u32[]{:S(2)}, u32[]{:S(2)}) collective-permute-start(f32[2,6,8,512]{3,2,1,0:T(8,128)S(1)} %carry.13), channel_id=1, source_target_pairs={{8,0},{16,8},{24,16},{9,1},{17,9},{25,17},{10,2},{18,10},{26,18},{... | collective-permute-start | bytes 589832 | tf_op jit(solution)/shard_map/ppermute | solution.py:372
  108.1 13.8 %collective-permute-start.23 = (f32[2,6,8,512]{3,2,1,0:T(8,128)S(1)}, f32[2,6,8,512]{3,2,1,0:T(8,128)S(1)}, u32[]{:S(2)}, u32[]{:S(2)}) collective-permute-start(f32[2,6,8,512]{3,2,1,0:T(8,128)S(1)} %carry.15), channel_id=1, source_target_pairs={{8,0},{16,8},{24,16},{9,1},{17,9},{25,17},{10,2},{18,10},{26,18},{... | collective-permute-start | bytes 589832 | tf_op jit(solution)/shard_map/ppermute | solution.py:372
  124.5 14.6 %all-to-all-start.1 = ((f32[8,5,8,512]{3,2,1,0:T(8,128)}), f32[8,5,8,512]{3,2,1,0:T(8,128)S(1)}, u32[]{:S(2)}, u32[]{:S(2)}) async-start(f32[8,5,8,512]{3,2,1,0:T(8,128)} %stencil.1), calls=%async_computation.1 | async-start | bytes 1310720 | tf_op jit(solution)/shard_map/all_to_all | solution.py:393

commit v3 on v2

--- a/solution.py
+++ b/solution.py
@@ -85,8 +85,8 @@
         )
 
 
-def unpack_state(in_ref):
-    tiles = [in_ref[0, j] for j in range(R)]
+def unpack_state(arrived):
+    tiles = [sum(in_ref[0, j] for in_ref in arrived) for j in range(R)]
     fields = [t[0:R] for t in tiles]
     fields.append(jnp.concatenate([t[6:7] for t in tiles], axis=0))
     fields.append(jnp.concatenate([t[7:8] for t in tiles], axis=0))
@@ -96,7 +96,7 @@
 def forward_kernel(groups, planes, chunk, length, *refs):
     strips = refs[: 2 * groups]
     obs_ref, noise_ref = refs[2 * groups : 2 * groups + 2]
-    defl_ref, shear_ref, m_ref, a_ref, src_ref, b_ref = refs[-6:]
+    map_ref, m_ref, a_ref, src_ref, b_ref = refs[-5:]
     step = pl.program_id(0)
     width = obs_ref.shape[-1]
     span = width // EDGE
@@ -148,18 +148,15 @@
             if own:
                 slope_rows = 0.5 * (row_up(psi) - row_down(psi))[:, EDGE:-EDGE]
                 slope_cols = 0.5 * (col_next(psi) - col_prev(psi))
-                defl_ref[k, 0] = slope_rows[0:R]
-                defl_ref[k, 1] = slope_cols[0:R]
                 shear = [
-                    1.0 - 0.5 * (a[0] + a[3])[0:R],
-                    0.5 * (a[3] - a[0])[0:R],
-                    -0.5 * (a[1] + a[2])[0:R],
+                    1.0 - 0.5 * (a[0] + a[3]),
+                    0.5 * (a[3] - a[0]),
+                    -0.5 * (a[1] + a[2]),
                 ]
+                for j, field in enumerate([slope_rows, slope_cols] + shear):
+                    map_ref[0, 5 * k + j] = field
                 noise = -0.5 * noise_ref[k]
-                r = []
-                for j in range(3):
-                    shear_ref[k, j] = shear[j]
-                    r.append(noise * (shear[j] - obs_ref[k, j]))
+                r = [noise * (shear[j][0:R] - obs_ref[k, j]) for j in range(3)]
                 src_ref[0, 3 * k, 0:R] = r[0] + r[1]
                 src_ref[0, 3 * k + 1, 0:R] = r[2]
                 src_ref[0, 3 * k + 2, 0:R] = r[0] - r[1]
@@ -174,8 +171,22 @@
     pack_state(b_ref, p + q)
 
 
+def assemble_kernel(*refs):
+    maps = refs[:-2]
+    defl_ref, shear_ref = refs[-2:]
+    steps, width = (maps[0].shape[0], maps[0].shape[-1])
+    for c, map_ref in enumerate(maps):
+        for i in range(steps):
+            start = (c * steps + i) * width
+            for k in range(defl_ref.shape[0]):
+                for j in range(2):
+                    defl_ref[k, j, :, start : start + width] = map_ref[i, 5 * k + j, 0:R]
+                for j in range(3):
+                    shear_ref[k, j, :, start : start + width] = map_ref[i, 5 * k + 2 + j, 0:R]
+
+
 def carry_kernel(planes, mix_ref, in_ref, b_ref, m_ref, out_ref):
-    fields = unpack_state(in_ref)
+    fields = unpack_state([in_ref])
     p, q = (fields[0:4], fields[4:8])
     for k in reversed(range(planes)):
         m0, m1, off = (m_ref[0, 3 * k + j, 0:R] for j in range(3))
@@ -184,9 +195,10 @@
     out_ref[...] += b_ref[...]
 
 
-def cotangent_kernel(planes, mix_ref, weight_ref, in_ref, src_ref, m_ref, a_ref, cot_ref):
-    width = in_ref.shape[-1]
-    fields = unpack_state(in_ref)
+def cotangent_kernel(planes, mix_ref, weight_ref, src_ref, m_ref, a_ref, *refs):
+    arrived, cot_ref = (refs[:-1], refs[-1])
+    width = cot_ref.shape[-1]
+    fields = unpack_state(arrived)
     p, q = (fields[0:4], fields[4:8])
     blank = jnp.zeros((SUB - R, width), F32)
     for k in reversed(range(planes)):
@@ -282,8 +294,12 @@
     length = tiles * slabs // CHUNKS
     span = SPAN * EDGE
     steps = length // SPAN
-    up_route = [(i, i + 1) for i in range(groups - 1)]
-    down_route = [(i + 1, i) for i in range(groups - 1)]
+
+    def climb(x, hop):
+        return lax.ppermute(x, "plane", [(i, i + 1) for i in range(hop, groups - 1)])
+
+    def descend(x, hop):
+        return lax.ppermute(x, "plane", [(groups - 1 - hop, groups - 2 - hop)])
 
     packed = pl.pallas_call(
         pack_kernel,
@@ -309,57 +325,41 @@
     for turn in range(CHUNKS + groups - 2):
         for c in range(CHUNKS):
             if 0 <= turn - c < groups - 1:
-                strips[c].insert(0, lax.ppermute(strips[c][0], "plane", up_route))
+                strips[c].insert(0, climb(strips[c][0], turn - c))
 
     state = block_of(R, SUB, span)
     triple = block_of(3 * planes, SUB, span)
     quad = block_of(4 * planes, SUB, span)
-    kept = pl.BlockSpec(memory_space=pl.ANY)
-
-    def columns_of(c, *dims):
-        return pl.BlockSpec(dims + (span,), lambda i: (0,) * len(dims) + (c * steps + i,))
-
-    deflection, shear = (None, None)
+    quint = block_of(5 * planes, SUB, span)
+    maps = []
     work = []
     for c in range(CHUNKS):
-        operands = [x for pair in zip(strips[c], strips[0]) for x in pair]
-        operands += [observed, noise_weight]
-        specs = [WHOLE] * (2 * groups) + [columns_of(c, planes, 3, R), columns_of(c, planes, R)]
-        aliases = {}
-        if c > 0:
-            aliases = {len(operands): 0, len(operands) + 1: 1}
-            operands += [deflection, shear]
-            specs += [kept, kept]
-        deflection, shear, *held = pl.pallas_call(
+
+        def columns_of(*dims, at=c * steps):
+            return pl.BlockSpec(dims + (span,), lambda i: (0,) * len(dims) + (at + i,))
+
+        map_piece, *held = pl.pallas_call(
             functools.partial(forward_kernel, groups, planes, c, length),
             grid=(steps,),
             out_shape=(
-                shape(planes, 2, R, columns),
-                shape(planes, 3, R, columns),
+                shape(steps, 5 * planes, SUB, span),
                 shape(steps, 3 * planes, SUB, span),
                 shape(steps, 4 * planes, SUB, span),
                 shape(steps, 3 * planes, SUB, span),
                 shape(steps, R, SUB, span),
             ),
-            in_specs=specs,
-            out_specs=(
-                columns_of(c, planes, 2, R),
-                columns_of(c, planes, 3, R),
-                triple,
-                quad,
-                triple,
-                state,
-            ),
-            input_output_aliases=aliases,
+            in_specs=[WHOLE] * (2 * groups) + [columns_of(planes, 3, R), columns_of(planes, R)],
+            out_specs=(quint, triple, quad, triple, state),
             compiler_params=params(),
             name="forward",
-        )(*operands)
+        )(*[x for pair in zip(strips[c], strips[0]) for x in pair], observed, noise_weight)
+        maps.append(map_piece)
         work.append(held)
 
     cots = []
     for matrices, states, sources, b in work:
-        incoming = lax.ppermute(b, "plane", down_route)
-        for hop in range(groups - 2):
+        arrived = [descend(b, 0)]
+        for hop in range(1, groups - 1):
             outgoing = pl.pallas_call(
                 functools.partial(carry_kernel, planes),
                 grid=(steps,),
@@ -368,18 +368,18 @@
                 out_specs=state,
                 compiler_params=params(),
                 name="carry",
-            )(mixing, incoming, b, matrices)
-            incoming = lax.ppermute(outgoing, "plane", down_route)
+            )(mixing, arrived[-1], b, matrices)
+            arrived.append(descend(outgoing, hop))
         cots.append(
             pl.pallas_call(
                 functools.partial(cotangent_kernel, planes),
                 grid=(steps,),
                 out_shape=shape(steps, 3 * planes, SUB, span),
-                in_specs=[SCALARS, SCALARS, state, triple, triple, quad],
+                in_specs=[SCALARS, SCALARS, triple, triple, quad] + [state] * (groups - 1),
                 out_specs=triple,
                 compiler_params=params(),
                 name="cotangent",
-            )(mixing, lens_weight, incoming, sources, matrices, states)
+            )(mixing, lens_weight, sources, matrices, states, *arrived)
         )
 
     partial = pl.pallas_call(
@@ -391,6 +391,14 @@
         name="stencil",
     )(*cots)
     returned = lax.all_to_all(partial, "slab", split_axis=0, concat_axis=0, tiled=True)
+    deflection, shear = pl.pallas_call(
+        assemble_kernel,
+        out_shape=(shape(planes, 2, R, columns), shape(planes, 3, R, columns)),
+        in_specs=[WHOLE] * CHUNKS,
+        out_specs=(WHOLE, WHOLE),
+        compiler_params=params(),
+        name="assemble",
+    )(*maps)
     potential_grad = pl.pallas_call(
         combine_kernel,
         out_shape=shape(planes, rows, width),

time: 141 us -> 127 us (0.901)
  starting transfers between devices: 56.7 us -> 31.8 us
  waiting for transfers between devices: 32 us -> 42.7 us
    ppermute x24, starting transfers between devices: 53.2 us -> 28.3 us  [the longest x12 17.7 us: climb(): lax.ppermute(x, 'plane', [(i, i + 1) for i in range(hop, groups - 1)])]
    ppermute x24, waiting for transfers between devices: 22.6 us -> 36 us  [the longest x12 32.8 us: descend(): return lax.ppermute(x, 'plane', [(groups - 1 - hop, groups - 2 - hop)])]
    pallas_call x4, Pallas kernels: 16.6 us -> 13.7 us  [on_device(): pl.pallas_call(functools.partial(forward_kernel, groups, planes, c, lengt...]
    all_to_all x1, waiting for transfers between devices: 9.38 us -> 6.68 us  [on_device(): lax.all_to_all(partial, 'slab', split_axis=0, concat_axis=0, tiled=True)]
    pallas_call x0 -> x1, Pallas kernels: none -> 1.55 us  [on_device(): pl.pallas_call(assemble_kernel, out_shape=(shape(planes, 2, R, columns),...]
    unnamed x15 -> x19, local copies, waits for them, and re-layouts: 4.12 us -> 5.34 us
  transfers between devices with their start and end apart: 25 -> 25, of which waited for: 10 -> 7; matrix products, arithmetic and copies ran while one was open for 1% -> 1% of each run, Pallas kernels for 18% -> 19%
where the time goes in v3:
time: 127 us; the launch traced here: 126 us
  waiting for transfers between devices  42.7 us (34%)
  starting transfers between devices  31.8 us (25%)
  Pallas kernels  28.8 us (23%)
  blocking collectives  16.1 us (13%)
  local copies, waits for them, and re-layouts  5.34 us (4%)
    ppermute x12, waiting for transfers between devices, descend(): return lax.ppermute(x, 'plane', [(groups - 1 - hop, groups - 2 - hop)])  32.8 us
    ppermute x12, starting transfers between devices, climb(): lax.ppermute(x, 'plane', [(i, i + 1) for i in range(hop, groups - 1)])  17.7 us
    all_to_all x1, blocking collectives, on_device(): lax.all_to_all(packed, 'slab', split_axis=0, concat_axis=0, tiled=True)  16.1 us
    pallas_call x4, Pallas kernels, on_device(): pl.pallas_call(functools.partial(forward_kernel, groups, planes, c, lengt...  13.7 us
    ppermute x12, starting transfers between devices, descend(): return lax.ppermute(x, 'plane', [(groups - 1 - hop, groups - 2 - hop)])  10.6 us
    all_to_all x1, waiting for transfers between devices, on_device(): lax.all_to_all(partial, 'slab', split_axis=0, concat_axis=0, tiled=True)  6.68 us
    pallas_call x8, Pallas kernels, on_device(): pl.pallas_call(functools.partial(carry_kernel, planes), grid=(steps,), ou...  6.18 us
    unnamed x19, local copies, waits for them, and re-layouts  5.34 us
  transfers between devices with their start and end apart: 25, of which 7 were waited for; matrix products, arithmetic and copies ran while one was open for 1% of the time, Pallas kernels for 19%

profile of v3, /device:TPU:0, one launch (start us, length us, event | category | flops | bytes accessed | tf_op | source)
XLA Modules:
  0.0 126.0 jit_solution(378723537580373895)
XLA Ops:
  0.7 1.2 copy-done.4
  2.5 0.7 pack.1
  3.2 16.1 %all_to_all.10 = f32[8,4,5,8,128]{4,3,2,1,0:T(8,128)S(1)} all-to-all(f32[8,4,5,8,128]{4,3,2,1,0:T(8,128)S(1)} %pack.1), channel_id=1, replica_groups=mesh['plane'=4,'slab'=8] {'slab'}, dimensions={0} | all-to-all | bytes 1310720 | tf_op jit(solution)/shard_map/all_to_all | solution.py:312
  20.6 3.5 %collective-permute-start = (f32[9,5,8,128]{3,2,1,0:T(8,128)S(1)}, f32[9,5,8,128]{3,2,1,0:T(8,128)S(1)}, u32[]{:S(2)}, u32[]{:S(2)}) collective-permute-start(f32[9,5,8,128]{3,2,1,0:T(8,128)S(1)} %get-tuple-element.29.refs_6_.refs_7_), channel_id=1, source_target_pairs={{0,8},{8,16},{16,24},{1,9},{9,17},{17,25},{2,10},{10,18},{18,26},{... | collective-permute-start | bytes 552968 | tf_op jit(solution)/shard_map/ppermute | solution.py:299
  24.1 3.5 %collective-permute-start.9 = (f32[8,5,8,128]{3,2,1,0:T(8,128)S(1)}, f32[8,5,8,128]{3,2,1,0:T(8,128)S(1)}, u32[]{:S(2)}, u32[]{:S(2)}) collective-permute-start(f32[8,5,8,128]{3,2,1,0:T(8,128)S(1)} %get-tuple-element.35.refs_6_), channel_id=1, source_target_pairs={{0,8},{8,16},{16,24},{1,9},{9,17},{17,25},{2,10},{10,18},{18,26},{... | collective-permute-start | bytes 491528 | tf_op jit(solution)/shard_map/ppermute | solution.py:299
  27.6 3.5 %collective-permute-start.6 = (f32[8,5,8,128]{3,2,1,0:T(8,128)S(1)}, f32[8,5,8,128]{3,2,1,0:T(8,128)S(1)}, u32[]{:S(2)}, u32[]{:S(2)}) collective-permute-start(f32[8,5,8,128]{3,2,1,0:T(8,128)S(1)} %get-tuple-element.33.refs_6_), channel_id=1, source_target_pairs={{0,8},{8,16},{16,24},{1,9},{9,17},{17,25},{2,10},{10,18},{18,26},{... | collective-permute-start | bytes 491528 | tf_op jit(solution)/shard_map/ppermute | solution.py:299
  31.1 1.9 %collective-permute-start.3 = (f32[8,5,8,128]{3,2,1,0:T(8,128)S(1)}, f32[8,5,8,128]{3,2,1,0:T(8,128)S(1)}, u32[]{:S(2)}, u32[]{:S(2)}) collective-permute-start(f32[8,5,8,128]{3,2,1,0:T(8,128)S(1)} %get-tuple-element.31.refs_6_), channel_id=1, source_target_pairs={{0,8},{8,16},{16,24},{1,9},{9,17},{17,25},{2,10},{10,18},{18,26},{... | collective-permute-start | bytes 491528 | tf_op jit(solution)/shard_map/ppermute | solution.py:299
  34.4 1.3 %collective-permute-done.6.refs_4_ = f32[8,5,8,128]{3,2,1,0:T(8,128)S(1)} collective-permute-done((f32[8,5,8,128]{3,2,1,0:T(8,128)S(1)}, f32[8,5,8,128]{3,2,1,0:T(8,128)S(1)}, u32[]{:S(2)}, u32[]{:S(2)}) %collective-permute-start.6) | collective-permute-done | bytes 163872 | tf_op jit(solution)/shard_map/ppermute | solution.py:299
  36.4 1.9 %collective-permute-done.3.refs_4_ = f32[8,5,8,128]{3,2,1,0:T(8,128)S(1)} collective-permute-done((f32[8,5,8,128]{3,2,1,0:T(8,128)S(1)}, f32[8,5,8,128]{3,2,1,0:T(8,128)S(1)}, u32[]{:S(2)}, u32[]{:S(2)}) %collective-permute-start.3) | collective-permute-done | bytes 163872 | tf_op jit(solution)/shard_map/ppermute | solution.py:299
  41.7 3.9 %forward.7 = (f32[2,25,8,512]{3,2,1,0:T(8,128)S(1)}, f32[2,15,8,512]{3,2,1,0:T(8,128)S(1)}, f32[2,20,8,512]{3,2,1,0:T(8,128)S(1)}, f32[2,15,8,512]{3,2,1,0:T(8,128)S(1)}, f32[2,6,8,512]{3,2,1,0:T(8,128)S(1)}) custom-call(f32[8,5,8,128]{3,2,1,0:T(8,128)S(1)} %collective-permute-done.11.refs_0_, f32[9,5,8,128]{3,2,1,0:T(8,128)S(1)} %collective-permute-done.2.refs_0_.refs_1_, ...), custom_call_target="tpu_custom_call" | custom-call | tf_op jit(solution)/shard_map/forward/pallas_call | solution.py:341
  45.7 0.7 collective-permute-start.21
  46.4 3.9 %forward.6 = (f32[2,25,8,512]{3,2,1,0:T(8,128)S(1)}, f32[2,15,8,512]{3,2,1,0:T(8,128)S(1)}, f32[2,20,8,512]{3,2,1,0:T(8,128)S(1)}, f32[2,15,8,512]{3,2,1,0:T(8,128)S(1)}, f32[2,6,8,512]{3,2,1,0:T(8,128)S(1)}) custom-call(f32[8,5,8,128]{3,2,1,0:T(8,128)S(1)} %collective-permute-done.8.refs_0_, f32[9,5,8,128]{3,2,1,0:T(8,128)S(1)} %collective-permute-done.2.refs_0_.refs_1_, ...), custom_call_target="tpu_custom_call" | custom-call | tf_op jit(solution)/shard_map/forward/pallas_call | solution.py:341
  50.3 0.7 collective-permute-start.18
  51.0 3.9 %forward.5 = (f32[2,25,8,512]{3,2,1,0:T(8,128)S(1)}, f32[2,15,8,512]{3,2,1,0:T(8,128)S(1)}, f32[2,20,8,512]{3,2,1,0:T(8,128)S(1)}, f32[2,15,8,512]{3,2,1,0:T(8,128)S(1)}, f32[2,6,8,512]{3,2,1,0:T(8,128)S(1)}) custom-call(f32[8,5,8,128]{3,2,1,0:T(8,128)S(1)} %collective-permute-done.5.refs_0_, f32[9,5,8,128]{3,2,1,0:T(8,128)S(1)} %collective-permute-done.2.refs_0_.refs_1_, ...), custom_call_target="tpu_custom_call" | custom-call | tf_op jit(solution)/shard_map/forward/pallas_call | solution.py:341
  54.9 0.7 collective-permute-start.15
  55.6 2.0 %forward.4 = (f32[2,25,8,512]{3,2,1,0:T(8,128)S(1)}, f32[2,15,8,512]{3,2,1,0:T(8,128)S(1)}, f32[2,20,8,512]{3,2,1,0:T(8,128)S(1)}, f32[2,15,8,512]{3,2,1,0:T(8,128)S(1)}, f32[2,6,8,512]{3,2,1,0:T(8,128)S(1)}) custom-call(f32[9,5,8,128]{3,2,1,0:T(8,128)S(1)} %collective-permute-done.2.refs_0_.refs_1_, ...), custom_call_target="tpu_custom_call" | custom-call | tf_op jit(solution)/shard_map/forward/pallas_call | solution.py:341
  57.5 0.7 collective-permute-start.12
  58.2 0.8 carry.14
  59.0 0.7 collective-permute-start.22
  59.7 0.8 carry.12
  60.5 0.7 collective-permute-start.19
  61.2 0.8 carry.10
  62.0 0.7 collective-permute-start.16
  62.6 0.8 carry.8
  63.5 0.7 collective-permute-start.13
  64.1 0.8 carry.15
  64.9 1.3 %collective-permute-start.23 = (f32[2,6,8,512]{3,2,1,0:T(8,128)S(1)}, f32[2,6,8,512]{3,2,1,0:T(8,128)S(1)}, u32[]{:S(2)}, u32[]{:S(2)}) collective-permute-start(f32[2,6,8,512]{3,2,1,0:T(8,128)S(1)} %carry.15), channel_id=1, source_target_pairs={{8,0},{9,1},{10,2},{11,3},{12,4},{13,5},{14,6},{15,7}} | collective-permute-start | bytes 589832 | tf_op jit(solution)/shard_map/ppermute | solution.py:302
  66.2 0.8 carry.13
  67.0 1.3 %collective-permute-start.20 = (f32[2,6,8,512]{3,2,1,0:T(8,128)S(1)}, f32[2,6,8,512]{3,2,1,0:T(8,128)S(1)}, u32[]{:S(2)}, u32[]{:S(2)}) collective-permute-start(f32[2,6,8,512]{3,2,1,0:T(8,128)S(1)} %carry.13), channel_id=1, source_target_pairs={{8,0},{9,1},{10,2},{11,3},{12,4},{13,5},{14,6},{15,7}} | collective-permute-start | bytes 589832 | tf_op jit(solution)/shard_map/ppermute | solution.py:302
  68.3 0.8 carry.11
  69.1 1.3 %collective-permute-start.17 = (f32[2,6,8,512]{3,2,1,0:T(8,128)S(1)}, f32[2,6,8,512]{3,2,1,0:T(8,128)S(1)}, u32[]{:S(2)}, u32[]{:S(2)}) collective-permute-start(f32[2,6,8,512]{3,2,1,0:T(8,128)S(1)} %carry.11), channel_id=1, source_target_pairs={{8,0},{9,1},{10,2},{11,3},{12,4},{13,5},{14,6},{15,7}} | collective-permute-start | bytes 589832 | tf_op jit(solution)/shard_map/ppermute | solution.py:302
  70.4 0.8 carry.9
  71.2 1.3 %collective-permute-start.14 = (f32[2,6,8,512]{3,2,1,0:T(8,128)S(1)}, f32[2,6,8,512]{3,2,1,0:T(8,128)S(1)}, u32[]{:S(2)}, u32[]{:S(2)}) collective-permute-start(f32[2,6,8,512]{3,2,1,0:T(8,128)S(1)} %carry.9), channel_id=1, source_target_pairs={{8,0},{9,1},{10,2},{11,3},{12,4},{13,5},{14,6},{15,7}} | collective-permute-start | bytes 589832 | tf_op jit(solution)/shard_map/ppermute | solution.py:302
  72.5 25.8 %collective-permute-done.23.refs_2_ = f32[2,6,8,512]{3,2,1,0:T(8,128)S(1)} collective-permute-done((f32[2,6,8,512]{3,2,1,0:T(8,128)S(1)}, f32[2,6,8,512]{3,2,1,0:T(8,128)S(1)}, u32[]{:S(2)}, u32[]{:S(2)}) %collective-permute-start.23) | collective-permute-done | bytes 196640 | tf_op jit(solution)/shard_map/ppermute | solution.py:302
  98.3 0.9 cotangent.7.refs_3_
  99.2 3.3 %collective-permute-done.20.refs_2_ = f32[2,6,8,512]{3,2,1,0:T(8,128)S(1)} collective-permute-done((f32[2,6,8,512]{3,2,1,0:T(8,128)S(1)}, f32[2,6,8,512]{3,2,1,0:T(8,128)S(1)}, u32[]{:S(2)}, u32[]{:S(2)}) %collective-permute-start.20) | collective-permute-done | bytes 196640 | tf_op jit(solution)/shard_map/ppermute | solution.py:302
  102.5 0.8 cotangent.6.refs_2_
  103.4 2.3 %collective-permute-done.17.refs_2_ = f32[2,6,8,512]{3,2,1,0:T(8,128)S(1)} collective-permute-done((f32[2,6,8,512]{3,2,1,0:T(8,128)S(1)}, f32[2,6,8,512]{3,2,1,0:T(8,128)S(1)}, u32[]{:S(2)}, u32[]{:S(2)}) %collective-permute-start.17) | collective-permute-done | bytes 196640 | tf_op jit(solution)/shard_map/ppermute | solution.py:302
  105.7 0.8 cotangent.5.refs_1_
  106.5 1.3 collective-permute-done.14.refs_2_
  107.8 0.8 cotangent.4.refs_0_
  108.7 1.8 %stencil.1 = f32[8,5,8,512]{3,2,1,0:T(8,128)} custom-call(f32[2,15,8,512]{3,2,1,0:T(8,128)S(1)} %cotangent.4.refs_0_, f32[2,15,8,512]{3,2,1,0:T(8,128)S(1)} %cotangent.5.refs_1_, f32[2,15,8,512]{3,2,1,0:T(8,128)S(1)} %cotangent.6.refs_2_, f32[2,15,8,512]{3,2,1,0:T(8,128)S(1)} %cotangent.7.refs_3_), custom_call_target="tpu_custom_call" | custom-call | tf_op jit(solution)/shard_map/stencil/pallas_call | solution.py:385
  110.4 3.5 %all-to-all-start.1 = ((f32[8,5,8,512]{3,2,1,0:T(8,128)}), f32[8,5,8,512]{3,2,1,0:T(8,128)S(1)}, u32[]{:S(2)}, u32[]{:S(2)}) async-start(f32[8,5,8,512]{3,2,1,0:T(8,128)} %stencil.1), calls=%async_computation.1 | async-start | bytes 1310720 | tf_op jit(solution)/shard_map/all_to_all | solution.py:393
  114.0 1.1 copy-done.3
  115.1 1.6 %assemble.1 = (f32[5,2,6,4096]{3,2,1,0:T(8,128)S(1)}, f32[5,3,6,4096]{3,2,1,0:T(8,128)}) custom-call(f32[2,25,8,512]{3,2,1,0:T(8,128)S(1)} %copy-done.3, f32[2,25,8,512]{3,2,1,0:T(8,128)S(1)} %get-tuple-element.32.refs_1_, f32[2,25,8,512]{3,2,1,0:T(8,128)S(1)} %get-tuple-element.34.refs_2_, f32[2,25,8,512]{3,2,1,0:T(8,128)S(1)} %get-tuple-element.36.refs_3_), custom_call_target="tpu_custom_call" | custom-call | tf_op jit(solution)/shard_map/assemble/pallas_call | solution.py:394
  116.7 1.7 %copy.8 = f32[5,2,6,4096]{3,1,2,0:T(2,128)} copy(f32[5,2,6,4096]{3,2,1,0:T(8,128)S(1)} %get-tuple-element.55) | data formatting | bytes 1966080
  118.4 6.7 %all-to-all-done.1.in_ref = f32[8,5,8,512]{3,2,1,0:T(8,128)S(1)} async-done(((f32[8,5,8,512]{3,2,1,0:T(8,128)}), f32[8,5,8,512]{3,2,1,0:T(8,128)S(1)}, u32[]{:S(2)}, u32[]{:S(2)}) %all-to-all-start.1) | async-done | bytes 655392 | tf_op jit(solution)/shard_map/all_to_all | solution.py:393
  125.1 0.9 combine.1
  (43 shorter events, 7.4 us)
Async XLA Ops:
  0.6 41.1 %copy-start = (f32[5,3,6,4096]{3,2,1,0:T(8,128)S(1)}, f32[5,3,6,4096]{3,2,1,0:T(8,128)}, u32[]{:S(2)}) copy-start(f32[5,3,6,4096]{3,2,1,0:T(8,128)} %refs_8_.7) | copy-start | bytes 4423684
  0.6 1.2 copy-start.4
  1.8 0.7 copy-start.7
  2.5 39.3 %copy-start.1 = (f32[5,6,4096]{2,1,0:T(8,128)S(1)}, f32[5,6,4096]{2,1,0:T(8,128)}, u32[]{:S(2)}) copy-start(f32[5,6,4096]{2,1,0:T(8,128)} %refs_9_.7) | copy-start | bytes 1474564
  19.3 0.7 copy-start.5
  20.6 12.4 %collective-permute-start = (f32[9,5,8,128]{3,2,1,0:T(8,128)S(1)}, f32[9,5,8,128]{3,2,1,0:T(8,128)S(1)}, u32[]{:S(2)}, u32[]{:S(2)}) collective-permute-start(f32[9,5,8,128]{3,2,1,0:T(8,128)S(1)} %get-tuple-element.29.refs_6_.refs_7_), channel_id=1, source_target_pairs={{0,8},{8,16},{16,24},{1,9},{9,17},{17,25},{2,10},{10,18},{18,26},{... | collective-permute-start | bytes 552968 | tf_op jit(solution)/shard_map/ppermute | solution.py:299
  24.1 9.6 %collective-permute-start.9 = (f32[8,5,8,128]{3,2,1,0:T(8,128)S(1)}, f32[8,5,8,128]{3,2,1,0:T(8,128)S(1)}, u32[]{:S(2)}, u32[]{:S(2)}) collective-permute-start(f32[8,5,8,128]{3,2,1,0:T(8,128)S(1)} %get-tuple-element.35.refs_6_), channel_id=1, source_target_pairs={{0,8},{8,16},{16,24},{1,9},{9,17},{17,25},{2,10},{10,18},{18,26},{... | collective-permute-start | bytes 491528 | tf_op jit(solution)/shard_map/ppermute | solution.py:299
  27.6 8.1 %collective-permute-start.6 = (f32[8,5,8,128]{3,2,1,0:T(8,128)S(1)}, f32[8,5,8,128]{3,2,1,0:T(8,128)S(1)}, u32[]{:S(2)}, u32[]{:S(2)}) collective-permute-start(f32[8,5,8,128]{3,2,1,0:T(8,128)S(1)} %get-tuple-element.33.refs_6_), channel_id=1, source_target_pairs={{0,8},{8,16},{16,24},{1,9},{9,17},{17,25},{2,10},{10,18},{18,26},{... | collective-permute-start | bytes 491528 | tf_op jit(solution)/shard_map/ppermute | solution.py:299
  31.1 7.2 %collective-permute-start.3 = (f32[8,5,8,128]{3,2,1,0:T(8,128)S(1)}, f32[8,5,8,128]{3,2,1,0:T(8,128)S(1)}, u32[]{:S(2)}, u32[]{:S(2)}) collective-permute-start(f32[8,5,8,128]{3,2,1,0:T(8,128)S(1)} %get-tuple-element.31.refs_6_), channel_id=1, source_target_pairs={{0,8},{8,16},{16,24},{1,9},{9,17},{17,25},{2,10},{10,18},{18,26},{... | collective-permute-start | bytes 491528 | tf_op jit(solution)/shard_map/ppermute | solution.py:299
  33.0 6.0 %collective-permute-start.1 = (f32[9,5,8,128]{3,2,1,0:T(8,128)S(1)}, f32[9,5,8,128]{3,2,1,0:T(8,128)S(1)}, u32[]{:S(2)}, u32[]{:S(2)}) collective-permute-start(f32[9,5,8,128]{3,2,1,0:T(8,128)S(1)} %collective-permute-done.refs_4_.refs_5_), channel_id=1, source_target_pairs={{8,16},{16,24},{9,17},{17,25},{10,18},{18,26},{11,19},{19,27},{12,... | collective-permute-start | bytes 552968 | tf_op jit(solution)/shard_map/ppermute | solution.py:299
  33.7 6.0 %collective-permute-start.10 = (f32[8,5,8,128]{3,2,1,0:T(8,128)S(1)}, f32[8,5,8,128]{3,2,1,0:T(8,128)S(1)}, u32[]{:S(2)}, u32[]{:S(2)}) collective-permute-start(f32[8,5,8,128]{3,2,1,0:T(8,128)S(1)} %collective-permute-done.9.refs_4_), channel_id=1, source_target_pairs={{8,16},{16,24},{9,17},{17,25},{10,18},{18,26},{11,19},{19,27},{12,... | collective-permute-start | bytes 491528 | tf_op jit(solution)/shard_map/ppermute | solution.py:299
  35.7 4.6 %collective-permute-start.7 = (f32[8,5,8,128]{3,2,1,0:T(8,128)S(1)}, f32[8,5,8,128]{3,2,1,0:T(8,128)S(1)}, u32[]{:S(2)}, u32[]{:S(2)}) collective-permute-start(f32[8,5,8,128]{3,2,1,0:T(8,128)S(1)} %collective-permute-done.6.refs_4_), channel_id=1, source_target_pairs={{8,16},{16,24},{9,17},{17,25},{10,18},{18,26},{11,19},{19,27},{12,... | collective-permute-start | bytes 491528 | tf_op jit(solution)/shard_map/ppermute | solution.py:299
  38.3 2.7 %collective-permute-start.4 = (f32[8,5,8,128]{3,2,1,0:T(8,128)S(1)}, f32[8,5,8,128]{3,2,1,0:T(8,128)S(1)}, u32[]{:S(2)}, u32[]{:S(2)}) collective-permute-start(f32[8,5,8,128]{3,2,1,0:T(8,128)S(1)} %collective-permute-done.3.refs_4_), channel_id=1, source_target_pairs={{8,16},{16,24},{9,17},{17,25},{10,18},{18,26},{11,19},{19,27},{12,... | collective-permute-start | bytes 491528 | tf_op jit(solution)/shard_map/ppermute | solution.py:299
  39.0 2.8 %collective-permute-start.2 = (f32[9,5,8,128]{3,2,1,0:T(8,128)S(1)}, f32[9,5,8,128]{3,2,1,0:T(8,128)S(1)}, u32[]{:S(2)}, u32[]{:S(2)}) collective-permute-start(f32[9,5,8,128]{3,2,1,0:T(8,128)S(1)} %collective-permute-done.1.refs_2_.refs_3_), channel_id=1, source_target_pairs={{16,24},{17,25},{18,26},{19,27},{20,28},{21,29},{22,30},{23,31}} | collective-permute-start | bytes 552968 | tf_op jit(solution)/shard_map/ppermute | solution.py:299
  39.6 2.1 %collective-permute-start.11 = (f32[8,5,8,128]{3,2,1,0:T(8,128)S(1)}, f32[8,5,8,128]{3,2,1,0:T(8,128)S(1)}, u32[]{:S(2)}, u32[]{:S(2)}) collective-permute-start(f32[8,5,8,128]{3,2,1,0:T(8,128)S(1)} %collective-permute-done.10.refs_2_), channel_id=1, source_target_pairs={{16,24},{17,25},{18,26},{19,27},{20,28},{21,29},{22,30},{23,31}} | collective-permute-start | bytes 491528 | tf_op jit(solution)/shard_map/ppermute | solution.py:299
  40.3 6.0 %collective-permute-start.8 = (f32[8,5,8,128]{3,2,1,0:T(8,128)S(1)}, f32[8,5,8,128]{3,2,1,0:T(8,128)S(1)}, u32[]{:S(2)}, u32[]{:S(2)}) collective-permute-start(f32[8,5,8,128]{3,2,1,0:T(8,128)S(1)} %collective-permute-done.7.refs_2_), channel_id=1, source_target_pairs={{16,24},{17,25},{18,26},{19,27},{20,28},{21,29},{22,30},{23,31}} | collective-permute-start | bytes 491528 | tf_op jit(solution)/shard_map/ppermute | solution.py:299
  41.0 9.9 %collective-permute-start.5 = (f32[8,5,8,128]{3,2,1,0:T(8,128)S(1)}, f32[8,5,8,128]{3,2,1,0:T(8,128)S(1)}, u32[]{:S(2)}, u32[]{:S(2)}) collective-permute-start(f32[8,5,8,128]{3,2,1,0:T(8,128)S(1)} %collective-permute-done.4.refs_2_), channel_id=1, source_target_pairs={{16,24},{17,25},{18,26},{19,27},{20,28},{21,29},{22,30},{23,31}} | collective-permute-start | bytes 491528 | tf_op jit(solution)/shard_map/ppermute | solution.py:299
  45.7 12.5 %collective-permute-start.21 = (f32[2,6,8,512]{3,2,1,0:T(8,128)S(1)}, f32[2,6,8,512]{3,2,1,0:T(8,128)S(1)}, u32[]{:S(2)}, u32[]{:S(2)}) collective-permute-start(f32[2,6,8,512]{3,2,1,0:T(8,128)S(1)} %get-tuple-element.54.b_ref), channel_id=1, source_target_pairs={{24,16},{25,17},{26,18},{27,19},{28,20},{29,21},{30,22},{31,23}} | collective-permute-start | bytes 589832 | tf_op jit(solution)/shard_map/ppermute | solution.py:302
  50.3 9.4 %collective-permute-start.18 = (f32[2,6,8,512]{3,2,1,0:T(8,128)S(1)}, f32[2,6,8,512]{3,2,1,0:T(8,128)S(1)}, u32[]{:S(2)}, u32[]{:S(2)}) collective-permute-start(f32[2,6,8,512]{3,2,1,0:T(8,128)S(1)} %get-tuple-element.50.b_ref), channel_id=1, source_target_pairs={{24,16},{25,17},{26,18},{27,19},{28,20},{29,21},{30,22},{31,23}} | collective-permute-start | bytes 589832 | tf_op jit(solution)/shard_map/ppermute | solution.py:302
  54.9 3.4 %copy-start.6 = (f32[5]{0:T(128)S(1)}, f32[5]{0:T(128)}, u32[]{:S(2)}) copy-start(f32[5]{0:T(128)} %mix_ref.25) | copy-start | bytes 64
  54.9 6.3 %collective-permute-start.15 = (f32[2,6,8,512]{3,2,1,0:T(8,128)S(1)}, f32[2,6,8,512]{3,2,1,0:T(8,128)S(1)}, u32[]{:S(2)}, u32[]{:S(2)}) collective-permute-start(f32[2,6,8,512]{3,2,1,0:T(8,128)S(1)} %get-tuple-element.46.b_ref), channel_id=1, source_target_pairs={{24,16},{25,17},{26,18},{27,19},{28,20},{29,21},{30,22},{31,23}} | collective-permute-start | bytes 589832 | tf_op jit(solution)/shard_map/ppermute | solution.py:302
  57.5 5.9 %copy-start.2 = (f32[2,25,8,512]{3,2,1,0:T(8,128)}, f32[2,25,8,512]{3,2,1,0:T(8,128)S(1)}, u32[]{:S(2)}) copy-start(f32[2,25,8,512]{3,2,1,0:T(8,128)S(1)} %get-tuple-element.30.refs_0_) | copy-start | bytes 2457604
  57.5 5.1 %collective-permute-start.12 = (f32[2,6,8,512]{3,2,1,0:T(8,128)S(1)}, f32[2,6,8,512]{3,2,1,0:T(8,128)S(1)}, u32[]{:S(2)}, u32[]{:S(2)}) collective-permute-start(f32[2,6,8,512]{3,2,1,0:T(8,128)S(1)} %get-tuple-element.42.b_ref), channel_id=1, source_target_pairs={{24,16},{25,17},{26,18},{27,19},{28,20},{29,21},{30,22},{31,23}} | collective-permute-start | bytes 589832 | tf_op jit(solution)/shard_map/ppermute | solution.py:302
  59.0 5.1 %collective-permute-start.22 = (f32[2,6,8,512]{3,2,1,0:T(8,128)S(1)}, f32[2,6,8,512]{3,2,1,0:T(8,128)S(1)}, u32[]{:S(2)}, u32[]{:S(2)}) collective-permute-start(f32[2,6,8,512]{3,2,1,0:T(8,128)S(1)} %carry.14), channel_id=1, source_target_pairs={{16,8},{17,9},{18,10},{19,11},{20,12},{21,13},{22,14},{23,15}} | collective-permute-start | bytes 589832 | tf_op jit(solution)/shard_map/ppermute | solution.py:302
  60.5 5.7 %collective-permute-start.19 = (f32[2,6,8,512]{3,2,1,0:T(8,128)S(1)}, f32[2,6,8,512]{3,2,1,0:T(8,128)S(1)}, u32[]{:S(2)}, u32[]{:S(2)}) collective-permute-start(f32[2,6,8,512]{3,2,1,0:T(8,128)S(1)} %carry.12), channel_id=1, source_target_pairs={{16,8},{17,9},{18,10},{19,11},{20,12},{21,13},{22,14},{23,15}} | collective-permute-start | bytes 589832 | tf_op jit(solution)/shard_map/ppermute | solution.py:302
  62.0 6.4 %collective-permute-start.16 = (f32[2,6,8,512]{3,2,1,0:T(8,128)S(1)}, f32[2,6,8,512]{3,2,1,0:T(8,128)S(1)}, u32[]{:S(2)}, u32[]{:S(2)}) collective-permute-start(f32[2,6,8,512]{3,2,1,0:T(8,128)S(1)} %carry.10), channel_id=1, source_target_pairs={{16,8},{17,9},{18,10},{19,11},{20,12},{21,13},{22,14},{23,15}} | collective-permute-start | bytes 589832 | tf_op jit(solution)/shard_map/ppermute | solution.py:302
  63.4 34.9 %copy-start.8 = (f32[5]{0:T(128)S(1)}, f32[5]{0:T(128)}, u32[]{:S(2)}) copy-start(f32[5]{0:T(128)} %weight_ref.9) | copy-start | bytes 64
  63.5 7.0 %collective-permute-start.13 = (f32[2,6,8,512]{3,2,1,0:T(8,128)S(1)}, f32[2,6,8,512]{3,2,1,0:T(8,128)S(1)}, u32[]{:S(2)}, u32[]{:S(2)}) collective-permute-start(f32[2,6,8,512]{3,2,1,0:T(8,128)S(1)} %carry.8), channel_id=1, source_target_pairs={{16,8},{17,9},{18,10},{19,11},{20,12},{21,13},{22,14},{23,15}} | collective-permute-start | bytes 589832 | tf_op jit(solution)/shard_map/ppermute | solution.py:302
  64.9 33.4 %collective-permute-start.23 = (f32[2,6,8,512]{3,2,1,0:T(8,128)S(1)}, f32[2,6,8,512]{3,2,1,0:T(8,128)S(1)}, u32[]{:S(2)}, u32[]{:S(2)}) collective-permute-start(f32[2,6,8,512]{3,2,1,0:T(8,128)S(1)} %carry.15), channel_id=1, source_target_pairs={{8,0},{9,1},{10,2},{11,3},{12,4},{13,5},{14,6},{15,7}} | collective-permute-start | bytes 589832 | tf_op jit(solution)/shard_map/ppermute | solution.py:302
  67.0 35.5 %collective-permute-start.20 = (f32[2,6,8,512]{3,2,1,0:T(8,128)S(1)}, f32[2,6,8,512]{3,2,1,0:T(8,128)S(1)}, u32[]{:S(2)}, u32[]{:S(2)}) collective-permute-start(f32[2,6,8,512]{3,2,1,0:T(8,128)S(1)} %carry.13), channel_id=1, source_target_pairs={{8,0},{9,1},{10,2},{11,3},{12,4},{13,5},{14,6},{15,7}} | collective-permute-start | bytes 589832 | tf_op jit(solution)/shard_map/ppermute | solution.py:302
  69.1 36.6 %collective-permute-start.17 = (f32[2,6,8,512]{3,2,1,0:T(8,128)S(1)}, f32[2,6,8,512]{3,2,1,0:T(8,128)S(1)}, u32[]{:S(2)}, u32[]{:S(2)}) collective-permute-start(f32[2,6,8,512]{3,2,1,0:T(8,128)S(1)} %carry.11), channel_id=1, source_target_pairs={{8,0},{9,1},{10,2},{11,3},{12,4},{13,5},{14,6},{15,7}} | collective-permute-start | bytes 589832 | tf_op jit(solution)/shard_map/ppermute | solution.py:302
  71.2 36.6 %collective-permute-start.14 = (f32[2,6,8,512]{3,2,1,0:T(8,128)S(1)}, f32[2,6,8,512]{3,2,1,0:T(8,128)S(1)}, u32[]{:S(2)}, u32[]{:S(2)}) collective-permute-start(f32[2,6,8,512]{3,2,1,0:T(8,128)S(1)} %carry.9), channel_id=1, source_target_pairs={{8,0},{9,1},{10,2},{11,3},{12,4},{13,5},{14,6},{15,7}} | collective-permute-start | bytes 589832 | tf_op jit(solution)/shard_map/ppermute | solution.py:302
  110.4 14.6 %all-to-all-start.1 = ((f32[8,5,8,512]{3,2,1,0:T(8,128)}), f32[8,5,8,512]{3,2,1,0:T(8,128)S(1)}, u32[]{:S(2)}, u32[]{:S(2)}) async-start(f32[8,5,8,512]{3,2,1,0:T(8,128)} %stencil.1), calls=%async_computation.1 | async-start | bytes 1310720 | tf_op jit(solution)/shard_map/all_to_all | solution.py:393
  114.0 1.1 copy-start.3

commit v4 on v3

--- a/solution.py
+++ b/solution.py
@@ -17,39 +17,64 @@
 MIX_LANE = 64
 
 
-def pack_kernel(weight_ref, p_ref, out_ref):
+def write_strips(column, k, out_ref):
+    rows, width = column.shape
+    for s in range(out_ref.shape[0]):
+        before = (R * s - 1) % rows
+        after = (R * (s + 1)) % rows
+        strip = jnp.concatenate(
+            [
+                column[R * s : R * (s + 1)],
+                column[after : after + 1],
+                column[before : before + 1],
+            ],
+            axis=0,
+        )
+        for t in range(width // EDGE):
+            out_ref[s, t, k] = strip[:, EDGE * t : EDGE * (t + 1)]
+
+
+def pack_kernel(weight_ref, mix_ref, p_ref, out_ref, column_ref):
     planes, rows, width = p_ref.shape
     for k in range(planes):
-        w = weight_ref[k]
-        for s in range(out_ref.shape[0]):
-            before = (R * s - 1) % rows
-            after = (R * (s + 1)) % rows
-            strip = w * jnp.concatenate(
-                [
-                    p_ref[k, R * s : R * (s + 1), :],
-                    p_ref[k, after : after + 1, :],
-                    p_ref[k, before : before + 1, :],
-                ],
-                axis=0,
-            )
-            for t in range(width // EDGE):
-                out_ref[s, t, k] = strip[:, EDGE * t : EDGE * (t + 1)]
-
-
-def split_kernel(mix_ref, in_ref, *outs):
+        column = weight_ref[k] * p_ref[k]
+        column_ref[k, 0:rows] = column
+        column_ref[k, rows:] = jnp.full((SUB, width), mix_ref[k] - 1.0, F32)
+        write_strips(column, k, out_ref)
+
+
+def repack_kernel(column_ref, out_ref):
+    for k in range(column_ref.shape[0]):
+        write_strips(column_ref[k, 0 : column_ref.shape[1] - SUB], k, out_ref)
+
+
+def split_kernel(column_ref, in_ref, *outs):
     tiles, planes = in_ref.shape[0:2]
     length = tiles // len(outs)
     lane = lax.broadcasted_iota(jnp.int32, (SUB, EDGE), 1)
     for c, out_ref in enumerate(outs):
         out_ref[0:length] = in_ref[length * c : length * (c + 1)]
     for k in range(planes):
-        edge = jnp.where(lane == MIX_LANE, mix_ref[k] - 1.0, 0.0)
+        edge = jnp.where(lane == MIX_LANE, column_ref[k, column_ref.shape[1] - SUB :, 0:EDGE], 0.0)
         for c in range(len(outs)):
             after = in_ref[(length * (c + 1)) % tiles, k]
             before = in_ref[(length * c - 1) % tiles, k]
             edge = jnp.where(lane == 2 * c, pltpu.roll(after, 2 * c, 1), edge)
             edge = jnp.where(lane == (2 * c - 1) % EDGE, pltpu.roll(before, 2 * c, 1), edge)
         outs[0][length, k] = edge
+
+
+def edges_kernel(*refs):
+    strips = refs[:-2]
+    beside_ref, excess_ref = refs[-2:]
+    for group, strip_ref in enumerate(strips):
+        planes = strip_ref.shape[1]
+        for k in range(planes):
+            edge = strip_ref[strip_ref.shape[0] - 1, k]
+            at = group * planes + k
+            excess_ref[at] = jnp.broadcast_to(edge[:, MIX_LANE : MIX_LANE + 1], edge.shape)
+            for c in range(CHUNKS):
+                beside_ref[c, at] = pltpu.roll(edge, (EDGE - 2 * c) % EDGE, 1)
 
 
 def row_up(x):
@@ -94,8 +119,8 @@
 
 
 def forward_kernel(groups, planes, chunk, length, *refs):
-    strips = refs[: 2 * groups]
-    obs_ref, noise_ref = refs[2 * groups : 2 * groups + 2]
+    strips = refs[:groups]
+    beside_ref, excess_ref, obs_ref, noise_ref = refs[groups : groups + 4]
     map_ref, m_ref, a_ref, src_ref, b_ref = refs[-5:]
     step = pl.program_id(0)
     width = obs_ref.shape[-1]
@@ -111,13 +136,15 @@
     psi_before = psi
     keeps = []
     for group in range(groups):
-        strip_ref, edge_ref = strips[2 * group : 2 * group + 2]
+        strip_ref = strips[group]
         own = group == groups - 1
         for k in range(planes):
-            edge = edge_ref[edge_ref.shape[0] - 1, k]
-            excess = edge[:, MIX_LANE : MIX_LANE + 1]
-            mix = 1.0 + excess
-            beside = pltpu.roll(edge, (EDGE - 2 * chunk) % EDGE, 1)
+            beside = beside_ref[chunk, group * planes + k]
+            excess_tile = excess_ref[group * planes + k]
+            excess_ext = jnp.concatenate([excess_tile] * (span + 2), axis=1)
+            excess = excess_ext[:, EDGE:-EDGE]
+            mix_ext = jnp.concatenate([1.0 + excess_tile] * (span + 2), axis=1)
+            mix = mix_ext[:, EDGE:-EDGE]
             left = jnp.where(at_start, beside, strip_ref[jnp.maximum(first - 1, 0), k])
             right = jnp.where(at_end, beside, strip_ref[jnp.minimum(first + span, length - 1), k])
             tiles = [strip_ref[first + t, k] for t in range(span)]
@@ -144,7 +171,7 @@
                 off * a[1] + m1 * a[3] - excess * a_before[3],
             ]
             a_before, a = (a, new_a)
-            psi, psi_before = (mix * psi - excess * psi_before - ext, psi)
+            psi, psi_before = (mix_ext * psi - excess_ext * psi_before - ext, psi)
             if own:
                 slope_rows = 0.5 * (row_up(psi) - row_down(psi))[:, EDGE:-EDGE]
                 slope_cols = 0.5 * (col_next(psi) - col_prev(psi))
@@ -301,31 +328,59 @@
     def descend(x, hop):
         return lax.ppermute(x, "plane", [(groups - 1 - hop, groups - 2 - hop)])
 
-    packed = pl.pallas_call(
+    packed_shape = shape(slabs, tiles, planes, SUB, EDGE)
+    packed, column = pl.pallas_call(
         pack_kernel,
-        out_shape=shape(slabs, tiles, planes, SUB, EDGE),
-        in_specs=[SCALARS, WHOLE],
+        out_shape=(packed_shape, shape(planes, rows + SUB, width)),
+        in_specs=[SCALARS, SCALARS, WHOLE],
+        out_specs=(WHOLE, WHOLE),
+        compiler_params=params(),
+        name="pack",
+    )(lens_weight, mixing, potential)
+
+    def to_rows(packed, column):
+        strip = lax.all_to_all(packed, "slab", split_axis=0, concat_axis=0, tiled=True)
+        return pl.pallas_call(
+            split_kernel,
+            out_shape=tuple(
+                shape(length + (c == 0), planes, SUB, EDGE) for c in range(CHUNKS)
+            ),
+            in_specs=[WHOLE, WHOLE],
+            out_specs=(WHOLE,) * CHUNKS,
+            compiler_params=params(),
+            name="split",
+        )(column, strip.reshape(slabs * tiles, planes, SUB, EDGE))
+
+    column_before = climb(column, 0)
+    pieces = to_rows(packed, column)
+    two_up = [(i, i + 2) for i in range(groups - 2)]
+    further = [[lax.ppermute(piece, "plane", two_up)] for piece in pieces]
+    packed_before = pl.pallas_call(
+        repack_kernel,
+        out_shape=packed_shape,
+        in_specs=[WHOLE],
         out_specs=WHOLE,
         compiler_params=params(),
-        name="pack",
-    )(lens_weight, potential)
-    own = lax.all_to_all(packed, "slab", split_axis=0, concat_axis=0, tiled=True)
-    own = own.reshape(slabs * tiles, planes, SUB, EDGE)
-    pieces = pl.pallas_call(
-        split_kernel,
-        out_shape=tuple(
-            shape(length + (c == 0), planes, SUB, EDGE) for c in range(CHUNKS)
+        name="repack",
+    )(column_before)
+    pieces_before = to_rows(packed_before, column_before)
+    for c in range(CHUNKS):
+        further[c][0] = lax.optimization_barrier((further[c][0], pieces_before[c]))[0]
+    for hop in range(2, groups - 1):
+        for c in range(CHUNKS):
+            further[c].insert(0, climb(further[c][0], hop))
+    strips = [further[c] + [pieces_before[c], pieces[c]] for c in range(CHUNKS)]
+    beside, excess = pl.pallas_call(
+        edges_kernel,
+        out_shape=(
+            shape(CHUNKS, groups * planes, SUB, EDGE),
+            shape(groups * planes, SUB, EDGE),
         ),
-        in_specs=[SCALARS, WHOLE],
-        out_specs=(WHOLE,) * CHUNKS,
-        compiler_params=params(),
-        name="split",
-    )(mixing, own)
-    strips = [[piece] for piece in pieces]
-    for turn in range(CHUNKS + groups - 2):
-        for c in range(CHUNKS):
-            if 0 <= turn - c < groups - 1:
-                strips[c].insert(0, climb(strips[c][0], turn - c))
+        in_specs=[WHOLE] * groups,
+        out_specs=(WHOLE, WHOLE),
+        compiler_params=params(),
+        name="edges",
+    )(*strips[0])
 
     state = block_of(R, SUB, span)
     triple = block_of(3 * planes, SUB, span)
@@ -348,11 +403,11 @@
                 shape(steps, 3 * planes, SUB, span),
                 shape(steps, R, SUB, span),
             ),
-            in_specs=[WHOLE] * (2 * groups) + [columns_of(planes, 3, R), columns_of(planes, R)],
+            in_specs=[WHOLE] * (groups + 2) + [columns_of(planes, 3, R), columns_of(planes, R)],
             out_specs=(quint, triple, quad, triple, state),
             compiler_params=params(),
             name="forward",
-        )(*[x for pair in zip(strips[c], strips[0]) for x in pair], observed, noise_weight)
+        )(*strips[c], beside, excess, observed, noise_weight)
         maps.append(map_piece)
         work.append(held)
 

time: 127 us -> 141 us (1.11)
  blocking collectives: 16.1 us -> 0 us
  waiting for transfers between devices: 42.7 us -> 56.7 us
  starting transfers between devices: 31.8 us -> 40.8 us
  local copies, waits for them, and re-layouts: 5.34 us -> 13.6 us
    all_to_all x1 -> x0, blocking collectives: 16.1 us -> none  [on_device(): lax.all_to_all(packed, 'slab', split_axis=0, concat_axis=0, tiled=True)]
    ppermute x0 -> x4, starting transfers between devices: none -> 11.3 us  [on_device(): further = [[lax.ppermute(piece, 'plane', two_up)] for piece in pieces]]
    ppermute x12 -> x5, starting transfers between devices: 17.7 us -> 7.6 us  [climb(): lax.ppermute(x, 'plane', [(i, i + 1) for i in range(hop, groups - 1)])]
    unnamed x19 -> x45, local copies, waits for them, and re-layouts: 5.34 us -> 13.6 us
    all_to_all x0 -> x2, starting transfers between devices: none -> 7.28 us  [to_rows(): lax.all_to_all(packed, 'slab', split_axis=0, concat_axis=0, tiled=True)]
    ppermute x0 -> x4, waiting for transfers between devices: none -> 5.53 us  [on_device(): further = [[lax.ppermute(piece, 'plane', two_up)] for piece in pieces]]
    ppermute x12 -> x5, waiting for transfers between devices: 3.27 us -> 8.46 us  [climb(): lax.ppermute(x, 'plane', [(i, i + 1) for i in range(hop, groups - 1)])]
    pallas_call x4, Pallas kernels: 13.7 us -> 10.1 us  [on_device(): pl.pallas_call(functools.partial(forward_kernel, groups, planes, c, lengt...]
  transfers between devices with their start and end apart: 25 -> 24, of which waited for: 7 -> 10; matrix products, arithmetic and copies ran while one was open for 1% -> 1% of each run, Pallas kernels for 19% -> 16%
where the time goes in v4:
time: 141 us; the launch traced here: 140 us
  waiting for transfers between devices  56.7 us (40%)
  starting transfers between devices  40.8 us (29%)
  Pallas kernels  27.4 us (19%)
  local copies, waits for them, and re-layouts  13.6 us (10%)
    ppermute x12, waiting for transfers between devices, descend(): return lax.ppermute(x, 'plane', [(groups - 1 - hop, groups - 2 - hop)])  35 us
    unnamed x45, local copies, waits for them, and re-layouts  13.6 us
    ppermute x4, starting transfers between devices, on_device(): further = [[lax.ppermute(piece, 'plane', two_up)] for piece in pieces]  11.3 us
    ppermute x12, starting transfers between devices, descend(): return lax.ppermute(x, 'plane', [(groups - 1 - hop, groups - 2 - hop)])  10.8 us
    pallas_call x4, Pallas kernels, on_device(): pl.pallas_call(functools.partial(forward_kernel, groups, planes, c, lengt...  10.1 us
    ppermute x5, waiting for transfers between devices, climb(): lax.ppermute(x, 'plane', [(i, i + 1) for i in range(hop, groups - 1)])  8.46 us
    ppermute x5, starting transfers between devices, climb(): lax.ppermute(x, 'plane', [(i, i + 1) for i in range(hop, groups - 1)])  7.6 us
    all_to_all x2, starting transfers between devices, to_rows(): lax.all_to_all(packed, 'slab', split_axis=0, concat_axis=0, tiled=True)  7.28 us
  transfers between devices with their start and end apart: 24, of which 10 were waited for; matrix products, arithmetic and copies ran while one was open for 1% of the time, Pallas kernels for 16%

profile of v4, /device:TPU:0, one launch (start us, length us, event | category | flops | bytes accessed | tf_op | source)
XLA Modules:
  0.0 139.6 jit_solution(800011203296852637)
XLA Ops:
  0.6 1.0 copy-done.17
  3.0 1.5 %pack.1 = (f32[8,4,5,8,128]{4,3,2,1,0:T(8,128)}, f32[5,56,512]{2,1,0:T(8,128)S(1)}) custom-call(f32[5]{0:T(128)S(1)} %copy-done.20, f32[5]{0:T(128)S(1)} %copy-done.18, f32[5,48,512]{2,1,0:T(8,128)S(1)} %copy-done.17), custom_call_target="tpu_custom_call" | custom-call | tf_op jit(solution)/shard_map/pack/pallas_call | solution.py:332
  4.5 5.0 %collective-permute-start.1 = (f32[5,56,512]{2,1,0:T(8,128)S(1)}, f32[5,56,512]{2,1,0:T(8,128)S(1)}, u32[]{:S(2)}, u32[]{:S(2)}) collective-permute-start(f32[5,56,512]{2,1,0:T(8,128)S(1)} %get-tuple-element.41.column_ref), channel_id=1, source_target_pairs={{0,8},{8,16},{16,24},{1,9},{9,17},{17,25},{2,10},{10,18},{18,26},{... | collective-permute-start | bytes 1720328 | tf_op jit(solution)/shard_map/ppermute | solution.py:326
  9.4 3.7 %all-to-all-start = ((f32[8,4,5,8,128]{4,3,2,1,0:T(8,128)}), f32[8,4,5,8,128]{4,3,2,1,0:T(8,128)S(1)}, u32[]{:S(2)}, u32[]{:S(2)}) async-start(f32[8,4,5,8,128]{4,3,2,1,0:T(8,128)} %get-tuple-element.42), calls=%async_computation | async-start | bytes 1310720 | tf_op jit(solution)/shard_map/all_to_all | solution.py:342
  13.2 8.4 %collective-permute-done.1.column_ref = f32[5,56,512]{2,1,0:T(8,128)S(1)} collective-permute-done((f32[5,56,512]{2,1,0:T(8,128)S(1)}, f32[5,56,512]{2,1,0:T(8,128)S(1)}, u32[]{:S(2)}, u32[]{:S(2)}) %collective-permute-start.1) | collective-permute-done | bytes 573472 | tf_op jit(solution)/shard_map/ppermute | solution.py:326
  21.7 0.8 copy-done.2
  22.5 0.8 copy-done.5
  23.4 0.9 all-to-all-done
  24.3 0.8 copy-done.3
  25.1 3.5 %all-to-all-start.1 = ((f32[8,4,5,8,128]{4,3,2,1,0:T(8,128)}), f32[8,4,5,8,128]{4,3,2,1,0:T(8,128)S(1)}, u32[]{:S(2)}, u32[]{:S(2)}) async-start(f32[8,4,5,8,128]{4,3,2,1,0:T(8,128)} %copy-done.2), calls=%async_computation.1 | async-start | bytes 1310720 | tf_op jit(solution)/shard_map/all_to_all | solution.py:342
  28.7 1.1 copy-done.4
  29.8 1.1 copy-done.16
  30.8 0.8 split.2
  31.6 5.4 %collective-permute-start = (f32[9,5,8,128]{3,2,1,0:T(8,128)S(1)}, f32[9,5,8,128]{3,2,1,0:T(8,128)}, u32[]{:S(2)}, u32[]{:S(2)}) collective-permute-start(f32[9,5,8,128]{3,2,1,0:T(8,128)S(1)} %get-tuple-element.43.refs_3_), channel_id=1, source_target_pairs={{0,16},{8,24},{1,17},{9,25},{2,18},{10,26},{3,19},{11,27},{4,20},{... | collective-permute-start | bytes 552968 | tf_op jit(solution)/shard_map/ppermute | solution.py:357
  37.1 1.9 %collective-permute-start.7 = (f32[8,5,8,128]{3,2,1,0:T(8,128)}, f32[8,5,8,128]{3,2,1,0:T(8,128)}, u32[]{:S(2)}, u32[]{:S(2)}) collective-permute-start(f32[8,5,8,128]{3,2,1,0:T(8,128)} %get-tuple-element.57.refs_3_), channel_id=1, source_target_pairs={{0,16},{8,24},{1,17},{9,25},{2,18},{10,26},{3,19},{11,27},{4,20},{... | collective-permute-start | bytes 491528 | tf_op jit(solution)/shard_map/ppermute | solution.py:357
  39.0 1.9 %collective-permute-start.5 = (f32[8,5,8,128]{3,2,1,0:T(8,128)}, f32[8,5,8,128]{3,2,1,0:T(8,128)}, u32[]{:S(2)}, u32[]{:S(2)}) collective-permute-start(f32[8,5,8,128]{3,2,1,0:T(8,128)} %get-tuple-element.53.refs_3_), channel_id=1, source_target_pairs={{0,16},{8,24},{1,17},{9,25},{2,18},{10,26},{3,19},{11,27},{4,20},{... | collective-permute-start | bytes 491528 | tf_op jit(solution)/shard_map/ppermute | solution.py:357
  41.0 2.0 %collective-permute-start.3 = (f32[8,5,8,128]{3,2,1,0:T(8,128)}, f32[8,5,8,128]{3,2,1,0:T(8,128)}, u32[]{:S(2)}, u32[]{:S(2)}) collective-permute-start(f32[8,5,8,128]{3,2,1,0:T(8,128)} %get-tuple-element.49.refs_3_), channel_id=1, source_target_pairs={{0,16},{8,24},{1,17},{9,25},{2,18},{10,26},{3,19},{11,27},{4,20},{... | collective-permute-start | bytes 491528 | tf_op jit(solution)/shard_map/ppermute | solution.py:357
  42.9 1.1 copy-done.6
  45.7 2.8 %collective-permute-done.5.refs_1_ = f32[8,5,8,128]{3,2,1,0:T(8,128)} collective-permute-done((f32[8,5,8,128]{3,2,1,0:T(8,128)}, f32[8,5,8,128]{3,2,1,0:T(8,128)}, u32[]{:S(2)}, u32[]{:S(2)}) %collective-permute-start.5) | collective-permute-done | bytes 163872 | tf_op jit(solution)/shard_map/ppermute | solution.py:357
  49.2 2.5 %collective-permute-done.3.refs_1_ = f32[8,5,8,128]{3,2,1,0:T(8,128)} collective-permute-done((f32[8,5,8,128]{3,2,1,0:T(8,128)}, f32[8,5,8,128]{3,2,1,0:T(8,128)}, u32[]{:S(2)}, u32[]{:S(2)}) %collective-permute-start.3) | collective-permute-done | bytes 163872 | tf_op jit(solution)/shard_map/ppermute | solution.py:357
  52.3 1.1 edges.1
  53.4 2.5 %forward.7 = (f32[2,25,8,512]{3,2,1,0:T(8,128)S(1)}, f32[2,15,8,512]{3,2,1,0:T(8,128)S(1)}, f32[2,20,8,512]{3,2,1,0:T(8,128)S(1)}, f32[2,15,8,512]{3,2,1,0:T(8,128)S(1)}, f32[2,6,8,512]{3,2,1,0:T(8,128)S(1)}) custom-call(f32[8,5,8,128]{3,2,1,0:T(8,128)S(1)} %collective-permute-done.8.refs_0_, f32[8,5,8,128]{3,2,1,0:T(8,128)} %collective-permute-done.7.refs_1_, ...), custom_call_target="tpu_custom_call" | custom-call | tf_op jit(solution)/shard_map/forward/pallas_call | solution.py:396
  56.7 2.5 %forward.6 = (f32[2,25,8,512]{3,2,1,0:T(8,128)S(1)}, f32[2,15,8,512]{3,2,1,0:T(8,128)S(1)}, f32[2,20,8,512]{3,2,1,0:T(8,128)S(1)}, f32[2,15,8,512]{3,2,1,0:T(8,128)S(1)}, f32[2,6,8,512]{3,2,1,0:T(8,128)S(1)}) custom-call(f32[8,5,8,128]{3,2,1,0:T(8,128)S(1)} %collective-permute-done.6.refs_0_, f32[8,5,8,128]{3,2,1,0:T(8,128)} %collective-permute-done.5.refs_1_, ...), custom_call_target="tpu_custom_call" | custom-call | tf_op jit(solution)/shard_map/forward/pallas_call | solution.py:396
  59.2 0.9 copy-done.7
  60.1 0.8 collective-permute-start.15
  60.9 2.5 %forward.5 = (f32[2,25,8,512]{3,2,1,0:T(8,128)S(1)}, f32[2,15,8,512]{3,2,1,0:T(8,128)S(1)}, f32[2,20,8,512]{3,2,1,0:T(8,128)S(1)}, f32[2,15,8,512]{3,2,1,0:T(8,128)S(1)}, f32[2,6,8,512]{3,2,1,0:T(8,128)S(1)}) custom-call(f32[8,5,8,128]{3,2,1,0:T(8,128)S(1)} %collective-permute-done.4.refs_0_, f32[8,5,8,128]{3,2,1,0:T(8,128)} %collective-permute-done.3.refs_1_, ...), custom_call_target="tpu_custom_call" | custom-call | tf_op jit(solution)/shard_map/forward/pallas_call | solution.py:396
  63.5 0.9 copy-done.9
  65.2 2.5 %forward.4 = (f32[2,25,8,512]{3,2,1,0:T(8,128)S(1)}, f32[2,15,8,512]{3,2,1,0:T(8,128)S(1)}, f32[2,20,8,512]{3,2,1,0:T(8,128)S(1)}, f32[2,15,8,512]{3,2,1,0:T(8,128)S(1)}, f32[2,6,8,512]{3,2,1,0:T(8,128)S(1)}) custom-call(f32[9,5,8,128]{3,2,1,0:T(8,128)S(1)} %collective-permute-done.2.refs_0_, f32[9,5,8,128]{3,2,1,0:T(8,128)} %collective-permute-done.refs_1_, ...), custom_call_target="tpu_custom_call" | custom-call | tf_op jit(solution)/shard_map/forward/pallas_call | solution.py:396
  67.7 0.9 copy-done.11
  75.9 1.3 collective-permute-start.20
  78.0 1.3 collective-permute-start.17
  80.1 1.3 collective-permute-start.14
  82.2 1.3 collective-permute-start.11
  83.5 24.9 %collective-permute-done.20.refs_2_ = f32[2,6,8,512]{3,2,1,0:T(8,128)S(1)} collective-permute-done((f32[2,6,8,512]{3,2,1,0:T(8,128)S(1)}, f32[2,6,8,512]{3,2,1,0:T(8,128)S(1)}, u32[]{:S(2)}, u32[]{:S(2)}) %collective-permute-start.20) | collective-permute-done | bytes 196640 | tf_op jit(solution)/shard_map/ppermute | solution.py:329
  108.4 0.8 cotangent.7.refs_3_
  109.2 3.4 %collective-permute-done.17.refs_2_ = f32[2,6,8,512]{3,2,1,0:T(8,128)S(1)} collective-permute-done((f32[2,6,8,512]{3,2,1,0:T(8,128)S(1)}, f32[2,6,8,512]{3,2,1,0:T(8,128)S(1)}, u32[]{:S(2)}, u32[]{:S(2)}) %collective-permute-start.17) | collective-permute-done | bytes 196640 | tf_op jit(solution)/shard_map/ppermute | solution.py:329
  112.6 0.8 cotangent.6.refs_2_
  113.4 3.4 %collective-permute-done.14.refs_2_ = f32[2,6,8,512]{3,2,1,0:T(8,128)S(1)} collective-permute-done((f32[2,6,8,512]{3,2,1,0:T(8,128)S(1)}, f32[2,6,8,512]{3,2,1,0:T(8,128)S(1)}, u32[]{:S(2)}, u32[]{:S(2)}) %collective-permute-start.14) | collective-permute-done | bytes 196640 | tf_op jit(solution)/shard_map/ppermute | solution.py:329
  116.8 0.8 cotangent.5.refs_1_
  117.7 3.4 %collective-permute-done.11.refs_2_ = f32[2,6,8,512]{3,2,1,0:T(8,128)S(1)} collective-permute-done((f32[2,6,8,512]{3,2,1,0:T(8,128)S(1)}, f32[2,6,8,512]{3,2,1,0:T(8,128)S(1)}, u32[]{:S(2)}, u32[]{:S(2)}) %collective-permute-start.11) | collective-permute-done | bytes 196640 | tf_op jit(solution)/shard_map/ppermute | solution.py:329
  121.0 0.8 cotangent.4.refs_0_
  121.9 1.8 %stencil.1 = f32[8,5,8,512]{3,2,1,0:T(8,128)} custom-call(f32[2,15,8,512]{3,2,1,0:T(8,128)S(1)} %cotangent.4.refs_0_, f32[2,15,8,512]{3,2,1,0:T(8,128)S(1)} %cotangent.5.refs_1_, f32[2,15,8,512]{3,2,1,0:T(8,128)S(1)} %cotangent.6.refs_2_, f32[2,15,8,512]{3,2,1,0:T(8,128)S(1)} %cotangent.7.refs_3_), custom_call_target="tpu_custom_call" | custom-call | tf_op jit(solution)/shard_map/stencil/pallas_call | solution.py:440
  123.7 3.8 %all-to-all-start.2 = ((f32[8,5,8,512]{3,2,1,0:T(8,128)}), f32[8,5,8,512]{3,2,1,0:T(8,128)S(1)}, u32[]{:S(2)}, u32[]{:S(2)}) async-start(f32[8,5,8,512]{3,2,1,0:T(8,128)} %stencil.1), calls=%async_computation.2 | async-start | bytes 1310720 | tf_op jit(solution)/shard_map/all_to_all | solution.py:448
  127.5 1.1 copy-done.12
  128.7 1.6 %assemble.1 = (f32[5,2,6,4096]{3,2,1,0:T(8,128)S(1)}, f32[5,3,6,4096]{3,2,1,0:T(8,128)}) custom-call(f32[2,25,8,512]{3,2,1,0:T(8,128)S(1)} %copy-done.12, f32[2,25,8,512]{3,2,1,0:T(8,128)S(1)} %copy-done.10, f32[2,25,8,512]{3,2,1,0:T(8,128)S(1)} %copy-done.8, f32[2,25,8,512]{3,2,1,0:T(8,128)S(1)} %get-tuple-element.60.refs_3_), custom_call_target="tpu_custom_call" | custom-call | tf_op jit(solution)/shard_map/assemble/pallas_call | solution.py:449
  130.2 1.7 %copy.8 = f32[5,2,6,4096]{3,1,2,0:T(2,128)} copy(f32[5,2,6,4096]{3,2,1,0:T(8,128)S(1)} %get-tuple-element.79) | data formatting | bytes 1966080
  131.9 6.7 %all-to-all-done.2.in_ref = f32[8,5,8,512]{3,2,1,0:T(8,128)S(1)} async-done(((f32[8,5,8,512]{3,2,1,0:T(8,128)}), f32[8,5,8,512]{3,2,1,0:T(8,128)S(1)}, u32[]{:S(2)}, u32[]{:S(2)}) %all-to-all-start.2) | async-done | bytes 655392 | tf_op jit(solution)/shard_map/all_to_all | solution.py:448
  138.7 0.9 combine.1
  (69 shorter events, 15.5 us)
Async XLA Ops:
  0.6 1.0 copy-start.17
  1.7 0.7 copy-start.18
  2.3 0.7 copy-start.20
  4.5 17.1 %copy-start.15 = (f32[5,56,512]{2,1,0:T(8,128)}, f32[5,56,512]{2,1,0:T(8,128)S(1)}, u32[]{:S(2)}) copy-start(f32[5,56,512]{2,1,0:T(8,128)S(1)} %get-tuple-element.41.column_ref) | copy-start | bytes 1720324
  4.5 17.1 %collective-permute-start.1 = (f32[5,56,512]{2,1,0:T(8,128)S(1)}, f32[5,56,512]{2,1,0:T(8,128)S(1)}, u32[]{:S(2)}, u32[]{:S(2)}) collective-permute-start(f32[5,56,512]{2,1,0:T(8,128)S(1)} %get-tuple-element.41.column_ref), channel_id=1, source_target_pairs={{0,8},{8,16},{16,24},{1,9},{9,17},{17,25},{2,10},{10,18},{18,26},{... | collective-permute-start | bytes 1720328 | tf_op jit(solution)/shard_map/ppermute | solution.py:326
  9.4 14.9 %all-to-all-start = ((f32[8,4,5,8,128]{4,3,2,1,0:T(8,128)}), f32[8,4,5,8,128]{4,3,2,1,0:T(8,128)S(1)}, u32[]{:S(2)}, u32[]{:S(2)}) async-start(f32[8,4,5,8,128]{4,3,2,1,0:T(8,128)} %get-tuple-element.42), calls=%async_computation | async-start | bytes 1310720 | tf_op jit(solution)/shard_map/all_to_all | solution.py:342
  21.7 0.8 copy-start.2
  22.5 0.8 copy-start.5
  23.4 30.0 %copy-start = (f32[5,3,6,4096]{3,2,1,0:T(8,128)S(1)}, f32[5,3,6,4096]{3,2,1,0:T(8,128)}, u32[]{:S(2)}) copy-start(f32[5,3,6,4096]{3,2,1,0:T(8,128)} %refs_6_.7) | copy-start | bytes 4423684
  23.4 30.1 %copy-start.1 = (f32[5,6,4096]{2,1,0:T(8,128)S(1)}, f32[5,6,4096]{2,1,0:T(8,128)}, u32[]{:S(2)}) copy-start(f32[5,6,4096]{2,1,0:T(8,128)} %refs_7_.7) | copy-start | bytes 1474564
  24.3 0.8 copy-start.3
  25.1 17.8 %all-to-all-start.1 = ((f32[8,4,5,8,128]{4,3,2,1,0:T(8,128)}), f32[8,4,5,8,128]{4,3,2,1,0:T(8,128)S(1)}, u32[]{:S(2)}, u32[]{:S(2)}) async-start(f32[8,4,5,8,128]{4,3,2,1,0:T(8,128)} %copy-done.2), calls=%async_computation.1 | async-start | bytes 1310720 | tf_op jit(solution)/shard_map/all_to_all | solution.py:342
  28.7 1.1 copy-start.4
  29.8 1.1 copy-start.16
  31.6 21.8 %copy-start.13 = (f32[9,5,8,128]{3,2,1,0:T(8,128)}, f32[9,5,8,128]{3,2,1,0:T(8,128)S(1)}, u32[]{:S(2)}) copy-start(f32[9,5,8,128]{3,2,1,0:T(8,128)S(1)} %get-tuple-element.43.refs_3_) | copy-start | bytes 552964
  31.6 12.5 %collective-permute-start = (f32[9,5,8,128]{3,2,1,0:T(8,128)S(1)}, f32[9,5,8,128]{3,2,1,0:T(8,128)}, u32[]{:S(2)}, u32[]{:S(2)}) collective-permute-start(f32[9,5,8,128]{3,2,1,0:T(8,128)S(1)} %get-tuple-element.43.refs_3_), channel_id=1, source_target_pairs={{0,16},{8,24},{1,17},{9,25},{2,18},{10,26},{3,19},{11,27},{4,20},{... | collective-permute-start | bytes 552968 | tf_op jit(solution)/shard_map/ppermute | solution.py:357
  37.1 7.9 %collective-permute-start.7 = (f32[8,5,8,128]{3,2,1,0:T(8,128)}, f32[8,5,8,128]{3,2,1,0:T(8,128)}, u32[]{:S(2)}, u32[]{:S(2)}) collective-permute-start(f32[8,5,8,128]{3,2,1,0:T(8,128)} %get-tuple-element.57.refs_3_), channel_id=1, source_target_pairs={{0,16},{8,24},{1,17},{9,25},{2,18},{10,26},{3,19},{11,27},{4,20},{... | collective-permute-start | bytes 491528 | tf_op jit(solution)/shard_map/ppermute | solution.py:357
  39.0 9.5 %collective-permute-start.5 = (f32[8,5,8,128]{3,2,1,0:T(8,128)}, f32[8,5,8,128]{3,2,1,0:T(8,128)}, u32[]{:S(2)}, u32[]{:S(2)}) collective-permute-start(f32[8,5,8,128]{3,2,1,0:T(8,128)} %get-tuple-element.53.refs_3_), channel_id=1, source_target_pairs={{0,16},{8,24},{1,17},{9,25},{2,18},{10,26},{3,19},{11,27},{4,20},{... | collective-permute-start | bytes 491528 | tf_op jit(solution)/shard_map/ppermute | solution.py:357
  41.0 10.7 %collective-permute-start.3 = (f32[8,5,8,128]{3,2,1,0:T(8,128)}, f32[8,5,8,128]{3,2,1,0:T(8,128)}, u32[]{:S(2)}, u32[]{:S(2)}) collective-permute-start(f32[8,5,8,128]{3,2,1,0:T(8,128)} %get-tuple-element.49.refs_3_), channel_id=1, source_target_pairs={{0,16},{8,24},{1,17},{9,25},{2,18},{10,26},{3,19},{11,27},{4,20},{... | collective-permute-start | bytes 491528 | tf_op jit(solution)/shard_map/ppermute | solution.py:357
  42.9 1.1 copy-start.6
  44.1 8.2 %collective-permute-start.2 = (f32[9,5,8,128]{3,2,1,0:T(8,128)}, f32[9,5,8,128]{3,2,1,0:T(8,128)S(1)}, u32[]{:S(2)}, u32[]{:S(2)}) collective-permute-start(f32[9,5,8,128]{3,2,1,0:T(8,128)} %collective-permute-done.refs_1_), channel_id=1, source_target_pairs={{16,24},{17,25},{18,26},{19,27},{20,28},{21,29},{22,30},{23,31}} | collective-permute-start | bytes 552968 | tf_op jit(solution)/shard_map/ppermute | solution.py:326
  45.0 8.4 %collective-permute-start.8 = (f32[8,5,8,128]{3,2,1,0:T(8,128)}, f32[8,5,8,128]{3,2,1,0:T(8,128)S(1)}, u32[]{:S(2)}, u32[]{:S(2)}) collective-permute-start(f32[8,5,8,128]{3,2,1,0:T(8,128)} %collective-permute-done.7.refs_1_), channel_id=1, source_target_pairs={{16,24},{17,25},{18,26},{19,27},{20,28},{21,29},{22,30},{23,31}} | collective-permute-start | bytes 491528 | tf_op jit(solution)/shard_map/ppermute | solution.py:326
  48.5 8.1 %collective-permute-start.6 = (f32[8,5,8,128]{3,2,1,0:T(8,128)}, f32[8,5,8,128]{3,2,1,0:T(8,128)S(1)}, u32[]{:S(2)}, u32[]{:S(2)}) collective-permute-start(f32[8,5,8,128]{3,2,1,0:T(8,128)} %collective-permute-done.5.refs_1_), channel_id=1, source_target_pairs={{16,24},{17,25},{18,26},{19,27},{20,28},{21,29},{22,30},{23,31}} | collective-permute-start | bytes 491528 | tf_op jit(solution)/shard_map/ppermute | solution.py:326
  51.6 9.3 %collective-permute-start.4 = (f32[8,5,8,128]{3,2,1,0:T(8,128)}, f32[8,5,8,128]{3,2,1,0:T(8,128)S(1)}, u32[]{:S(2)}, u32[]{:S(2)}) collective-permute-start(f32[8,5,8,128]{3,2,1,0:T(8,128)} %collective-permute-done.3.refs_1_), channel_id=1, source_target_pairs={{16,24},{17,25},{18,26},{19,27},{20,28},{21,29},{22,30},{23,31}} | collective-permute-start | bytes 491528 | tf_op jit(solution)/shard_map/ppermute | solution.py:326
  56.0 13.2 %collective-permute-start.18 = (f32[2,6,8,512]{3,2,1,0:T(8,128)S(1)}, f32[2,6,8,512]{3,2,1,0:T(8,128)S(1)}, u32[]{:S(2)}, u32[]{:S(2)}) collective-permute-start(f32[2,6,8,512]{3,2,1,0:T(8,128)S(1)} %get-tuple-element.78.b_ref), channel_id=1, source_target_pairs={{24,16},{25,17},{26,18},{27,19},{28,20},{29,21},{30,22},{31,23}} | collective-permute-start | bytes 589832 | tf_op jit(solution)/shard_map/ppermute | solution.py:329
  59.2 0.9 copy-start.7
  60.1 5.1 %copy-start.14 = (f32[9,5,8,128]{3,2,1,0:T(8,128)S(1)}, f32[9,5,8,128]{3,2,1,0:T(8,128)}, u32[]{:S(2)}) copy-start(f32[9,5,8,128]{3,2,1,0:T(8,128)} %copy-done.13) | copy-start | bytes 552964
  60.1 10.6 %collective-permute-start.15 = (f32[2,6,8,512]{3,2,1,0:T(8,128)S(1)}, f32[2,6,8,512]{3,2,1,0:T(8,128)S(1)}, u32[]{:S(2)}, u32[]{:S(2)}) collective-permute-start(f32[2,6,8,512]{3,2,1,0:T(8,128)S(1)} %get-tuple-element.74.b_ref), channel_id=1, source_target_pairs={{24,16},{25,17},{26,18},{27,19},{28,20},{29,21},{30,22},{31,23}} | collective-permute-start | bytes 589832 | tf_op jit(solution)/shard_map/ppermute | solution.py:329
  63.5 0.9 copy-start.9
  64.4 4.8 %copy-start.19 = (f32[5]{0:T(128)S(1)}, f32[5]{0:T(128)}, u32[]{:S(2)}) copy-start(f32[5]{0:T(128)} %mix_ref.25) | copy-start | bytes 64
  64.4 7.8 %collective-permute-start.12 = (f32[2,6,8,512]{3,2,1,0:T(8,128)S(1)}, f32[2,6,8,512]{3,2,1,0:T(8,128)S(1)}, u32[]{:S(2)}, u32[]{:S(2)}) collective-permute-start(f32[2,6,8,512]{3,2,1,0:T(8,128)S(1)} %get-tuple-element.70.b_ref), channel_id=1, source_target_pairs={{24,16},{25,17},{26,18},{27,19},{28,20},{29,21},{30,22},{31,23}} | collective-permute-start | bytes 589832 | tf_op jit(solution)/shard_map/ppermute | solution.py:329
  67.6 0.9 copy-start.11
  68.5 5.1 %collective-permute-start.9 = (f32[2,6,8,512]{3,2,1,0:T(8,128)S(1)}, f32[2,6,8,512]{3,2,1,0:T(8,128)S(1)}, u32[]{:S(2)}, u32[]{:S(2)}) collective-permute-start(f32[2,6,8,512]{3,2,1,0:T(8,128)S(1)} %get-tuple-element.66.b_ref), channel_id=1, source_target_pairs={{24,16},{25,17},{26,18},{27,19},{28,20},{29,21},{30,22},{31,23}} | collective-permute-start | bytes 589832 | tf_op jit(solution)/shard_map/ppermute | solution.py:329
  70.0 5.1 %collective-permute-start.19 = (f32[2,6,8,512]{3,2,1,0:T(8,128)S(1)}, f32[2,6,8,512]{3,2,1,0:T(8,128)S(1)}, u32[]{:S(2)}, u32[]{:S(2)}) collective-permute-start(f32[2,6,8,512]{3,2,1,0:T(8,128)S(1)} %carry.14), channel_id=1, source_target_pairs={{16,8},{17,9},{18,10},{19,11},{20,12},{21,13},{22,14},{23,15}} | collective-permute-start | bytes 589832 | tf_op jit(solution)/shard_map/ppermute | solution.py:329
  71.5 5.7 %collective-permute-start.16 = (f32[2,6,8,512]{3,2,1,0:T(8,128)S(1)}, f32[2,6,8,512]{3,2,1,0:T(8,128)S(1)}, u32[]{:S(2)}, u32[]{:S(2)}) collective-permute-start(f32[2,6,8,512]{3,2,1,0:T(8,128)S(1)} %carry.12), channel_id=1, source_target_pairs={{16,8},{17,9},{18,10},{19,11},{20,12},{21,13},{22,14},{23,15}} | collective-permute-start | bytes 589832 | tf_op jit(solution)/shard_map/ppermute | solution.py:329
  73.0 6.3 %collective-permute-start.13 = (f32[2,6,8,512]{3,2,1,0:T(8,128)S(1)}, f32[2,6,8,512]{3,2,1,0:T(8,128)S(1)}, u32[]{:S(2)}, u32[]{:S(2)}) collective-permute-start(f32[2,6,8,512]{3,2,1,0:T(8,128)S(1)} %carry.10), channel_id=1, source_target_pairs={{16,8},{17,9},{18,10},{19,11},{20,12},{21,13},{22,14},{23,15}} | collective-permute-start | bytes 589832 | tf_op jit(solution)/shard_map/ppermute | solution.py:329
  74.4 34.0 %copy-start.21 = (f32[5]{0:T(128)S(1)}, f32[5]{0:T(128)}, u32[]{:S(2)}) copy-start(f32[5]{0:T(128)} %weight_ref.9) | copy-start | bytes 64
  74.4 7.0 %collective-permute-start.10 = (f32[2,6,8,512]{3,2,1,0:T(8,128)S(1)}, f32[2,6,8,512]{3,2,1,0:T(8,128)S(1)}, u32[]{:S(2)}, u32[]{:S(2)}) collective-permute-start(f32[2,6,8,512]{3,2,1,0:T(8,128)S(1)} %carry.8), channel_id=1, source_target_pairs={{16,8},{17,9},{18,10},{19,11},{20,12},{21,13},{22,14},{23,15}} | collective-permute-start | bytes 589832 | tf_op jit(solution)/shard_map/ppermute | solution.py:329
  75.9 32.5 %collective-permute-start.20 = (f32[2,6,8,512]{3,2,1,0:T(8,128)S(1)}, f32[2,6,8,512]{3,2,1,0:T(8,128)S(1)}, u32[]{:S(2)}, u32[]{:S(2)}) collective-permute-start(f32[2,6,8,512]{3,2,1,0:T(8,128)S(1)} %carry.15), channel_id=1, source_target_pairs={{8,0},{9,1},{10,2},{11,3},{12,4},{13,5},{14,6},{15,7}} | collective-permute-start | bytes 589832 | tf_op jit(solution)/shard_map/ppermute | solution.py:329
  78.0 34.6 %collective-permute-start.17 = (f32[2,6,8,512]{3,2,1,0:T(8,128)S(1)}, f32[2,6,8,512]{3,2,1,0:T(8,128)S(1)}, u32[]{:S(2)}, u32[]{:S(2)}) collective-permute-start(f32[2,6,8,512]{3,2,1,0:T(8,128)S(1)} %carry.13), channel_id=1, source_target_pairs={{8,0},{9,1},{10,2},{11,3},{12,4},{13,5},{14,6},{15,7}} | collective-permute-start | bytes 589832 | tf_op jit(solution)/shard_map/ppermute | solution.py:329
  80.1 36.7 %collective-permute-start.14 = (f32[2,6,8,512]{3,2,1,0:T(8,128)S(1)}, f32[2,6,8,512]{3,2,1,0:T(8,128)S(1)}, u32[]{:S(2)}, u32[]{:S(2)}) collective-permute-start(f32[2,6,8,512]{3,2,1,0:T(8,128)S(1)} %carry.11), channel_id=1, source_target_pairs={{8,0},{9,1},{10,2},{11,3},{12,4},{13,5},{14,6},{15,7}} | collective-permute-start | bytes 589832 | tf_op jit(solution)/shard_map/ppermute | solution.py:329
  82.2 38.8 %collective-permute-start.11 = (f32[2,6,8,512]{3,2,1,0:T(8,128)S(1)}, f32[2,6,8,512]{3,2,1,0:T(8,128)S(1)}, u32[]{:S(2)}, u32[]{:S(2)}) collective-permute-start(f32[2,6,8,512]{3,2,1,0:T(8,128)S(1)} %carry.9), channel_id=1, source_target_pairs={{8,0},{9,1},{10,2},{11,3},{12,4},{13,5},{14,6},{15,7}} | collective-permute-start | bytes 589832 | tf_op jit(solution)/shard_map/ppermute | solution.py:329
  121.9 5.6 %copy-start.8 = (f32[2,25,8,512]{3,2,1,0:T(8,128)S(1)}, f32[2,25,8,512]{3,2,1,0:T(8,128)}, u32[]{:S(2)}) copy-start(f32[2,25,8,512]{3,2,1,0:T(8,128)} %copy-done.7) | copy-start | bytes 2457604
  121.9 5.6 %copy-start.10 = (f32[2,25,8,512]{3,2,1,0:T(8,128)S(1)}, f32[2,25,8,512]{3,2,1,0:T(8,128)}, u32[]{:S(2)}) copy-start(f32[2,25,8,512]{3,2,1,0:T(8,128)} %copy-done.9) | copy-start | bytes 2457604
  123.7 15.0 %all-to-all-start.2 = ((f32[8,5,8,512]{3,2,1,0:T(8,128)}), f32[8,5,8,512]{3,2,1,0:T(8,128)S(1)}, u32[]{:S(2)}, u32[]{:S(2)}) async-start(f32[8,5,8,512]{3,2,1,0:T(8,128)} %stencil.1), calls=%async_computation.2 | async-start | bytes 1310720 | tf_op jit(solution)/shard_map/all_to_all | solution.py:448
  127.5 1.1 copy-start.12

commit v5 on v3

--- a/solution.py
+++ b/solution.py
@@ -11,7 +11,7 @@
 SUB = 8
 EDGE = 128
 F32 = jnp.float32
-VMEM_LIMIT = 32 * 1024 * 1024
+VMEM_LIMIT = 16 * 1024 * 1024
 CHUNKS = 4
 SPAN = 4
 MIX_LANE = 64
@@ -52,6 +52,19 @@
         outs[0][length, k] = edge
 
 
+def edges_kernel(*refs):
+    strips = refs[:-2]
+    beside_ref, excess_ref = refs[-2:]
+    for group, strip_ref in enumerate(strips):
+        planes = strip_ref.shape[1]
+        for k in range(planes):
+            edge = strip_ref[strip_ref.shape[0] - 1, k]
+            at = group * planes + k
+            excess_ref[at] = jnp.broadcast_to(edge[:, MIX_LANE : MIX_LANE + 1], edge.shape)
+            for c in range(CHUNKS):
+                beside_ref[c, at] = pltpu.roll(edge, (EDGE - 2 * c) % EDGE, 1)
+
+
 def row_up(x):
     return pltpu.roll(x, SUB - 1, 0)
 
@@ -94,8 +107,8 @@
 
 
 def forward_kernel(groups, planes, chunk, length, *refs):
-    strips = refs[: 2 * groups]
-    obs_ref, noise_ref = refs[2 * groups : 2 * groups + 2]
+    strips = refs[:groups]
+    beside_ref, excess_ref, obs_ref, noise_ref = refs[groups : groups + 4]
     map_ref, m_ref, a_ref, src_ref, b_ref = refs[-5:]
     step = pl.program_id(0)
     width = obs_ref.shape[-1]
@@ -111,13 +124,15 @@
     psi_before = psi
     keeps = []
     for group in range(groups):
-        strip_ref, edge_ref = strips[2 * group : 2 * group + 2]
+        strip_ref = strips[group]
         own = group == groups - 1
         for k in range(planes):
-            edge = edge_ref[edge_ref.shape[0] - 1, k]
-            excess = edge[:, MIX_LANE : MIX_LANE + 1]
-            mix = 1.0 + excess
-            beside = pltpu.roll(edge, (EDGE - 2 * chunk) % EDGE, 1)
+            beside = beside_ref[chunk, group * planes + k]
+            excess_tile = excess_ref[group * planes + k]
+            excess_ext = jnp.concatenate([excess_tile] * (span + 2), axis=1)
+            excess = excess_ext[:, EDGE:-EDGE]
+            mix_ext = jnp.concatenate([1.0 + excess_tile] * (span + 2), axis=1)
+            mix = mix_ext[:, EDGE:-EDGE]
             left = jnp.where(at_start, beside, strip_ref[jnp.maximum(first - 1, 0), k])
             right = jnp.where(at_end, beside, strip_ref[jnp.minimum(first + span, length - 1), k])
             tiles = [strip_ref[first + t, k] for t in range(span)]
@@ -144,7 +159,7 @@
                 off * a[1] + m1 * a[3] - excess * a_before[3],
             ]
             a_before, a = (a, new_a)
-            psi, psi_before = (mix * psi - excess * psi_before - ext, psi)
+            psi, psi_before = (mix_ext * psi - excess_ext * psi_before - ext, psi)
             if own:
                 slope_rows = 0.5 * (row_up(psi) - row_down(psi))[:, EDGE:-EDGE]
                 slope_cols = 0.5 * (col_next(psi) - col_prev(psi))
@@ -327,6 +342,18 @@
             if 0 <= turn - c < groups - 1:
                 strips[c].insert(0, climb(strips[c][0], turn - c))
 
+    beside, excess = pl.pallas_call(
+        edges_kernel,
+        out_shape=(
+            shape(CHUNKS, groups * planes, SUB, EDGE),
+            shape(groups * planes, SUB, EDGE),
+        ),
+        in_specs=[WHOLE] * groups,
+        out_specs=(WHOLE, WHOLE),
+        compiler_params=params(),
+        name="edges",
+    )(*strips[0])
+
     state = block_of(R, SUB, span)
     triple = block_of(3 * planes, SUB, span)
     quad = block_of(4 * planes, SUB, span)
@@ -348,11 +375,11 @@
                 shape(steps, 3 * planes, SUB, span),
                 shape(steps, R, SUB, span),
             ),
-            in_specs=[WHOLE] * (2 * groups) + [columns_of(planes, 3, R), columns_of(planes, R)],
+            in_specs=[WHOLE] * (groups + 2) + [columns_of(planes, 3, R), columns_of(planes, R)],
             out_specs=(quint, triple, quad, triple, state),
             compiler_params=params(),
             name="forward",
-        )(*[x for pair in zip(strips[c], strips[0]) for x in pair], observed, noise_weight)
+        )(*strips[c], beside, excess, observed, noise_weight)
         maps.append(map_piece)
         work.append(held)
 

time: 127 us -> 120 us (0.945)
  Pallas kernels: 28.8 us -> 21.5 us
    pallas_call x4, Pallas kernels: 13.7 us -> 6.27 us  [on_device(): pl.pallas_call(functools.partial(forward_kernel, groups, planes, c, lengt...]
  transfers between devices with their start and end apart: 25 -> 25, of which waited for: 7 -> 7; matrix products, arithmetic and copies ran while one was open for 1% -> 1% of each run, Pallas kernels for 19% -> 14%
where the time goes in v5:
time: 120 us; the launch traced here: 119 us
  waiting for transfers between devices  43.4 us (36%)
  starting transfers between devices  31.8 us (26%)
  Pallas kernels  21.5 us (18%)
  blocking collectives  16.1 us (13%)
  local copies, waits for them, and re-layouts  5.34 us (4%)
  between operations  1.2 us (1%)
    ppermute x12, waiting for transfers between devices, descend(): return lax.ppermute(x, 'plane', [(groups - 1 - hop, groups - 2 - hop)])  33.5 us
    ppermute x12, starting transfers between devices, climb(): lax.ppermute(x, 'plane', [(i, i + 1) for i in range(hop, groups - 1)])  17.7 us
    all_to_all x1, blocking collectives, on_device(): lax.all_to_all(packed, 'slab', split_axis=0, concat_axis=0, tiled=True)  16.1 us
    ppermute x12, starting transfers between devices, descend(): return lax.ppermute(x, 'plane', [(groups - 1 - hop, groups - 2 - hop)])  10.6 us
    all_to_all x1, waiting for transfers between devices, on_device(): lax.all_to_all(partial, 'slab', split_axis=0, concat_axis=0, tiled=True)  6.68 us
    pallas_call x4, Pallas kernels, on_device(): pl.pallas_call(functools.partial(forward_kernel, groups, planes, c, lengt...  6.27 us
    pallas_call x8, Pallas kernels, on_device(): pl.pallas_call(functools.partial(carry_kernel, planes), grid=(steps,), ou...  6.18 us
    unnamed x19, local copies, waits for them, and re-layouts  5.34 us
  transfers between devices with their start and end apart: 25, of which 7 were waited for; matrix products, arithmetic and copies ran while one was open for 1% of the time, Pallas kernels for 14%

profile of v5, /device:TPU:0, one launch (start us, length us, event | category | flops | bytes accessed | tf_op | source)
XLA Modules:
  0.0 119.4 jit_solution(1863343573622589590)
XLA Ops:
  0.7 1.2 copy-done.4
  2.5 0.7 pack.1
  3.2 16.1 %all_to_all.10 = f32[8,4,5,8,128]{4,3,2,1,0:T(8,128)S(1)} all-to-all(f32[8,4,5,8,128]{4,3,2,1,0:T(8,128)S(1)} %pack.1), channel_id=1, replica_groups=mesh['plane'=4,'slab'=8] {'slab'}, dimensions={0} | all-to-all | bytes 1310720 | tf_op jit(solution)/shard_map/all_to_all | solution.py:327
  20.6 3.5 %collective-permute-start = (f32[9,5,8,128]{3,2,1,0:T(8,128)S(1)}, f32[9,5,8,128]{3,2,1,0:T(8,128)S(1)}, u32[]{:S(2)}, u32[]{:S(2)}) collective-permute-start(f32[9,5,8,128]{3,2,1,0:T(8,128)S(1)} %get-tuple-element.31.refs_3_), channel_id=1, source_target_pairs={{0,8},{8,16},{16,24},{1,9},{9,17},{17,25},{2,10},{10,18},{18,26},{... | collective-permute-start | bytes 552968 | tf_op jit(solution)/shard_map/ppermute | solution.py:314
  24.1 3.5 %collective-permute-start.9 = (f32[8,5,8,128]{3,2,1,0:T(8,128)S(1)}, f32[8,5,8,128]{3,2,1,0:T(8,128)S(1)}, u32[]{:S(2)}, u32[]{:S(2)}) collective-permute-start(f32[8,5,8,128]{3,2,1,0:T(8,128)S(1)} %get-tuple-element.39.refs_3_), channel_id=1, source_target_pairs={{0,8},{8,16},{16,24},{1,9},{9,17},{17,25},{2,10},{10,18},{18,26},{... | collective-permute-start | bytes 491528 | tf_op jit(solution)/shard_map/ppermute | solution.py:314
  27.6 3.5 %collective-permute-start.6 = (f32[8,5,8,128]{3,2,1,0:T(8,128)S(1)}, f32[8,5,8,128]{3,2,1,0:T(8,128)S(1)}, u32[]{:S(2)}, u32[]{:S(2)}) collective-permute-start(f32[8,5,8,128]{3,2,1,0:T(8,128)S(1)} %get-tuple-element.37.refs_3_), channel_id=1, source_target_pairs={{0,8},{8,16},{16,24},{1,9},{9,17},{17,25},{2,10},{10,18},{18,26},{... | collective-permute-start | bytes 491528 | tf_op jit(solution)/shard_map/ppermute | solution.py:314
  31.1 1.9 %collective-permute-start.3 = (f32[8,5,8,128]{3,2,1,0:T(8,128)S(1)}, f32[8,5,8,128]{3,2,1,0:T(8,128)S(1)}, u32[]{:S(2)}, u32[]{:S(2)}) collective-permute-start(f32[8,5,8,128]{3,2,1,0:T(8,128)S(1)} %get-tuple-element.35.refs_3_), channel_id=1, source_target_pairs={{0,8},{8,16},{16,24},{1,9},{9,17},{17,25},{2,10},{10,18},{18,26},{... | collective-permute-start | bytes 491528 | tf_op jit(solution)/shard_map/ppermute | solution.py:314
  34.4 1.3 %collective-permute-done.6.refs_2_ = f32[8,5,8,128]{3,2,1,0:T(8,128)S(1)} collective-permute-done((f32[8,5,8,128]{3,2,1,0:T(8,128)S(1)}, f32[8,5,8,128]{3,2,1,0:T(8,128)S(1)}, u32[]{:S(2)}, u32[]{:S(2)}) %collective-permute-start.6) | collective-permute-done | bytes 163872 | tf_op jit(solution)/shard_map/ppermute | solution.py:314
  36.4 1.9 %collective-permute-done.3.refs_2_ = f32[8,5,8,128]{3,2,1,0:T(8,128)S(1)} collective-permute-done((f32[8,5,8,128]{3,2,1,0:T(8,128)S(1)}, f32[8,5,8,128]{3,2,1,0:T(8,128)S(1)}, u32[]{:S(2)}, u32[]{:S(2)}) %collective-permute-start.3) | collective-permute-done | bytes 163872 | tf_op jit(solution)/shard_map/ppermute | solution.py:314
  41.9 1.6 %forward.7 = (f32[2,25,8,512]{3,2,1,0:T(8,128)S(1)}, f32[2,15,8,512]{3,2,1,0:T(8,128)S(1)}, f32[2,20,8,512]{3,2,1,0:T(8,128)S(1)}, f32[2,15,8,512]{3,2,1,0:T(8,128)S(1)}, f32[2,6,8,512]{3,2,1,0:T(8,128)S(1)}) custom-call(f32[8,5,8,128]{3,2,1,0:T(8,128)S(1)} %collective-permute-done.11.refs_0_, f32[8,5,8,128]{3,2,1,0:T(8,128)S(1)} %collective-permute-done.10.refs_1_, ...), custom_call_target="tpu_custom_call" | custom-call | tf_op jit(solution)/shard_map/forward/pallas_call | solution.py:368
  43.5 0.7 collective-permute-start.21
  44.2 1.6 %forward.6 = (f32[2,25,8,512]{3,2,1,0:T(8,128)S(1)}, f32[2,15,8,512]{3,2,1,0:T(8,128)S(1)}, f32[2,20,8,512]{3,2,1,0:T(8,128)S(1)}, f32[2,15,8,512]{3,2,1,0:T(8,128)S(1)}, f32[2,6,8,512]{3,2,1,0:T(8,128)S(1)}) custom-call(f32[8,5,8,128]{3,2,1,0:T(8,128)S(1)} %collective-permute-done.8.refs_0_, f32[8,5,8,128]{3,2,1,0:T(8,128)S(1)} %collective-permute-done.7.refs_1_, ...), custom_call_target="tpu_custom_call" | custom-call | tf_op jit(solution)/shard_map/forward/pallas_call | solution.py:368
  45.7 0.7 collective-permute-start.18
  46.4 1.6 %forward.5 = (f32[2,25,8,512]{3,2,1,0:T(8,128)S(1)}, f32[2,15,8,512]{3,2,1,0:T(8,128)S(1)}, f32[2,20,8,512]{3,2,1,0:T(8,128)S(1)}, f32[2,15,8,512]{3,2,1,0:T(8,128)S(1)}, f32[2,6,8,512]{3,2,1,0:T(8,128)S(1)}) custom-call(f32[8,5,8,128]{3,2,1,0:T(8,128)S(1)} %collective-permute-done.5.refs_0_, f32[8,5,8,128]{3,2,1,0:T(8,128)S(1)} %collective-permute-done.4.refs_1_, ...), custom_call_target="tpu_custom_call" | custom-call | tf_op jit(solution)/shard_map/forward/pallas_call | solution.py:368
  48.0 0.7 collective-permute-start.15
  48.7 1.6 %forward.4 = (f32[2,25,8,512]{3,2,1,0:T(8,128)S(1)}, f32[2,15,8,512]{3,2,1,0:T(8,128)S(1)}, f32[2,20,8,512]{3,2,1,0:T(8,128)S(1)}, f32[2,15,8,512]{3,2,1,0:T(8,128)S(1)}, f32[2,6,8,512]{3,2,1,0:T(8,128)S(1)}) custom-call(f32[9,5,8,128]{3,2,1,0:T(8,128)S(1)} %collective-permute-done.2.refs_0_, f32[9,5,8,128]{3,2,1,0:T(8,128)S(1)} %collective-permute-done.1.refs_1_, ...), custom_call_target="tpu_custom_call" | custom-call | tf_op jit(solution)/shard_map/forward/pallas_call | solution.py:368
  50.3 0.7 collective-permute-start.12
  51.0 0.8 carry.14
  51.8 0.7 collective-permute-start.22
  52.5 0.8 carry.12
  53.2 0.7 collective-permute-start.19
  53.9 0.8 carry.10
  54.7 0.7 collective-permute-start.16
  55.4 0.8 carry.8
  56.2 0.7 collective-permute-start.13
  56.9 0.8 carry.15
  57.7 1.3 %collective-permute-start.23 = (f32[2,6,8,512]{3,2,1,0:T(8,128)S(1)}, f32[2,6,8,512]{3,2,1,0:T(8,128)S(1)}, u32[]{:S(2)}, u32[]{:S(2)}) collective-permute-start(f32[2,6,8,512]{3,2,1,0:T(8,128)S(1)} %carry.15), channel_id=1, source_target_pairs={{8,0},{9,1},{10,2},{11,3},{12,4},{13,5},{14,6},{15,7}} | collective-permute-start | bytes 589832 | tf_op jit(solution)/shard_map/ppermute | solution.py:317
  59.0 0.8 carry.13
  59.8 1.3 %collective-permute-start.20 = (f32[2,6,8,512]{3,2,1,0:T(8,128)S(1)}, f32[2,6,8,512]{3,2,1,0:T(8,128)S(1)}, u32[]{:S(2)}, u32[]{:S(2)}) collective-permute-start(f32[2,6,8,512]{3,2,1,0:T(8,128)S(1)} %carry.13), channel_id=1, source_target_pairs={{8,0},{9,1},{10,2},{11,3},{12,4},{13,5},{14,6},{15,7}} | collective-permute-start | bytes 589832 | tf_op jit(solution)/shard_map/ppermute | solution.py:317
  61.1 0.8 carry.11
  61.9 1.3 %collective-permute-start.17 = (f32[2,6,8,512]{3,2,1,0:T(8,128)S(1)}, f32[2,6,8,512]{3,2,1,0:T(8,128)S(1)}, u32[]{:S(2)}, u32[]{:S(2)}) collective-permute-start(f32[2,6,8,512]{3,2,1,0:T(8,128)S(1)} %carry.11), channel_id=1, source_target_pairs={{8,0},{9,1},{10,2},{11,3},{12,4},{13,5},{14,6},{15,7}} | collective-permute-start | bytes 589832 | tf_op jit(solution)/shard_map/ppermute | solution.py:317
  63.2 0.8 carry.9
  63.9 1.3 %collective-permute-start.14 = (f32[2,6,8,512]{3,2,1,0:T(8,128)S(1)}, f32[2,6,8,512]{3,2,1,0:T(8,128)S(1)}, u32[]{:S(2)}, u32[]{:S(2)}) collective-permute-start(f32[2,6,8,512]{3,2,1,0:T(8,128)S(1)} %carry.9), channel_id=1, source_target_pairs={{8,0},{9,1},{10,2},{11,3},{12,4},{13,5},{14,6},{15,7}} | collective-permute-start | bytes 589832 | tf_op jit(solution)/shard_map/ppermute | solution.py:317
  65.2 25.5 %collective-permute-done.23.refs_2_ = f32[2,6,8,512]{3,2,1,0:T(8,128)S(1)} collective-permute-done((f32[2,6,8,512]{3,2,1,0:T(8,128)S(1)}, f32[2,6,8,512]{3,2,1,0:T(8,128)S(1)}, u32[]{:S(2)}, u32[]{:S(2)}) %collective-permute-start.23) | collective-permute-done | bytes 196640 | tf_op jit(solution)/shard_map/ppermute | solution.py:317
  90.7 0.8 cotangent.7.refs_3_
  91.6 3.4 %collective-permute-done.20.refs_2_ = f32[2,6,8,512]{3,2,1,0:T(8,128)S(1)} collective-permute-done((f32[2,6,8,512]{3,2,1,0:T(8,128)S(1)}, f32[2,6,8,512]{3,2,1,0:T(8,128)S(1)}, u32[]{:S(2)}, u32[]{:S(2)}) %collective-permute-start.20) | collective-permute-done | bytes 196640 | tf_op jit(solution)/shard_map/ppermute | solution.py:317
  94.9 0.8 cotangent.6.refs_2_
  95.8 3.4 %collective-permute-done.17.refs_2_ = f32[2,6,8,512]{3,2,1,0:T(8,128)S(1)} collective-permute-done((f32[2,6,8,512]{3,2,1,0:T(8,128)S(1)}, f32[2,6,8,512]{3,2,1,0:T(8,128)S(1)}, u32[]{:S(2)}, u32[]{:S(2)}) %collective-permute-start.17) | collective-permute-done | bytes 196640 | tf_op jit(solution)/shard_map/ppermute | solution.py:317
  99.1 0.8 cotangent.5.refs_1_
  100.0 1.2 %collective-permute-done.14.refs_2_ = f32[2,6,8,512]{3,2,1,0:T(8,128)S(1)} collective-permute-done((f32[2,6,8,512]{3,2,1,0:T(8,128)S(1)}, f32[2,6,8,512]{3,2,1,0:T(8,128)S(1)}, u32[]{:S(2)}, u32[]{:S(2)}) %collective-permute-start.14) | collective-permute-done | bytes 196640 | tf_op jit(solution)/shard_map/ppermute | solution.py:317
  101.2 0.8 cotangent.4.refs_0_
  102.1 1.8 %stencil.1 = f32[8,5,8,512]{3,2,1,0:T(8,128)} custom-call(f32[2,15,8,512]{3,2,1,0:T(8,128)S(1)} %cotangent.4.refs_0_, f32[2,15,8,512]{3,2,1,0:T(8,128)S(1)} %cotangent.5.refs_1_, f32[2,15,8,512]{3,2,1,0:T(8,128)S(1)} %cotangent.6.refs_2_, f32[2,15,8,512]{3,2,1,0:T(8,128)S(1)} %cotangent.7.refs_3_), custom_call_target="tpu_custom_call" | custom-call | tf_op jit(solution)/shard_map/stencil/pallas_call | solution.py:412
  103.9 3.5 %all-to-all-start.1 = ((f32[8,5,8,512]{3,2,1,0:T(8,128)}), f32[8,5,8,512]{3,2,1,0:T(8,128)S(1)}, u32[]{:S(2)}, u32[]{:S(2)}) async-start(f32[8,5,8,512]{3,2,1,0:T(8,128)} %stencil.1), calls=%async_computation.1 | async-start | bytes 1310720 | tf_op jit(solution)/shard_map/all_to_all | solution.py:420
  107.4 1.1 copy-done.3
  108.6 1.6 %assemble.1 = (f32[5,2,6,4096]{3,2,1,0:T(8,128)S(1)}, f32[5,3,6,4096]{3,2,1,0:T(8,128)}) custom-call(f32[2,25,8,512]{3,2,1,0:T(8,128)S(1)} %copy-done.3, f32[2,25,8,512]{3,2,1,0:T(8,128)S(1)} %get-tuple-element.36.refs_1_, f32[2,25,8,512]{3,2,1,0:T(8,128)S(1)} %get-tuple-element.38.refs_2_, f32[2,25,8,512]{3,2,1,0:T(8,128)S(1)} %get-tuple-element.40.refs_3_), custom_call_target="tpu_custom_call" | custom-call | tf_op jit(solution)/shard_map/assemble/pallas_call | solution.py:421
  110.1 1.7 %copy.8 = f32[5,2,6,4096]{3,1,2,0:T(2,128)} copy(f32[5,2,6,4096]{3,2,1,0:T(8,128)S(1)} %get-tuple-element.59) | data formatting | bytes 1966080
  111.8 6.7 %all-to-all-done.1.in_ref = f32[8,5,8,512]{3,2,1,0:T(8,128)S(1)} async-done(((f32[8,5,8,512]{3,2,1,0:T(8,128)}), f32[8,5,8,512]{3,2,1,0:T(8,128)S(1)}, u32[]{:S(2)}, u32[]{:S(2)}) %all-to-all-start.1) | async-done | bytes 655392 | tf_op jit(solution)/shard_map/all_to_all | solution.py:420
  118.5 0.9 combine.1
  (44 shorter events, 7.5 us)
Async XLA Ops:
  0.6 41.2 %copy-start = (f32[5,3,6,4096]{3,2,1,0:T(8,128)S(1)}, f32[5,3,6,4096]{3,2,1,0:T(8,128)}, u32[]{:S(2)}) copy-start(f32[5,3,6,4096]{3,2,1,0:T(8,128)} %refs_6_.7) | copy-start | bytes 4423684
  0.6 1.2 copy-start.4
  1.8 0.7 copy-start.7
  2.5 39.4 %copy-start.1 = (f32[5,6,4096]{2,1,0:T(8,128)S(1)}, f32[5,6,4096]{2,1,0:T(8,128)}, u32[]{:S(2)}) copy-start(f32[5,6,4096]{2,1,0:T(8,128)} %refs_7_.7) | copy-start | bytes 1474564
  19.3 0.7 copy-start.5
  20.6 12.4 %collective-permute-start = (f32[9,5,8,128]{3,2,1,0:T(8,128)S(1)}, f32[9,5,8,128]{3,2,1,0:T(8,128)S(1)}, u32[]{:S(2)}, u32[]{:S(2)}) collective-permute-start(f32[9,5,8,128]{3,2,1,0:T(8,128)S(1)} %get-tuple-element.31.refs_3_), channel_id=1, source_target_pairs={{0,8},{8,16},{16,24},{1,9},{9,17},{17,25},{2,10},{10,18},{18,26},{... | collective-permute-start | bytes 552968 | tf_op jit(solution)/shard_map/ppermute | solution.py:314
  24.1 9.6 %collective-permute-start.9 = (f32[8,5,8,128]{3,2,1,0:T(8,128)S(1)}, f32[8,5,8,128]{3,2,1,0:T(8,128)S(1)}, u32[]{:S(2)}, u32[]{:S(2)}) collective-permute-start(f32[8,5,8,128]{3,2,1,0:T(8,128)S(1)} %get-tuple-element.39.refs_3_), channel_id=1, source_target_pairs={{0,8},{8,16},{16,24},{1,9},{9,17},{17,25},{2,10},{10,18},{18,26},{... | collective-permute-start | bytes 491528 | tf_op jit(solution)/shard_map/ppermute | solution.py:314
  27.6 8.1 %collective-permute-start.6 = (f32[8,5,8,128]{3,2,1,0:T(8,128)S(1)}, f32[8,5,8,128]{3,2,1,0:T(8,128)S(1)}, u32[]{:S(2)}, u32[]{:S(2)}) collective-permute-start(f32[8,5,8,128]{3,2,1,0:T(8,128)S(1)} %get-tuple-element.37.refs_3_), channel_id=1, source_target_pairs={{0,8},{8,16},{16,24},{1,9},{9,17},{17,25},{2,10},{10,18},{18,26},{... | collective-permute-start | bytes 491528 | tf_op jit(solution)/shard_map/ppermute | solution.py:314
  31.1 7.2 %collective-permute-start.3 = (f32[8,5,8,128]{3,2,1,0:T(8,128)S(1)}, f32[8,5,8,128]{3,2,1,0:T(8,128)S(1)}, u32[]{:S(2)}, u32[]{:S(2)}) collective-permute-start(f32[8,5,8,128]{3,2,1,0:T(8,128)S(1)} %get-tuple-element.35.refs_3_), channel_id=1, source_target_pairs={{0,8},{8,16},{16,24},{1,9},{9,17},{17,25},{2,10},{10,18},{18,26},{... | collective-permute-start | bytes 491528 | tf_op jit(solution)/shard_map/ppermute | solution.py:314
  33.0 6.0 %collective-permute-start.1 = (f32[9,5,8,128]{3,2,1,0:T(8,128)S(1)}, f32[9,5,8,128]{3,2,1,0:T(8,128)S(1)}, u32[]{:S(2)}, u32[]{:S(2)}) collective-permute-start(f32[9,5,8,128]{3,2,1,0:T(8,128)S(1)} %collective-permute-done.refs_2_), channel_id=1, source_target_pairs={{8,16},{16,24},{9,17},{17,25},{10,18},{18,26},{11,19},{19,27},{12,... | collective-permute-start | bytes 552968 | tf_op jit(solution)/shard_map/ppermute | solution.py:314
  33.7 6.0 %collective-permute-start.10 = (f32[8,5,8,128]{3,2,1,0:T(8,128)S(1)}, f32[8,5,8,128]{3,2,1,0:T(8,128)S(1)}, u32[]{:S(2)}, u32[]{:S(2)}) collective-permute-start(f32[8,5,8,128]{3,2,1,0:T(8,128)S(1)} %collective-permute-done.9.refs_2_), channel_id=1, source_target_pairs={{8,16},{16,24},{9,17},{17,25},{10,18},{18,26},{11,19},{19,27},{12,... | collective-permute-start | bytes 491528 | tf_op jit(solution)/shard_map/ppermute | solution.py:314
  35.7 4.6 %collective-permute-start.7 = (f32[8,5,8,128]{3,2,1,0:T(8,128)S(1)}, f32[8,5,8,128]{3,2,1,0:T(8,128)S(1)}, u32[]{:S(2)}, u32[]{:S(2)}) collective-permute-start(f32[8,5,8,128]{3,2,1,0:T(8,128)S(1)} %collective-permute-done.6.refs_2_), channel_id=1, source_target_pairs={{8,16},{16,24},{9,17},{17,25},{10,18},{18,26},{11,19},{19,27},{12,... | collective-permute-start | bytes 491528 | tf_op jit(solution)/shard_map/ppermute | solution.py:314
  38.3 2.7 %collective-permute-start.4 = (f32[8,5,8,128]{3,2,1,0:T(8,128)S(1)}, f32[8,5,8,128]{3,2,1,0:T(8,128)S(1)}, u32[]{:S(2)}, u32[]{:S(2)}) collective-permute-start(f32[8,5,8,128]{3,2,1,0:T(8,128)S(1)} %collective-permute-done.3.refs_2_), channel_id=1, source_target_pairs={{8,16},{16,24},{9,17},{17,25},{10,18},{18,26},{11,19},{19,27},{12,... | collective-permute-start | bytes 491528 | tf_op jit(solution)/shard_map/ppermute | solution.py:314
  39.0 2.8 %collective-permute-start.2 = (f32[9,5,8,128]{3,2,1,0:T(8,128)S(1)}, f32[9,5,8,128]{3,2,1,0:T(8,128)S(1)}, u32[]{:S(2)}, u32[]{:S(2)}) collective-permute-start(f32[9,5,8,128]{3,2,1,0:T(8,128)S(1)} %collective-permute-done.1.refs_1_), channel_id=1, source_target_pairs={{16,24},{17,25},{18,26},{19,27},{20,28},{21,29},{22,30},{23,31}} | collective-permute-start | bytes 552968 | tf_op jit(solution)/shard_map/ppermute | solution.py:314
  39.6 2.2 %collective-permute-start.11 = (f32[8,5,8,128]{3,2,1,0:T(8,128)S(1)}, f32[8,5,8,128]{3,2,1,0:T(8,128)S(1)}, u32[]{:S(2)}, u32[]{:S(2)}) collective-permute-start(f32[8,5,8,128]{3,2,1,0:T(8,128)S(1)} %collective-permute-done.10.refs_1_), channel_id=1, source_target_pairs={{16,24},{17,25},{18,26},{19,27},{20,28},{21,29},{22,30},{23,31}} | collective-permute-start | bytes 491528 | tf_op jit(solution)/shard_map/ppermute | solution.py:314
  40.3 3.8 %collective-permute-start.8 = (f32[8,5,8,128]{3,2,1,0:T(8,128)S(1)}, f32[8,5,8,128]{3,2,1,0:T(8,128)S(1)}, u32[]{:S(2)}, u32[]{:S(2)}) collective-permute-start(f32[8,5,8,128]{3,2,1,0:T(8,128)S(1)} %collective-permute-done.7.refs_1_), channel_id=1, source_target_pairs={{16,24},{17,25},{18,26},{19,27},{20,28},{21,29},{22,30},{23,31}} | collective-permute-start | bytes 491528 | tf_op jit(solution)/shard_map/ppermute | solution.py:314
  41.0 5.4 %collective-permute-start.5 = (f32[8,5,8,128]{3,2,1,0:T(8,128)S(1)}, f32[8,5,8,128]{3,2,1,0:T(8,128)S(1)}, u32[]{:S(2)}, u32[]{:S(2)}) collective-permute-start(f32[8,5,8,128]{3,2,1,0:T(8,128)S(1)} %collective-permute-done.4.refs_1_), channel_id=1, source_target_pairs={{16,24},{17,25},{18,26},{19,27},{20,28},{21,29},{22,30},{23,31}} | collective-permute-start | bytes 491528 | tf_op jit(solution)/shard_map/ppermute | solution.py:314
  43.5 7.5 %collective-permute-start.21 = (f32[2,6,8,512]{3,2,1,0:T(8,128)S(1)}, f32[2,6,8,512]{3,2,1,0:T(8,128)S(1)}, u32[]{:S(2)}, u32[]{:S(2)}) collective-permute-start(f32[2,6,8,512]{3,2,1,0:T(8,128)S(1)} %get-tuple-element.58.b_ref), channel_id=1, source_target_pairs={{24,16},{25,17},{26,18},{27,19},{28,20},{29,21},{30,22},{31,23}} | collective-permute-start | bytes 589832 | tf_op jit(solution)/shard_map/ppermute | solution.py:317
  45.7 6.7 %collective-permute-start.18 = (f32[2,6,8,512]{3,2,1,0:T(8,128)S(1)}, f32[2,6,8,512]{3,2,1,0:T(8,128)S(1)}, u32[]{:S(2)}, u32[]{:S(2)}) collective-permute-start(f32[2,6,8,512]{3,2,1,0:T(8,128)S(1)} %get-tuple-element.54.b_ref), channel_id=1, source_target_pairs={{24,16},{25,17},{26,18},{27,19},{28,20},{29,21},{30,22},{31,23}} | collective-permute-start | bytes 589832 | tf_op jit(solution)/shard_map/ppermute | solution.py:317
  48.0 3.0 %copy-start.6 = (f32[5]{0:T(128)S(1)}, f32[5]{0:T(128)}, u32[]{:S(2)}) copy-start(f32[5]{0:T(128)} %mix_ref.25) | copy-start | bytes 64
  48.0 5.9 %collective-permute-start.15 = (f32[2,6,8,512]{3,2,1,0:T(8,128)S(1)}, f32[2,6,8,512]{3,2,1,0:T(8,128)S(1)}, u32[]{:S(2)}, u32[]{:S(2)}) collective-permute-start(f32[2,6,8,512]{3,2,1,0:T(8,128)S(1)} %get-tuple-element.50.b_ref), channel_id=1, source_target_pairs={{24,16},{25,17},{26,18},{27,19},{28,20},{29,21},{30,22},{31,23}} | collective-permute-start | bytes 589832 | tf_op jit(solution)/shard_map/ppermute | solution.py:317
  50.3 5.9 %copy-start.2 = (f32[2,25,8,512]{3,2,1,0:T(8,128)}, f32[2,25,8,512]{3,2,1,0:T(8,128)S(1)}, u32[]{:S(2)}) copy-start(f32[2,25,8,512]{3,2,1,0:T(8,128)S(1)} %get-tuple-element.34.refs_0_) | copy-start | bytes 2457604
  50.3 5.1 %collective-permute-start.12 = (f32[2,6,8,512]{3,2,1,0:T(8,128)S(1)}, f32[2,6,8,512]{3,2,1,0:T(8,128)S(1)}, u32[]{:S(2)}, u32[]{:S(2)}) collective-permute-start(f32[2,6,8,512]{3,2,1,0:T(8,128)S(1)} %get-tuple-element.46.b_ref), channel_id=1, source_target_pairs={{24,16},{25,17},{26,18},{27,19},{28,20},{29,21},{30,22},{31,23}} | collective-permute-start | bytes 589832 | tf_op jit(solution)/shard_map/ppermute | solution.py:317
  51.8 5.1 %collective-permute-start.22 = (f32[2,6,8,512]{3,2,1,0:T(8,128)S(1)}, f32[2,6,8,512]{3,2,1,0:T(8,128)S(1)}, u32[]{:S(2)}, u32[]{:S(2)}) collective-permute-start(f32[2,6,8,512]{3,2,1,0:T(8,128)S(1)} %carry.14), channel_id=1, source_target_pairs={{16,8},{17,9},{18,10},{19,11},{20,12},{21,13},{22,14},{23,15}} | collective-permute-start | bytes 589832 | tf_op jit(solution)/shard_map/ppermute | solution.py:317
  53.2 5.7 %collective-permute-start.19 = (f32[2,6,8,512]{3,2,1,0:T(8,128)S(1)}, f32[2,6,8,512]{3,2,1,0:T(8,128)S(1)}, u32[]{:S(2)}, u32[]{:S(2)}) collective-permute-start(f32[2,6,8,512]{3,2,1,0:T(8,128)S(1)} %carry.12), channel_id=1, source_target_pairs={{16,8},{17,9},{18,10},{19,11},{20,12},{21,13},{22,14},{23,15}} | collective-permute-start | bytes 589832 | tf_op jit(solution)/shard_map/ppermute | solution.py:317
  54.7 6.4 %collective-permute-start.16 = (f32[2,6,8,512]{3,2,1,0:T(8,128)S(1)}, f32[2,6,8,512]{3,2,1,0:T(8,128)S(1)}, u32[]{:S(2)}, u32[]{:S(2)}) collective-permute-start(f32[2,6,8,512]{3,2,1,0:T(8,128)S(1)} %carry.10), channel_id=1, source_target_pairs={{16,8},{17,9},{18,10},{19,11},{20,12},{21,13},{22,14},{23,15}} | collective-permute-start | bytes 589832 | tf_op jit(solution)/shard_map/ppermute | solution.py:317
  56.2 34.5 %copy-start.8 = (f32[5]{0:T(128)S(1)}, f32[5]{0:T(128)}, u32[]{:S(2)}) copy-start(f32[5]{0:T(128)} %weight_ref.9) | copy-start | bytes 64
  56.2 7.0 %collective-permute-start.13 = (f32[2,6,8,512]{3,2,1,0:T(8,128)S(1)}, f32[2,6,8,512]{3,2,1,0:T(8,128)S(1)}, u32[]{:S(2)}, u32[]{:S(2)}) collective-permute-start(f32[2,6,8,512]{3,2,1,0:T(8,128)S(1)} %carry.8), channel_id=1, source_target_pairs={{16,8},{17,9},{18,10},{19,11},{20,12},{21,13},{22,14},{23,15}} | collective-permute-start | bytes 589832 | tf_op jit(solution)/shard_map/ppermute | solution.py:317
  57.7 33.0 %collective-permute-start.23 = (f32[2,6,8,512]{3,2,1,0:T(8,128)S(1)}, f32[2,6,8,512]{3,2,1,0:T(8,128)S(1)}, u32[]{:S(2)}, u32[]{:S(2)}) collective-permute-start(f32[2,6,8,512]{3,2,1,0:T(8,128)S(1)} %carry.15), channel_id=1, source_target_pairs={{8,0},{9,1},{10,2},{11,3},{12,4},{13,5},{14,6},{15,7}} | collective-permute-start | bytes 589832 | tf_op jit(solution)/shard_map/ppermute | solution.py:317
  59.8 35.2 %collective-permute-start.20 = (f32[2,6,8,512]{3,2,1,0:T(8,128)S(1)}, f32[2,6,8,512]{3,2,1,0:T(8,128)S(1)}, u32[]{:S(2)}, u32[]{:S(2)}) collective-permute-start(f32[2,6,8,512]{3,2,1,0:T(8,128)S(1)} %carry.13), channel_id=1, source_target_pairs={{8,0},{9,1},{10,2},{11,3},{12,4},{13,5},{14,6},{15,7}} | collective-permute-start | bytes 589832 | tf_op jit(solution)/shard_map/ppermute | solution.py:317
  61.9 37.3 %collective-permute-start.17 = (f32[2,6,8,512]{3,2,1,0:T(8,128)S(1)}, f32[2,6,8,512]{3,2,1,0:T(8,128)S(1)}, u32[]{:S(2)}, u32[]{:S(2)}) collective-permute-start(f32[2,6,8,512]{3,2,1,0:T(8,128)S(1)} %carry.11), channel_id=1, source_target_pairs={{8,0},{9,1},{10,2},{11,3},{12,4},{13,5},{14,6},{15,7}} | collective-permute-start | bytes 589832 | tf_op jit(solution)/shard_map/ppermute | solution.py:317
  63.9 37.3 %collective-permute-start.14 = (f32[2,6,8,512]{3,2,1,0:T(8,128)S(1)}, f32[2,6,8,512]{3,2,1,0:T(8,128)S(1)}, u32[]{:S(2)}, u32[]{:S(2)}) collective-permute-start(f32[2,6,8,512]{3,2,1,0:T(8,128)S(1)} %carry.9), channel_id=1, source_target_pairs={{8,0},{9,1},{10,2},{11,3},{12,4},{13,5},{14,6},{15,7}} | collective-permute-start | bytes 589832 | tf_op jit(solution)/shard_map/ppermute | solution.py:317
  103.9 14.6 %all-to-all-start.1 = ((f32[8,5,8,512]{3,2,1,0:T(8,128)}), f32[8,5,8,512]{3,2,1,0:T(8,128)S(1)}, u32[]{:S(2)}, u32[]{:S(2)}) async-start(f32[8,5,8,512]{3,2,1,0:T(8,128)} %stencil.1), calls=%async_computation.1 | async-start | bytes 1310720 | tf_op jit(solution)/shard_map/all_to_all | solution.py:420
  107.4 1.1 copy-start.3

commit v6 on v5

--- a/solution.py
+++ b/solution.py
@@ -17,10 +17,10 @@
 MIX_LANE = 64
 
 
-def pack_kernel(weight_ref, p_ref, out_ref):
+def pack_kernel(coef_ref, p_ref, out_ref):
     planes, rows, width = p_ref.shape
     for k in range(planes):
-        w = weight_ref[k]
+        w = coef_ref[0, k]
         for s in range(out_ref.shape[0]):
             before = (R * s - 1) % rows
             after = (R * (s + 1)) % rows
@@ -36,14 +36,14 @@
                 out_ref[s, t, k] = strip[:, EDGE * t : EDGE * (t + 1)]
 
 
-def split_kernel(mix_ref, in_ref, *outs):
+def split_kernel(coef_ref, in_ref, *outs):
     tiles, planes = in_ref.shape[0:2]
     length = tiles // len(outs)
     lane = lax.broadcasted_iota(jnp.int32, (SUB, EDGE), 1)
     for c, out_ref in enumerate(outs):
         out_ref[0:length] = in_ref[length * c : length * (c + 1)]
     for k in range(planes):
-        edge = jnp.where(lane == MIX_LANE, mix_ref[k] - 1.0, 0.0)
+        edge = jnp.where(lane == MIX_LANE, coef_ref[1, k] - 1.0, 0.0)
         for c in range(len(outs)):
             after = in_ref[(length * (c + 1)) % tiles, k]
             before = in_ref[(length * c - 1) % tiles, k]
@@ -91,31 +91,30 @@
     return (new_p, [keep * x for x in p])
 
 
-def pack_state(out_ref, fields):
+def pack_state(out_ref, step, fields, extra_ref=None):
     for j in range(R):
-        out_ref[0, j] = jnp.concatenate(
+        tile = jnp.concatenate(
             [fields[j], fields[6][j : j + 1], fields[7][j : j + 1]], axis=0
         )
-
-
-def unpack_state(arrived):
-    tiles = [sum(in_ref[0, j] for in_ref in arrived) for j in range(R)]
+        out_ref[step, j] = tile if extra_ref is None else tile + extra_ref[step, j]
+
+
+def unpack_state(arrived, step):
+    tiles = [sum(in_ref[step, j] for in_ref in arrived) for j in range(R)]
     fields = [t[0:R] for t in tiles]
     fields.append(jnp.concatenate([t[6:7] for t in tiles], axis=0))
     fields.append(jnp.concatenate([t[7:8] for t in tiles], axis=0))
     return fields
 
 
-def forward_kernel(groups, planes, chunk, length, *refs):
+def forward_block(groups, planes, chunk, length, step, *refs):
     strips = refs[:groups]
     beside_ref, excess_ref, obs_ref, noise_ref = refs[groups : groups + 4]
     map_ref, m_ref, a_ref, src_ref, b_ref = refs[-5:]
-    step = pl.program_id(0)
-    width = obs_ref.shape[-1]
+    width = m_ref.shape[-1]
     span = width // EDGE
     first = step * span
-    at_start = first == 0
-    at_end = first + span == length
+    start = EDGE * (chunk * length + first)
     one = jnp.ones((SUB, width), F32)
     zero = jnp.zeros((SUB, width), F32)
     a = [one, zero, zero, one]
@@ -133,8 +132,8 @@
             excess = excess_ext[:, EDGE:-EDGE]
             mix_ext = jnp.concatenate([1.0 + excess_tile] * (span + 2), axis=1)
             mix = mix_ext[:, EDGE:-EDGE]
-            left = jnp.where(at_start, beside, strip_ref[jnp.maximum(first - 1, 0), k])
-            right = jnp.where(at_end, beside, strip_ref[jnp.minimum(first + span, length - 1), k])
+            left = strip_ref[first - 1, k] if first > 0 else beside
+            right = strip_ref[first + span, k] if first + span < length else beside
             tiles = [strip_ref[first + t, k] for t in range(span)]
             mid = jnp.concatenate(tiles, axis=1)
             ext = jnp.concatenate([left] + tiles + [right], axis=1)
@@ -146,12 +145,12 @@
             m1 = mix - (col_next(ext) + col_prev(ext) - twice)
             off = 0.25 * (col_prev(across) - col_next(across))
             if own:
-                m_ref[0, 3 * k] = m0
-                m_ref[0, 3 * k + 1] = m1
-                m_ref[0, 3 * k + 2] = off
+                m_ref[step, 3 * k] = m0
+                m_ref[step, 3 * k + 1] = m1
+                m_ref[step, 3 * k + 2] = off
                 keeps.append(-excess[0:R])
                 for j in range(4):
-                    a_ref[0, 4 * k + j] = a[j]
+                    a_ref[step, 4 * k + j] = a[j]
             new_a = [
                 m0 * a[0] + off * a[2] - excess * a_before[0],
                 m0 * a[1] + off * a[3] - excess * a_before[1],
@@ -169,21 +168,29 @@
                     -0.5 * (a[1] + a[2]),
                 ]
                 for j, field in enumerate([slope_rows, slope_cols] + shear):
-                    map_ref[0, 5 * k + j] = field
-                noise = -0.5 * noise_ref[k]
-                r = [noise * (shear[j][0:R] - obs_ref[k, j]) for j in range(3)]
-                src_ref[0, 3 * k, 0:R] = r[0] + r[1]
-                src_ref[0, 3 * k + 1, 0:R] = r[2]
-                src_ref[0, 3 * k + 2, 0:R] = r[0] - r[1]
+                    map_ref[step, 5 * k + j] = field
+                noise = -0.5 * noise_ref[k, :, start : start + width]
+                r = [
+                    noise * (shear[j][0:R] - obs_ref[k, j, :, start : start + width])
+                    for j in range(3)
+                ]
+                src_ref[step, 3 * k, 0:R] = r[0] + r[1]
+                src_ref[step, 3 * k + 1, 0:R] = r[2]
+                src_ref[step, 3 * k + 2, 0:R] = r[0] - r[1]
     none = jnp.zeros((R, width), F32)
     p = [none] * 4
     q = [none] * 4
     for k in reversed(range(planes)):
-        s0, s1, s3 = (src_ref[0, 3 * k + j, 0:R] for j in range(3))
+        s0, s1, s3 = (src_ref[step, 3 * k + j, 0:R] for j in range(3))
         p = [p[0] + s0, p[1] + s1, p[2] + s1, p[3] + s3]
-        m0, m1, off = (m_ref[0, 3 * k + j, 0:R] for j in range(3))
+        m0, m1, off = (m_ref[step, 3 * k + j, 0:R] for j in range(3))
         p, q = transposed_step(m0, m1, off, p, q, keeps[k])
-    pack_state(b_ref, p + q)
+    pack_state(b_ref, step, p + q)
+
+
+def forward_kernel(groups, planes, chunk, length, *refs):
+    for step in range(refs[-1].shape[0]):
+        forward_block(groups, planes, chunk, length, step, *refs)
 
 
 def assemble_kernel(*refs):
@@ -200,36 +207,38 @@
                     shear_ref[k, j, :, start : start + width] = map_ref[i, 5 * k + 2 + j, 0:R]
 
 
-def carry_kernel(planes, mix_ref, in_ref, b_ref, m_ref, out_ref):
-    fields = unpack_state([in_ref])
-    p, q = (fields[0:4], fields[4:8])
-    for k in reversed(range(planes)):
-        m0, m1, off = (m_ref[0, 3 * k + j, 0:R] for j in range(3))
-        p, q = transposed_step(m0, m1, off, p, q, 1.0 - mix_ref[k])
-    pack_state(out_ref, p + q)
-    out_ref[...] += b_ref[...]
-
-
-def cotangent_kernel(planes, mix_ref, weight_ref, src_ref, m_ref, a_ref, *refs):
+def carry_kernel(planes, sender, coef_ref, in_ref, b_ref, m_ref, out_ref):
+    @pl.when(lax.axis_index("plane") == sender)
+    def _():
+        for step in range(out_ref.shape[0]):
+            fields = unpack_state([in_ref], step)
+            p, q = (fields[0:4], fields[4:8])
+            for k in reversed(range(planes)):
+                m0, m1, off = (m_ref[step, 3 * k + j, 0:R] for j in range(3))
+                p, q = transposed_step(m0, m1, off, p, q, 1.0 - coef_ref[1, k])
+            pack_state(out_ref, step, p + q, b_ref)
+
+
+def cotangent_kernel(planes, coef_ref, src_ref, m_ref, a_ref, *refs):
     arrived, cot_ref = (refs[:-1], refs[-1])
-    width = cot_ref.shape[-1]
-    fields = unpack_state(arrived)
-    p, q = (fields[0:4], fields[4:8])
-    blank = jnp.zeros((SUB - R, width), F32)
-    for k in reversed(range(planes)):
-        s0, s1, s3 = (src_ref[0, 3 * k + j, 0:R] for j in range(3))
-        p = [p[0] + s0, p[1] + s1, p[2] + s1, p[3] + s3]
-        a = [a_ref[0, 4 * k + j, 0:R] for j in range(4)]
-        w = -weight_ref[k]
-        cots = [
-            w * (p[0] * a[0] + p[1] * a[1]),
-            w * (p[2] * a[2] + p[3] * a[3]),
-            (0.25 * w) * (p[0] * a[2] + p[1] * a[3] + p[2] * a[0] + p[3] * a[1]),
-        ]
-        for j in range(3):
-            cot_ref[0, 3 * k + j] = jnp.concatenate([cots[j], blank], axis=0)
-        m0, m1, off = (m_ref[0, 3 * k + j, 0:R] for j in range(3))
-        p, q = transposed_step(m0, m1, off, p, q, 1.0 - mix_ref[k])
+    blank = jnp.zeros((SUB - R, cot_ref.shape[-1]), F32)
+    for step in range(cot_ref.shape[0]):
+        fields = unpack_state(arrived, step)
+        p, q = (fields[0:4], fields[4:8])
+        for k in reversed(range(planes)):
+            s0, s1, s3 = (src_ref[step, 3 * k + j, 0:R] for j in range(3))
+            p = [p[0] + s0, p[1] + s1, p[2] + s1, p[3] + s3]
+            a = [a_ref[step, 4 * k + j, 0:R] for j in range(4)]
+            w = -coef_ref[0, k]
+            cots = [
+                w * (p[0] * a[0] + p[1] * a[1]),
+                w * (p[2] * a[2] + p[3] * a[3]),
+                (0.25 * w) * (p[0] * a[2] + p[1] * a[3] + p[2] * a[0] + p[3] * a[1]),
+            ]
+            for j in range(3):
+                cot_ref[step, 3 * k + j] = jnp.concatenate([cots[j], blank], axis=0)
+            m0, m1, off = (m_ref[step, 3 * k + j, 0:R] for j in range(3))
+            p, q = transposed_step(m0, m1, off, p, q, 1.0 - coef_ref[1, k])
 
 
 def stencil_kernel(planes, *refs):
@@ -291,10 +300,6 @@
     return pltpu.CompilerParams(vmem_limit_bytes=VMEM_LIMIT)
 
 
-def block_of(*dims):
-    return pl.BlockSpec((1,) + dims, lambda c: (c,) + (0,) * len(dims))
-
-
 SCALARS = pl.BlockSpec(memory_space=pltpu.SMEM)
 WHOLE = pl.BlockSpec(memory_space=pltpu.VMEM)
 
@@ -316,6 +321,7 @@
     def descend(x, hop):
         return lax.ppermute(x, "plane", [(groups - 1 - hop, groups - 2 - hop)])
 
+    coef = jnp.stack([lens_weight, mixing])
     packed = pl.pallas_call(
         pack_kernel,
         out_shape=shape(slabs, tiles, planes, SUB, EDGE),
@@ -323,7 +329,7 @@
         out_specs=WHOLE,
         compiler_params=params(),
         name="pack",
-    )(lens_weight, potential)
+    )(coef, potential)
     own = lax.all_to_all(packed, "slab", split_axis=0, concat_axis=0, tiled=True)
     own = own.reshape(slabs * tiles, planes, SUB, EDGE)
     pieces = pl.pallas_call(
@@ -335,7 +341,7 @@
         out_specs=(WHOLE,) * CHUNKS,
         compiler_params=params(),
         name="split",
-    )(mixing, own)
+    )(coef, own)
     strips = [[piece] for piece in pieces]
     for turn in range(CHUNKS + groups - 2):
         for c in range(CHUNKS):
@@ -354,20 +360,11 @@
         name="edges",
     )(*strips[0])
 
-    state = block_of(R, SUB, span)
-    triple = block_of(3 * planes, SUB, span)
-    quad = block_of(4 * planes, SUB, span)
-    quint = block_of(5 * planes, SUB, span)
     maps = []
     work = []
     for c in range(CHUNKS):
-
-        def columns_of(*dims, at=c * steps):
-            return pl.BlockSpec(dims + (span,), lambda i: (0,) * len(dims) + (at + i,))
-
         map_piece, *held = pl.pallas_call(
             functools.partial(forward_kernel, groups, planes, c, length),
-            grid=(steps,),
             out_shape=(
                 shape(steps, 5 * planes, SUB, span),
                 shape(steps, 3 * planes, SUB, span),
@@ -375,8 +372,8 @@
                 shape(steps, 3 * planes, SUB, span),
                 shape(steps, R, SUB, span),
             ),
-            in_specs=[WHOLE] * (groups + 2) + [columns_of(planes, 3, R), columns_of(planes, R)],
-            out_specs=(quint, triple, quad, triple, state),
+            in_specs=[WHOLE] * (groups + 4),
+            out_specs=(WHOLE,) * 5,
             compiler_params=params(),
             name="forward",
         )(*strips[c], beside, excess, observed, noise_weight)
@@ -388,25 +385,23 @@
         arrived = [descend(b, 0)]
         for hop in range(1, groups - 1):
             outgoing = pl.pallas_call(
-                functools.partial(carry_kernel, planes),
-                grid=(steps,),
+                functools.partial(carry_kernel, planes, groups - 1 - hop),
                 out_shape=shape(steps, R, SUB, span),
-                in_specs=[SCALARS, state, state, triple],
-                out_specs=state,
+                in_specs=[SCALARS] + [WHOLE] * 3,
+                out_specs=WHOLE,
                 compiler_params=params(),
                 name="carry",
-            )(mixing, arrived[-1], b, matrices)
+            )(coef, arrived[-1], b, matrices)
             arrived.append(descend(outgoing, hop))
         cots.append(
             pl.pallas_call(
                 functools.partial(cotangent_kernel, planes),
-                grid=(steps,),
                 out_shape=shape(steps, 3 * planes, SUB, span),
-                in_specs=[SCALARS, SCALARS, triple, triple, quad] + [state] * (groups - 1),
-                out_specs=triple,
+                in_specs=[SCALARS] + [WHOLE] * (groups + 2),
+                out_specs=WHOLE,
                 compiler_params=params(),
                 name="cotangent",
-            )(mixing, lens_weight, sources, matrices, states, *arrived)
+            )(coef, sources, matrices, states, *arrived)
         )
 
     partial = pl.pallas_call(

time: 120 us -> 119 us (level)
  Pallas kernels: 21.5 us -> 19 us
  waiting for transfers between devices: 43.4 us -> 45.7 us
  local copies, waits for them, and re-layouts: 5.34 us -> 3.89 us
    ppermute x12, waiting for transfers between devices: 33.5 us -> 35.7 us  [descend(): return lax.ppermute(x, 'plane', [(groups - 1 - hop, groups - 2 - hop)])]
    pallas_call x12, Pallas kernels: 9.56 us -> 7.73 us  [the longest x8 4.52 us: on_device(): pl.pallas_call(functools.partial(carry_kernel, planes, groups - 1 - hop),...]
    unnamed x19 -> x11, local copies, waits for them, and re-layouts: 5.34 us -> 3.89 us
  transfers between devices with their start and end apart: 25 -> 25, of which waited for: 7 -> 7; matrix products, arithmetic and copies ran while one was open for 1% -> 1% of each run, Pallas kernels for 14% -> 12%
where the time goes in v6:
time: 119 us
  waiting for transfers between devices  45.7 us (38%)
  starting transfers between devices  31.8 us (27%)
  Pallas kernels  19 us (16%)
  blocking collectives  16.1 us (14%)
  local copies, waits for them, and re-layouts  3.89 us (3%)
    ppermute x12, waiting for transfers between devices, descend(): return lax.ppermute(x, 'plane', [(groups - 1 - hop, groups - 2 - hop)])  35.7 us
    ppermute x12, starting transfers between devices, climb(): lax.ppermute(x, 'plane', [(i, i + 1) for i in range(hop, groups - 1)])  17.7 us
    all_to_all x1, blocking collectives, on_device(): lax.all_to_all(packed, 'slab', split_axis=0, concat_axis=0, tiled=True)  16.1 us
    ppermute x12, starting transfers between devices, descend(): return lax.ppermute(x, 'plane', [(groups - 1 - hop, groups - 2 - hop)])  10.6 us
    all_to_all x1, waiting for transfers between devices, on_device(): lax.all_to_all(partial, 'slab', split_axis=0, concat_axis=0, tiled=True)  6.68 us
    pallas_call x4, Pallas kernels, on_device(): pl.pallas_call(functools.partial(forward_kernel, groups, planes, c, lengt...  5.59 us
    pallas_call x8, Pallas kernels, on_device(): pl.pallas_call(functools.partial(carry_kernel, planes, groups - 1 - hop),...  4.52 us
    unnamed x11, local copies, waits for them, and re-layouts  3.89 us
  transfers between devices with their start and end apart: 25, of which 7 were waited for; matrix products, arithmetic and copies ran while one was open for 1% of the time, Pallas kernels for 12%

profile of v6, /device:TPU:0, one launch (start us, length us, event | category | flops | bytes accessed | tf_op | source)
XLA Modules:
  0.0 118.5 jit_solution(9363069926982709458)
XLA Ops:
  0.7 0.8 pad_maximum_fusion.coef_ref
  1.5 1.0 copy-done.4
  2.5 0.7 pack.1
  3.2 16.1 %all_to_all.10 = f32[8,4,5,8,128]{4,3,2,1,0:T(8,128)S(1)} all-to-all(f32[8,4,5,8,128]{4,3,2,1,0:T(8,128)S(1)} %pack.1), channel_id=1, replica_groups=mesh['plane'=4,'slab'=8] {'slab'}, dimensions={0} | all-to-all | bytes 1310720 | tf_op jit(solution)/shard_map/all_to_all | solution.py:333
  20.0 3.5 %collective-permute-start = (f32[9,5,8,128]{3,2,1,0:T(8,128)S(1)}, f32[9,5,8,128]{3,2,1,0:T(8,128)S(1)}, u32[]{:S(2)}, u32[]{:S(2)}) collective-permute-start(f32[9,5,8,128]{3,2,1,0:T(8,128)S(1)} %get-tuple-element.31.refs_3_), channel_id=1, source_target_pairs={{0,8},{8,16},{16,24},{1,9},{9,17},{17,25},{2,10},{10,18},{18,26},{... | collective-permute-start | bytes 552968 | tf_op jit(solution)/shard_map/ppermute | solution.py:319
  23.5 3.5 %collective-permute-start.9 = (f32[8,5,8,128]{3,2,1,0:T(8,128)S(1)}, f32[8,5,8,128]{3,2,1,0:T(8,128)S(1)}, u32[]{:S(2)}, u32[]{:S(2)}) collective-permute-start(f32[8,5,8,128]{3,2,1,0:T(8,128)S(1)} %get-tuple-element.39.refs_3_), channel_id=1, source_target_pairs={{0,8},{8,16},{16,24},{1,9},{9,17},{17,25},{2,10},{10,18},{18,26},{... | collective-permute-start | bytes 491528 | tf_op jit(solution)/shard_map/ppermute | solution.py:319
  27.0 3.5 %collective-permute-start.6 = (f32[8,5,8,128]{3,2,1,0:T(8,128)S(1)}, f32[8,5,8,128]{3,2,1,0:T(8,128)S(1)}, u32[]{:S(2)}, u32[]{:S(2)}) collective-permute-start(f32[8,5,8,128]{3,2,1,0:T(8,128)S(1)} %get-tuple-element.37.refs_3_), channel_id=1, source_target_pairs={{0,8},{8,16},{16,24},{1,9},{9,17},{17,25},{2,10},{10,18},{18,26},{... | collective-permute-start | bytes 491528 | tf_op jit(solution)/shard_map/ppermute | solution.py:319
  30.5 1.9 %collective-permute-start.3 = (f32[8,5,8,128]{3,2,1,0:T(8,128)S(1)}, f32[8,5,8,128]{3,2,1,0:T(8,128)S(1)}, u32[]{:S(2)}, u32[]{:S(2)}) collective-permute-start(f32[8,5,8,128]{3,2,1,0:T(8,128)S(1)} %get-tuple-element.35.refs_3_), channel_id=1, source_target_pairs={{0,8},{8,16},{16,24},{1,9},{9,17},{17,25},{2,10},{10,18},{18,26},{... | collective-permute-start | bytes 491528 | tf_op jit(solution)/shard_map/ppermute | solution.py:319
  32.4 0.7 collective-permute-start.1
  33.1 0.7 collective-permute-start.10
  33.8 1.3 %collective-permute-done.6.refs_2_ = f32[8,5,8,128]{3,2,1,0:T(8,128)S(1)} collective-permute-done((f32[8,5,8,128]{3,2,1,0:T(8,128)S(1)}, f32[8,5,8,128]{3,2,1,0:T(8,128)S(1)}, u32[]{:S(2)}, u32[]{:S(2)}) %collective-permute-start.6) | collective-permute-done | bytes 163872 | tf_op jit(solution)/shard_map/ppermute | solution.py:319
  35.1 0.7 collective-permute-start.7
  35.8 1.9 %collective-permute-done.3.refs_2_ = f32[8,5,8,128]{3,2,1,0:T(8,128)S(1)} collective-permute-done((f32[8,5,8,128]{3,2,1,0:T(8,128)S(1)}, f32[8,5,8,128]{3,2,1,0:T(8,128)S(1)}, u32[]{:S(2)}, u32[]{:S(2)}) %collective-permute-start.3) | collective-permute-done | bytes 163872 | tf_op jit(solution)/shard_map/ppermute | solution.py:319
  38.4 0.7 collective-permute-start.2
  39.1 0.7 collective-permute-start.11
  39.7 0.7 collective-permute-start.8
  40.4 0.7 collective-permute-start.5
  41.3 1.4 %forward.7 = (f32[2,25,8,512]{3,2,1,0:T(8,128)S(1)}, f32[2,15,8,512]{3,2,1,0:T(8,128)S(1)}, f32[2,20,8,512]{3,2,1,0:T(8,128)S(1)}, f32[2,15,8,512]{3,2,1,0:T(8,128)S(1)}, f32[2,6,8,512]{3,2,1,0:T(8,128)S(1)}) custom-call(f32[8,5,8,128]{3,2,1,0:T(8,128)S(1)} %collective-permute-done.11.refs_0_, f32[8,5,8,128]{3,2,1,0:T(8,128)S(1)} %collective-permute-done.10.refs_1_, ...), custom_call_target="tpu_custom_call" | custom-call | tf_op jit(solution)/shard_map/forward/pallas_call | solution.py:366
  42.7 0.7 collective-permute-start.21
  43.4 1.4 %forward.6 = (f32[2,25,8,512]{3,2,1,0:T(8,128)S(1)}, f32[2,15,8,512]{3,2,1,0:T(8,128)S(1)}, f32[2,20,8,512]{3,2,1,0:T(8,128)S(1)}, f32[2,15,8,512]{3,2,1,0:T(8,128)S(1)}, f32[2,6,8,512]{3,2,1,0:T(8,128)S(1)}) custom-call(f32[8,5,8,128]{3,2,1,0:T(8,128)S(1)} %collective-permute-done.8.refs_0_, f32[8,5,8,128]{3,2,1,0:T(8,128)S(1)} %collective-permute-done.7.refs_1_, ...), custom_call_target="tpu_custom_call" | custom-call | tf_op jit(solution)/shard_map/forward/pallas_call | solution.py:366
  44.8 0.7 collective-permute-start.18
  45.5 1.4 %forward.5 = (f32[2,25,8,512]{3,2,1,0:T(8,128)S(1)}, f32[2,15,8,512]{3,2,1,0:T(8,128)S(1)}, f32[2,20,8,512]{3,2,1,0:T(8,128)S(1)}, f32[2,15,8,512]{3,2,1,0:T(8,128)S(1)}, f32[2,6,8,512]{3,2,1,0:T(8,128)S(1)}) custom-call(f32[8,5,8,128]{3,2,1,0:T(8,128)S(1)} %collective-permute-done.5.refs_0_, f32[8,5,8,128]{3,2,1,0:T(8,128)S(1)} %collective-permute-done.4.refs_1_, ...), custom_call_target="tpu_custom_call" | custom-call | tf_op jit(solution)/shard_map/forward/pallas_call | solution.py:366
  46.9 0.7 collective-permute-start.15
  47.6 1.4 %forward.4 = (f32[2,25,8,512]{3,2,1,0:T(8,128)S(1)}, f32[2,15,8,512]{3,2,1,0:T(8,128)S(1)}, f32[2,20,8,512]{3,2,1,0:T(8,128)S(1)}, f32[2,15,8,512]{3,2,1,0:T(8,128)S(1)}, f32[2,6,8,512]{3,2,1,0:T(8,128)S(1)}) custom-call(f32[9,5,8,128]{3,2,1,0:T(8,128)S(1)} %collective-permute-done.2.refs_0_, f32[9,5,8,128]{3,2,1,0:T(8,128)S(1)} %collective-permute-done.1.refs_1_, ...), custom_call_target="tpu_custom_call" | custom-call | tf_op jit(solution)/shard_map/forward/pallas_call | solution.py:366
  49.0 0.7 collective-permute-start.12
  50.3 0.7 collective-permute-start.22
  51.5 0.7 collective-permute-start.19
  52.8 0.7 collective-permute-start.16
  54.1 0.7 collective-permute-start.13
  55.3 1.3 %collective-permute-start.23 = (f32[2,6,8,512]{3,2,1,0:T(8,128)S(1)}, f32[2,6,8,512]{3,2,1,0:T(8,128)S(1)}, u32[]{:S(2)}, u32[]{:S(2)}) collective-permute-start(f32[2,6,8,512]{3,2,1,0:T(8,128)S(1)} %carry.15), channel_id=1, source_target_pairs={{8,0},{9,1},{10,2},{11,3},{12,4},{13,5},{14,6},{15,7}} | collective-permute-start | bytes 589832 | tf_op jit(solution)/shard_map/ppermute | solution.py:322
  57.2 1.3 %collective-permute-start.20 = (f32[2,6,8,512]{3,2,1,0:T(8,128)S(1)}, f32[2,6,8,512]{3,2,1,0:T(8,128)S(1)}, u32[]{:S(2)}, u32[]{:S(2)}) collective-permute-start(f32[2,6,8,512]{3,2,1,0:T(8,128)S(1)} %carry.13), channel_id=1, source_target_pairs={{8,0},{9,1},{10,2},{11,3},{12,4},{13,5},{14,6},{15,7}} | collective-permute-start | bytes 589832 | tf_op jit(solution)/shard_map/ppermute | solution.py:322
  59.1 1.3 %collective-permute-start.17 = (f32[2,6,8,512]{3,2,1,0:T(8,128)S(1)}, f32[2,6,8,512]{3,2,1,0:T(8,128)S(1)}, u32[]{:S(2)}, u32[]{:S(2)}) collective-permute-start(f32[2,6,8,512]{3,2,1,0:T(8,128)S(1)} %carry.11), channel_id=1, source_target_pairs={{8,0},{9,1},{10,2},{11,3},{12,4},{13,5},{14,6},{15,7}} | collective-permute-start | bytes 589832 | tf_op jit(solution)/shard_map/ppermute | solution.py:322
  61.0 1.3 %collective-permute-start.14 = (f32[2,6,8,512]{3,2,1,0:T(8,128)S(1)}, f32[2,6,8,512]{3,2,1,0:T(8,128)S(1)}, u32[]{:S(2)}, u32[]{:S(2)}) collective-permute-start(f32[2,6,8,512]{3,2,1,0:T(8,128)S(1)} %carry.9), channel_id=1, source_target_pairs={{8,0},{9,1},{10,2},{11,3},{12,4},{13,5},{14,6},{15,7}} | collective-permute-start | bytes 589832 | tf_op jit(solution)/shard_map/ppermute | solution.py:322
  62.3 27.6 %collective-permute-done.23.refs_2_ = f32[2,6,8,512]{3,2,1,0:T(8,128)S(1)} collective-permute-done((f32[2,6,8,512]{3,2,1,0:T(8,128)S(1)}, f32[2,6,8,512]{3,2,1,0:T(8,128)S(1)}, u32[]{:S(2)}, u32[]{:S(2)}) %collective-permute-start.23) | collective-permute-done | bytes 196640 | tf_op jit(solution)/shard_map/ppermute | solution.py:322
  89.9 0.8 cotangent.7.refs_3_
  90.7 3.4 %collective-permute-done.20.refs_2_ = f32[2,6,8,512]{3,2,1,0:T(8,128)S(1)} collective-permute-done((f32[2,6,8,512]{3,2,1,0:T(8,128)S(1)}, f32[2,6,8,512]{3,2,1,0:T(8,128)S(1)}, u32[]{:S(2)}, u32[]{:S(2)}) %collective-permute-start.20) | collective-permute-done | bytes 196640 | tf_op jit(solution)/shard_map/ppermute | solution.py:322
  94.1 0.8 cotangent.6.refs_2_
  94.9 3.4 %collective-permute-done.17.refs_2_ = f32[2,6,8,512]{3,2,1,0:T(8,128)S(1)} collective-permute-done((f32[2,6,8,512]{3,2,1,0:T(8,128)S(1)}, f32[2,6,8,512]{3,2,1,0:T(8,128)S(1)}, u32[]{:S(2)}, u32[]{:S(2)}) %collective-permute-start.17) | collective-permute-done | bytes 196640 | tf_op jit(solution)/shard_map/ppermute | solution.py:322
  98.3 0.8 cotangent.5.refs_1_
  99.1 1.3 %collective-permute-done.14.refs_2_ = f32[2,6,8,512]{3,2,1,0:T(8,128)S(1)} collective-permute-done((f32[2,6,8,512]{3,2,1,0:T(8,128)S(1)}, f32[2,6,8,512]{3,2,1,0:T(8,128)S(1)}, u32[]{:S(2)}, u32[]{:S(2)}) %collective-permute-start.14) | collective-permute-done | bytes 196640 | tf_op jit(solution)/shard_map/ppermute | solution.py:322
  100.4 0.8 cotangent.4.refs_0_
  101.2 1.8 %stencil.1 = f32[8,5,8,512]{3,2,1,0:T(8,128)} custom-call(f32[2,15,8,512]{3,2,1,0:T(8,128)S(1)} %cotangent.4.refs_0_, f32[2,15,8,512]{3,2,1,0:T(8,128)S(1)} %cotangent.5.refs_1_, f32[2,15,8,512]{3,2,1,0:T(8,128)S(1)} %cotangent.6.refs_2_, f32[2,15,8,512]{3,2,1,0:T(8,128)S(1)} %cotangent.7.refs_3_), custom_call_target="tpu_custom_call" | custom-call | tf_op jit(solution)/shard_map/stencil/pallas_call | solution.py:407
  103.0 3.5 %all-to-all-start.1 = ((f32[8,5,8,512]{3,2,1,0:T(8,128)}), f32[8,5,8,512]{3,2,1,0:T(8,128)S(1)}, u32[]{:S(2)}, u32[]{:S(2)}) async-start(f32[8,5,8,512]{3,2,1,0:T(8,128)} %stencil.1), calls=%async_computation.1 | async-start | bytes 1310720 | tf_op jit(solution)/shard_map/all_to_all | solution.py:415
  106.5 1.1 copy-done.3
  107.7 1.6 %assemble.1 = (f32[5,2,6,4096]{3,2,1,0:T(8,128)S(1)}, f32[5,3,6,4096]{3,2,1,0:T(8,128)}) custom-call(f32[2,25,8,512]{3,2,1,0:T(8,128)S(1)} %copy-done.3, f32[2,25,8,512]{3,2,1,0:T(8,128)S(1)} %get-tuple-element.36.refs_1_, f32[2,25,8,512]{3,2,1,0:T(8,128)S(1)} %get-tuple-element.38.refs_2_, f32[2,25,8,512]{3,2,1,0:T(8,128)S(1)} %get-tuple-element.40.refs_3_), custom_call_target="tpu_custom_call" | custom-call | tf_op jit(solution)/shard_map/assemble/pallas_call | solution.py:416
  109.2 1.7 %copy.8 = f32[5,2,6,4096]{3,1,2,0:T(2,128)} copy(f32[5,2,6,4096]{3,2,1,0:T(8,128)S(1)} %get-tuple-element.59) | data formatting | bytes 1966080
  110.9 6.7 %all-to-all-done.1.in_ref = f32[8,5,8,512]{3,2,1,0:T(8,128)S(1)} async-done(((f32[8,5,8,512]{3,2,1,0:T(8,128)}), f32[8,5,8,512]{3,2,1,0:T(8,128)S(1)}, u32[]{:S(2)}, u32[]{:S(2)}) %all-to-all-start.1) | async-done | bytes 655392 | tf_op jit(solution)/shard_map/all_to_all | solution.py:415
  117.6 0.9 combine.1
  (37 shorter events, 6.0 us)
Async XLA Ops:
  0.6 40.6 %copy-start = (f32[5,3,6,4096]{3,2,1,0:T(8,128)S(1)}, f32[5,3,6,4096]{3,2,1,0:T(8,128)}, u32[]{:S(2)}) copy-start(f32[5,3,6,4096]{3,2,1,0:T(8,128)} %refs_6_.7) | copy-start | bytes 4423684
  0.6 40.6 %copy-start.1 = (f32[5,6,4096]{2,1,0:T(8,128)S(1)}, f32[5,6,4096]{2,1,0:T(8,128)}, u32[]{:S(2)}) copy-start(f32[5,6,4096]{2,1,0:T(8,128)} %refs_7_.7) | copy-start | bytes 1474564
  1.5 1.0 copy-start.4
  20.0 12.4 %collective-permute-start = (f32[9,5,8,128]{3,2,1,0:T(8,128)S(1)}, f32[9,5,8,128]{3,2,1,0:T(8,128)S(1)}, u32[]{:S(2)}, u32[]{:S(2)}) collective-permute-start(f32[9,5,8,128]{3,2,1,0:T(8,128)S(1)} %get-tuple-element.31.refs_3_), channel_id=1, source_target_pairs={{0,8},{8,16},{16,24},{1,9},{9,17},{17,25},{2,10},{10,18},{18,26},{... | collective-permute-start | bytes 552968 | tf_op jit(solution)/shard_map/ppermute | solution.py:319
  23.5 9.6 %collective-permute-start.9 = (f32[8,5,8,128]{3,2,1,0:T(8,128)S(1)}, f32[8,5,8,128]{3,2,1,0:T(8,128)S(1)}, u32[]{:S(2)}, u32[]{:S(2)}) collective-permute-start(f32[8,5,8,128]{3,2,1,0:T(8,128)S(1)} %get-tuple-element.39.refs_3_), channel_id=1, source_target_pairs={{0,8},{8,16},{16,24},{1,9},{9,17},{17,25},{2,10},{10,18},{18,26},{... | collective-permute-start | bytes 491528 | tf_op jit(solution)/shard_map/ppermute | solution.py:319
  27.0 8.1 %collective-permute-start.6 = (f32[8,5,8,128]{3,2,1,0:T(8,128)S(1)}, f32[8,5,8,128]{3,2,1,0:T(8,128)S(1)}, u32[]{:S(2)}, u32[]{:S(2)}) collective-permute-start(f32[8,5,8,128]{3,2,1,0:T(8,128)S(1)} %get-tuple-element.37.refs_3_), channel_id=1, source_target_pairs={{0,8},{8,16},{16,24},{1,9},{9,17},{17,25},{2,10},{10,18},{18,26},{... | collective-permute-start | bytes 491528 | tf_op jit(solution)/shard_map/ppermute | solution.py:319
  30.5 7.2 %collective-permute-start.3 = (f32[8,5,8,128]{3,2,1,0:T(8,128)S(1)}, f32[8,5,8,128]{3,2,1,0:T(8,128)S(1)}, u32[]{:S(2)}, u32[]{:S(2)}) collective-permute-start(f32[8,5,8,128]{3,2,1,0:T(8,128)S(1)} %get-tuple-element.35.refs_3_), channel_id=1, source_target_pairs={{0,8},{8,16},{16,24},{1,9},{9,17},{17,25},{2,10},{10,18},{18,26},{... | collective-permute-start | bytes 491528 | tf_op jit(solution)/shard_map/ppermute | solution.py:319
  32.4 6.0 %collective-permute-start.1 = (f32[9,5,8,128]{3,2,1,0:T(8,128)S(1)}, f32[9,5,8,128]{3,2,1,0:T(8,128)S(1)}, u32[]{:S(2)}, u32[]{:S(2)}) collective-permute-start(f32[9,5,8,128]{3,2,1,0:T(8,128)S(1)} %collective-permute-done.refs_2_), channel_id=1, source_target_pairs={{8,16},{16,24},{9,17},{17,25},{10,18},{18,26},{11,19},{19,27},{12,... | collective-permute-start | bytes 552968 | tf_op jit(solution)/shard_map/ppermute | solution.py:319
  33.1 6.0 %collective-permute-start.10 = (f32[8,5,8,128]{3,2,1,0:T(8,128)S(1)}, f32[8,5,8,128]{3,2,1,0:T(8,128)S(1)}, u32[]{:S(2)}, u32[]{:S(2)}) collective-permute-start(f32[8,5,8,128]{3,2,1,0:T(8,128)S(1)} %collective-permute-done.9.refs_2_), channel_id=1, source_target_pairs={{8,16},{16,24},{9,17},{17,25},{10,18},{18,26},{11,19},{19,27},{12,... | collective-permute-start | bytes 491528 | tf_op jit(solution)/shard_map/ppermute | solution.py:319
  35.1 4.6 %collective-permute-start.7 = (f32[8,5,8,128]{3,2,1,0:T(8,128)S(1)}, f32[8,5,8,128]{3,2,1,0:T(8,128)S(1)}, u32[]{:S(2)}, u32[]{:S(2)}) collective-permute-start(f32[8,5,8,128]{3,2,1,0:T(8,128)S(1)} %collective-permute-done.6.refs_2_), channel_id=1, source_target_pairs={{8,16},{16,24},{9,17},{17,25},{10,18},{18,26},{11,19},{19,27},{12,... | collective-permute-start | bytes 491528 | tf_op jit(solution)/shard_map/ppermute | solution.py:319
  37.7 2.7 %collective-permute-start.4 = (f32[8,5,8,128]{3,2,1,0:T(8,128)S(1)}, f32[8,5,8,128]{3,2,1,0:T(8,128)S(1)}, u32[]{:S(2)}, u32[]{:S(2)}) collective-permute-start(f32[8,5,8,128]{3,2,1,0:T(8,128)S(1)} %collective-permute-done.3.refs_2_), channel_id=1, source_target_pairs={{8,16},{16,24},{9,17},{17,25},{10,18},{18,26},{11,19},{19,27},{12,... | collective-permute-start | bytes 491528 | tf_op jit(solution)/shard_map/ppermute | solution.py:319
  38.4 2.8 %collective-permute-start.2 = (f32[9,5,8,128]{3,2,1,0:T(8,128)S(1)}, f32[9,5,8,128]{3,2,1,0:T(8,128)S(1)}, u32[]{:S(2)}, u32[]{:S(2)}) collective-permute-start(f32[9,5,8,128]{3,2,1,0:T(8,128)S(1)} %collective-permute-done.1.refs_1_), channel_id=1, source_target_pairs={{16,24},{17,25},{18,26},{19,27},{20,28},{21,29},{22,30},{23,31}} | collective-permute-start | bytes 552968 | tf_op jit(solution)/shard_map/ppermute | solution.py:319
  39.1 2.2 %collective-permute-start.11 = (f32[8,5,8,128]{3,2,1,0:T(8,128)S(1)}, f32[8,5,8,128]{3,2,1,0:T(8,128)S(1)}, u32[]{:S(2)}, u32[]{:S(2)}) collective-permute-start(f32[8,5,8,128]{3,2,1,0:T(8,128)S(1)} %collective-permute-done.10.refs_1_), channel_id=1, source_target_pairs={{16,24},{17,25},{18,26},{19,27},{20,28},{21,29},{22,30},{23,31}} | collective-permute-start | bytes 491528 | tf_op jit(solution)/shard_map/ppermute | solution.py:319
  39.7 3.6 %collective-permute-start.8 = (f32[8,5,8,128]{3,2,1,0:T(8,128)S(1)}, f32[8,5,8,128]{3,2,1,0:T(8,128)S(1)}, u32[]{:S(2)}, u32[]{:S(2)}) collective-permute-start(f32[8,5,8,128]{3,2,1,0:T(8,128)S(1)} %collective-permute-done.7.refs_1_), channel_id=1, source_target_pairs={{16,24},{17,25},{18,26},{19,27},{20,28},{21,29},{22,30},{23,31}} | collective-permute-start | bytes 491528 | tf_op jit(solution)/shard_map/ppermute | solution.py:319
  40.4 5.0 %collective-permute-start.5 = (f32[8,5,8,128]{3,2,1,0:T(8,128)S(1)}, f32[8,5,8,128]{3,2,1,0:T(8,128)S(1)}, u32[]{:S(2)}, u32[]{:S(2)}) collective-permute-start(f32[8,5,8,128]{3,2,1,0:T(8,128)S(1)} %collective-permute-done.4.refs_1_), channel_id=1, source_target_pairs={{16,24},{17,25},{18,26},{19,27},{20,28},{21,29},{22,30},{23,31}} | collective-permute-start | bytes 491528 | tf_op jit(solution)/shard_map/ppermute | solution.py:319
  42.7 7.0 %collective-permute-start.21 = (f32[2,6,8,512]{3,2,1,0:T(8,128)S(1)}, f32[2,6,8,512]{3,2,1,0:T(8,128)S(1)}, u32[]{:S(2)}, u32[]{:S(2)}) collective-permute-start(f32[2,6,8,512]{3,2,1,0:T(8,128)S(1)} %get-tuple-element.58.b_ref), channel_id=1, source_target_pairs={{24,16},{25,17},{26,18},{27,19},{28,20},{29,21},{30,22},{31,23}} | collective-permute-start | bytes 589832 | tf_op jit(solution)/shard_map/ppermute | solution.py:322
  44.8 6.1 %collective-permute-start.18 = (f32[2,6,8,512]{3,2,1,0:T(8,128)S(1)}, f32[2,6,8,512]{3,2,1,0:T(8,128)S(1)}, u32[]{:S(2)}, u32[]{:S(2)}) collective-permute-start(f32[2,6,8,512]{3,2,1,0:T(8,128)S(1)} %get-tuple-element.54.b_ref), channel_id=1, source_target_pairs={{24,16},{25,17},{26,18},{27,19},{28,20},{29,21},{30,22},{31,23}} | collective-permute-start | bytes 589832 | tf_op jit(solution)/shard_map/ppermute | solution.py:322
  46.9 5.3 %collective-permute-start.15 = (f32[2,6,8,512]{3,2,1,0:T(8,128)S(1)}, f32[2,6,8,512]{3,2,1,0:T(8,128)S(1)}, u32[]{:S(2)}, u32[]{:S(2)}) collective-permute-start(f32[2,6,8,512]{3,2,1,0:T(8,128)S(1)} %get-tuple-element.50.b_ref), channel_id=1, source_target_pairs={{24,16},{25,17},{26,18},{27,19},{28,20},{29,21},{30,22},{31,23}} | collective-permute-start | bytes 589832 | tf_op jit(solution)/shard_map/ppermute | solution.py:322
  49.0 5.1 %copy-start.2 = (f32[2,25,8,512]{3,2,1,0:T(8,128)}, f32[2,25,8,512]{3,2,1,0:T(8,128)S(1)}, u32[]{:S(2)}) copy-start(f32[2,25,8,512]{3,2,1,0:T(8,128)S(1)} %get-tuple-element.34.refs_0_) | copy-start | bytes 2457604
  49.0 4.5 %collective-permute-start.12 = (f32[2,6,8,512]{3,2,1,0:T(8,128)S(1)}, f32[2,6,8,512]{3,2,1,0:T(8,128)S(1)}, u32[]{:S(2)}, u32[]{:S(2)}) collective-permute-start(f32[2,6,8,512]{3,2,1,0:T(8,128)S(1)} %get-tuple-element.46.b_ref), channel_id=1, source_target_pairs={{24,16},{25,17},{26,18},{27,19},{28,20},{29,21},{30,22},{31,23}} | collective-permute-start | bytes 589832 | tf_op jit(solution)/shard_map/ppermute | solution.py:322
  50.3 4.5 %collective-permute-start.22 = (f32[2,6,8,512]{3,2,1,0:T(8,128)S(1)}, f32[2,6,8,512]{3,2,1,0:T(8,128)S(1)}, u32[]{:S(2)}, u32[]{:S(2)}) collective-permute-start(f32[2,6,8,512]{3,2,1,0:T(8,128)S(1)} %carry.14), channel_id=1, source_target_pairs={{16,8},{17,9},{18,10},{19,11},{20,12},{21,13},{22,14},{23,15}} | collective-permute-start | bytes 589832 | tf_op jit(solution)/shard_map/ppermute | solution.py:322
  51.5 5.1 %collective-permute-start.19 = (f32[2,6,8,512]{3,2,1,0:T(8,128)S(1)}, f32[2,6,8,512]{3,2,1,0:T(8,128)S(1)}, u32[]{:S(2)}, u32[]{:S(2)}) collective-permute-start(f32[2,6,8,512]{3,2,1,0:T(8,128)S(1)} %carry.12), channel_id=1, source_target_pairs={{16,8},{17,9},{18,10},{19,11},{20,12},{21,13},{22,14},{23,15}} | collective-permute-start | bytes 589832 | tf_op jit(solution)/shard_map/ppermute | solution.py:322
  52.8 5.7 %collective-permute-start.16 = (f32[2,6,8,512]{3,2,1,0:T(8,128)S(1)}, f32[2,6,8,512]{3,2,1,0:T(8,128)S(1)}, u32[]{:S(2)}, u32[]{:S(2)}) collective-permute-start(f32[2,6,8,512]{3,2,1,0:T(8,128)S(1)} %carry.10), channel_id=1, source_target_pairs={{16,8},{17,9},{18,10},{19,11},{20,12},{21,13},{22,14},{23,15}} | collective-permute-start | bytes 589832 | tf_op jit(solution)/shard_map/ppermute | solution.py:322
  54.1 6.3 %collective-permute-start.13 = (f32[2,6,8,512]{3,2,1,0:T(8,128)S(1)}, f32[2,6,8,512]{3,2,1,0:T(8,128)S(1)}, u32[]{:S(2)}, u32[]{:S(2)}) collective-permute-start(f32[2,6,8,512]{3,2,1,0:T(8,128)S(1)} %carry.8), channel_id=1, source_target_pairs={{16,8},{17,9},{18,10},{19,11},{20,12},{21,13},{22,14},{23,15}} | collective-permute-start | bytes 589832 | tf_op jit(solution)/shard_map/ppermute | solution.py:322
  55.3 34.5 %collective-permute-start.23 = (f32[2,6,8,512]{3,2,1,0:T(8,128)S(1)}, f32[2,6,8,512]{3,2,1,0:T(8,128)S(1)}, u32[]{:S(2)}, u32[]{:S(2)}) collective-permute-start(f32[2,6,8,512]{3,2,1,0:T(8,128)S(1)} %carry.15), channel_id=1, source_target_pairs={{8,0},{9,1},{10,2},{11,3},{12,4},{13,5},{14,6},{15,7}} | collective-permute-start | bytes 589832 | tf_op jit(solution)/shard_map/ppermute | solution.py:322
  57.2 36.9 %collective-permute-start.20 = (f32[2,6,8,512]{3,2,1,0:T(8,128)S(1)}, f32[2,6,8,512]{3,2,1,0:T(8,128)S(1)}, u32[]{:S(2)}, u32[]{:S(2)}) collective-permute-start(f32[2,6,8,512]{3,2,1,0:T(8,128)S(1)} %carry.13), channel_id=1, source_target_pairs={{8,0},{9,1},{10,2},{11,3},{12,4},{13,5},{14,6},{15,7}} | collective-permute-start | bytes 589832 | tf_op jit(solution)/shard_map/ppermute | solution.py:322
  59.1 39.2 %collective-permute-start.17 = (f32[2,6,8,512]{3,2,1,0:T(8,128)S(1)}, f32[2,6,8,512]{3,2,1,0:T(8,128)S(1)}, u32[]{:S(2)}, u32[]{:S(2)}) collective-permute-start(f32[2,6,8,512]{3,2,1,0:T(8,128)S(1)} %carry.11), channel_id=1, source_target_pairs={{8,0},{9,1},{10,2},{11,3},{12,4},{13,5},{14,6},{15,7}} | collective-permute-start | bytes 589832 | tf_op jit(solution)/shard_map/ppermute | solution.py:322
  61.0 39.4 %collective-permute-start.14 = (f32[2,6,8,512]{3,2,1,0:T(8,128)S(1)}, f32[2,6,8,512]{3,2,1,0:T(8,128)S(1)}, u32[]{:S(2)}, u32[]{:S(2)}) collective-permute-start(f32[2,6,8,512]{3,2,1,0:T(8,128)S(1)} %carry.9), channel_id=1, source_target_pairs={{8,0},{9,1},{10,2},{11,3},{12,4},{13,5},{14,6},{15,7}} | collective-permute-start | bytes 589832 | tf_op jit(solution)/shard_map/ppermute | solution.py:322
  103.0 14.6 %all-to-all-start.1 = ((f32[8,5,8,512]{3,2,1,0:T(8,128)}), f32[8,5,8,512]{3,2,1,0:T(8,128)S(1)}, u32[]{:S(2)}, u32[]{:S(2)}) async-start(f32[8,5,8,512]{3,2,1,0:T(8,128)} %stencil.1), calls=%async_computation.1 | async-start | bytes 1310720 | tf_op jit(solution)/shard_map/all_to_all | solution.py:415
  106.5 1.1 copy-start.3

commit v7 on v6

--- a/solution.py
+++ b/solution.py
@@ -13,14 +13,16 @@
 F32 = jnp.float32
 VMEM_LIMIT = 16 * 1024 * 1024
 CHUNKS = 4
+WAVE = 2
 SPAN = 4
 MIX_LANE = 64
 
 
-def pack_kernel(coef_ref, p_ref, out_ref):
+def pack_kernel(coef_ref, p_ref, out_ref, weight_ref):
     planes, rows, width = p_ref.shape
     for k in range(planes):
         w = coef_ref[0, k]
+        weight_ref[k] = jnp.full((SUB, EDGE), w, F32)
         for s in range(out_ref.shape[0]):
             before = (R * s - 1) % rows
             after = (R * (s + 1)) % rows
@@ -207,7 +209,12 @@
                     shear_ref[k, j, :, start : start + width] = map_ref[i, 5 * k + 2 + j, 0:R]
 
 
-def carry_kernel(planes, sender, coef_ref, in_ref, b_ref, m_ref, out_ref):
+def own_tile(ref, k, planes, like):
+    tile = ref[ref.shape[0] - planes + k, 0:R]
+    return jnp.concatenate([tile] * (like.shape[1] // EDGE), axis=1)
+
+
+def carry_kernel(planes, sender, in_ref, excess_ref, b_ref, m_ref, out_ref):
     @pl.when(lax.axis_index("plane") == sender)
     def _():
         for step in range(out_ref.shape[0]):
@@ -215,11 +222,11 @@
             p, q = (fields[0:4], fields[4:8])
             for k in reversed(range(planes)):
                 m0, m1, off = (m_ref[step, 3 * k + j, 0:R] for j in range(3))
-                p, q = transposed_step(m0, m1, off, p, q, 1.0 - coef_ref[1, k])
+                p, q = transposed_step(m0, m1, off, p, q, -own_tile(excess_ref, k, planes, m0))
             pack_state(out_ref, step, p + q, b_ref)
 
 
-def cotangent_kernel(planes, coef_ref, src_ref, m_ref, a_ref, *refs):
+def cotangent_kernel(planes, excess_ref, weight_ref, src_ref, m_ref, a_ref, *refs):
     arrived, cot_ref = (refs[:-1], refs[-1])
     blank = jnp.zeros((SUB - R, cot_ref.shape[-1]), F32)
     for step in range(cot_ref.shape[0]):
@@ -229,7 +236,7 @@
             s0, s1, s3 = (src_ref[step, 3 * k + j, 0:R] for j in range(3))
             p = [p[0] + s0, p[1] + s1, p[2] + s1, p[3] + s3]
             a = [a_ref[step, 4 * k + j, 0:R] for j in range(4)]
-            w = -coef_ref[0, k]
+            w = -own_tile(weight_ref, k, planes, s0)
             cots = [
                 w * (p[0] * a[0] + p[1] * a[1]),
                 w * (p[2] * a[2] + p[3] * a[3]),
@@ -238,7 +245,7 @@
             for j in range(3):
                 cot_ref[step, 3 * k + j] = jnp.concatenate([cots[j], blank], axis=0)
             m0, m1, off = (m_ref[step, 3 * k + j, 0:R] for j in range(3))
-            p, q = transposed_step(m0, m1, off, p, q, 1.0 - coef_ref[1, k])
+            p, q = transposed_step(m0, m1, off, p, q, -own_tile(excess_ref, k, planes, m0))
 
 
 def stencil_kernel(planes, *refs):
@@ -322,11 +329,11 @@
         return lax.ppermute(x, "plane", [(groups - 1 - hop, groups - 2 - hop)])
 
     coef = jnp.stack([lens_weight, mixing])
-    packed = pl.pallas_call(
+    packed, weights = pl.pallas_call(
         pack_kernel,
-        out_shape=shape(slabs, tiles, planes, SUB, EDGE),
+        out_shape=(shape(slabs, tiles, planes, SUB, EDGE), shape(planes, SUB, EDGE)),
         in_specs=[SCALARS, WHOLE],
-        out_specs=WHOLE,
+        out_specs=(WHOLE, WHOLE),
         compiler_params=params(),
         name="pack",
     )(coef, potential)
@@ -342,28 +349,38 @@
         compiler_params=params(),
         name="split",
     )(coef, own)
-    strips = [[piece] for piece in pieces]
-    for turn in range(CHUNKS + groups - 2):
-        for c in range(CHUNKS):
-            if 0 <= turn - c < groups - 1:
-                strips[c].insert(0, climb(strips[c][0], turn - c))
-
-    beside, excess = pl.pallas_call(
-        edges_kernel,
-        out_shape=(
-            shape(CHUNKS, groups * planes, SUB, EDGE),
-            shape(groups * planes, SUB, EDGE),
-        ),
-        in_specs=[WHOLE] * groups,
-        out_specs=(WHOLE, WHOLE),
-        compiler_params=params(),
-        name="edges",
-    )(*strips[0])
-
+    events = [[] for c in range(CHUNKS)]
+
+    def ordered(c, x):
+        place = len(events[c]) + 1
+        if c < WAVE or place >= len(events[c - WAVE]):
+            return x
+        return lax.optimization_barrier((x, events[c - WAVE][place]))[0]
+
+    strips = []
     maps = []
-    work = []
+    cots = []
+    beside, excess = (None, None)
     for c in range(CHUNKS):
-        map_piece, *held = pl.pallas_call(
+        line = [pieces[c]]
+        for hop in range(groups - 1):
+            line.insert(0, climb(ordered(c, line[0]), hop))
+            events[c].append(line[0])
+        strips.append(line)
+        if c == 0:
+            beside, excess = pl.pallas_call(
+                edges_kernel,
+                out_shape=(
+                    shape(CHUNKS, groups * planes, SUB, EDGE),
+                    shape(groups * planes, SUB, EDGE),
+                ),
+                in_specs=[WHOLE] * groups,
+                out_specs=(WHOLE, WHOLE),
+                compiler_params=params(),
+                name="edges",
+            )(*line)
+        line = [ordered(c, line[0])] + line[1:]
+        map_piece, matrices, states, sources, b = pl.pallas_call(
             functools.partial(forward_kernel, groups, planes, c, length),
             out_shape=(
                 shape(steps, 5 * planes, SUB, span),
@@ -376,33 +393,32 @@
             out_specs=(WHOLE,) * 5,
             compiler_params=params(),
             name="forward",
-        )(*strips[c], beside, excess, observed, noise_weight)
+        )(*line, beside, excess, observed, noise_weight)
         maps.append(map_piece)
-        work.append(held)
-
-    cots = []
-    for matrices, states, sources, b in work:
+        events[c].append(b)
         arrived = [descend(b, 0)]
         for hop in range(1, groups - 1):
             outgoing = pl.pallas_call(
                 functools.partial(carry_kernel, planes, groups - 1 - hop),
                 out_shape=shape(steps, R, SUB, span),
-                in_specs=[SCALARS] + [WHOLE] * 3,
+                in_specs=[WHOLE] * 4,
                 out_specs=WHOLE,
                 compiler_params=params(),
                 name="carry",
-            )(coef, arrived[-1], b, matrices)
+            )(ordered(c, arrived[-1]), excess, b, matrices)
+            events[c].append(outgoing)
             arrived.append(descend(outgoing, hop))
         cots.append(
             pl.pallas_call(
                 functools.partial(cotangent_kernel, planes),
                 out_shape=shape(steps, 3 * planes, SUB, span),
-                in_specs=[SCALARS] + [WHOLE] * (groups + 2),
+                in_specs=[WHOLE] * (groups + 4),
                 out_specs=WHOLE,
                 compiler_params=params(),
                 name="cotangent",
-            )(coef, sources, matrices, states, *arrived)
+            )(excess, weights, sources, matrices, states, *arrived)
         )
+        events[c].append(cots[-1])
 
     partial = pl.pallas_call(
         functools.partial(stencil_kernel, planes),

time: 119 us -> 119 us (level)
  starting transfers between devices: 31.8 us -> 46.4 us
  waiting for transfers between devices: 45.7 us -> 37.4 us
  Pallas kernels: 19 us -> 12.5 us
    ppermute x12, starting transfers between devices: 17.7 us -> 32.3 us  [climb(): lax.ppermute(x, 'plane', [(i, i + 1) for i in range(hop, groups - 1)])]
    ppermute x12, waiting for transfers between devices: 35.7 us -> 25.6 us  [descend(): return lax.ppermute(x, 'plane', [(groups - 1 - hop, groups - 2 - hop)])]
    pallas_call x8, Pallas kernels: 4.52 us -> 0.13 us  [on_device(): pl.pallas_call(functools.partial(carry_kernel, planes, groups - 1 - hop),...]
    pallas_call x4, Pallas kernels: 3.21 us -> 1.03 us  [on_device(): pl.pallas_call(functools.partial(cotangent_kernel, planes), out_shape=sha...]
    ppermute x12, waiting for transfers between devices: 3.27 us -> 5.16 us  [climb(): lax.ppermute(x, 'plane', [(i, i + 1) for i in range(hop, groups - 1)])]
  transfers between devices with their start and end apart: 25 -> 25, of which waited for: 7 -> 8; matrix products, arithmetic and copies ran while one was open for 1% -> 1% of each run, Pallas kernels for 12% -> 7%
where the time goes in v7:
time: 119 us; the launch traced here: 118 us
  starting transfers between devices  46.4 us (39%)
  waiting for transfers between devices  37.4 us (31%)
  blocking collectives  16.1 us (14%)
  Pallas kernels  12.5 us (11%)
  local copies, waits for them, and re-layouts  3.89 us (3%)
    ppermute x12, starting transfers between devices, climb(): lax.ppermute(x, 'plane', [(i, i + 1) for i in range(hop, groups - 1)])  32.3 us
    ppermute x12, waiting for transfers between devices, descend(): return lax.ppermute(x, 'plane', [(groups - 1 - hop, groups - 2 - hop)])  25.6 us
    all_to_all x1, blocking collectives, on_device(): lax.all_to_all(packed, 'slab', split_axis=0, concat_axis=0, tiled=True)  16.1 us
    ppermute x12, starting transfers between devices, descend(): return lax.ppermute(x, 'plane', [(groups - 1 - hop, groups - 2 - hop)])  10.6 us
    all_to_all x1, waiting for transfers between devices, on_device(): lax.all_to_all(partial, 'slab', split_axis=0, concat_axis=0, tiled=True)  6.68 us
    pallas_call x4, Pallas kernels, on_device(): pl.pallas_call(functools.partial(forward_kernel, groups, planes, c, lengt...  5.62 us
    ppermute x12, waiting for transfers between devices, climb(): lax.ppermute(x, 'plane', [(i, i + 1) for i in range(hop, groups - 1)])  5.16 us
    unnamed x11, local copies, waits for them, and re-layouts  3.89 us
  transfers between devices with their start and end apart: 25, of which 8 were waited for; matrix products, arithmetic and copies ran while one was open for 1% of the time, Pallas kernels for 7%

profile of v7, /device:TPU:0, one launch (start us, length us, event | category | flops | bytes accessed | tf_op | source)
XLA Modules:
  0.0 118.4 jit_solution(8036690899683700271)
XLA Ops:
  0.7 0.8 pad_maximum_fusion.coef_ref
  1.5 1.0 copy-done.4
  2.5 0.7 pack.1
  3.2 16.1 %all_to_all.10 = f32[8,4,5,8,128]{4,3,2,1,0:T(8,128)S(1)} all-to-all(f32[8,4,5,8,128]{4,3,2,1,0:T(8,128)S(1)} %get-tuple-element.45), channel_id=1, replica_groups=mesh['plane'=4,'slab'=8] {'slab'}, dimensions={0} | all-to-all | bytes 1310720 | tf_op jit(solution)/shard_map/all_to_all | solution.py:340
  19.3 0.7 split.1
  20.0 3.5 %collective-permute-start = (f32[9,5,8,128]{3,2,1,0:T(8,128)S(1)}, f32[9,5,8,128]{3,2,1,0:T(8,128)S(1)}, u32[]{:S(2)}, u32[]{:S(2)}) collective-permute-start(f32[9,5,8,128]{3,2,1,0:T(8,128)S(1)} %get-tuple-element.46.refs_3_), channel_id=1, source_target_pairs={{0,8},{8,16},{16,24},{1,9},{9,17},{17,25},{2,10},{10,18},{18,26},{... | collective-permute-start | bytes 552968 | tf_op jit(solution)/shard_map/ppermute | solution.py:326
  23.5 3.5 %collective-permute-start.3 = (f32[8,5,8,128]{3,2,1,0:T(8,128)S(1)}, f32[8,5,8,128]{3,2,1,0:T(8,128)S(1)}, u32[]{:S(2)}, u32[]{:S(2)}) collective-permute-start(f32[8,5,8,128]{3,2,1,0:T(8,128)S(1)} %get-tuple-element.50.refs_3_), channel_id=1, source_target_pairs={{0,8},{8,16},{16,24},{1,9},{9,17},{17,25},{2,10},{10,18},{18,26},{... | collective-permute-start | bytes 491528 | tf_op jit(solution)/shard_map/ppermute | solution.py:326
  27.0 0.8 collective-permute-done.refs_2_
  27.8 0.7 collective-permute-start.1
  28.5 2.2 %collective-permute-done.3.refs_2_ = f32[8,5,8,128]{3,2,1,0:T(8,128)S(1)} collective-permute-done((f32[8,5,8,128]{3,2,1,0:T(8,128)S(1)}, f32[8,5,8,128]{3,2,1,0:T(8,128)S(1)}, u32[]{:S(2)}, u32[]{:S(2)}) %collective-permute-start.3) | collective-permute-done | bytes 163872 | tf_op jit(solution)/shard_map/ppermute | solution.py:326
  30.7 0.7 collective-permute-start.4
  31.3 0.7 collective-permute-start.2
  32.0 0.7 collective-permute-start.5
  32.7 10.7 %collective-permute-start.10 = (f32[8,5,8,128]{3,2,1,0:T(8,128)S(1)}, f32[8,5,8,128]{3,2,1,0:T(8,128)S(1)}, u32[]{:S(2)}, u32[]{:S(2)}) collective-permute-start(f32[8,5,8,128]{3,2,1,0:T(8,128)S(1)} %get-tuple-element.61.refs_3_), channel_id=1, source_target_pairs={{0,8},{8,16},{16,24},{1,9},{9,17},{17,25},{2,10},{10,18},{18,26},{... | collective-permute-start | bytes 491528 | tf_op jit(solution)/shard_map/ppermute | solution.py:326
  43.4 9.3 %collective-permute-start.6 = (f32[8,5,8,128]{3,2,1,0:T(8,128)S(1)}, f32[8,5,8,128]{3,2,1,0:T(8,128)S(1)}, u32[]{:S(2)}, u32[]{:S(2)}) collective-permute-start(f32[8,5,8,128]{3,2,1,0:T(8,128)S(1)} %get-tuple-element.53.refs_3_), channel_id=1, source_target_pairs={{0,8},{8,16},{16,24},{1,9},{9,17},{17,25},{2,10},{10,18},{18,26},{... | collective-permute-start | bytes 491528 | tf_op jit(solution)/shard_map/ppermute | solution.py:326
  52.7 0.7 collective-permute-start.11
  53.4 2.1 %collective-permute-done.6.refs_2_ = f32[8,5,8,128]{3,2,1,0:T(8,128)S(1)} collective-permute-done((f32[8,5,8,128]{3,2,1,0:T(8,128)S(1)}, f32[8,5,8,128]{3,2,1,0:T(8,128)S(1)}, u32[]{:S(2)}, u32[]{:S(2)}) %collective-permute-start.6) | collective-permute-done | bytes 163872 | tf_op jit(solution)/shard_map/ppermute | solution.py:326
  55.5 0.7 collective-permute-start.7
  56.4 1.4 %forward.5 = (f32[2,25,8,512]{3,2,1,0:T(8,128)S(1)}, f32[2,15,8,512]{3,2,1,0:T(8,128)S(1)}, f32[2,20,8,512]{3,2,1,0:T(8,128)S(1)}, f32[2,15,8,512]{3,2,1,0:T(8,128)S(1)}, f32[2,6,8,512]{3,2,1,0:T(8,128)S(1)}) custom-call(f32[8,5,8,128]{3,2,1,0:T(8,128)S(1)} %collective-permute-done.5.refs_0_, f32[8,5,8,128]{3,2,1,0:T(8,128)S(1)} %collective-permute-done.4.refs_1_, ...), custom_call_target="tpu_custom_call" | custom-call | tf_op jit(solution)/shard_map/forward/pallas_call | solution.py:383
  57.8 0.7 collective-permute-start.13
  58.5 1.4 %forward.4 = (f32[2,25,8,512]{3,2,1,0:T(8,128)S(1)}, f32[2,15,8,512]{3,2,1,0:T(8,128)S(1)}, f32[2,20,8,512]{3,2,1,0:T(8,128)S(1)}, f32[2,15,8,512]{3,2,1,0:T(8,128)S(1)}, f32[2,6,8,512]{3,2,1,0:T(8,128)S(1)}) custom-call(f32[9,5,8,128]{3,2,1,0:T(8,128)S(1)} %collective-permute-done.2.refs_0_, f32[9,5,8,128]{3,2,1,0:T(8,128)S(1)} %collective-permute-done.1.refs_1_, ...), custom_call_target="tpu_custom_call" | custom-call | tf_op jit(solution)/shard_map/forward/pallas_call | solution.py:383
  59.9 0.7 collective-permute-start.9
  60.6 0.7 collective-permute-start.12
  61.2 0.7 collective-permute-start.8
  62.0 0.7 collective-permute-start.16
  62.7 0.7 collective-permute-start.14
  63.4 1.4 %forward.7 = (f32[2,25,8,512]{3,2,1,0:T(8,128)S(1)}, f32[2,15,8,512]{3,2,1,0:T(8,128)S(1)}, f32[2,20,8,512]{3,2,1,0:T(8,128)S(1)}, f32[2,15,8,512]{3,2,1,0:T(8,128)S(1)}, f32[2,6,8,512]{3,2,1,0:T(8,128)S(1)}) custom-call(f32[8,5,8,128]{3,2,1,0:T(8,128)S(1)} %collective-permute-done.12.refs_0_, f32[8,5,8,128]{3,2,1,0:T(8,128)S(1)} %collective-permute-done.11.refs_1_, ...), custom_call_target="tpu_custom_call" | custom-call | tf_op jit(solution)/shard_map/forward/pallas_call | solution.py:383
  64.8 0.7 collective-permute-start.21
  65.5 1.4 %forward.6 = (f32[2,25,8,512]{3,2,1,0:T(8,128)S(1)}, f32[2,15,8,512]{3,2,1,0:T(8,128)S(1)}, f32[2,20,8,512]{3,2,1,0:T(8,128)S(1)}, f32[2,15,8,512]{3,2,1,0:T(8,128)S(1)}, f32[2,6,8,512]{3,2,1,0:T(8,128)S(1)}) custom-call(f32[8,5,8,128]{3,2,1,0:T(8,128)S(1)} %collective-permute-done.8.refs_0_, f32[8,5,8,128]{3,2,1,0:T(8,128)S(1)} %collective-permute-done.7.refs_1_, ...), custom_call_target="tpu_custom_call" | custom-call | tf_op jit(solution)/shard_map/forward/pallas_call | solution.py:383
  66.9 0.7 collective-permute-start.18
  67.6 1.3 %collective-permute-start.17 = (f32[2,6,8,512]{3,2,1,0:T(8,128)S(1)}, f32[2,6,8,512]{3,2,1,0:T(8,128)S(1)}, u32[]{:S(2)}, u32[]{:S(2)}) collective-permute-start(f32[2,6,8,512]{3,2,1,0:T(8,128)S(1)} %carry.11), channel_id=1, source_target_pairs={{8,0},{9,1},{10,2},{11,3},{12,4},{13,5},{14,6},{15,7}} | collective-permute-start | bytes 589832 | tf_op jit(solution)/shard_map/ppermute | solution.py:329
  69.0 1.3 %collective-permute-start.15 = (f32[2,6,8,512]{3,2,1,0:T(8,128)S(1)}, f32[2,6,8,512]{3,2,1,0:T(8,128)S(1)}, u32[]{:S(2)}, u32[]{:S(2)}) collective-permute-start(f32[2,6,8,512]{3,2,1,0:T(8,128)S(1)} %carry.10), channel_id=1, source_target_pairs={{8,0},{9,1},{10,2},{11,3},{12,4},{13,5},{14,6},{15,7}} | collective-permute-start | bytes 589832 | tf_op jit(solution)/shard_map/ppermute | solution.py:329
  70.3 0.7 collective-permute-start.22
  71.0 0.7 collective-permute-start.19
  71.7 14.3 %collective-permute-done.17.refs_2_ = f32[2,6,8,512]{3,2,1,0:T(8,128)S(1)} collective-permute-done((f32[2,6,8,512]{3,2,1,0:T(8,128)S(1)}, f32[2,6,8,512]{3,2,1,0:T(8,128)S(1)}, u32[]{:S(2)}, u32[]{:S(2)}) %collective-permute-start.17) | collective-permute-done | bytes 196640 | tf_op jit(solution)/shard_map/ppermute | solution.py:329
  86.3 4.0 %collective-permute-done.15.refs_2_ = f32[2,6,8,512]{3,2,1,0:T(8,128)S(1)} collective-permute-done((f32[2,6,8,512]{3,2,1,0:T(8,128)S(1)}, f32[2,6,8,512]{3,2,1,0:T(8,128)S(1)}, u32[]{:S(2)}, u32[]{:S(2)}) %collective-permute-start.15) | collective-permute-done | bytes 196640 | tf_op jit(solution)/shard_map/ppermute | solution.py:329
  90.6 1.3 %collective-permute-start.23 = (f32[2,6,8,512]{3,2,1,0:T(8,128)S(1)}, f32[2,6,8,512]{3,2,1,0:T(8,128)S(1)}, u32[]{:S(2)}, u32[]{:S(2)}) collective-permute-start(f32[2,6,8,512]{3,2,1,0:T(8,128)S(1)} %carry.15), channel_id=1, source_target_pairs={{8,0},{9,1},{10,2},{11,3},{12,4},{13,5},{14,6},{15,7}} | collective-permute-start | bytes 589832 | tf_op jit(solution)/shard_map/ppermute | solution.py:329
  91.9 1.3 %collective-permute-start.20 = (f32[2,6,8,512]{3,2,1,0:T(8,128)S(1)}, f32[2,6,8,512]{3,2,1,0:T(8,128)S(1)}, u32[]{:S(2)}, u32[]{:S(2)}) collective-permute-start(f32[2,6,8,512]{3,2,1,0:T(8,128)S(1)} %carry.13), channel_id=1, source_target_pairs={{8,0},{9,1},{10,2},{11,3},{12,4},{13,5},{14,6},{15,7}} | collective-permute-start | bytes 589832 | tf_op jit(solution)/shard_map/ppermute | solution.py:329
  93.2 4.9 %collective-permute-done.23.refs_2_ = f32[2,6,8,512]{3,2,1,0:T(8,128)S(1)} collective-permute-done((f32[2,6,8,512]{3,2,1,0:T(8,128)S(1)}, f32[2,6,8,512]{3,2,1,0:T(8,128)S(1)}, u32[]{:S(2)}, u32[]{:S(2)}) %collective-permute-start.23) | collective-permute-done | bytes 196640 | tf_op jit(solution)/shard_map/ppermute | solution.py:329
  98.1 0.3 cotangent.7.refs_3_
  98.4 2.4 %collective-permute-done.20.refs_2_ = f32[2,6,8,512]{3,2,1,0:T(8,128)S(1)} collective-permute-done((f32[2,6,8,512]{3,2,1,0:T(8,128)S(1)}, f32[2,6,8,512]{3,2,1,0:T(8,128)S(1)}, u32[]{:S(2)}, u32[]{:S(2)}) %collective-permute-start.20) | collective-permute-done | bytes 196640 | tf_op jit(solution)/shard_map/ppermute | solution.py:329
  101.0 1.8 %stencil.1 = f32[8,5,8,512]{3,2,1,0:T(8,128)} custom-call(f32[2,15,8,512]{3,2,1,0:T(8,128)S(1)} %cotangent.4.refs_0_, f32[2,15,8,512]{3,2,1,0:T(8,128)S(1)} %cotangent.5.refs_1_, f32[2,15,8,512]{3,2,1,0:T(8,128)S(1)} %cotangent.6.refs_2_, f32[2,15,8,512]{3,2,1,0:T(8,128)S(1)} %cotangent.7.refs_3_), custom_call_target="tpu_custom_call" | custom-call | tf_op jit(solution)/shard_map/stencil/pallas_call | solution.py:423
  102.8 3.5 %all-to-all-start.1 = ((f32[8,5,8,512]{3,2,1,0:T(8,128)}), f32[8,5,8,512]{3,2,1,0:T(8,128)S(1)}, u32[]{:S(2)}, u32[]{:S(2)}) async-start(f32[8,5,8,512]{3,2,1,0:T(8,128)} %stencil.1), calls=%async_computation.1 | async-start | bytes 1310720 | tf_op jit(solution)/shard_map/all_to_all | solution.py:431
  106.4 1.1 copy-done.3
  107.5 1.6 %assemble.1 = (f32[5,2,6,4096]{3,2,1,0:T(8,128)S(1)}, f32[5,3,6,4096]{3,2,1,0:T(8,128)}) custom-call(f32[2,25,8,512]{3,2,1,0:T(8,128)S(1)} %get-tuple-element.49.refs_0_, f32[2,25,8,512]{3,2,1,0:T(8,128)S(1)} %get-tuple-element.51.refs_1_, f32[2,25,8,512]{3,2,1,0:T(8,128)S(1)} %copy-done.3, f32[2,25,8,512]{3,2,1,0:T(8,128)S(1)} %get-tuple-element.67.refs_3_), custom_call_target="tpu_custom_call" | custom-call | tf_op jit(solution)/shard_map/assemble/pallas_call | solution.py:432
  109.0 1.7 %copy.8 = f32[5,2,6,4096]{3,1,2,0:T(2,128)} copy(f32[5,2,6,4096]{3,2,1,0:T(8,128)S(1)} %get-tuple-element.87) | data formatting | bytes 1966080
  110.7 6.7 %all-to-all-done.1.in_ref = f32[8,5,8,512]{3,2,1,0:T(8,128)S(1)} async-done(((f32[8,5,8,512]{3,2,1,0:T(8,128)}), f32[8,5,8,512]{3,2,1,0:T(8,128)S(1)}, u32[]{:S(2)}, u32[]{:S(2)}) %all-to-all-start.1) | async-done | bytes 655392 | tf_op jit(solution)/shard_map/all_to_all | solution.py:431
  117.4 0.9 combine.1
  (37 shorter events, 1.1 us)
Async XLA Ops:
  0.6 55.7 %copy-start = (f32[5,3,6,4096]{3,2,1,0:T(8,128)S(1)}, f32[5,3,6,4096]{3,2,1,0:T(8,128)}, u32[]{:S(2)}) copy-start(f32[5,3,6,4096]{3,2,1,0:T(8,128)} %refs_6_.7) | copy-start | bytes 4423684
  0.6 55.7 %copy-start.1 = (f32[5,6,4096]{2,1,0:T(8,128)S(1)}, f32[5,6,4096]{2,1,0:T(8,128)}, u32[]{:S(2)}) copy-start(f32[5,6,4096]{2,1,0:T(8,128)} %refs_7_.7) | copy-start | bytes 1474564
  1.5 1.0 copy-start.4
  20.0 7.8 %collective-permute-start = (f32[9,5,8,128]{3,2,1,0:T(8,128)S(1)}, f32[9,5,8,128]{3,2,1,0:T(8,128)S(1)}, u32[]{:S(2)}, u32[]{:S(2)}) collective-permute-start(f32[9,5,8,128]{3,2,1,0:T(8,128)S(1)} %get-tuple-element.46.refs_3_), channel_id=1, source_target_pairs={{0,8},{8,16},{16,24},{1,9},{9,17},{17,25},{2,10},{10,18},{18,26},{... | collective-permute-start | bytes 552968 | tf_op jit(solution)/shard_map/ppermute | solution.py:326
  23.5 7.2 %collective-permute-start.3 = (f32[8,5,8,128]{3,2,1,0:T(8,128)S(1)}, f32[8,5,8,128]{3,2,1,0:T(8,128)S(1)}, u32[]{:S(2)}, u32[]{:S(2)}) collective-permute-start(f32[8,5,8,128]{3,2,1,0:T(8,128)S(1)} %get-tuple-element.50.refs_3_), channel_id=1, source_target_pairs={{0,8},{8,16},{16,24},{1,9},{9,17},{17,25},{2,10},{10,18},{18,26},{... | collective-permute-start | bytes 491528 | tf_op jit(solution)/shard_map/ppermute | solution.py:326
  27.8 3.5 %collective-permute-start.1 = (f32[9,5,8,128]{3,2,1,0:T(8,128)S(1)}, f32[9,5,8,128]{3,2,1,0:T(8,128)S(1)}, u32[]{:S(2)}, u32[]{:S(2)}) collective-permute-start(f32[9,5,8,128]{3,2,1,0:T(8,128)S(1)} %collective-permute-done.refs_2_), channel_id=1, source_target_pairs={{8,16},{16,24},{9,17},{17,25},{10,18},{18,26},{11,19},{19,27},{12,... | collective-permute-start | bytes 552968 | tf_op jit(solution)/shard_map/ppermute | solution.py:326
  30.7 1.4 %collective-permute-start.4 = (f32[8,5,8,128]{3,2,1,0:T(8,128)S(1)}, f32[8,5,8,128]{3,2,1,0:T(8,128)S(1)}, u32[]{:S(2)}, u32[]{:S(2)}) collective-permute-start(f32[8,5,8,128]{3,2,1,0:T(8,128)S(1)} %collective-permute-done.3.refs_2_), channel_id=1, source_target_pairs={{8,16},{16,24},{9,17},{17,25},{10,18},{18,26},{11,19},{19,27},{12,... | collective-permute-start | bytes 491528 | tf_op jit(solution)/shard_map/ppermute | solution.py:326
  31.3 24.2 %collective-permute-start.2 = (f32[9,5,8,128]{3,2,1,0:T(8,128)S(1)}, f32[9,5,8,128]{3,2,1,0:T(8,128)S(1)}, u32[]{:S(2)}, u32[]{:S(2)}) collective-permute-start(f32[9,5,8,128]{3,2,1,0:T(8,128)S(1)} %collective-permute-done.1.refs_1_), channel_id=1, source_target_pairs={{16,24},{17,25},{18,26},{19,27},{20,28},{21,29},{22,30},{23,31}} | collective-permute-start | bytes 552968 | tf_op jit(solution)/shard_map/ppermute | solution.py:326
  32.0 20.7 %collective-permute-start.5 = (f32[8,5,8,128]{3,2,1,0:T(8,128)S(1)}, f32[8,5,8,128]{3,2,1,0:T(8,128)S(1)}, u32[]{:S(2)}, u32[]{:S(2)}) collective-permute-start(f32[8,5,8,128]{3,2,1,0:T(8,128)S(1)} %collective-permute-done.4.refs_1_), channel_id=1, source_target_pairs={{16,24},{17,25},{18,26},{19,27},{20,28},{21,29},{22,30},{23,31}} | collective-permute-start | bytes 491528 | tf_op jit(solution)/shard_map/ppermute | solution.py:326
  32.7 20.0 %collective-permute-start.10 = (f32[8,5,8,128]{3,2,1,0:T(8,128)S(1)}, f32[8,5,8,128]{3,2,1,0:T(8,128)S(1)}, u32[]{:S(2)}, u32[]{:S(2)}) collective-permute-start(f32[8,5,8,128]{3,2,1,0:T(8,128)S(1)} %get-tuple-element.61.refs_3_), channel_id=1, source_target_pairs={{0,8},{8,16},{16,24},{1,9},{9,17},{17,25},{2,10},{10,18},{18,26},{... | collective-permute-start | bytes 491528 | tf_op jit(solution)/shard_map/ppermute | solution.py:326
  43.4 12.1 %collective-permute-start.6 = (f32[8,5,8,128]{3,2,1,0:T(8,128)S(1)}, f32[8,5,8,128]{3,2,1,0:T(8,128)S(1)}, u32[]{:S(2)}, u32[]{:S(2)}) collective-permute-start(f32[8,5,8,128]{3,2,1,0:T(8,128)S(1)} %get-tuple-element.53.refs_3_), channel_id=1, source_target_pairs={{0,8},{8,16},{16,24},{1,9},{9,17},{17,25},{2,10},{10,18},{18,26},{... | collective-permute-start | bytes 491528 | tf_op jit(solution)/shard_map/ppermute | solution.py:326
  52.7 7.8 %collective-permute-start.11 = (f32[8,5,8,128]{3,2,1,0:T(8,128)S(1)}, f32[8,5,8,128]{3,2,1,0:T(8,128)S(1)}, u32[]{:S(2)}, u32[]{:S(2)}) collective-permute-start(f32[8,5,8,128]{3,2,1,0:T(8,128)S(1)} %collective-permute-done.10.refs_2_), channel_id=1, source_target_pairs={{8,16},{16,24},{9,17},{17,25},{10,18},{18,26},{11,19},{19,27},{12,... | collective-permute-start | bytes 491528 | tf_op jit(solution)/shard_map/ppermute | solution.py:326
  55.5 5.7 %collective-permute-start.7 = (f32[8,5,8,128]{3,2,1,0:T(8,128)S(1)}, f32[8,5,8,128]{3,2,1,0:T(8,128)S(1)}, u32[]{:S(2)}, u32[]{:S(2)}) collective-permute-start(f32[8,5,8,128]{3,2,1,0:T(8,128)S(1)} %collective-permute-done.6.refs_2_), channel_id=1, source_target_pairs={{8,16},{16,24},{9,17},{17,25},{10,18},{18,26},{11,19},{19,27},{12,... | collective-permute-start | bytes 491528 | tf_op jit(solution)/shard_map/ppermute | solution.py:326
  57.8 4.2 %collective-permute-start.13 = (f32[2,6,8,512]{3,2,1,0:T(8,128)S(1)}, f32[2,6,8,512]{3,2,1,0:T(8,128)S(1)}, u32[]{:S(2)}, u32[]{:S(2)}) collective-permute-start(f32[2,6,8,512]{3,2,1,0:T(8,128)S(1)} %get-tuple-element.63.b_ref), channel_id=1, source_target_pairs={{24,16},{25,17},{26,18},{27,19},{28,20},{29,21},{30,22},{31,23}} | collective-permute-start | bytes 589832 | tf_op jit(solution)/shard_map/ppermute | solution.py:329
  59.9 2.8 %collective-permute-start.9 = (f32[2,6,8,512]{3,2,1,0:T(8,128)S(1)}, f32[2,6,8,512]{3,2,1,0:T(8,128)S(1)}, u32[]{:S(2)}, u32[]{:S(2)}) collective-permute-start(f32[2,6,8,512]{3,2,1,0:T(8,128)S(1)} %get-tuple-element.55.b_ref), channel_id=1, source_target_pairs={{24,16},{25,17},{26,18},{27,19},{28,20},{29,21},{30,22},{31,23}} | collective-permute-start | bytes 589832 | tf_op jit(solution)/shard_map/ppermute | solution.py:329
  60.6 2.8 %collective-permute-start.12 = (f32[8,5,8,128]{3,2,1,0:T(8,128)S(1)}, f32[8,5,8,128]{3,2,1,0:T(8,128)S(1)}, u32[]{:S(2)}, u32[]{:S(2)}) collective-permute-start(f32[8,5,8,128]{3,2,1,0:T(8,128)S(1)} %collective-permute-done.11.refs_1_), channel_id=1, source_target_pairs={{16,24},{17,25},{18,26},{19,27},{20,28},{21,29},{22,30},{23,31}} | collective-permute-start | bytes 491528 | tf_op jit(solution)/shard_map/ppermute | solution.py:326
  61.2 4.2 %collective-permute-start.8 = (f32[8,5,8,128]{3,2,1,0:T(8,128)S(1)}, f32[8,5,8,128]{3,2,1,0:T(8,128)S(1)}, u32[]{:S(2)}, u32[]{:S(2)}) collective-permute-start(f32[8,5,8,128]{3,2,1,0:T(8,128)S(1)} %collective-permute-done.7.refs_1_), channel_id=1, source_target_pairs={{16,24},{17,25},{18,26},{19,27},{20,28},{21,29},{22,30},{23,31}} | collective-permute-start | bytes 491528 | tf_op jit(solution)/shard_map/ppermute | solution.py:326
  62.0 5.6 %collective-permute-start.16 = (f32[2,6,8,512]{3,2,1,0:T(8,128)S(1)}, f32[2,6,8,512]{3,2,1,0:T(8,128)S(1)}, u32[]{:S(2)}, u32[]{:S(2)}) collective-permute-start(f32[2,6,8,512]{3,2,1,0:T(8,128)S(1)} %carry.9), channel_id=1, source_target_pairs={{16,8},{17,9},{18,10},{19,11},{20,12},{21,13},{22,14},{23,15}} | collective-permute-start | bytes 589832 | tf_op jit(solution)/shard_map/ppermute | solution.py:329
  62.7 6.2 %collective-permute-start.14 = (f32[2,6,8,512]{3,2,1,0:T(8,128)S(1)}, f32[2,6,8,512]{3,2,1,0:T(8,128)S(1)}, u32[]{:S(2)}, u32[]{:S(2)}) collective-permute-start(f32[2,6,8,512]{3,2,1,0:T(8,128)S(1)} %carry.8), channel_id=1, source_target_pairs={{16,8},{17,9},{18,10},{19,11},{20,12},{21,13},{22,14},{23,15}} | collective-permute-start | bytes 589832 | tf_op jit(solution)/shard_map/ppermute | solution.py:329
  64.8 5.5 %collective-permute-start.21 = (f32[2,6,8,512]{3,2,1,0:T(8,128)S(1)}, f32[2,6,8,512]{3,2,1,0:T(8,128)S(1)}, u32[]{:S(2)}, u32[]{:S(2)}) collective-permute-start(f32[2,6,8,512]{3,2,1,0:T(8,128)S(1)} %get-tuple-element.84.b_ref), channel_id=1, source_target_pairs={{24,16},{25,17},{26,18},{27,19},{28,20},{29,21},{30,22},{31,23}} | collective-permute-start | bytes 589832 | tf_op jit(solution)/shard_map/ppermute | solution.py:329
  66.9 4.1 %copy-start.2 = (f32[2,25,8,512]{3,2,1,0:T(8,128)}, f32[2,25,8,512]{3,2,1,0:T(8,128)S(1)}, u32[]{:S(2)}) copy-start(f32[2,25,8,512]{3,2,1,0:T(8,128)S(1)} %get-tuple-element.59.refs_2_) | copy-start | bytes 2457604
  66.9 4.1 %collective-permute-start.18 = (f32[2,6,8,512]{3,2,1,0:T(8,128)S(1)}, f32[2,6,8,512]{3,2,1,0:T(8,128)S(1)}, u32[]{:S(2)}, u32[]{:S(2)}) collective-permute-start(f32[2,6,8,512]{3,2,1,0:T(8,128)S(1)} %get-tuple-element.78.b_ref), channel_id=1, source_target_pairs={{24,16},{25,17},{26,18},{27,19},{28,20},{29,21},{30,22},{31,23}} | collective-permute-start | bytes 589832 | tf_op jit(solution)/shard_map/ppermute | solution.py:329
  67.6 18.4 %collective-permute-start.17 = (f32[2,6,8,512]{3,2,1,0:T(8,128)S(1)}, f32[2,6,8,512]{3,2,1,0:T(8,128)S(1)}, u32[]{:S(2)}, u32[]{:S(2)}) collective-permute-start(f32[2,6,8,512]{3,2,1,0:T(8,128)S(1)} %carry.11), channel_id=1, source_target_pairs={{8,0},{9,1},{10,2},{11,3},{12,4},{13,5},{14,6},{15,7}} | collective-permute-start | bytes 589832 | tf_op jit(solution)/shard_map/ppermute | solution.py:329
  69.0 21.3 %collective-permute-start.15 = (f32[2,6,8,512]{3,2,1,0:T(8,128)S(1)}, f32[2,6,8,512]{3,2,1,0:T(8,128)S(1)}, u32[]{:S(2)}, u32[]{:S(2)}) collective-permute-start(f32[2,6,8,512]{3,2,1,0:T(8,128)S(1)} %carry.10), channel_id=1, source_target_pairs={{8,0},{9,1},{10,2},{11,3},{12,4},{13,5},{14,6},{15,7}} | collective-permute-start | bytes 589832 | tf_op jit(solution)/shard_map/ppermute | solution.py:329
  70.3 20.2 %collective-permute-start.22 = (f32[2,6,8,512]{3,2,1,0:T(8,128)S(1)}, f32[2,6,8,512]{3,2,1,0:T(8,128)S(1)}, u32[]{:S(2)}, u32[]{:S(2)}) collective-permute-start(f32[2,6,8,512]{3,2,1,0:T(8,128)S(1)} %carry.14), channel_id=1, source_target_pairs={{16,8},{17,9},{18,10},{19,11},{20,12},{21,13},{22,14},{23,15}} | collective-permute-start | bytes 589832 | tf_op jit(solution)/shard_map/ppermute | solution.py:329
  71.0 20.9 %collective-permute-start.19 = (f32[2,6,8,512]{3,2,1,0:T(8,128)S(1)}, f32[2,6,8,512]{3,2,1,0:T(8,128)S(1)}, u32[]{:S(2)}, u32[]{:S(2)}) collective-permute-start(f32[2,6,8,512]{3,2,1,0:T(8,128)S(1)} %carry.12), channel_id=1, source_target_pairs={{16,8},{17,9},{18,10},{19,11},{20,12},{21,13},{22,14},{23,15}} | collective-permute-start | bytes 589832 | tf_op jit(solution)/shard_map/ppermute | solution.py:329
  90.6 7.6 %collective-permute-start.23 = (f32[2,6,8,512]{3,2,1,0:T(8,128)S(1)}, f32[2,6,8,512]{3,2,1,0:T(8,128)S(1)}, u32[]{:S(2)}, u32[]{:S(2)}) collective-permute-start(f32[2,6,8,512]{3,2,1,0:T(8,128)S(1)} %carry.15), channel_id=1, source_target_pairs={{8,0},{9,1},{10,2},{11,3},{12,4},{13,5},{14,6},{15,7}} | collective-permute-start | bytes 589832 | tf_op jit(solution)/shard_map/ppermute | solution.py:329
  91.9 8.8 %collective-permute-start.20 = (f32[2,6,8,512]{3,2,1,0:T(8,128)S(1)}, f32[2,6,8,512]{3,2,1,0:T(8,128)S(1)}, u32[]{:S(2)}, u32[]{:S(2)}) collective-permute-start(f32[2,6,8,512]{3,2,1,0:T(8,128)S(1)} %carry.13), channel_id=1, source_target_pairs={{8,0},{9,1},{10,2},{11,3},{12,4},{13,5},{14,6},{15,7}} | collective-permute-start | bytes 589832 | tf_op jit(solution)/shard_map/ppermute | solution.py:329
  102.8 14.6 %all-to-all-start.1 = ((f32[8,5,8,512]{3,2,1,0:T(8,128)}), f32[8,5,8,512]{3,2,1,0:T(8,128)S(1)}, u32[]{:S(2)}, u32[]{:S(2)}) async-start(f32[8,5,8,512]{3,2,1,0:T(8,128)} %stencil.1), calls=%async_computation.1 | async-start | bytes 1310720 | tf_op jit(solution)/shard_map/all_to_all | solution.py:431
  106.3 1.1 copy-start.3

commit v8 on v6

--- a/solution.py
+++ b/solution.py
@@ -13,14 +13,16 @@
 F32 = jnp.float32
 VMEM_LIMIT = 16 * 1024 * 1024
 CHUNKS = 4
+WAVE = 2
 SPAN = 4
 MIX_LANE = 64
 
 
-def pack_kernel(coef_ref, p_ref, out_ref):
+def pack_kernel(coef_ref, p_ref, out_ref, weight_ref):
     planes, rows, width = p_ref.shape
     for k in range(planes):
         w = coef_ref[0, k]
+        weight_ref[k] = jnp.full((SUB, EDGE), w, F32)
         for s in range(out_ref.shape[0]):
             before = (R * s - 1) % rows
             after = (R * (s + 1)) % rows
@@ -207,7 +209,12 @@
                     shear_ref[k, j, :, start : start + width] = map_ref[i, 5 * k + 2 + j, 0:R]
 
 
-def carry_kernel(planes, sender, coef_ref, in_ref, b_ref, m_ref, out_ref):
+def own_tile(ref, k, planes, like):
+    tile = ref[ref.shape[0] - planes + k, 0:R]
+    return jnp.concatenate([tile] * (like.shape[1] // EDGE), axis=1)
+
+
+def carry_kernel(planes, sender, in_ref, excess_ref, b_ref, m_ref, out_ref):
     @pl.when(lax.axis_index("plane") == sender)
     def _():
         for step in range(out_ref.shape[0]):
@@ -215,11 +222,11 @@
             p, q = (fields[0:4], fields[4:8])
             for k in reversed(range(planes)):
                 m0, m1, off = (m_ref[step, 3 * k + j, 0:R] for j in range(3))
-                p, q = transposed_step(m0, m1, off, p, q, 1.0 - coef_ref[1, k])
+                p, q = transposed_step(m0, m1, off, p, q, -own_tile(excess_ref, k, planes, m0))
             pack_state(out_ref, step, p + q, b_ref)
 
 
-def cotangent_kernel(planes, coef_ref, src_ref, m_ref, a_ref, *refs):
+def cotangent_kernel(planes, excess_ref, weight_ref, src_ref, m_ref, a_ref, *refs):
     arrived, cot_ref = (refs[:-1], refs[-1])
     blank = jnp.zeros((SUB - R, cot_ref.shape[-1]), F32)
     for step in range(cot_ref.shape[0]):
@@ -229,7 +236,7 @@
             s0, s1, s3 = (src_ref[step, 3 * k + j, 0:R] for j in range(3))
             p = [p[0] + s0, p[1] + s1, p[2] + s1, p[3] + s3]
             a = [a_ref[step, 4 * k + j, 0:R] for j in range(4)]
-            w = -coef_ref[0, k]
+            w = -own_tile(weight_ref, k, planes, s0)
             cots = [
                 w * (p[0] * a[0] + p[1] * a[1]),
                 w * (p[2] * a[2] + p[3] * a[3]),
@@ -238,7 +245,7 @@
             for j in range(3):
                 cot_ref[step, 3 * k + j] = jnp.concatenate([cots[j], blank], axis=0)
             m0, m1, off = (m_ref[step, 3 * k + j, 0:R] for j in range(3))
-            p, q = transposed_step(m0, m1, off, p, q, 1.0 - coef_ref[1, k])
+            p, q = transposed_step(m0, m1, off, p, q, -own_tile(excess_ref, k, planes, m0))
 
 
 def stencil_kernel(planes, *refs):
@@ -322,11 +329,11 @@
         return lax.ppermute(x, "plane", [(groups - 1 - hop, groups - 2 - hop)])
 
     coef = jnp.stack([lens_weight, mixing])
-    packed = pl.pallas_call(
+    packed, weights = pl.pallas_call(
         pack_kernel,
-        out_shape=shape(slabs, tiles, planes, SUB, EDGE),
+        out_shape=(shape(slabs, tiles, planes, SUB, EDGE), shape(planes, SUB, EDGE)),
         in_specs=[SCALARS, WHOLE],
-        out_specs=WHOLE,
+        out_specs=(WHOLE, WHOLE),
         compiler_params=params(),
         name="pack",
     )(coef, potential)
@@ -347,7 +354,6 @@
         for c in range(CHUNKS):
             if 0 <= turn - c < groups - 1:
                 strips[c].insert(0, climb(strips[c][0], turn - c))
-
     beside, excess = pl.pallas_call(
         edges_kernel,
         out_shape=(
@@ -360,10 +366,13 @@
         name="edges",
     )(*strips[0])
 
-    maps = []
-    work = []
-    for c in range(CHUNKS):
-        map_piece, *held = pl.pallas_call(
+    sequence = list(reversed(range(2, CHUNKS))) + [0, 1]
+    maps = [None] * CHUNKS
+    work = [None] * CHUNKS
+    for c in sequence:
+        if c == 1:
+            strips[1][0] = lax.optimization_barrier((strips[1][0], work[0][-1]))[0]
+        maps[c], *work[c] = pl.pallas_call(
             functools.partial(forward_kernel, groups, planes, c, length),
             out_shape=(
                 shape(steps, 5 * planes, SUB, span),
@@ -377,32 +386,36 @@
             compiler_params=params(),
             name="forward",
         )(*strips[c], beside, excess, observed, noise_weight)
-        maps.append(map_piece)
-        work.append(held)
-
-    cots = []
-    for matrices, states, sources, b in work:
+
+    events = [[] for c in range(CHUNKS)]
+    cots = [None] * CHUNKS
+    for place, c in enumerate(sequence):
+        matrices, states, sources, b = work[c]
         arrived = [descend(b, 0)]
         for hop in range(1, groups - 1):
+            incoming = arrived[-1]
+            if place >= WAVE:
+                ahead = events[sequence[place - WAVE]]
+                incoming = lax.optimization_barrier((incoming, ahead[hop]))[0]
             outgoing = pl.pallas_call(
                 functools.partial(carry_kernel, planes, groups - 1 - hop),
                 out_shape=shape(steps, R, SUB, span),
-                in_specs=[SCALARS] + [WHOLE] * 3,
+                in_specs=[WHOLE] * 4,
                 out_specs=WHOLE,
                 compiler_params=params(),
                 name="carry",
-            )(coef, arrived[-1], b, matrices)
+            )(incoming, excess, b, matrices)
+            events[c].append(outgoing)
             arrived.append(descend(outgoing, hop))
-        cots.append(
-            pl.pallas_call(
-                functools.partial(cotangent_kernel, planes),
-                out_shape=shape(steps, 3 * planes, SUB, span),
-                in_specs=[SCALARS] + [WHOLE] * (groups + 2),
-                out_specs=WHOLE,
-                compiler_params=params(),
-                name="cotangent",
-            )(coef, sources, matrices, states, *arrived)
-        )
+        cots[c] = pl.pallas_call(
+            functools.partial(cotangent_kernel, planes),
+            out_shape=shape(steps, 3 * planes, SUB, span),
+            in_specs=[WHOLE] * (groups + 4),
+            out_specs=WHOLE,
+            compiler_params=params(),
+            name="cotangent",
+        )(excess, weights, sources, matrices, states, *arrived)
+        events[c].append(cots[c])
 
     partial = pl.pallas_call(
         functools.partial(stencil_kernel, planes),

time: 119 us -> 118 us (level)
  starting transfers between devices: 31.8 us -> 38.5 us
  Pallas kernels: 19 us -> 12.5 us
  waiting for transfers between devices: 45.7 us -> 44.4 us
    ppermute x12, starting transfers between devices: 17.7 us -> 24.4 us  [climb(): lax.ppermute(x, 'plane', [(i, i + 1) for i in range(hop, groups - 1)])]
    pallas_call x8, Pallas kernels: 4.52 us -> 0.13 us  [on_device(): pl.pallas_call(functools.partial(carry_kernel, planes, groups - 1 - hop),...]
    pallas_call x4, Pallas kernels: 3.21 us -> 1.05 us  [on_device(): pl.pallas_call(functools.partial(cotangent_kernel, planes), out_shape=sha...]
  transfers between devices with their start and end apart: 25 -> 25, of which waited for: 7 -> 8; matrix products, arithmetic and copies ran while one was open for 1% -> 1% of each run, Pallas kernels for 12% -> 7%
where the time goes in v8:
time: 118 us; the launch traced here: 117 us
  waiting for transfers between devices  44.4 us (38%)
  starting transfers between devices  38.5 us (33%)
  blocking collectives  16.1 us (14%)
  Pallas kernels  12.5 us (11%)
  local copies, waits for them, and re-layouts  3.89 us (3%)
    ppermute x12, waiting for transfers between devices, descend(): return lax.ppermute(x, 'plane', [(groups - 1 - hop, groups - 2 - hop)])  34.6 us
    ppermute x12, starting transfers between devices, climb(): lax.ppermute(x, 'plane', [(i, i + 1) for i in range(hop, groups - 1)])  24.4 us
    all_to_all x1, blocking collectives, on_device(): lax.all_to_all(packed, 'slab', split_axis=0, concat_axis=0, tiled=True)  16.1 us
    ppermute x12, starting transfers between devices, descend(): return lax.ppermute(x, 'plane', [(groups - 1 - hop, groups - 2 - hop)])  10.6 us
    all_to_all x1, waiting for transfers between devices, on_device(): lax.all_to_all(partial, 'slab', split_axis=0, concat_axis=0, tiled=True)  6.68 us
    pallas_call x4, Pallas kernels, on_device(): pl.pallas_call(functools.partial(forward_kernel, groups, planes, c, lengt...  5.62 us
    unnamed x11, local copies, waits for them, and re-layouts  3.89 us
    all_to_all x1, starting transfers between devices, on_device(): lax.all_to_all(partial, 'slab', split_axis=0, concat_axis=0, tiled=True)  3.54 us
  transfers between devices with their start and end apart: 25, of which 8 were waited for; matrix products, arithmetic and copies ran while one was open for 1% of the time, Pallas kernels for 7%

profile of v8, /device:TPU:0, one launch (start us, length us, event | category | flops | bytes accessed | tf_op | source)
XLA Modules:
  0.0 117.4 jit_solution(1816991459721728620)
XLA Ops:
  0.7 0.8 pad_maximum_fusion.coef_ref
  1.5 1.0 copy-done.4
  2.5 0.7 pack.1
  3.2 16.1 %all_to_all.10 = f32[8,4,5,8,128]{4,3,2,1,0:T(8,128)S(1)} all-to-all(f32[8,4,5,8,128]{4,3,2,1,0:T(8,128)S(1)} %get-tuple-element.38), channel_id=1, replica_groups=mesh['plane'=4,'slab'=8] {'slab'}, dimensions={0} | all-to-all | bytes 1310720 | tf_op jit(solution)/shard_map/all_to_all | solution.py:340
  19.3 0.7 split.1
  20.0 3.5 %collective-permute-start = (f32[9,5,8,128]{3,2,1,0:T(8,128)S(1)}, f32[9,5,8,128]{3,2,1,0:T(8,128)S(1)}, u32[]{:S(2)}, u32[]{:S(2)}) collective-permute-start(f32[9,5,8,128]{3,2,1,0:T(8,128)S(1)} %get-tuple-element.39.refs_3_), channel_id=1, source_target_pairs={{0,8},{8,16},{16,24},{1,9},{9,17},{17,25},{2,10},{10,18},{18,26},{... | collective-permute-start | bytes 552968 | tf_op jit(solution)/shard_map/ppermute | solution.py:326
  23.5 3.5 %collective-permute-start.6 = (f32[8,5,8,128]{3,2,1,0:T(8,128)S(1)}, f32[8,5,8,128]{3,2,1,0:T(8,128)S(1)}, u32[]{:S(2)}, u32[]{:S(2)}) collective-permute-start(f32[8,5,8,128]{3,2,1,0:T(8,128)S(1)} %get-tuple-element.47.refs_3_), channel_id=1, source_target_pairs={{0,8},{8,16},{16,24},{1,9},{9,17},{17,25},{2,10},{10,18},{18,26},{... | collective-permute-start | bytes 491528 | tf_op jit(solution)/shard_map/ppermute | solution.py:326
  27.0 3.5 %collective-permute-start.9 = (f32[8,5,8,128]{3,2,1,0:T(8,128)S(1)}, f32[8,5,8,128]{3,2,1,0:T(8,128)S(1)}, u32[]{:S(2)}, u32[]{:S(2)}) collective-permute-start(f32[8,5,8,128]{3,2,1,0:T(8,128)S(1)} %get-tuple-element.49.refs_3_), channel_id=1, source_target_pairs={{0,8},{8,16},{16,24},{1,9},{9,17},{17,25},{2,10},{10,18},{18,26},{... | collective-permute-start | bytes 491528 | tf_op jit(solution)/shard_map/ppermute | solution.py:326
  30.5 0.7 collective-permute-start.1
  31.2 0.4 collective-permute-done.6.refs_2_
  31.6 0.7 collective-permute-start.7
  32.3 1.9 %collective-permute-done.9.refs_2_ = f32[8,5,8,128]{3,2,1,0:T(8,128)S(1)} collective-permute-done((f32[8,5,8,128]{3,2,1,0:T(8,128)S(1)}, f32[8,5,8,128]{3,2,1,0:T(8,128)S(1)}, u32[]{:S(2)}, u32[]{:S(2)}) %collective-permute-start.9) | collective-permute-done | bytes 163872 | tf_op jit(solution)/shard_map/ppermute | solution.py:326
  34.2 0.7 collective-permute-start.10
  34.8 8.6 %collective-permute-start.3 = (f32[8,5,8,128]{3,2,1,0:T(8,128)S(1)}, f32[8,5,8,128]{3,2,1,0:T(8,128)S(1)}, u32[]{:S(2)}, u32[]{:S(2)}) collective-permute-start(f32[8,5,8,128]{3,2,1,0:T(8,128)S(1)} %get-tuple-element.43.refs_3_), channel_id=1, source_target_pairs={{0,8},{8,16},{16,24},{1,9},{9,17},{17,25},{2,10},{10,18},{18,26},{... | collective-permute-start | bytes 491528 | tf_op jit(solution)/shard_map/ppermute | solution.py:326
  43.4 0.7 collective-permute-start.2
  44.1 0.7 collective-permute-start.8
  44.8 0.7 collective-permute-start.11
  45.5 0.7 collective-permute-done.3.refs_2_
  46.2 0.7 collective-permute-start.4
  47.1 1.4 %forward.6 = (f32[2,25,8,512]{3,2,1,0:T(8,128)S(1)}, f32[2,15,8,512]{3,2,1,0:T(8,128)S(1)}, f32[2,20,8,512]{3,2,1,0:T(8,128)S(1)}, f32[2,15,8,512]{3,2,1,0:T(8,128)S(1)}, f32[2,6,8,512]{3,2,1,0:T(8,128)S(1)}) custom-call(f32[8,5,8,128]{3,2,1,0:T(8,128)S(1)} %collective-permute-done.8.refs_0_, f32[8,5,8,128]{3,2,1,0:T(8,128)S(1)} %collective-permute-done.7.refs_1_, ...), custom_call_target="tpu_custom_call" | custom-call | tf_op jit(solution)/shard_map/forward/pallas_call | solution.py:375
  48.5 0.7 collective-permute-start.19
  49.2 1.4 %forward.7 = (f32[2,25,8,512]{3,2,1,0:T(8,128)S(1)}, f32[2,15,8,512]{3,2,1,0:T(8,128)S(1)}, f32[2,20,8,512]{3,2,1,0:T(8,128)S(1)}, f32[2,15,8,512]{3,2,1,0:T(8,128)S(1)}, f32[2,6,8,512]{3,2,1,0:T(8,128)S(1)}) custom-call(f32[8,5,8,128]{3,2,1,0:T(8,128)S(1)} %collective-permute-done.11.refs_0_, f32[8,5,8,128]{3,2,1,0:T(8,128)S(1)} %collective-permute-done.10.refs_1_, ...), custom_call_target="tpu_custom_call" | custom-call | tf_op jit(solution)/shard_map/forward/pallas_call | solution.py:375
  50.6 0.7 collective-permute-start.13
  51.3 0.7 collective-permute-start.5
  52.0 1.4 %forward.4 = (f32[2,25,8,512]{3,2,1,0:T(8,128)S(1)}, f32[2,15,8,512]{3,2,1,0:T(8,128)S(1)}, f32[2,20,8,512]{3,2,1,0:T(8,128)S(1)}, f32[2,15,8,512]{3,2,1,0:T(8,128)S(1)}, f32[2,6,8,512]{3,2,1,0:T(8,128)S(1)}) custom-call(f32[9,5,8,128]{3,2,1,0:T(8,128)S(1)} %collective-permute-done.2.refs_0_, f32[9,5,8,128]{3,2,1,0:T(8,128)S(1)} %collective-permute-done.1.refs_1_, ...), custom_call_target="tpu_custom_call" | custom-call | tf_op jit(solution)/shard_map/forward/pallas_call | solution.py:375
  53.4 0.7 collective-permute-start.20
  54.1 1.4 %forward.5 = (f32[2,25,8,512]{3,2,1,0:T(8,128)S(1)}, f32[2,15,8,512]{3,2,1,0:T(8,128)S(1)}, f32[2,20,8,512]{3,2,1,0:T(8,128)S(1)}, f32[2,15,8,512]{3,2,1,0:T(8,128)S(1)}, f32[2,6,8,512]{3,2,1,0:T(8,128)S(1)}) custom-call(f32[8,5,8,128]{3,2,1,0:T(8,128)S(1)} %collective-permute-done.5.refs_0_, f32[8,5,8,128]{3,2,1,0:T(8,128)S(1)} %collective-permute-done.4.refs_1_, ...), custom_call_target="tpu_custom_call" | custom-call | tf_op jit(solution)/shard_map/forward/pallas_call | solution.py:375
  55.5 0.7 collective-permute-start.18
  56.3 0.7 collective-permute-start.14
  56.9 0.7 collective-permute-start.12
  57.7 1.3 %collective-permute-start.22 = (f32[2,6,8,512]{3,2,1,0:T(8,128)S(1)}, f32[2,6,8,512]{3,2,1,0:T(8,128)S(1)}, u32[]{:S(2)}, u32[]{:S(2)}) collective-permute-start(f32[2,6,8,512]{3,2,1,0:T(8,128)S(1)} %carry.13), channel_id=1, source_target_pairs={{8,0},{9,1},{10,2},{11,3},{12,4},{13,5},{14,6},{15,7}} | collective-permute-start | bytes 589832 | tf_op jit(solution)/shard_map/ppermute | solution.py:329
  59.0 0.7 collective-permute-start.21
  59.7 1.3 %collective-permute-start.16 = (f32[2,6,8,512]{3,2,1,0:T(8,128)S(1)}, f32[2,6,8,512]{3,2,1,0:T(8,128)S(1)}, u32[]{:S(2)}, u32[]{:S(2)}) collective-permute-start(f32[2,6,8,512]{3,2,1,0:T(8,128)S(1)} %carry.9), channel_id=1, source_target_pairs={{8,0},{9,1},{10,2},{11,3},{12,4},{13,5},{14,6},{15,7}} | collective-permute-start | bytes 589832 | tf_op jit(solution)/shard_map/ppermute | solution.py:329
  61.0 0.7 collective-permute-start.15
  61.7 26.1 %collective-permute-done.22.refs_2_ = f32[2,6,8,512]{3,2,1,0:T(8,128)S(1)} collective-permute-done((f32[2,6,8,512]{3,2,1,0:T(8,128)S(1)}, f32[2,6,8,512]{3,2,1,0:T(8,128)S(1)}, u32[]{:S(2)}, u32[]{:S(2)}) %collective-permute-start.22) | collective-permute-done | bytes 196640 | tf_op jit(solution)/shard_map/ppermute | solution.py:329
  88.1 1.3 %collective-permute-start.23 = (f32[2,6,8,512]{3,2,1,0:T(8,128)S(1)}, f32[2,6,8,512]{3,2,1,0:T(8,128)S(1)}, u32[]{:S(2)}, u32[]{:S(2)}) collective-permute-start(f32[2,6,8,512]{3,2,1,0:T(8,128)S(1)} %carry.15), channel_id=1, source_target_pairs={{8,0},{9,1},{10,2},{11,3},{12,4},{13,5},{14,6},{15,7}} | collective-permute-start | bytes 589832 | tf_op jit(solution)/shard_map/ppermute | solution.py:329
  89.4 2.5 %collective-permute-done.16.refs_2_ = f32[2,6,8,512]{3,2,1,0:T(8,128)S(1)} collective-permute-done((f32[2,6,8,512]{3,2,1,0:T(8,128)S(1)}, f32[2,6,8,512]{3,2,1,0:T(8,128)S(1)}, u32[]{:S(2)}, u32[]{:S(2)}) %collective-permute-start.16) | collective-permute-done | bytes 196640 | tf_op jit(solution)/shard_map/ppermute | solution.py:329
  92.2 1.3 %collective-permute-start.17 = (f32[2,6,8,512]{3,2,1,0:T(8,128)S(1)}, f32[2,6,8,512]{3,2,1,0:T(8,128)S(1)}, u32[]{:S(2)}, u32[]{:S(2)}) collective-permute-start(f32[2,6,8,512]{3,2,1,0:T(8,128)S(1)} %carry.11), channel_id=1, source_target_pairs={{8,0},{9,1},{10,2},{11,3},{12,4},{13,5},{14,6},{15,7}} | collective-permute-start | bytes 589832 | tf_op jit(solution)/shard_map/ppermute | solution.py:329
  93.5 3.2 %collective-permute-done.23.refs_2_ = f32[2,6,8,512]{3,2,1,0:T(8,128)S(1)} collective-permute-done((f32[2,6,8,512]{3,2,1,0:T(8,128)S(1)}, f32[2,6,8,512]{3,2,1,0:T(8,128)S(1)}, u32[]{:S(2)}, u32[]{:S(2)}) %collective-permute-start.23) | collective-permute-done | bytes 196640 | tf_op jit(solution)/shard_map/ppermute | solution.py:329
  96.7 0.3 cotangent.7.refs_1_
  97.0 2.8 %collective-permute-done.17.refs_2_ = f32[2,6,8,512]{3,2,1,0:T(8,128)S(1)} collective-permute-done((f32[2,6,8,512]{3,2,1,0:T(8,128)S(1)}, f32[2,6,8,512]{3,2,1,0:T(8,128)S(1)}, u32[]{:S(2)}, u32[]{:S(2)}) %collective-permute-start.17) | collective-permute-done | bytes 196640 | tf_op jit(solution)/shard_map/ppermute | solution.py:329
  100.1 1.8 %stencil.1 = f32[8,5,8,512]{3,2,1,0:T(8,128)} custom-call(f32[2,15,8,512]{3,2,1,0:T(8,128)S(1)} %cotangent.5.refs_0_, f32[2,15,8,512]{3,2,1,0:T(8,128)S(1)} %cotangent.7.refs_1_, f32[2,15,8,512]{3,2,1,0:T(8,128)S(1)} %cotangent.6.refs_2_, f32[2,15,8,512]{3,2,1,0:T(8,128)S(1)} %cotangent.4.refs_3_), custom_call_target="tpu_custom_call" | custom-call | tf_op jit(solution)/shard_map/stencil/pallas_call | solution.py:420
  101.8 3.5 %all-to-all-start.1 = ((f32[8,5,8,512]{3,2,1,0:T(8,128)}), f32[8,5,8,512]{3,2,1,0:T(8,128)S(1)}, u32[]{:S(2)}, u32[]{:S(2)}) async-start(f32[8,5,8,512]{3,2,1,0:T(8,128)} %stencil.1), calls=%async_computation.1 | async-start | bytes 1310720 | tf_op jit(solution)/shard_map/all_to_all | solution.py:428
  105.4 1.1 copy-done.3
  106.5 1.6 %assemble.1 = (f32[5,2,6,4096]{3,2,1,0:T(8,128)S(1)}, f32[5,3,6,4096]{3,2,1,0:T(8,128)}) custom-call(f32[2,25,8,512]{3,2,1,0:T(8,128)S(1)} %get-tuple-element.42.refs_0_, f32[2,25,8,512]{3,2,1,0:T(8,128)S(1)} %copy-done.3, f32[2,25,8,512]{3,2,1,0:T(8,128)S(1)} %get-tuple-element.48.refs_2_, f32[2,25,8,512]{3,2,1,0:T(8,128)S(1)} %get-tuple-element.50.refs_3_), custom_call_target="tpu_custom_call" | custom-call | tf_op jit(solution)/shard_map/assemble/pallas_call | solution.py:429
  108.1 1.7 %copy.8 = f32[5,2,6,4096]{3,1,2,0:T(2,128)} copy(f32[5,2,6,4096]{3,2,1,0:T(8,128)S(1)} %get-tuple-element.73) | data formatting | bytes 1966080
  109.8 6.7 %all-to-all-done.1.in_ref = f32[8,5,8,512]{3,2,1,0:T(8,128)S(1)} async-done(((f32[8,5,8,512]{3,2,1,0:T(8,128)}), f32[8,5,8,512]{3,2,1,0:T(8,128)S(1)}, u32[]{:S(2)}, u32[]{:S(2)}) %all-to-all-start.1) | async-done | bytes 655392 | tf_op jit(solution)/shard_map/all_to_all | solution.py:428
  116.5 0.9 combine.1
  (37 shorter events, 1.1 us)
Async XLA Ops:
  0.6 46.4 %copy-start = (f32[5,3,6,4096]{3,2,1,0:T(8,128)S(1)}, f32[5,3,6,4096]{3,2,1,0:T(8,128)}, u32[]{:S(2)}) copy-start(f32[5,3,6,4096]{3,2,1,0:T(8,128)} %refs_6_.7) | copy-start | bytes 4423684
  0.6 46.4 %copy-start.1 = (f32[5,6,4096]{2,1,0:T(8,128)S(1)}, f32[5,6,4096]{2,1,0:T(8,128)}, u32[]{:S(2)}) copy-start(f32[5,6,4096]{2,1,0:T(8,128)} %refs_7_.7) | copy-start | bytes 1474564
  1.5 1.0 copy-start.4
  20.0 10.5 %collective-permute-start = (f32[9,5,8,128]{3,2,1,0:T(8,128)S(1)}, f32[9,5,8,128]{3,2,1,0:T(8,128)S(1)}, u32[]{:S(2)}, u32[]{:S(2)}) collective-permute-start(f32[9,5,8,128]{3,2,1,0:T(8,128)S(1)} %get-tuple-element.39.refs_3_), channel_id=1, source_target_pairs={{0,8},{8,16},{16,24},{1,9},{9,17},{17,25},{2,10},{10,18},{18,26},{... | collective-permute-start | bytes 552968 | tf_op jit(solution)/shard_map/ppermute | solution.py:326
  23.5 8.1 %collective-permute-start.6 = (f32[8,5,8,128]{3,2,1,0:T(8,128)S(1)}, f32[8,5,8,128]{3,2,1,0:T(8,128)S(1)}, u32[]{:S(2)}, u32[]{:S(2)}) collective-permute-start(f32[8,5,8,128]{3,2,1,0:T(8,128)S(1)} %get-tuple-element.47.refs_3_), channel_id=1, source_target_pairs={{0,8},{8,16},{16,24},{1,9},{9,17},{17,25},{2,10},{10,18},{18,26},{... | collective-permute-start | bytes 491528 | tf_op jit(solution)/shard_map/ppermute | solution.py:326
  27.0 7.2 %collective-permute-start.9 = (f32[8,5,8,128]{3,2,1,0:T(8,128)S(1)}, f32[8,5,8,128]{3,2,1,0:T(8,128)S(1)}, u32[]{:S(2)}, u32[]{:S(2)}) collective-permute-start(f32[8,5,8,128]{3,2,1,0:T(8,128)S(1)} %get-tuple-element.49.refs_3_), channel_id=1, source_target_pairs={{0,8},{8,16},{16,24},{1,9},{9,17},{17,25},{2,10},{10,18},{18,26},{... | collective-permute-start | bytes 491528 | tf_op jit(solution)/shard_map/ppermute | solution.py:326
  30.5 13.0 %collective-permute-start.1 = (f32[9,5,8,128]{3,2,1,0:T(8,128)S(1)}, f32[9,5,8,128]{3,2,1,0:T(8,128)S(1)}, u32[]{:S(2)}, u32[]{:S(2)}) collective-permute-start(f32[9,5,8,128]{3,2,1,0:T(8,128)S(1)} %collective-permute-done.refs_2_), channel_id=1, source_target_pairs={{8,16},{16,24},{9,17},{17,25},{10,18},{18,26},{11,19},{19,27},{12,... | collective-permute-start | bytes 552968 | tf_op jit(solution)/shard_map/ppermute | solution.py:326
  31.6 12.5 %collective-permute-start.7 = (f32[8,5,8,128]{3,2,1,0:T(8,128)S(1)}, f32[8,5,8,128]{3,2,1,0:T(8,128)S(1)}, u32[]{:S(2)}, u32[]{:S(2)}) collective-permute-start(f32[8,5,8,128]{3,2,1,0:T(8,128)S(1)} %collective-permute-done.6.refs_2_), channel_id=1, source_target_pairs={{8,16},{16,24},{9,17},{17,25},{10,18},{18,26},{11,19},{19,27},{12,... | collective-permute-start | bytes 491528 | tf_op jit(solution)/shard_map/ppermute | solution.py:326
  34.2 10.6 %collective-permute-start.10 = (f32[8,5,8,128]{3,2,1,0:T(8,128)S(1)}, f32[8,5,8,128]{3,2,1,0:T(8,128)S(1)}, u32[]{:S(2)}, u32[]{:S(2)}) collective-permute-start(f32[8,5,8,128]{3,2,1,0:T(8,128)S(1)} %collective-permute-done.9.refs_2_), channel_id=1, source_target_pairs={{8,16},{16,24},{9,17},{17,25},{10,18},{18,26},{11,19},{19,27},{12,... | collective-permute-start | bytes 491528 | tf_op jit(solution)/shard_map/ppermute | solution.py:326
  34.8 11.4 %collective-permute-start.3 = (f32[8,5,8,128]{3,2,1,0:T(8,128)S(1)}, f32[8,5,8,128]{3,2,1,0:T(8,128)S(1)}, u32[]{:S(2)}, u32[]{:S(2)}) collective-permute-start(f32[8,5,8,128]{3,2,1,0:T(8,128)S(1)} %get-tuple-element.43.refs_3_), channel_id=1, source_target_pairs={{0,8},{8,16},{16,24},{1,9},{9,17},{17,25},{2,10},{10,18},{18,26},{... | collective-permute-start | bytes 491528 | tf_op jit(solution)/shard_map/ppermute | solution.py:326
  43.4 3.5 %collective-permute-start.2 = (f32[9,5,8,128]{3,2,1,0:T(8,128)S(1)}, f32[9,5,8,128]{3,2,1,0:T(8,128)S(1)}, u32[]{:S(2)}, u32[]{:S(2)}) collective-permute-start(f32[9,5,8,128]{3,2,1,0:T(8,128)S(1)} %collective-permute-done.1.refs_1_), channel_id=1, source_target_pairs={{16,24},{17,25},{18,26},{19,27},{20,28},{21,29},{22,30},{23,31}} | collective-permute-start | bytes 552968 | tf_op jit(solution)/shard_map/ppermute | solution.py:326
  44.1 2.9 %collective-permute-start.8 = (f32[8,5,8,128]{3,2,1,0:T(8,128)S(1)}, f32[8,5,8,128]{3,2,1,0:T(8,128)S(1)}, u32[]{:S(2)}, u32[]{:S(2)}) collective-permute-start(f32[8,5,8,128]{3,2,1,0:T(8,128)S(1)} %collective-permute-done.7.refs_1_), channel_id=1, source_target_pairs={{16,24},{17,25},{18,26},{19,27},{20,28},{21,29},{22,30},{23,31}} | collective-permute-start | bytes 491528 | tf_op jit(solution)/shard_map/ppermute | solution.py:326
  44.8 4.4 %collective-permute-start.11 = (f32[8,5,8,128]{3,2,1,0:T(8,128)S(1)}, f32[8,5,8,128]{3,2,1,0:T(8,128)S(1)}, u32[]{:S(2)}, u32[]{:S(2)}) collective-permute-start(f32[8,5,8,128]{3,2,1,0:T(8,128)S(1)} %collective-permute-done.10.refs_1_), channel_id=1, source_target_pairs={{16,24},{17,25},{18,26},{19,27},{20,28},{21,29},{22,30},{23,31}} | collective-permute-start | bytes 491528 | tf_op jit(solution)/shard_map/ppermute | solution.py:326
  46.2 5.0 %collective-permute-start.4 = (f32[8,5,8,128]{3,2,1,0:T(8,128)S(1)}, f32[8,5,8,128]{3,2,1,0:T(8,128)S(1)}, u32[]{:S(2)}, u32[]{:S(2)}) collective-permute-start(f32[8,5,8,128]{3,2,1,0:T(8,128)S(1)} %collective-permute-done.3.refs_2_), channel_id=1, source_target_pairs={{8,16},{16,24},{9,17},{17,25},{10,18},{18,26},{11,19},{19,27},{12,... | collective-permute-start | bytes 491528 | tf_op jit(solution)/shard_map/ppermute | solution.py:326
  48.5 4.9 %collective-permute-start.19 = (f32[2,6,8,512]{3,2,1,0:T(8,128)S(1)}, f32[2,6,8,512]{3,2,1,0:T(8,128)S(1)}, u32[]{:S(2)}, u32[]{:S(2)}) collective-permute-start(f32[2,6,8,512]{3,2,1,0:T(8,128)S(1)} %get-tuple-element.67.b_ref), channel_id=1, source_target_pairs={{24,16},{25,17},{26,18},{27,19},{28,20},{29,21},{30,22},{31,23}} | collective-permute-start | bytes 589832 | tf_op jit(solution)/shard_map/ppermute | solution.py:329
  50.6 5.6 %collective-permute-start.13 = (f32[2,6,8,512]{3,2,1,0:T(8,128)S(1)}, f32[2,6,8,512]{3,2,1,0:T(8,128)S(1)}, u32[]{:S(2)}, u32[]{:S(2)}) collective-permute-start(f32[2,6,8,512]{3,2,1,0:T(8,128)S(1)} %get-tuple-element.57.b_ref), channel_id=1, source_target_pairs={{24,16},{25,17},{26,18},{27,19},{28,20},{29,21},{30,22},{31,23}} | collective-permute-start | bytes 589832 | tf_op jit(solution)/shard_map/ppermute | solution.py:329
  51.3 2.1 %collective-permute-start.5 = (f32[8,5,8,128]{3,2,1,0:T(8,128)S(1)}, f32[8,5,8,128]{3,2,1,0:T(8,128)S(1)}, u32[]{:S(2)}, u32[]{:S(2)}) collective-permute-start(f32[8,5,8,128]{3,2,1,0:T(8,128)S(1)} %collective-permute-done.4.refs_1_), channel_id=1, source_target_pairs={{16,24},{17,25},{18,26},{19,27},{20,28},{21,29},{22,30},{23,31}} | collective-permute-start | bytes 491528 | tf_op jit(solution)/shard_map/ppermute | solution.py:326
  53.4 4.2 %collective-permute-start.20 = (f32[2,6,8,512]{3,2,1,0:T(8,128)S(1)}, f32[2,6,8,512]{3,2,1,0:T(8,128)S(1)}, u32[]{:S(2)}, u32[]{:S(2)}) collective-permute-start(f32[2,6,8,512]{3,2,1,0:T(8,128)S(1)} %carry.12), channel_id=1, source_target_pairs={{16,8},{17,9},{18,10},{19,11},{20,12},{21,13},{22,14},{23,15}} | collective-permute-start | bytes 589832 | tf_op jit(solution)/shard_map/ppermute | solution.py:329
  55.5 4.2 %copy-start.2 = (f32[2,25,8,512]{3,2,1,0:T(8,128)}, f32[2,25,8,512]{3,2,1,0:T(8,128)S(1)}, u32[]{:S(2)}) copy-start(f32[2,25,8,512]{3,2,1,0:T(8,128)S(1)} %get-tuple-element.46.refs_1_) | copy-start | bytes 2457604
  55.5 3.4 %collective-permute-start.18 = (f32[2,6,8,512]{3,2,1,0:T(8,128)S(1)}, f32[2,6,8,512]{3,2,1,0:T(8,128)S(1)}, u32[]{:S(2)}, u32[]{:S(2)}) collective-permute-start(f32[2,6,8,512]{3,2,1,0:T(8,128)S(1)} %get-tuple-element.66.b_ref), channel_id=1, source_target_pairs={{24,16},{25,17},{26,18},{27,19},{28,20},{29,21},{30,22},{31,23}} | collective-permute-start | bytes 589832 | tf_op jit(solution)/shard_map/ppermute | solution.py:329
  56.3 3.4 %collective-permute-start.14 = (f32[2,6,8,512]{3,2,1,0:T(8,128)S(1)}, f32[2,6,8,512]{3,2,1,0:T(8,128)S(1)}, u32[]{:S(2)}, u32[]{:S(2)}) collective-permute-start(f32[2,6,8,512]{3,2,1,0:T(8,128)S(1)} %carry.8), channel_id=1, source_target_pairs={{16,8},{17,9},{18,10},{19,11},{20,12},{21,13},{22,14},{23,15}} | collective-permute-start | bytes 589832 | tf_op jit(solution)/shard_map/ppermute | solution.py:329
  56.9 4.1 %collective-permute-start.12 = (f32[2,6,8,512]{3,2,1,0:T(8,128)S(1)}, f32[2,6,8,512]{3,2,1,0:T(8,128)S(1)}, u32[]{:S(2)}, u32[]{:S(2)}) collective-permute-start(f32[2,6,8,512]{3,2,1,0:T(8,128)S(1)} %get-tuple-element.44.b_ref), channel_id=1, source_target_pairs={{24,16},{25,17},{26,18},{27,19},{28,20},{29,21},{30,22},{31,23}} | collective-permute-start | bytes 589832 | tf_op jit(solution)/shard_map/ppermute | solution.py:329
  57.7 30.1 %collective-permute-start.22 = (f32[2,6,8,512]{3,2,1,0:T(8,128)S(1)}, f32[2,6,8,512]{3,2,1,0:T(8,128)S(1)}, u32[]{:S(2)}, u32[]{:S(2)}) collective-permute-start(f32[2,6,8,512]{3,2,1,0:T(8,128)S(1)} %carry.13), channel_id=1, source_target_pairs={{8,0},{9,1},{10,2},{11,3},{12,4},{13,5},{14,6},{15,7}} | collective-permute-start | bytes 589832 | tf_op jit(solution)/shard_map/ppermute | solution.py:329
  59.0 29.1 %collective-permute-start.21 = (f32[2,6,8,512]{3,2,1,0:T(8,128)S(1)}, f32[2,6,8,512]{3,2,1,0:T(8,128)S(1)}, u32[]{:S(2)}, u32[]{:S(2)}) collective-permute-start(f32[2,6,8,512]{3,2,1,0:T(8,128)S(1)} %carry.14), channel_id=1, source_target_pairs={{16,8},{17,9},{18,10},{19,11},{20,12},{21,13},{22,14},{23,15}} | collective-permute-start | bytes 589832 | tf_op jit(solution)/shard_map/ppermute | solution.py:329
  59.7 32.2 %collective-permute-start.16 = (f32[2,6,8,512]{3,2,1,0:T(8,128)S(1)}, f32[2,6,8,512]{3,2,1,0:T(8,128)S(1)}, u32[]{:S(2)}, u32[]{:S(2)}) collective-permute-start(f32[2,6,8,512]{3,2,1,0:T(8,128)S(1)} %carry.9), channel_id=1, source_target_pairs={{8,0},{9,1},{10,2},{11,3},{12,4},{13,5},{14,6},{15,7}} | collective-permute-start | bytes 589832 | tf_op jit(solution)/shard_map/ppermute | solution.py:329
  61.0 31.1 %collective-permute-start.15 = (f32[2,6,8,512]{3,2,1,0:T(8,128)S(1)}, f32[2,6,8,512]{3,2,1,0:T(8,128)S(1)}, u32[]{:S(2)}, u32[]{:S(2)}) collective-permute-start(f32[2,6,8,512]{3,2,1,0:T(8,128)S(1)} %carry.10), channel_id=1, source_target_pairs={{16,8},{17,9},{18,10},{19,11},{20,12},{21,13},{22,14},{23,15}} | collective-permute-start | bytes 589832 | tf_op jit(solution)/shard_map/ppermute | solution.py:329
  88.1 8.6 %collective-permute-start.23 = (f32[2,6,8,512]{3,2,1,0:T(8,128)S(1)}, f32[2,6,8,512]{3,2,1,0:T(8,128)S(1)}, u32[]{:S(2)}, u32[]{:S(2)}) collective-permute-start(f32[2,6,8,512]{3,2,1,0:T(8,128)S(1)} %carry.15), channel_id=1, source_target_pairs={{8,0},{9,1},{10,2},{11,3},{12,4},{13,5},{14,6},{15,7}} | collective-permute-start | bytes 589832 | tf_op jit(solution)/shard_map/ppermute | solution.py:329
  92.2 7.6 %collective-permute-start.17 = (f32[2,6,8,512]{3,2,1,0:T(8,128)S(1)}, f32[2,6,8,512]{3,2,1,0:T(8,128)S(1)}, u32[]{:S(2)}, u32[]{:S(2)}) collective-permute-start(f32[2,6,8,512]{3,2,1,0:T(8,128)S(1)} %carry.11), channel_id=1, source_target_pairs={{8,0},{9,1},{10,2},{11,3},{12,4},{13,5},{14,6},{15,7}} | collective-permute-start | bytes 589832 | tf_op jit(solution)/shard_map/ppermute | solution.py:329
  101.8 14.6 %all-to-all-start.1 = ((f32[8,5,8,512]{3,2,1,0:T(8,128)}), f32[8,5,8,512]{3,2,1,0:T(8,128)S(1)}, u32[]{:S(2)}, u32[]{:S(2)}) async-start(f32[8,5,8,512]{3,2,1,0:T(8,128)} %stencil.1), calls=%async_computation.1 | async-start | bytes 1310720 | tf_op jit(solution)/shard_map/all_to_all | solution.py:428
  105.4 1.1 copy-start.3

commit v9 on v8

--- a/solution.py
+++ b/solution.py
@@ -394,6 +394,9 @@
         arrived = [descend(b, 0)]
         for hop in range(1, groups - 1):
             incoming = arrived[-1]
+            if place > 0:
+                ahead = events[sequence[place - 1]]
+                incoming = lax.optimization_barrier((incoming, ahead[hop - 1]))[0]
             if place >= WAVE:
                 ahead = events[sequence[place - WAVE]]
                 incoming = lax.optimization_barrier((incoming, ahead[hop]))[0]
@@ -407,6 +410,9 @@
             )(incoming, excess, b, matrices)
             events[c].append(outgoing)
             arrived.append(descend(outgoing, hop))
+        if place > 0:
+            ahead = cots[sequence[place - 1]]
+            arrived[-1] = lax.optimization_barrier((arrived[-1], ahead))[0]
         cots[c] = pl.pallas_call(
             functools.partial(cotangent_kernel, planes),
             out_shape=shape(steps, 3 * planes, SUB, span),

time: 118 us -> 119 us (level)
  no operation moved by 1% of the time
where the time goes in v9:
time: 119 us; the launch traced here: 118 us
  waiting for transfers between devices  45 us (38%)
  starting transfers between devices  38.5 us (32%)
  blocking collectives  16.1 us (14%)
  Pallas kernels  12.5 us (11%)
  local copies, waits for them, and re-layouts  3.89 us (3%)
    ppermute x12, waiting for transfers between devices, descend(): return lax.ppermute(x, 'plane', [(groups - 1 - hop, groups - 2 - hop)])  35.2 us
    ppermute x12, starting transfers between devices, climb(): lax.ppermute(x, 'plane', [(i, i + 1) for i in range(hop, groups - 1)])  24.4 us
    all_to_all x1, blocking collectives, on_device(): lax.all_to_all(packed, 'slab', split_axis=0, concat_axis=0, tiled=True)  16.1 us
    ppermute x12, starting transfers between devices, descend(): return lax.ppermute(x, 'plane', [(groups - 1 - hop, groups - 2 - hop)])  10.6 us
    all_to_all x1, waiting for transfers between devices, on_device(): lax.all_to_all(partial, 'slab', split_axis=0, concat_axis=0, tiled=True)  6.68 us
    pallas_call x4, Pallas kernels, on_device(): pl.pallas_call(functools.partial(forward_kernel, groups, planes, c, lengt...  5.63 us
    unnamed x11, local copies, waits for them, and re-layouts  3.89 us
    all_to_all x1, starting transfers between devices, on_device(): lax.all_to_all(partial, 'slab', split_axis=0, concat_axis=0, tiled=True)  3.54 us
  transfers between devices with their start and end apart: 25, of which 8 were waited for; matrix products, arithmetic and copies ran while one was open for 1% of the time, Pallas kernels for 7%

profile of v9, /device:TPU:0, one launch (start us, length us, event | category | flops | bytes accessed | tf_op | source)
XLA Modules:
  0.0 118.0 jit_solution(10407661349887913244)
XLA Ops:
  0.7 0.8 pad_maximum_fusion.coef_ref
  1.5 1.0 copy-done.4
  2.5 0.7 pack.1
  3.2 16.1 %all_to_all.10 = f32[8,4,5,8,128]{4,3,2,1,0:T(8,128)S(1)} all-to-all(f32[8,4,5,8,128]{4,3,2,1,0:T(8,128)S(1)} %get-tuple-element.47), channel_id=1, replica_groups=mesh['plane'=4,'slab'=8] {'slab'}, dimensions={0} | all-to-all | bytes 1310720 | tf_op jit(solution)/shard_map/all_to_all | solution.py:340
  19.3 0.7 split.1
  20.0 3.5 %collective-permute-start = (f32[9,5,8,128]{3,2,1,0:T(8,128)S(1)}, f32[9,5,8,128]{3,2,1,0:T(8,128)S(1)}, u32[]{:S(2)}, u32[]{:S(2)}) collective-permute-start(f32[9,5,8,128]{3,2,1,0:T(8,128)S(1)} %get-tuple-element.48.refs_3_), channel_id=1, source_target_pairs={{0,8},{8,16},{16,24},{1,9},{9,17},{17,25},{2,10},{10,18},{18,26},{... | collective-permute-start | bytes 552968 | tf_op jit(solution)/shard_map/ppermute | solution.py:326
  23.5 3.5 %collective-permute-start.9 = (f32[8,5,8,128]{3,2,1,0:T(8,128)S(1)}, f32[8,5,8,128]{3,2,1,0:T(8,128)S(1)}, u32[]{:S(2)}, u32[]{:S(2)}) collective-permute-start(f32[8,5,8,128]{3,2,1,0:T(8,128)S(1)} %get-tuple-element.58.refs_3_), channel_id=1, source_target_pairs={{0,8},{8,16},{16,24},{1,9},{9,17},{17,25},{2,10},{10,18},{18,26},{... | collective-permute-start | bytes 491528 | tf_op jit(solution)/shard_map/ppermute | solution.py:326
  27.0 3.5 %collective-permute-start.6 = (f32[8,5,8,128]{3,2,1,0:T(8,128)S(1)}, f32[8,5,8,128]{3,2,1,0:T(8,128)S(1)}, u32[]{:S(2)}, u32[]{:S(2)}) collective-permute-start(f32[8,5,8,128]{3,2,1,0:T(8,128)S(1)} %get-tuple-element.56.refs_3_), channel_id=1, source_target_pairs={{0,8},{8,16},{16,24},{1,9},{9,17},{17,25},{2,10},{10,18},{18,26},{... | collective-permute-start | bytes 491528 | tf_op jit(solution)/shard_map/ppermute | solution.py:326
  30.5 0.7 collective-permute-start.1
  31.2 0.4 collective-permute-done.9.refs_2_
  31.6 0.7 collective-permute-start.10
  32.3 1.9 %collective-permute-done.6.refs_2_ = f32[8,5,8,128]{3,2,1,0:T(8,128)S(1)} collective-permute-done((f32[8,5,8,128]{3,2,1,0:T(8,128)S(1)}, f32[8,5,8,128]{3,2,1,0:T(8,128)S(1)}, u32[]{:S(2)}, u32[]{:S(2)}) %collective-permute-start.6) | collective-permute-done | bytes 163872 | tf_op jit(solution)/shard_map/ppermute | solution.py:326
  34.2 0.7 collective-permute-start.7
  34.8 8.6 %collective-permute-start.3 = (f32[8,5,8,128]{3,2,1,0:T(8,128)S(1)}, f32[8,5,8,128]{3,2,1,0:T(8,128)S(1)}, u32[]{:S(2)}, u32[]{:S(2)}) collective-permute-start(f32[8,5,8,128]{3,2,1,0:T(8,128)S(1)} %get-tuple-element.52.refs_3_), channel_id=1, source_target_pairs={{0,8},{8,16},{16,24},{1,9},{9,17},{17,25},{2,10},{10,18},{18,26},{... | collective-permute-start | bytes 491528 | tf_op jit(solution)/shard_map/ppermute | solution.py:326
  43.4 0.7 collective-permute-start.2
  44.1 0.7 collective-permute-start.11
  44.8 0.7 collective-permute-start.8
  45.5 0.7 collective-permute-done.3.refs_2_
  46.2 0.7 collective-permute-start.4
  47.1 1.4 %forward.7 = (f32[2,25,8,512]{3,2,1,0:T(8,128)S(1)}, f32[2,15,8,512]{3,2,1,0:T(8,128)S(1)}, f32[2,20,8,512]{3,2,1,0:T(8,128)S(1)}, f32[2,15,8,512]{3,2,1,0:T(8,128)S(1)}, f32[2,6,8,512]{3,2,1,0:T(8,128)S(1)}) custom-call(f32[8,5,8,128]{3,2,1,0:T(8,128)S(1)} %collective-permute-done.11.refs_0_, f32[8,5,8,128]{3,2,1,0:T(8,128)S(1)} %collective-permute-done.10.refs_1_, ...), custom_call_target="tpu_custom_call" | custom-call | tf_op jit(solution)/shard_map/forward/pallas_call | solution.py:375
  48.5 0.7 collective-permute-start.14
  49.2 1.4 %forward.6 = (f32[2,25,8,512]{3,2,1,0:T(8,128)S(1)}, f32[2,15,8,512]{3,2,1,0:T(8,128)S(1)}, f32[2,20,8,512]{3,2,1,0:T(8,128)S(1)}, f32[2,15,8,512]{3,2,1,0:T(8,128)S(1)}, f32[2,6,8,512]{3,2,1,0:T(8,128)S(1)}) custom-call(f32[8,5,8,128]{3,2,1,0:T(8,128)S(1)} %collective-permute-done.8.refs_0_, f32[8,5,8,128]{3,2,1,0:T(8,128)S(1)} %collective-permute-done.7.refs_1_, ...), custom_call_target="tpu_custom_call" | custom-call | tf_op jit(solution)/shard_map/forward/pallas_call | solution.py:375
  50.6 0.7 collective-permute-start.13
  51.3 0.7 collective-permute-start.5
  52.0 1.4 %forward.4 = (f32[2,25,8,512]{3,2,1,0:T(8,128)S(1)}, f32[2,15,8,512]{3,2,1,0:T(8,128)S(1)}, f32[2,20,8,512]{3,2,1,0:T(8,128)S(1)}, f32[2,15,8,512]{3,2,1,0:T(8,128)S(1)}, f32[2,6,8,512]{3,2,1,0:T(8,128)S(1)}) custom-call(f32[9,5,8,128]{3,2,1,0:T(8,128)S(1)} %collective-permute-done.2.refs_0_, f32[9,5,8,128]{3,2,1,0:T(8,128)S(1)} %collective-permute-done.1.refs_1_, ...), custom_call_target="tpu_custom_call" | custom-call | tf_op jit(solution)/shard_map/forward/pallas_call | solution.py:375
  53.4 0.7 collective-permute-start.12
  54.1 0.7 collective-permute-start.15
  54.8 1.4 %forward.5 = (f32[2,25,8,512]{3,2,1,0:T(8,128)S(1)}, f32[2,15,8,512]{3,2,1,0:T(8,128)S(1)}, f32[2,20,8,512]{3,2,1,0:T(8,128)S(1)}, f32[2,15,8,512]{3,2,1,0:T(8,128)S(1)}, f32[2,6,8,512]{3,2,1,0:T(8,128)S(1)}) custom-call(f32[8,5,8,128]{3,2,1,0:T(8,128)S(1)} %collective-permute-done.5.refs_0_, f32[8,5,8,128]{3,2,1,0:T(8,128)S(1)} %collective-permute-done.4.refs_1_, ...), custom_call_target="tpu_custom_call" | custom-call | tf_op jit(solution)/shard_map/forward/pallas_call | solution.py:375
  56.2 0.7 collective-permute-start.21
  56.9 0.7 collective-permute-start.17
  57.7 1.3 %collective-permute-start.18 = (f32[2,6,8,512]{3,2,1,0:T(8,128)S(1)}, f32[2,6,8,512]{3,2,1,0:T(8,128)S(1)}, u32[]{:S(2)}, u32[]{:S(2)}) collective-permute-start(f32[2,6,8,512]{3,2,1,0:T(8,128)S(1)} %carry.10), channel_id=1, source_target_pairs={{8,0},{9,1},{10,2},{11,3},{12,4},{13,5},{14,6},{15,7}} | collective-permute-start | bytes 589832 | tf_op jit(solution)/shard_map/ppermute | solution.py:329
  59.0 0.7 collective-permute-start.16
  59.8 0.7 collective-permute-start.22
  60.4 1.3 %collective-permute-start.20 = (f32[2,6,8,512]{3,2,1,0:T(8,128)S(1)}, f32[2,6,8,512]{3,2,1,0:T(8,128)S(1)}, u32[]{:S(2)}, u32[]{:S(2)}) collective-permute-start(f32[2,6,8,512]{3,2,1,0:T(8,128)S(1)} %carry.12), channel_id=1, source_target_pairs={{8,0},{9,1},{10,2},{11,3},{12,4},{13,5},{14,6},{15,7}} | collective-permute-start | bytes 589832 | tf_op jit(solution)/shard_map/ppermute | solution.py:329
  61.7 23.7 %collective-permute-done.18.refs_2_ = f32[2,6,8,512]{3,2,1,0:T(8,128)S(1)} collective-permute-done((f32[2,6,8,512]{3,2,1,0:T(8,128)S(1)}, f32[2,6,8,512]{3,2,1,0:T(8,128)S(1)}, u32[]{:S(2)}, u32[]{:S(2)}) %collective-permute-start.18) | collective-permute-done | bytes 196640 | tf_op jit(solution)/shard_map/ppermute | solution.py:329
  85.7 1.3 %collective-permute-start.19 = (f32[2,6,8,512]{3,2,1,0:T(8,128)S(1)}, f32[2,6,8,512]{3,2,1,0:T(8,128)S(1)}, u32[]{:S(2)}, u32[]{:S(2)}) collective-permute-start(f32[2,6,8,512]{3,2,1,0:T(8,128)S(1)} %carry.13), channel_id=1, source_target_pairs={{8,0},{9,1},{10,2},{11,3},{12,4},{13,5},{14,6},{15,7}} | collective-permute-start | bytes 589832 | tf_op jit(solution)/shard_map/ppermute | solution.py:329
  87.0 5.5 %collective-permute-done.20.refs_2_ = f32[2,6,8,512]{3,2,1,0:T(8,128)S(1)} collective-permute-done((f32[2,6,8,512]{3,2,1,0:T(8,128)S(1)}, f32[2,6,8,512]{3,2,1,0:T(8,128)S(1)}, u32[]{:S(2)}, u32[]{:S(2)}) %collective-permute-start.20) | collective-permute-done | bytes 196640 | tf_op jit(solution)/shard_map/ppermute | solution.py:329
  92.5 0.3 cotangent.5.refs_2_
  92.8 1.3 %collective-permute-start.23 = (f32[2,6,8,512]{3,2,1,0:T(8,128)S(1)}, f32[2,6,8,512]{3,2,1,0:T(8,128)S(1)}, u32[]{:S(2)}, u32[]{:S(2)}) collective-permute-start(f32[2,6,8,512]{3,2,1,0:T(8,128)S(1)} %carry.15), channel_id=1, source_target_pairs={{8,0},{9,1},{10,2},{11,3},{12,4},{13,5},{14,6},{15,7}} | collective-permute-start | bytes 589832 | tf_op jit(solution)/shard_map/ppermute | solution.py:329
  94.1 2.3 %collective-permute-done.19.refs_2_ = f32[2,6,8,512]{3,2,1,0:T(8,128)S(1)} collective-permute-done((f32[2,6,8,512]{3,2,1,0:T(8,128)S(1)}, f32[2,6,8,512]{3,2,1,0:T(8,128)S(1)}, u32[]{:S(2)}, u32[]{:S(2)}) %collective-permute-start.19) | collective-permute-done | bytes 196640 | tf_op jit(solution)/shard_map/ppermute | solution.py:329
  96.7 3.7 %collective-permute-done.23.refs_2_ = f32[2,6,8,512]{3,2,1,0:T(8,128)S(1)} collective-permute-done((f32[2,6,8,512]{3,2,1,0:T(8,128)S(1)}, f32[2,6,8,512]{3,2,1,0:T(8,128)S(1)}, u32[]{:S(2)}, u32[]{:S(2)}) %collective-permute-start.23) | collective-permute-done | bytes 196640 | tf_op jit(solution)/shard_map/ppermute | solution.py:329
  100.6 1.8 %stencil.1 = f32[8,5,8,512]{3,2,1,0:T(8,128)} custom-call(f32[2,15,8,512]{3,2,1,0:T(8,128)S(1)} %cotangent.6.refs_0_, f32[2,15,8,512]{3,2,1,0:T(8,128)S(1)} %cotangent.7.refs_1_, f32[2,15,8,512]{3,2,1,0:T(8,128)S(1)} %cotangent.5.refs_2_, f32[2,15,8,512]{3,2,1,0:T(8,128)S(1)} %cotangent.4.refs_3_), custom_call_target="tpu_custom_call" | custom-call | tf_op jit(solution)/shard_map/stencil/pallas_call | solution.py:426
  102.4 3.5 %all-to-all-start.1 = ((f32[8,5,8,512]{3,2,1,0:T(8,128)}), f32[8,5,8,512]{3,2,1,0:T(8,128)S(1)}, u32[]{:S(2)}, u32[]{:S(2)}) async-start(f32[8,5,8,512]{3,2,1,0:T(8,128)} %stencil.1), calls=%async_computation.1 | async-start | bytes 1310720 | tf_op jit(solution)/shard_map/all_to_all | solution.py:434
  106.0 1.1 copy-done.3
  107.1 1.6 %assemble.1 = (f32[5,2,6,4096]{3,2,1,0:T(8,128)S(1)}, f32[5,3,6,4096]{3,2,1,0:T(8,128)}) custom-call(f32[2,25,8,512]{3,2,1,0:T(8,128)S(1)} %get-tuple-element.51.refs_0_, f32[2,25,8,512]{3,2,1,0:T(8,128)S(1)} %copy-done.3, f32[2,25,8,512]{3,2,1,0:T(8,128)S(1)} %get-tuple-element.57.refs_2_, f32[2,25,8,512]{3,2,1,0:T(8,128)S(1)} %get-tuple-element.59.refs_3_), custom_call_target="tpu_custom_call" | custom-call | tf_op jit(solution)/shard_map/assemble/pallas_call | solution.py:435
  108.7 1.7 %copy.8 = f32[5,2,6,4096]{3,1,2,0:T(2,128)} copy(f32[5,2,6,4096]{3,2,1,0:T(8,128)S(1)} %get-tuple-element.91) | data formatting | bytes 1966080
  110.4 6.7 %all-to-all-done.1.in_ref = f32[8,5,8,512]{3,2,1,0:T(8,128)S(1)} async-done(((f32[8,5,8,512]{3,2,1,0:T(8,128)}), f32[8,5,8,512]{3,2,1,0:T(8,128)S(1)}, u32[]{:S(2)}, u32[]{:S(2)}) %all-to-all-start.1) | async-done | bytes 655392 | tf_op jit(solution)/shard_map/all_to_all | solution.py:434
  117.0 0.9 combine.1
  (37 shorter events, 1.1 us)
Async XLA Ops:
  0.6 46.4 %copy-start = (f32[5,3,6,4096]{3,2,1,0:T(8,128)S(1)}, f32[5,3,6,4096]{3,2,1,0:T(8,128)}, u32[]{:S(2)}) copy-start(f32[5,3,6,4096]{3,2,1,0:T(8,128)} %refs_6_.7) | copy-start | bytes 4423684
  0.6 46.4 %copy-start.1 = (f32[5,6,4096]{2,1,0:T(8,128)S(1)}, f32[5,6,4096]{2,1,0:T(8,128)}, u32[]{:S(2)}) copy-start(f32[5,6,4096]{2,1,0:T(8,128)} %refs_7_.7) | copy-start | bytes 1474564
  1.5 1.0 copy-start.4
  20.0 10.5 %collective-permute-start = (f32[9,5,8,128]{3,2,1,0:T(8,128)S(1)}, f32[9,5,8,128]{3,2,1,0:T(8,128)S(1)}, u32[]{:S(2)}, u32[]{:S(2)}) collective-permute-start(f32[9,5,8,128]{3,2,1,0:T(8,128)S(1)} %get-tuple-element.48.refs_3_), channel_id=1, source_target_pairs={{0,8},{8,16},{16,24},{1,9},{9,17},{17,25},{2,10},{10,18},{18,26},{... | collective-permute-start | bytes 552968 | tf_op jit(solution)/shard_map/ppermute | solution.py:326
  23.5 8.1 %collective-permute-start.9 = (f32[8,5,8,128]{3,2,1,0:T(8,128)S(1)}, f32[8,5,8,128]{3,2,1,0:T(8,128)S(1)}, u32[]{:S(2)}, u32[]{:S(2)}) collective-permute-start(f32[8,5,8,128]{3,2,1,0:T(8,128)S(1)} %get-tuple-element.58.refs_3_), channel_id=1, source_target_pairs={{0,8},{8,16},{16,24},{1,9},{9,17},{17,25},{2,10},{10,18},{18,26},{... | collective-permute-start | bytes 491528 | tf_op jit(solution)/shard_map/ppermute | solution.py:326
  27.0 7.2 %collective-permute-start.6 = (f32[8,5,8,128]{3,2,1,0:T(8,128)S(1)}, f32[8,5,8,128]{3,2,1,0:T(8,128)S(1)}, u32[]{:S(2)}, u32[]{:S(2)}) collective-permute-start(f32[8,5,8,128]{3,2,1,0:T(8,128)S(1)} %get-tuple-element.56.refs_3_), channel_id=1, source_target_pairs={{0,8},{8,16},{16,24},{1,9},{9,17},{17,25},{2,10},{10,18},{18,26},{... | collective-permute-start | bytes 491528 | tf_op jit(solution)/shard_map/ppermute | solution.py:326
  30.5 13.0 %collective-permute-start.1 = (f32[9,5,8,128]{3,2,1,0:T(8,128)S(1)}, f32[9,5,8,128]{3,2,1,0:T(8,128)S(1)}, u32[]{:S(2)}, u32[]{:S(2)}) collective-permute-start(f32[9,5,8,128]{3,2,1,0:T(8,128)S(1)} %collective-permute-done.refs_2_), channel_id=1, source_target_pairs={{8,16},{16,24},{9,17},{17,25},{10,18},{18,26},{11,19},{19,27},{12,... | collective-permute-start | bytes 552968 | tf_op jit(solution)/shard_map/ppermute | solution.py:326
  31.6 12.5 %collective-permute-start.10 = (f32[8,5,8,128]{3,2,1,0:T(8,128)S(1)}, f32[8,5,8,128]{3,2,1,0:T(8,128)S(1)}, u32[]{:S(2)}, u32[]{:S(2)}) collective-permute-start(f32[8,5,8,128]{3,2,1,0:T(8,128)S(1)} %collective-permute-done.9.refs_2_), channel_id=1, source_target_pairs={{8,16},{16,24},{9,17},{17,25},{10,18},{18,26},{11,19},{19,27},{12,... | collective-permute-start | bytes 491528 | tf_op jit(solution)/shard_map/ppermute | solution.py:326
  34.2 10.6 %collective-permute-start.7 = (f32[8,5,8,128]{3,2,1,0:T(8,128)S(1)}, f32[8,5,8,128]{3,2,1,0:T(8,128)S(1)}, u32[]{:S(2)}, u32[]{:S(2)}) collective-permute-start(f32[8,5,8,128]{3,2,1,0:T(8,128)S(1)} %collective-permute-done.6.refs_2_), channel_id=1, source_target_pairs={{8,16},{16,24},{9,17},{17,25},{10,18},{18,26},{11,19},{19,27},{12,... | collective-permute-start | bytes 491528 | tf_op jit(solution)/shard_map/ppermute | solution.py:326
  34.8 11.4 %collective-permute-start.3 = (f32[8,5,8,128]{3,2,1,0:T(8,128)S(1)}, f32[8,5,8,128]{3,2,1,0:T(8,128)S(1)}, u32[]{:S(2)}, u32[]{:S(2)}) collective-permute-start(f32[8,5,8,128]{3,2,1,0:T(8,128)S(1)} %get-tuple-element.52.refs_3_), channel_id=1, source_target_pairs={{0,8},{8,16},{16,24},{1,9},{9,17},{17,25},{2,10},{10,18},{18,26},{... | collective-permute-start | bytes 491528 | tf_op jit(solution)/shard_map/ppermute | solution.py:326
  43.4 3.5 %collective-permute-start.2 = (f32[9,5,8,128]{3,2,1,0:T(8,128)S(1)}, f32[9,5,8,128]{3,2,1,0:T(8,128)S(1)}, u32[]{:S(2)}, u32[]{:S(2)}) collective-permute-start(f32[9,5,8,128]{3,2,1,0:T(8,128)S(1)} %collective-permute-done.1.refs_1_), channel_id=1, source_target_pairs={{16,24},{17,25},{18,26},{19,27},{20,28},{21,29},{22,30},{23,31}} | collective-permute-start | bytes 552968 | tf_op jit(solution)/shard_map/ppermute | solution.py:326
  44.1 2.9 %collective-permute-start.11 = (f32[8,5,8,128]{3,2,1,0:T(8,128)S(1)}, f32[8,5,8,128]{3,2,1,0:T(8,128)S(1)}, u32[]{:S(2)}, u32[]{:S(2)}) collective-permute-start(f32[8,5,8,128]{3,2,1,0:T(8,128)S(1)} %collective-permute-done.10.refs_1_), channel_id=1, source_target_pairs={{16,24},{17,25},{18,26},{19,27},{20,28},{21,29},{22,30},{23,31}} | collective-permute-start | bytes 491528 | tf_op jit(solution)/shard_map/ppermute | solution.py:326
  44.8 4.4 %collective-permute-start.8 = (f32[8,5,8,128]{3,2,1,0:T(8,128)S(1)}, f32[8,5,8,128]{3,2,1,0:T(8,128)S(1)}, u32[]{:S(2)}, u32[]{:S(2)}) collective-permute-start(f32[8,5,8,128]{3,2,1,0:T(8,128)S(1)} %collective-permute-done.7.refs_1_), channel_id=1, source_target_pairs={{16,24},{17,25},{18,26},{19,27},{20,28},{21,29},{22,30},{23,31}} | collective-permute-start | bytes 491528 | tf_op jit(solution)/shard_map/ppermute | solution.py:326
  46.2 5.1 %collective-permute-start.4 = (f32[8,5,8,128]{3,2,1,0:T(8,128)S(1)}, f32[8,5,8,128]{3,2,1,0:T(8,128)S(1)}, u32[]{:S(2)}, u32[]{:S(2)}) collective-permute-start(f32[8,5,8,128]{3,2,1,0:T(8,128)S(1)} %collective-permute-done.3.refs_2_), channel_id=1, source_target_pairs={{8,16},{16,24},{9,17},{17,25},{10,18},{18,26},{11,19},{19,27},{12,... | collective-permute-start | bytes 491528 | tf_op jit(solution)/shard_map/ppermute | solution.py:326
  48.5 5.6 %collective-permute-start.14 = (f32[2,6,8,512]{3,2,1,0:T(8,128)S(1)}, f32[2,6,8,512]{3,2,1,0:T(8,128)S(1)}, u32[]{:S(2)}, u32[]{:S(2)}) collective-permute-start(f32[2,6,8,512]{3,2,1,0:T(8,128)S(1)} %get-tuple-element.67.b_ref), channel_id=1, source_target_pairs={{24,16},{25,17},{26,18},{27,19},{28,20},{29,21},{30,22},{31,23}} | collective-permute-start | bytes 589832 | tf_op jit(solution)/shard_map/ppermute | solution.py:329
  50.6 6.3 %collective-permute-start.13 = (f32[2,6,8,512]{3,2,1,0:T(8,128)S(1)}, f32[2,6,8,512]{3,2,1,0:T(8,128)S(1)}, u32[]{:S(2)}, u32[]{:S(2)}) collective-permute-start(f32[2,6,8,512]{3,2,1,0:T(8,128)S(1)} %get-tuple-element.66.b_ref), channel_id=1, source_target_pairs={{24,16},{25,17},{26,18},{27,19},{28,20},{29,21},{30,22},{31,23}} | collective-permute-start | bytes 589832 | tf_op jit(solution)/shard_map/ppermute | solution.py:329
  51.3 3.5 %collective-permute-start.5 = (f32[8,5,8,128]{3,2,1,0:T(8,128)S(1)}, f32[8,5,8,128]{3,2,1,0:T(8,128)S(1)}, u32[]{:S(2)}, u32[]{:S(2)}) collective-permute-start(f32[8,5,8,128]{3,2,1,0:T(8,128)S(1)} %collective-permute-done.4.refs_1_), channel_id=1, source_target_pairs={{16,24},{17,25},{18,26},{19,27},{20,28},{21,29},{22,30},{23,31}} | collective-permute-start | bytes 491528 | tf_op jit(solution)/shard_map/ppermute | solution.py:326
  53.4 4.2 %collective-permute-start.12 = (f32[2,6,8,512]{3,2,1,0:T(8,128)S(1)}, f32[2,6,8,512]{3,2,1,0:T(8,128)S(1)}, u32[]{:S(2)}, u32[]{:S(2)}) collective-permute-start(f32[2,6,8,512]{3,2,1,0:T(8,128)S(1)} %get-tuple-element.53.b_ref), channel_id=1, source_target_pairs={{24,16},{25,17},{26,18},{27,19},{28,20},{29,21},{30,22},{31,23}} | collective-permute-start | bytes 589832 | tf_op jit(solution)/shard_map/ppermute | solution.py:329
  54.1 3.5 %collective-permute-start.15 = (f32[2,6,8,512]{3,2,1,0:T(8,128)S(1)}, f32[2,6,8,512]{3,2,1,0:T(8,128)S(1)}, u32[]{:S(2)}, u32[]{:S(2)}) collective-permute-start(f32[2,6,8,512]{3,2,1,0:T(8,128)S(1)} %carry.8), channel_id=1, source_target_pairs={{16,8},{17,9},{18,10},{19,11},{20,12},{21,13},{22,14},{23,15}} | collective-permute-start | bytes 589832 | tf_op jit(solution)/shard_map/ppermute | solution.py:329
  56.2 3.5 %copy-start.2 = (f32[2,25,8,512]{3,2,1,0:T(8,128)}, f32[2,25,8,512]{3,2,1,0:T(8,128)S(1)}, u32[]{:S(2)}) copy-start(f32[2,25,8,512]{3,2,1,0:T(8,128)S(1)} %get-tuple-element.55.refs_1_) | copy-start | bytes 2457604
  56.2 3.5 %collective-permute-start.21 = (f32[2,6,8,512]{3,2,1,0:T(8,128)S(1)}, f32[2,6,8,512]{3,2,1,0:T(8,128)S(1)}, u32[]{:S(2)}, u32[]{:S(2)}) collective-permute-start(f32[2,6,8,512]{3,2,1,0:T(8,128)S(1)} %get-tuple-element.85.b_ref), channel_id=1, source_target_pairs={{24,16},{25,17},{26,18},{27,19},{28,20},{29,21},{30,22},{31,23}} | collective-permute-start | bytes 589832 | tf_op jit(solution)/shard_map/ppermute | solution.py:329
  56.9 2.7 %collective-permute-start.17 = (f32[2,6,8,512]{3,2,1,0:T(8,128)S(1)}, f32[2,6,8,512]{3,2,1,0:T(8,128)S(1)}, u32[]{:S(2)}, u32[]{:S(2)}) collective-permute-start(f32[2,6,8,512]{3,2,1,0:T(8,128)S(1)} %carry.9), channel_id=1, source_target_pairs={{16,8},{17,9},{18,10},{19,11},{20,12},{21,13},{22,14},{23,15}} | collective-permute-start | bytes 589832 | tf_op jit(solution)/shard_map/ppermute | solution.py:329
  57.7 27.8 %collective-permute-start.18 = (f32[2,6,8,512]{3,2,1,0:T(8,128)S(1)}, f32[2,6,8,512]{3,2,1,0:T(8,128)S(1)}, u32[]{:S(2)}, u32[]{:S(2)}) collective-permute-start(f32[2,6,8,512]{3,2,1,0:T(8,128)S(1)} %carry.10), channel_id=1, source_target_pairs={{8,0},{9,1},{10,2},{11,3},{12,4},{13,5},{14,6},{15,7}} | collective-permute-start | bytes 589832 | tf_op jit(solution)/shard_map/ppermute | solution.py:329
  59.0 2.7 %collective-permute-start.16 = (f32[2,6,8,512]{3,2,1,0:T(8,128)S(1)}, f32[2,6,8,512]{3,2,1,0:T(8,128)S(1)}, u32[]{:S(2)}, u32[]{:S(2)}) collective-permute-start(f32[2,6,8,512]{3,2,1,0:T(8,128)S(1)} %carry.11), channel_id=1, source_target_pairs={{16,8},{17,9},{18,10},{19,11},{20,12},{21,13},{22,14},{23,15}} | collective-permute-start | bytes 589832 | tf_op jit(solution)/shard_map/ppermute | solution.py:329
  59.8 27.3 %collective-permute-start.22 = (f32[2,6,8,512]{3,2,1,0:T(8,128)S(1)}, f32[2,6,8,512]{3,2,1,0:T(8,128)S(1)}, u32[]{:S(2)}, u32[]{:S(2)}) collective-permute-start(f32[2,6,8,512]{3,2,1,0:T(8,128)S(1)} %carry.14), channel_id=1, source_target_pairs={{16,8},{17,9},{18,10},{19,11},{20,12},{21,13},{22,14},{23,15}} | collective-permute-start | bytes 589832 | tf_op jit(solution)/shard_map/ppermute | solution.py:329
  60.4 32.1 %collective-permute-start.20 = (f32[2,6,8,512]{3,2,1,0:T(8,128)S(1)}, f32[2,6,8,512]{3,2,1,0:T(8,128)S(1)}, u32[]{:S(2)}, u32[]{:S(2)}) collective-permute-start(f32[2,6,8,512]{3,2,1,0:T(8,128)S(1)} %carry.12), channel_id=1, source_target_pairs={{8,0},{9,1},{10,2},{11,3},{12,4},{13,5},{14,6},{15,7}} | collective-permute-start | bytes 589832 | tf_op jit(solution)/shard_map/ppermute | solution.py:329
  85.7 10.7 %collective-permute-start.19 = (f32[2,6,8,512]{3,2,1,0:T(8,128)S(1)}, f32[2,6,8,512]{3,2,1,0:T(8,128)S(1)}, u32[]{:S(2)}, u32[]{:S(2)}) collective-permute-start(f32[2,6,8,512]{3,2,1,0:T(8,128)S(1)} %carry.13), channel_id=1, source_target_pairs={{8,0},{9,1},{10,2},{11,3},{12,4},{13,5},{14,6},{15,7}} | collective-permute-start | bytes 589832 | tf_op jit(solution)/shard_map/ppermute | solution.py:329
  92.8 7.6 %collective-permute-start.23 = (f32[2,6,8,512]{3,2,1,0:T(8,128)S(1)}, f32[2,6,8,512]{3,2,1,0:T(8,128)S(1)}, u32[]{:S(2)}, u32[]{:S(2)}) collective-permute-start(f32[2,6,8,512]{3,2,1,0:T(8,128)S(1)} %carry.15), channel_id=1, source_target_pairs={{8,0},{9,1},{10,2},{11,3},{12,4},{13,5},{14,6},{15,7}} | collective-permute-start | bytes 589832 | tf_op jit(solution)/shard_map/ppermute | solution.py:329
  102.4 14.6 %all-to-all-start.1 = ((f32[8,5,8,512]{3,2,1,0:T(8,128)}), f32[8,5,8,512]{3,2,1,0:T(8,128)S(1)}, u32[]{:S(2)}, u32[]{:S(2)}) async-start(f32[8,5,8,512]{3,2,1,0:T(8,128)} %stencil.1), calls=%async_computation.1 | async-start | bytes 1310720 | tf_op jit(solution)/shard_map/all_to_all | solution.py:434
  106.0 1.1 copy-start.3

commit v10 on v8

--- a/solution.py
+++ b/solution.py
@@ -13,7 +13,6 @@
 F32 = jnp.float32
 VMEM_LIMIT = 16 * 1024 * 1024
 CHUNKS = 4
-WAVE = 2
 SPAN = 4
 MIX_LANE = 64
 
@@ -366,12 +365,9 @@
         name="edges",
     )(*strips[0])
 
-    sequence = list(reversed(range(2, CHUNKS))) + [0, 1]
     maps = [None] * CHUNKS
     work = [None] * CHUNKS
-    for c in sequence:
-        if c == 1:
-            strips[1][0] = lax.optimization_barrier((strips[1][0], work[0][-1]))[0]
+    for c in range(CHUNKS):
         maps[c], *work[c] = pl.pallas_call(
             functools.partial(forward_kernel, groups, planes, c, length),
             out_shape=(
@@ -387,16 +383,11 @@
             name="forward",
         )(*strips[c], beside, excess, observed, noise_weight)
 
-    events = [[] for c in range(CHUNKS)]
     cots = [None] * CHUNKS
-    for place, c in enumerate(sequence):
+    for c in range(CHUNKS):
         matrices, states, sources, b = work[c]
         arrived = [descend(b, 0)]
         for hop in range(1, groups - 1):
-            incoming = arrived[-1]
-            if place >= WAVE:
-                ahead = events[sequence[place - WAVE]]
-                incoming = lax.optimization_barrier((incoming, ahead[hop]))[0]
             outgoing = pl.pallas_call(
                 functools.partial(carry_kernel, planes, groups - 1 - hop),
                 out_shape=shape(steps, R, SUB, span),
@@ -404,8 +395,7 @@
                 out_specs=WHOLE,
                 compiler_params=params(),
                 name="carry",
-            )(incoming, excess, b, matrices)
-            events[c].append(outgoing)
+            )(arrived[-1], excess, b, matrices)
             arrived.append(descend(outgoing, hop))
         cots[c] = pl.pallas_call(
             functools.partial(cotangent_kernel, planes),
@@ -415,7 +405,6 @@
             compiler_params=params(),
             name="cotangent",
         )(excess, weights, sources, matrices, states, *arrived)
-        events[c].append(cots[c])
 
     partial = pl.pallas_call(
         functools.partial(stencil_kernel, planes),

time: 118 us -> 118 us (level)
  starting transfers between devices: 38.5 us -> 31.8 us
  waiting for transfers between devices: 44.4 us -> 50.5 us
    ppermute x12, starting transfers between devices: 24.4 us -> 17.7 us  [climb(): lax.ppermute(x, 'plane', [(i, i + 1) for i in range(hop, groups - 1)])]
    ppermute x12, waiting for transfers between devices: 34.6 us -> 40.5 us  [descend(): return lax.ppermute(x, 'plane', [(groups - 1 - hop, groups - 2 - hop)])]
  transfers between devices with their start and end apart: 25 -> 25, of which waited for: 8 -> 7; matrix products, arithmetic and copies ran while one was open for 1% -> 1% of each run, Pallas kernels for 7% -> 7%
where the time goes in v10:
time: 118 us; the launch traced here: 117 us
  waiting for transfers between devices  50.5 us (43%)
  starting transfers between devices  31.8 us (27%)
  blocking collectives  16.1 us (14%)
  Pallas kernels  12.6 us (11%)
  local copies, waits for them, and re-layouts  3.89 us (3%)
    ppermute x12, waiting for transfers between devices, descend(): return lax.ppermute(x, 'plane', [(groups - 1 - hop, groups - 2 - hop)])  40.5 us
    ppermute x12, starting transfers between devices, climb(): lax.ppermute(x, 'plane', [(i, i + 1) for i in range(hop, groups - 1)])  17.7 us
    all_to_all x1, blocking collectives, on_device(): lax.all_to_all(packed, 'slab', split_axis=0, concat_axis=0, tiled=True)  16.1 us
    ppermute x12, starting transfers between devices, descend(): return lax.ppermute(x, 'plane', [(groups - 1 - hop, groups - 2 - hop)])  10.6 us
    all_to_all x1, waiting for transfers between devices, on_device(): lax.all_to_all(partial, 'slab', split_axis=0, concat_axis=0, tiled=True)  6.68 us
    pallas_call x4, Pallas kernels, on_device(): pl.pallas_call(functools.partial(forward_kernel, groups, planes, c, lengt...  5.62 us
    unnamed x11, local copies, waits for them, and re-layouts  3.89 us
    all_to_all x1, starting transfers between devices, on_device(): lax.all_to_all(partial, 'slab', split_axis=0, concat_axis=0, tiled=True)  3.54 us
  transfers between devices with their start and end apart: 25, of which 7 were waited for; matrix products, arithmetic and copies ran while one was open for 1% of the time, Pallas kernels for 7%

profile of v10, /device:TPU:0, one launch (start us, length us, event | category | flops | bytes accessed | tf_op | source)
XLA Modules:
  0.0 116.9 jit_solution(10732925881130861085)
XLA Ops:
  0.7 0.8 pad_maximum_fusion.coef_ref
  1.5 1.0 copy-done.4
  2.5 0.7 pack.1
  3.2 16.1 %all_to_all.10 = f32[8,4,5,8,128]{4,3,2,1,0:T(8,128)S(1)} all-to-all(f32[8,4,5,8,128]{4,3,2,1,0:T(8,128)S(1)} %get-tuple-element.33), channel_id=1, replica_groups=mesh['plane'=4,'slab'=8] {'slab'}, dimensions={0} | all-to-all | bytes 1310720 | tf_op jit(solution)/shard_map/all_to_all | solution.py:339
  19.3 0.7 split.1
  20.0 3.5 %collective-permute-start = (f32[9,5,8,128]{3,2,1,0:T(8,128)S(1)}, f32[9,5,8,128]{3,2,1,0:T(8,128)S(1)}, u32[]{:S(2)}, u32[]{:S(2)}) collective-permute-start(f32[9,5,8,128]{3,2,1,0:T(8,128)S(1)} %get-tuple-element.34.refs_3_), channel_id=1, source_target_pairs={{0,8},{8,16},{16,24},{1,9},{9,17},{17,25},{2,10},{10,18},{18,26},{... | collective-permute-start | bytes 552968 | tf_op jit(solution)/shard_map/ppermute | solution.py:325
  23.5 3.5 %collective-permute-start.9 = (f32[8,5,8,128]{3,2,1,0:T(8,128)S(1)}, f32[8,5,8,128]{3,2,1,0:T(8,128)S(1)}, u32[]{:S(2)}, u32[]{:S(2)}) collective-permute-start(f32[8,5,8,128]{3,2,1,0:T(8,128)S(1)} %get-tuple-element.42.refs_3_), channel_id=1, source_target_pairs={{0,8},{8,16},{16,24},{1,9},{9,17},{17,25},{2,10},{10,18},{18,26},{... | collective-permute-start | bytes 491528 | tf_op jit(solution)/shard_map/ppermute | solution.py:325
  27.0 3.5 %collective-permute-start.6 = (f32[8,5,8,128]{3,2,1,0:T(8,128)S(1)}, f32[8,5,8,128]{3,2,1,0:T(8,128)S(1)}, u32[]{:S(2)}, u32[]{:S(2)}) collective-permute-start(f32[8,5,8,128]{3,2,1,0:T(8,128)S(1)} %get-tuple-element.40.refs_3_), channel_id=1, source_target_pairs={{0,8},{8,16},{16,24},{1,9},{9,17},{17,25},{2,10},{10,18},{18,26},{... | collective-permute-start | bytes 491528 | tf_op jit(solution)/shard_map/ppermute | solution.py:325
  30.5 1.9 %collective-permute-start.3 = (f32[8,5,8,128]{3,2,1,0:T(8,128)S(1)}, f32[8,5,8,128]{3,2,1,0:T(8,128)S(1)}, u32[]{:S(2)}, u32[]{:S(2)}) collective-permute-start(f32[8,5,8,128]{3,2,1,0:T(8,128)S(1)} %get-tuple-element.38.refs_3_), channel_id=1, source_target_pairs={{0,8},{8,16},{16,24},{1,9},{9,17},{17,25},{2,10},{10,18},{18,26},{... | collective-permute-start | bytes 491528 | tf_op jit(solution)/shard_map/ppermute | solution.py:325
  32.4 0.7 collective-permute-start.1
  33.1 0.7 collective-permute-start.10
  33.8 1.3 %collective-permute-done.6.refs_2_ = f32[8,5,8,128]{3,2,1,0:T(8,128)S(1)} collective-permute-done((f32[8,5,8,128]{3,2,1,0:T(8,128)S(1)}, f32[8,5,8,128]{3,2,1,0:T(8,128)S(1)}, u32[]{:S(2)}, u32[]{:S(2)}) %collective-permute-start.6) | collective-permute-done | bytes 163872 | tf_op jit(solution)/shard_map/ppermute | solution.py:325
  35.1 0.7 collective-permute-start.7
  35.8 1.9 %collective-permute-done.3.refs_2_ = f32[8,5,8,128]{3,2,1,0:T(8,128)S(1)} collective-permute-done((f32[8,5,8,128]{3,2,1,0:T(8,128)S(1)}, f32[8,5,8,128]{3,2,1,0:T(8,128)S(1)}, u32[]{:S(2)}, u32[]{:S(2)}) %collective-permute-start.3) | collective-permute-done | bytes 163872 | tf_op jit(solution)/shard_map/ppermute | solution.py:325
  37.7 0.7 collective-permute-start.4
  38.4 0.7 collective-permute-start.2
  39.1 0.7 collective-permute-start.11
  39.7 0.7 collective-permute-start.8
  40.4 0.7 collective-permute-start.5
  41.3 1.4 %forward.7 = (f32[2,25,8,512]{3,2,1,0:T(8,128)S(1)}, f32[2,15,8,512]{3,2,1,0:T(8,128)S(1)}, f32[2,20,8,512]{3,2,1,0:T(8,128)S(1)}, f32[2,15,8,512]{3,2,1,0:T(8,128)S(1)}, f32[2,6,8,512]{3,2,1,0:T(8,128)S(1)}) custom-call(f32[8,5,8,128]{3,2,1,0:T(8,128)S(1)} %collective-permute-done.11.refs_0_, f32[8,5,8,128]{3,2,1,0:T(8,128)S(1)} %collective-permute-done.10.refs_1_, ...), custom_call_target="tpu_custom_call" | custom-call | tf_op jit(solution)/shard_map/forward/pallas_call | solution.py:371
  42.7 0.7 collective-permute-start.21
  43.4 1.4 %forward.6 = (f32[2,25,8,512]{3,2,1,0:T(8,128)S(1)}, f32[2,15,8,512]{3,2,1,0:T(8,128)S(1)}, f32[2,20,8,512]{3,2,1,0:T(8,128)S(1)}, f32[2,15,8,512]{3,2,1,0:T(8,128)S(1)}, f32[2,6,8,512]{3,2,1,0:T(8,128)S(1)}) custom-call(f32[8,5,8,128]{3,2,1,0:T(8,128)S(1)} %collective-permute-done.8.refs_0_, f32[8,5,8,128]{3,2,1,0:T(8,128)S(1)} %collective-permute-done.7.refs_1_, ...), custom_call_target="tpu_custom_call" | custom-call | tf_op jit(solution)/shard_map/forward/pallas_call | solution.py:371
  44.8 0.7 collective-permute-start.18
  45.5 1.4 %forward.5 = (f32[2,25,8,512]{3,2,1,0:T(8,128)S(1)}, f32[2,15,8,512]{3,2,1,0:T(8,128)S(1)}, f32[2,20,8,512]{3,2,1,0:T(8,128)S(1)}, f32[2,15,8,512]{3,2,1,0:T(8,128)S(1)}, f32[2,6,8,512]{3,2,1,0:T(8,128)S(1)}) custom-call(f32[8,5,8,128]{3,2,1,0:T(8,128)S(1)} %collective-permute-done.5.refs_0_, f32[8,5,8,128]{3,2,1,0:T(8,128)S(1)} %collective-permute-done.4.refs_1_, ...), custom_call_target="tpu_custom_call" | custom-call | tf_op jit(solution)/shard_map/forward/pallas_call | solution.py:371
  46.9 0.7 collective-permute-start.15
  47.6 1.4 %forward.4 = (f32[2,25,8,512]{3,2,1,0:T(8,128)S(1)}, f32[2,15,8,512]{3,2,1,0:T(8,128)S(1)}, f32[2,20,8,512]{3,2,1,0:T(8,128)S(1)}, f32[2,15,8,512]{3,2,1,0:T(8,128)S(1)}, f32[2,6,8,512]{3,2,1,0:T(8,128)S(1)}) custom-call(f32[9,5,8,128]{3,2,1,0:T(8,128)S(1)} %collective-permute-done.2.refs_0_, f32[9,5,8,128]{3,2,1,0:T(8,128)S(1)} %collective-permute-done.1.refs_1_, ...), custom_call_target="tpu_custom_call" | custom-call | tf_op jit(solution)/shard_map/forward/pallas_call | solution.py:371
  49.0 0.7 collective-permute-start.12
  49.7 0.7 collective-permute-start.22
  50.5 0.7 collective-permute-start.19
  51.2 0.7 collective-permute-start.16
  51.9 0.7 collective-permute-start.13
  52.6 1.3 %collective-permute-start.23 = (f32[2,6,8,512]{3,2,1,0:T(8,128)S(1)}, f32[2,6,8,512]{3,2,1,0:T(8,128)S(1)}, u32[]{:S(2)}, u32[]{:S(2)}) collective-permute-start(f32[2,6,8,512]{3,2,1,0:T(8,128)S(1)} %carry.15), channel_id=1, source_target_pairs={{8,0},{9,1},{10,2},{11,3},{12,4},{13,5},{14,6},{15,7}} | collective-permute-start | bytes 589832 | tf_op jit(solution)/shard_map/ppermute | solution.py:328
  54.0 1.3 %collective-permute-start.20 = (f32[2,6,8,512]{3,2,1,0:T(8,128)S(1)}, f32[2,6,8,512]{3,2,1,0:T(8,128)S(1)}, u32[]{:S(2)}, u32[]{:S(2)}) collective-permute-start(f32[2,6,8,512]{3,2,1,0:T(8,128)S(1)} %carry.13), channel_id=1, source_target_pairs={{8,0},{9,1},{10,2},{11,3},{12,4},{13,5},{14,6},{15,7}} | collective-permute-start | bytes 589832 | tf_op jit(solution)/shard_map/ppermute | solution.py:328
  55.3 1.3 %collective-permute-start.17 = (f32[2,6,8,512]{3,2,1,0:T(8,128)S(1)}, f32[2,6,8,512]{3,2,1,0:T(8,128)S(1)}, u32[]{:S(2)}, u32[]{:S(2)}) collective-permute-start(f32[2,6,8,512]{3,2,1,0:T(8,128)S(1)} %carry.11), channel_id=1, source_target_pairs={{8,0},{9,1},{10,2},{11,3},{12,4},{13,5},{14,6},{15,7}} | collective-permute-start | bytes 589832 | tf_op jit(solution)/shard_map/ppermute | solution.py:328
  56.6 1.3 %collective-permute-start.14 = (f32[2,6,8,512]{3,2,1,0:T(8,128)S(1)}, f32[2,6,8,512]{3,2,1,0:T(8,128)S(1)}, u32[]{:S(2)}, u32[]{:S(2)}) collective-permute-start(f32[2,6,8,512]{3,2,1,0:T(8,128)S(1)} %carry.9), channel_id=1, source_target_pairs={{8,0},{9,1},{10,2},{11,3},{12,4},{13,5},{14,6},{15,7}} | collective-permute-start | bytes 589832 | tf_op jit(solution)/shard_map/ppermute | solution.py:328
  57.9 30.8 %collective-permute-done.23.refs_2_ = f32[2,6,8,512]{3,2,1,0:T(8,128)S(1)} collective-permute-done((f32[2,6,8,512]{3,2,1,0:T(8,128)S(1)}, f32[2,6,8,512]{3,2,1,0:T(8,128)S(1)}, u32[]{:S(2)}, u32[]{:S(2)}) %collective-permute-start.23) | collective-permute-done | bytes 196640 | tf_op jit(solution)/shard_map/ppermute | solution.py:328
  88.7 0.3 cotangent.7.refs_3_
  89.0 3.9 %collective-permute-done.20.refs_2_ = f32[2,6,8,512]{3,2,1,0:T(8,128)S(1)} collective-permute-done((f32[2,6,8,512]{3,2,1,0:T(8,128)S(1)}, f32[2,6,8,512]{3,2,1,0:T(8,128)S(1)}, u32[]{:S(2)}, u32[]{:S(2)}) %collective-permute-start.20) | collective-permute-done | bytes 196640 | tf_op jit(solution)/shard_map/ppermute | solution.py:328
  93.2 3.9 %collective-permute-done.17.refs_2_ = f32[2,6,8,512]{3,2,1,0:T(8,128)S(1)} collective-permute-done((f32[2,6,8,512]{3,2,1,0:T(8,128)S(1)}, f32[2,6,8,512]{3,2,1,0:T(8,128)S(1)}, u32[]{:S(2)}, u32[]{:S(2)}) %collective-permute-start.17) | collective-permute-done | bytes 196640 | tf_op jit(solution)/shard_map/ppermute | solution.py:328
  97.4 1.8 %collective-permute-done.14.refs_2_ = f32[2,6,8,512]{3,2,1,0:T(8,128)S(1)} collective-permute-done((f32[2,6,8,512]{3,2,1,0:T(8,128)S(1)}, f32[2,6,8,512]{3,2,1,0:T(8,128)S(1)}, u32[]{:S(2)}, u32[]{:S(2)}) %collective-permute-start.14) | collective-permute-done | bytes 196640 | tf_op jit(solution)/shard_map/ppermute | solution.py:328
  99.3 0.3 cotangent.4.refs_0_
  99.5 1.8 %stencil.1 = f32[8,5,8,512]{3,2,1,0:T(8,128)} custom-call(f32[2,15,8,512]{3,2,1,0:T(8,128)S(1)} %cotangent.4.refs_0_, f32[2,15,8,512]{3,2,1,0:T(8,128)S(1)} %cotangent.5.refs_1_, f32[2,15,8,512]{3,2,1,0:T(8,128)S(1)} %cotangent.6.refs_2_, f32[2,15,8,512]{3,2,1,0:T(8,128)S(1)} %cotangent.7.refs_3_), custom_call_target="tpu_custom_call" | custom-call | tf_op jit(solution)/shard_map/stencil/pallas_call | solution.py:409
  101.3 3.5 %all-to-all-start.1 = ((f32[8,5,8,512]{3,2,1,0:T(8,128)}), f32[8,5,8,512]{3,2,1,0:T(8,128)S(1)}, u32[]{:S(2)}, u32[]{:S(2)}) async-start(f32[8,5,8,512]{3,2,1,0:T(8,128)} %stencil.1), calls=%async_computation.1 | async-start | bytes 1310720 | tf_op jit(solution)/shard_map/all_to_all | solution.py:417
  104.9 1.1 copy-done.3
  106.0 1.6 %assemble.1 = (f32[5,2,6,4096]{3,2,1,0:T(8,128)S(1)}, f32[5,3,6,4096]{3,2,1,0:T(8,128)}) custom-call(f32[2,25,8,512]{3,2,1,0:T(8,128)S(1)} %copy-done.3, f32[2,25,8,512]{3,2,1,0:T(8,128)S(1)} %get-tuple-element.39.refs_1_, f32[2,25,8,512]{3,2,1,0:T(8,128)S(1)} %get-tuple-element.41.refs_2_, f32[2,25,8,512]{3,2,1,0:T(8,128)S(1)} %get-tuple-element.43.refs_3_), custom_call_target="tpu_custom_call" | custom-call | tf_op jit(solution)/shard_map/assemble/pallas_call | solution.py:418
  107.6 1.7 %copy.8 = f32[5,2,6,4096]{3,1,2,0:T(2,128)} copy(f32[5,2,6,4096]{3,2,1,0:T(8,128)S(1)} %get-tuple-element.63) | data formatting | bytes 1966080
  109.3 6.7 %all-to-all-done.1.in_ref = f32[8,5,8,512]{3,2,1,0:T(8,128)S(1)} async-done(((f32[8,5,8,512]{3,2,1,0:T(8,128)}), f32[8,5,8,512]{3,2,1,0:T(8,128)S(1)}, u32[]{:S(2)}, u32[]{:S(2)}) %all-to-all-start.1) | async-done | bytes 655392 | tf_op jit(solution)/shard_map/all_to_all | solution.py:417
  115.9 0.9 combine.1
  (37 shorter events, 0.9 us)
Async XLA Ops:
  0.6 40.6 %copy-start = (f32[5,3,6,4096]{3,2,1,0:T(8,128)S(1)}, f32[5,3,6,4096]{3,2,1,0:T(8,128)}, u32[]{:S(2)}) copy-start(f32[5,3,6,4096]{3,2,1,0:T(8,128)} %refs_6_.7) | copy-start | bytes 4423684
  0.6 40.6 %copy-start.1 = (f32[5,6,4096]{2,1,0:T(8,128)S(1)}, f32[5,6,4096]{2,1,0:T(8,128)}, u32[]{:S(2)}) copy-start(f32[5,6,4096]{2,1,0:T(8,128)} %refs_7_.7) | copy-start | bytes 1474564
  1.5 1.0 copy-start.4
  20.0 12.4 %collective-permute-start = (f32[9,5,8,128]{3,2,1,0:T(8,128)S(1)}, f32[9,5,8,128]{3,2,1,0:T(8,128)S(1)}, u32[]{:S(2)}, u32[]{:S(2)}) collective-permute-start(f32[9,5,8,128]{3,2,1,0:T(8,128)S(1)} %get-tuple-element.34.refs_3_), channel_id=1, source_target_pairs={{0,8},{8,16},{16,24},{1,9},{9,17},{17,25},{2,10},{10,18},{18,26},{... | collective-permute-start | bytes 552968 | tf_op jit(solution)/shard_map/ppermute | solution.py:325
  23.5 9.6 %collective-permute-start.9 = (f32[8,5,8,128]{3,2,1,0:T(8,128)S(1)}, f32[8,5,8,128]{3,2,1,0:T(8,128)S(1)}, u32[]{:S(2)}, u32[]{:S(2)}) collective-permute-start(f32[8,5,8,128]{3,2,1,0:T(8,128)S(1)} %get-tuple-element.42.refs_3_), channel_id=1, source_target_pairs={{0,8},{8,16},{16,24},{1,9},{9,17},{17,25},{2,10},{10,18},{18,26},{... | collective-permute-start | bytes 491528 | tf_op jit(solution)/shard_map/ppermute | solution.py:325
  27.0 8.1 %collective-permute-start.6 = (f32[8,5,8,128]{3,2,1,0:T(8,128)S(1)}, f32[8,5,8,128]{3,2,1,0:T(8,128)S(1)}, u32[]{:S(2)}, u32[]{:S(2)}) collective-permute-start(f32[8,5,8,128]{3,2,1,0:T(8,128)S(1)} %get-tuple-element.40.refs_3_), channel_id=1, source_target_pairs={{0,8},{8,16},{16,24},{1,9},{9,17},{17,25},{2,10},{10,18},{18,26},{... | collective-permute-start | bytes 491528 | tf_op jit(solution)/shard_map/ppermute | solution.py:325
  30.5 7.2 %collective-permute-start.3 = (f32[8,5,8,128]{3,2,1,0:T(8,128)S(1)}, f32[8,5,8,128]{3,2,1,0:T(8,128)S(1)}, u32[]{:S(2)}, u32[]{:S(2)}) collective-permute-start(f32[8,5,8,128]{3,2,1,0:T(8,128)S(1)} %get-tuple-element.38.refs_3_), channel_id=1, source_target_pairs={{0,8},{8,16},{16,24},{1,9},{9,17},{17,25},{2,10},{10,18},{18,26},{... | collective-permute-start | bytes 491528 | tf_op jit(solution)/shard_map/ppermute | solution.py:325
  32.4 6.0 %collective-permute-start.1 = (f32[9,5,8,128]{3,2,1,0:T(8,128)S(1)}, f32[9,5,8,128]{3,2,1,0:T(8,128)S(1)}, u32[]{:S(2)}, u32[]{:S(2)}) collective-permute-start(f32[9,5,8,128]{3,2,1,0:T(8,128)S(1)} %collective-permute-done.refs_2_), channel_id=1, source_target_pairs={{8,16},{16,24},{9,17},{17,25},{10,18},{18,26},{11,19},{19,27},{12,... | collective-permute-start | bytes 552968 | tf_op jit(solution)/shard_map/ppermute | solution.py:325
  33.1 6.0 %collective-permute-start.10 = (f32[8,5,8,128]{3,2,1,0:T(8,128)S(1)}, f32[8,5,8,128]{3,2,1,0:T(8,128)S(1)}, u32[]{:S(2)}, u32[]{:S(2)}) collective-permute-start(f32[8,5,8,128]{3,2,1,0:T(8,128)S(1)} %collective-permute-done.9.refs_2_), channel_id=1, source_target_pairs={{8,16},{16,24},{9,17},{17,25},{10,18},{18,26},{11,19},{19,27},{12,... | collective-permute-start | bytes 491528 | tf_op jit(solution)/shard_map/ppermute | solution.py:325
  35.1 4.6 %collective-permute-start.7 = (f32[8,5,8,128]{3,2,1,0:T(8,128)S(1)}, f32[8,5,8,128]{3,2,1,0:T(8,128)S(1)}, u32[]{:S(2)}, u32[]{:S(2)}) collective-permute-start(f32[8,5,8,128]{3,2,1,0:T(8,128)S(1)} %collective-permute-done.6.refs_2_), channel_id=1, source_target_pairs={{8,16},{16,24},{9,17},{17,25},{10,18},{18,26},{11,19},{19,27},{12,... | collective-permute-start | bytes 491528 | tf_op jit(solution)/shard_map/ppermute | solution.py:325
  37.7 2.7 %collective-permute-start.4 = (f32[8,5,8,128]{3,2,1,0:T(8,128)S(1)}, f32[8,5,8,128]{3,2,1,0:T(8,128)S(1)}, u32[]{:S(2)}, u32[]{:S(2)}) collective-permute-start(f32[8,5,8,128]{3,2,1,0:T(8,128)S(1)} %collective-permute-done.3.refs_2_), channel_id=1, source_target_pairs={{8,16},{16,24},{9,17},{17,25},{10,18},{18,26},{11,19},{19,27},{12,... | collective-permute-start | bytes 491528 | tf_op jit(solution)/shard_map/ppermute | solution.py:325
  38.4 2.8 %collective-permute-start.2 = (f32[9,5,8,128]{3,2,1,0:T(8,128)S(1)}, f32[9,5,8,128]{3,2,1,0:T(8,128)S(1)}, u32[]{:S(2)}, u32[]{:S(2)}) collective-permute-start(f32[9,5,8,128]{3,2,1,0:T(8,128)S(1)} %collective-permute-done.1.refs_1_), channel_id=1, source_target_pairs={{16,24},{17,25},{18,26},{19,27},{20,28},{21,29},{22,30},{23,31}} | collective-permute-start | bytes 552968 | tf_op jit(solution)/shard_map/ppermute | solution.py:325
  39.1 2.2 %collective-permute-start.11 = (f32[8,5,8,128]{3,2,1,0:T(8,128)S(1)}, f32[8,5,8,128]{3,2,1,0:T(8,128)S(1)}, u32[]{:S(2)}, u32[]{:S(2)}) collective-permute-start(f32[8,5,8,128]{3,2,1,0:T(8,128)S(1)} %collective-permute-done.10.refs_1_), channel_id=1, source_target_pairs={{16,24},{17,25},{18,26},{19,27},{20,28},{21,29},{22,30},{23,31}} | collective-permute-start | bytes 491528 | tf_op jit(solution)/shard_map/ppermute | solution.py:325
  39.7 3.6 %collective-permute-start.8 = (f32[8,5,8,128]{3,2,1,0:T(8,128)S(1)}, f32[8,5,8,128]{3,2,1,0:T(8,128)S(1)}, u32[]{:S(2)}, u32[]{:S(2)}) collective-permute-start(f32[8,5,8,128]{3,2,1,0:T(8,128)S(1)} %collective-permute-done.7.refs_1_), channel_id=1, source_target_pairs={{16,24},{17,25},{18,26},{19,27},{20,28},{21,29},{22,30},{23,31}} | collective-permute-start | bytes 491528 | tf_op jit(solution)/shard_map/ppermute | solution.py:325
  40.4 5.1 %collective-permute-start.5 = (f32[8,5,8,128]{3,2,1,0:T(8,128)S(1)}, f32[8,5,8,128]{3,2,1,0:T(8,128)S(1)}, u32[]{:S(2)}, u32[]{:S(2)}) collective-permute-start(f32[8,5,8,128]{3,2,1,0:T(8,128)S(1)} %collective-permute-done.4.refs_1_), channel_id=1, source_target_pairs={{16,24},{17,25},{18,26},{19,27},{20,28},{21,29},{22,30},{23,31}} | collective-permute-start | bytes 491528 | tf_op jit(solution)/shard_map/ppermute | solution.py:325
  42.7 7.0 %collective-permute-start.21 = (f32[2,6,8,512]{3,2,1,0:T(8,128)S(1)}, f32[2,6,8,512]{3,2,1,0:T(8,128)S(1)}, u32[]{:S(2)}, u32[]{:S(2)}) collective-permute-start(f32[2,6,8,512]{3,2,1,0:T(8,128)S(1)} %get-tuple-element.62.b_ref), channel_id=1, source_target_pairs={{24,16},{25,17},{26,18},{27,19},{28,20},{29,21},{30,22},{31,23}} | collective-permute-start | bytes 589832 | tf_op jit(solution)/shard_map/ppermute | solution.py:328
  44.8 5.6 %collective-permute-start.18 = (f32[2,6,8,512]{3,2,1,0:T(8,128)S(1)}, f32[2,6,8,512]{3,2,1,0:T(8,128)S(1)}, u32[]{:S(2)}, u32[]{:S(2)}) collective-permute-start(f32[2,6,8,512]{3,2,1,0:T(8,128)S(1)} %get-tuple-element.58.b_ref), channel_id=1, source_target_pairs={{24,16},{25,17},{26,18},{27,19},{28,20},{29,21},{30,22},{31,23}} | collective-permute-start | bytes 589832 | tf_op jit(solution)/shard_map/ppermute | solution.py:328
  46.9 4.2 %collective-permute-start.15 = (f32[2,6,8,512]{3,2,1,0:T(8,128)S(1)}, f32[2,6,8,512]{3,2,1,0:T(8,128)S(1)}, u32[]{:S(2)}, u32[]{:S(2)}) collective-permute-start(f32[2,6,8,512]{3,2,1,0:T(8,128)S(1)} %get-tuple-element.54.b_ref), channel_id=1, source_target_pairs={{24,16},{25,17},{26,18},{27,19},{28,20},{29,21},{30,22},{31,23}} | collective-permute-start | bytes 589832 | tf_op jit(solution)/shard_map/ppermute | solution.py:328
  49.0 2.9 %copy-start.2 = (f32[2,25,8,512]{3,2,1,0:T(8,128)}, f32[2,25,8,512]{3,2,1,0:T(8,128)S(1)}, u32[]{:S(2)}) copy-start(f32[2,25,8,512]{3,2,1,0:T(8,128)S(1)} %get-tuple-element.37.refs_0_) | copy-start | bytes 2457604
  49.0 2.8 %collective-permute-start.12 = (f32[2,6,8,512]{3,2,1,0:T(8,128)S(1)}, f32[2,6,8,512]{3,2,1,0:T(8,128)S(1)}, u32[]{:S(2)}, u32[]{:S(2)}) collective-permute-start(f32[2,6,8,512]{3,2,1,0:T(8,128)S(1)} %get-tuple-element.50.b_ref), channel_id=1, source_target_pairs={{24,16},{25,17},{26,18},{27,19},{28,20},{29,21},{30,22},{31,23}} | collective-permute-start | bytes 589832 | tf_op jit(solution)/shard_map/ppermute | solution.py:328
  49.7 2.8 %collective-permute-start.22 = (f32[2,6,8,512]{3,2,1,0:T(8,128)S(1)}, f32[2,6,8,512]{3,2,1,0:T(8,128)S(1)}, u32[]{:S(2)}, u32[]{:S(2)}) collective-permute-start(f32[2,6,8,512]{3,2,1,0:T(8,128)S(1)} %carry.14), channel_id=1, source_target_pairs={{16,8},{17,9},{18,10},{19,11},{20,12},{21,13},{22,14},{23,15}} | collective-permute-start | bytes 589832 | tf_op jit(solution)/shard_map/ppermute | solution.py:328
  50.5 3.5 %collective-permute-start.19 = (f32[2,6,8,512]{3,2,1,0:T(8,128)S(1)}, f32[2,6,8,512]{3,2,1,0:T(8,128)S(1)}, u32[]{:S(2)}, u32[]{:S(2)}) collective-permute-start(f32[2,6,8,512]{3,2,1,0:T(8,128)S(1)} %carry.12), channel_id=1, source_target_pairs={{16,8},{17,9},{18,10},{19,11},{20,12},{21,13},{22,14},{23,15}} | collective-permute-start | bytes 589832 | tf_op jit(solution)/shard_map/ppermute | solution.py:328
  51.2 4.1 %collective-permute-start.16 = (f32[2,6,8,512]{3,2,1,0:T(8,128)S(1)}, f32[2,6,8,512]{3,2,1,0:T(8,128)S(1)}, u32[]{:S(2)}, u32[]{:S(2)}) collective-permute-start(f32[2,6,8,512]{3,2,1,0:T(8,128)S(1)} %carry.10), channel_id=1, source_target_pairs={{16,8},{17,9},{18,10},{19,11},{20,12},{21,13},{22,14},{23,15}} | collective-permute-start | bytes 589832 | tf_op jit(solution)/shard_map/ppermute | solution.py:328
  51.9 4.7 %collective-permute-start.13 = (f32[2,6,8,512]{3,2,1,0:T(8,128)S(1)}, f32[2,6,8,512]{3,2,1,0:T(8,128)S(1)}, u32[]{:S(2)}, u32[]{:S(2)}) collective-permute-start(f32[2,6,8,512]{3,2,1,0:T(8,128)S(1)} %carry.8), channel_id=1, source_target_pairs={{16,8},{17,9},{18,10},{19,11},{20,12},{21,13},{22,14},{23,15}} | collective-permute-start | bytes 589832 | tf_op jit(solution)/shard_map/ppermute | solution.py:328
  52.6 36.1 %collective-permute-start.23 = (f32[2,6,8,512]{3,2,1,0:T(8,128)S(1)}, f32[2,6,8,512]{3,2,1,0:T(8,128)S(1)}, u32[]{:S(2)}, u32[]{:S(2)}) collective-permute-start(f32[2,6,8,512]{3,2,1,0:T(8,128)S(1)} %carry.15), channel_id=1, source_target_pairs={{8,0},{9,1},{10,2},{11,3},{12,4},{13,5},{14,6},{15,7}} | collective-permute-start | bytes 589832 | tf_op jit(solution)/shard_map/ppermute | solution.py:328
  54.0 39.0 %collective-permute-start.20 = (f32[2,6,8,512]{3,2,1,0:T(8,128)S(1)}, f32[2,6,8,512]{3,2,1,0:T(8,128)S(1)}, u32[]{:S(2)}, u32[]{:S(2)}) collective-permute-start(f32[2,6,8,512]{3,2,1,0:T(8,128)S(1)} %carry.13), channel_id=1, source_target_pairs={{8,0},{9,1},{10,2},{11,3},{12,4},{13,5},{14,6},{15,7}} | collective-permute-start | bytes 589832 | tf_op jit(solution)/shard_map/ppermute | solution.py:328
  55.3 41.9 %collective-permute-start.17 = (f32[2,6,8,512]{3,2,1,0:T(8,128)S(1)}, f32[2,6,8,512]{3,2,1,0:T(8,128)S(1)}, u32[]{:S(2)}, u32[]{:S(2)}) collective-permute-start(f32[2,6,8,512]{3,2,1,0:T(8,128)S(1)} %carry.11), channel_id=1, source_target_pairs={{8,0},{9,1},{10,2},{11,3},{12,4},{13,5},{14,6},{15,7}} | collective-permute-start | bytes 589832 | tf_op jit(solution)/shard_map/ppermute | solution.py:328
  56.6 42.6 %collective-permute-start.14 = (f32[2,6,8,512]{3,2,1,0:T(8,128)S(1)}, f32[2,6,8,512]{3,2,1,0:T(8,128)S(1)}, u32[]{:S(2)}, u32[]{:S(2)}) collective-permute-start(f32[2,6,8,512]{3,2,1,0:T(8,128)S(1)} %carry.9), channel_id=1, source_target_pairs={{8,0},{9,1},{10,2},{11,3},{12,4},{13,5},{14,6},{15,7}} | collective-permute-start | bytes 589832 | tf_op jit(solution)/shard_map/ppermute | solution.py:328
  101.3 14.6 %all-to-all-start.1 = ((f32[8,5,8,512]{3,2,1,0:T(8,128)}), f32[8,5,8,512]{3,2,1,0:T(8,128)S(1)}, u32[]{:S(2)}, u32[]{:S(2)}) async-start(f32[8,5,8,512]{3,2,1,0:T(8,128)} %stencil.1), calls=%async_computation.1 | async-start | bytes 1310720 | tf_op jit(solution)/shard_map/all_to_all | solution.py:417
  104.9 1.1 copy-start.3

commit v11 on v10

--- a/solution.py
+++ b/solution.py
@@ -368,6 +368,8 @@
     maps = [None] * CHUNKS
     work = [None] * CHUNKS
     for c in range(CHUNKS):
+        if c == CHUNKS - 1:
+            strips[c][0] = lax.optimization_barrier((strips[c][0], work[0][-1]))[0]
         maps[c], *work[c] = pl.pallas_call(
             functools.partial(forward_kernel, groups, planes, c, length),
             out_shape=(

time: 118 us -> 117 us (level)
  no operation moved by 1% of the time
where the time goes in v11:
time: 117 us; the launch traced here: 116 us
  waiting for transfers between devices  49.9 us (43%)
  starting transfers between devices  31.8 us (27%)
  blocking collectives  16.1 us (14%)
  Pallas kernels  12.5 us (11%)
  local copies, waits for them, and re-layouts  3.89 us (3%)
    ppermute x12, waiting for transfers between devices, descend(): return lax.ppermute(x, 'plane', [(groups - 1 - hop, groups - 2 - hop)])  40 us
    ppermute x12, starting transfers between devices, climb(): lax.ppermute(x, 'plane', [(i, i + 1) for i in range(hop, groups - 1)])  17.7 us
    all_to_all x1, blocking collectives, on_device(): lax.all_to_all(packed, 'slab', split_axis=0, concat_axis=0, tiled=True)  16.1 us
    ppermute x12, starting transfers between devices, descend(): return lax.ppermute(x, 'plane', [(groups - 1 - hop, groups - 2 - hop)])  10.6 us
    all_to_all x1, waiting for transfers between devices, on_device(): lax.all_to_all(partial, 'slab', split_axis=0, concat_axis=0, tiled=True)  6.68 us
    pallas_call x4, Pallas kernels, on_device(): pl.pallas_call(functools.partial(forward_kernel, groups, planes, c, lengt...  5.56 us
    unnamed x11, local copies, waits for them, and re-layouts  3.89 us
    all_to_all x1, starting transfers between devices, on_device(): lax.all_to_all(partial, 'slab', split_axis=0, concat_axis=0, tiled=True)  3.54 us
  transfers between devices with their start and end apart: 25, of which 7 were waited for; matrix products, arithmetic and copies ran while one was open for 1% of the time, Pallas kernels for 7%

profile of v11, /device:TPU:0, one launch (start us, length us, event | category | flops | bytes accessed | tf_op | source)
XLA Modules:
  0.0 116.2 jit_solution(15203956441672838508)
XLA Ops:
  0.7 0.8 pad_maximum_fusion.coef_ref
  1.5 1.0 copy-done.4
  2.5 0.7 pack.1
  3.2 16.1 %all_to_all.10 = f32[8,4,5,8,128]{4,3,2,1,0:T(8,128)S(1)} all-to-all(f32[8,4,5,8,128]{4,3,2,1,0:T(8,128)S(1)} %get-tuple-element.34), channel_id=1, replica_groups=mesh['plane'=4,'slab'=8] {'slab'}, dimensions={0} | all-to-all | bytes 1310720 | tf_op jit(solution)/shard_map/all_to_all | solution.py:339
  19.3 0.7 split.1
  20.0 3.5 %collective-permute-start = (f32[9,5,8,128]{3,2,1,0:T(8,128)S(1)}, f32[9,5,8,128]{3,2,1,0:T(8,128)S(1)}, u32[]{:S(2)}, u32[]{:S(2)}) collective-permute-start(f32[9,5,8,128]{3,2,1,0:T(8,128)S(1)} %get-tuple-element.35.refs_3_), channel_id=1, source_target_pairs={{0,8},{8,16},{16,24},{1,9},{9,17},{17,25},{2,10},{10,18},{18,26},{... | collective-permute-start | bytes 552968 | tf_op jit(solution)/shard_map/ppermute | solution.py:325
  23.5 3.5 %collective-permute-start.9 = (f32[8,5,8,128]{3,2,1,0:T(8,128)S(1)}, f32[8,5,8,128]{3,2,1,0:T(8,128)S(1)}, u32[]{:S(2)}, u32[]{:S(2)}) collective-permute-start(f32[8,5,8,128]{3,2,1,0:T(8,128)S(1)} %get-tuple-element.43.refs_3_), channel_id=1, source_target_pairs={{0,8},{8,16},{16,24},{1,9},{9,17},{17,25},{2,10},{10,18},{18,26},{... | collective-permute-start | bytes 491528 | tf_op jit(solution)/shard_map/ppermute | solution.py:325
  27.0 3.5 %collective-permute-start.6 = (f32[8,5,8,128]{3,2,1,0:T(8,128)S(1)}, f32[8,5,8,128]{3,2,1,0:T(8,128)S(1)}, u32[]{:S(2)}, u32[]{:S(2)}) collective-permute-start(f32[8,5,8,128]{3,2,1,0:T(8,128)S(1)} %get-tuple-element.41.refs_3_), channel_id=1, source_target_pairs={{0,8},{8,16},{16,24},{1,9},{9,17},{17,25},{2,10},{10,18},{18,26},{... | collective-permute-start | bytes 491528 | tf_op jit(solution)/shard_map/ppermute | solution.py:325
  30.5 1.9 %collective-permute-start.3 = (f32[8,5,8,128]{3,2,1,0:T(8,128)S(1)}, f32[8,5,8,128]{3,2,1,0:T(8,128)S(1)}, u32[]{:S(2)}, u32[]{:S(2)}) collective-permute-start(f32[8,5,8,128]{3,2,1,0:T(8,128)S(1)} %get-tuple-element.39.refs_3_), channel_id=1, source_target_pairs={{0,8},{8,16},{16,24},{1,9},{9,17},{17,25},{2,10},{10,18},{18,26},{... | collective-permute-start | bytes 491528 | tf_op jit(solution)/shard_map/ppermute | solution.py:325
  32.4 0.7 collective-permute-start.1
  33.1 0.7 collective-permute-start.10
  33.8 1.3 %collective-permute-done.6.refs_2_ = f32[8,5,8,128]{3,2,1,0:T(8,128)S(1)} collective-permute-done((f32[8,5,8,128]{3,2,1,0:T(8,128)S(1)}, f32[8,5,8,128]{3,2,1,0:T(8,128)S(1)}, u32[]{:S(2)}, u32[]{:S(2)}) %collective-permute-start.6) | collective-permute-done | bytes 163872 | tf_op jit(solution)/shard_map/ppermute | solution.py:325
  35.1 0.7 collective-permute-start.7
  35.8 1.9 %collective-permute-done.3.refs_2_ = f32[8,5,8,128]{3,2,1,0:T(8,128)S(1)} collective-permute-done((f32[8,5,8,128]{3,2,1,0:T(8,128)S(1)}, f32[8,5,8,128]{3,2,1,0:T(8,128)S(1)}, u32[]{:S(2)}, u32[]{:S(2)}) %collective-permute-start.3) | collective-permute-done | bytes 163872 | tf_op jit(solution)/shard_map/ppermute | solution.py:325
  37.7 0.7 collective-permute-start.4
  38.4 0.7 collective-permute-start.2
  39.1 0.7 collective-permute-start.11
  39.7 0.7 collective-permute-start.8
  40.4 0.7 collective-permute-start.5
  41.3 1.4 %forward.4 = (f32[2,25,8,512]{3,2,1,0:T(8,128)S(1)}, f32[2,15,8,512]{3,2,1,0:T(8,128)S(1)}, f32[2,20,8,512]{3,2,1,0:T(8,128)S(1)}, f32[2,15,8,512]{3,2,1,0:T(8,128)S(1)}, f32[2,6,8,512]{3,2,1,0:T(8,128)S(1)}) custom-call(f32[9,5,8,128]{3,2,1,0:T(8,128)S(1)} %collective-permute-done.2.refs_0_, f32[9,5,8,128]{3,2,1,0:T(8,128)S(1)} %collective-permute-done.1.refs_1_, ...), custom_call_target="tpu_custom_call" | custom-call | tf_op jit(solution)/shard_map/forward/pallas_call | solution.py:373
  42.7 1.4 %forward.7 = (f32[2,25,8,512]{3,2,1,0:T(8,128)S(1)}, f32[2,15,8,512]{3,2,1,0:T(8,128)S(1)}, f32[2,20,8,512]{3,2,1,0:T(8,128)S(1)}, f32[2,15,8,512]{3,2,1,0:T(8,128)S(1)}, f32[2,6,8,512]{3,2,1,0:T(8,128)S(1)}) custom-call(f32[8,5,8,128]{3,2,1,0:T(8,128)S(1)} %collective-permute-done.11.refs_0_, f32[8,5,8,128]{3,2,1,0:T(8,128)S(1)} %collective-permute-done.10.refs_1_, ...), custom_call_target="tpu_custom_call" | custom-call | tf_op jit(solution)/shard_map/forward/pallas_call | solution.py:373
  44.1 0.7 collective-permute-start.21
  44.8 1.4 %forward.6 = (f32[2,25,8,512]{3,2,1,0:T(8,128)S(1)}, f32[2,15,8,512]{3,2,1,0:T(8,128)S(1)}, f32[2,20,8,512]{3,2,1,0:T(8,128)S(1)}, f32[2,15,8,512]{3,2,1,0:T(8,128)S(1)}, f32[2,6,8,512]{3,2,1,0:T(8,128)S(1)}) custom-call(f32[8,5,8,128]{3,2,1,0:T(8,128)S(1)} %collective-permute-done.8.refs_0_, f32[8,5,8,128]{3,2,1,0:T(8,128)S(1)} %collective-permute-done.7.refs_1_, ...), custom_call_target="tpu_custom_call" | custom-call | tf_op jit(solution)/shard_map/forward/pallas_call | solution.py:373
  46.2 0.7 collective-permute-start.18
  46.9 1.4 %forward.5 = (f32[2,25,8,512]{3,2,1,0:T(8,128)S(1)}, f32[2,15,8,512]{3,2,1,0:T(8,128)S(1)}, f32[2,20,8,512]{3,2,1,0:T(8,128)S(1)}, f32[2,15,8,512]{3,2,1,0:T(8,128)S(1)}, f32[2,6,8,512]{3,2,1,0:T(8,128)S(1)}) custom-call(f32[8,5,8,128]{3,2,1,0:T(8,128)S(1)} %collective-permute-done.5.refs_0_, f32[8,5,8,128]{3,2,1,0:T(8,128)S(1)} %collective-permute-done.4.refs_1_, ...), custom_call_target="tpu_custom_call" | custom-call | tf_op jit(solution)/shard_map/forward/pallas_call | solution.py:373
  48.3 0.7 collective-permute-start.15
  49.0 0.7 collective-permute-start.12
  49.7 0.7 collective-permute-start.22
  50.4 0.7 collective-permute-start.19
  51.1 0.7 collective-permute-start.16
  51.8 0.7 collective-permute-start.13
  52.6 1.3 %collective-permute-start.23 = (f32[2,6,8,512]{3,2,1,0:T(8,128)S(1)}, f32[2,6,8,512]{3,2,1,0:T(8,128)S(1)}, u32[]{:S(2)}, u32[]{:S(2)}) collective-permute-start(f32[2,6,8,512]{3,2,1,0:T(8,128)S(1)} %carry.15), channel_id=1, source_target_pairs={{8,0},{9,1},{10,2},{11,3},{12,4},{13,5},{14,6},{15,7}} | collective-permute-start | bytes 589832 | tf_op jit(solution)/shard_map/ppermute | solution.py:328
  53.9 1.3 %collective-permute-start.20 = (f32[2,6,8,512]{3,2,1,0:T(8,128)S(1)}, f32[2,6,8,512]{3,2,1,0:T(8,128)S(1)}, u32[]{:S(2)}, u32[]{:S(2)}) collective-permute-start(f32[2,6,8,512]{3,2,1,0:T(8,128)S(1)} %carry.13), channel_id=1, source_target_pairs={{8,0},{9,1},{10,2},{11,3},{12,4},{13,5},{14,6},{15,7}} | collective-permute-start | bytes 589832 | tf_op jit(solution)/shard_map/ppermute | solution.py:328
  55.2 1.3 %collective-permute-start.17 = (f32[2,6,8,512]{3,2,1,0:T(8,128)S(1)}, f32[2,6,8,512]{3,2,1,0:T(8,128)S(1)}, u32[]{:S(2)}, u32[]{:S(2)}) collective-permute-start(f32[2,6,8,512]{3,2,1,0:T(8,128)S(1)} %carry.11), channel_id=1, source_target_pairs={{8,0},{9,1},{10,2},{11,3},{12,4},{13,5},{14,6},{15,7}} | collective-permute-start | bytes 589832 | tf_op jit(solution)/shard_map/ppermute | solution.py:328
  56.6 1.3 %collective-permute-start.14 = (f32[2,6,8,512]{3,2,1,0:T(8,128)S(1)}, f32[2,6,8,512]{3,2,1,0:T(8,128)S(1)}, u32[]{:S(2)}, u32[]{:S(2)}) collective-permute-start(f32[2,6,8,512]{3,2,1,0:T(8,128)S(1)} %carry.9), channel_id=1, source_target_pairs={{8,0},{9,1},{10,2},{11,3},{12,4},{13,5},{14,6},{15,7}} | collective-permute-start | bytes 589832 | tf_op jit(solution)/shard_map/ppermute | solution.py:328
  57.9 30.2 %collective-permute-done.23.refs_2_ = f32[2,6,8,512]{3,2,1,0:T(8,128)S(1)} collective-permute-done((f32[2,6,8,512]{3,2,1,0:T(8,128)S(1)}, f32[2,6,8,512]{3,2,1,0:T(8,128)S(1)}, u32[]{:S(2)}, u32[]{:S(2)}) %collective-permute-start.23) | collective-permute-done | bytes 196640 | tf_op jit(solution)/shard_map/ppermute | solution.py:328
  88.3 4.0 %collective-permute-done.20.refs_2_ = f32[2,6,8,512]{3,2,1,0:T(8,128)S(1)} collective-permute-done((f32[2,6,8,512]{3,2,1,0:T(8,128)S(1)}, f32[2,6,8,512]{3,2,1,0:T(8,128)S(1)}, u32[]{:S(2)}, u32[]{:S(2)}) %collective-permute-start.20) | collective-permute-done | bytes 196640 | tf_op jit(solution)/shard_map/ppermute | solution.py:328
  92.5 4.0 %collective-permute-done.17.refs_2_ = f32[2,6,8,512]{3,2,1,0:T(8,128)S(1)} collective-permute-done((f32[2,6,8,512]{3,2,1,0:T(8,128)S(1)}, f32[2,6,8,512]{3,2,1,0:T(8,128)S(1)}, u32[]{:S(2)}, u32[]{:S(2)}) %collective-permute-start.17) | collective-permute-done | bytes 196640 | tf_op jit(solution)/shard_map/ppermute | solution.py:328
  96.5 0.3 cotangent.5.refs_1_
  96.8 1.8 %collective-permute-done.14.refs_2_ = f32[2,6,8,512]{3,2,1,0:T(8,128)S(1)} collective-permute-done((f32[2,6,8,512]{3,2,1,0:T(8,128)S(1)}, f32[2,6,8,512]{3,2,1,0:T(8,128)S(1)}, u32[]{:S(2)}, u32[]{:S(2)}) %collective-permute-start.14) | collective-permute-done | bytes 196640 | tf_op jit(solution)/shard_map/ppermute | solution.py:328
  98.6 0.3 cotangent.4.refs_0_
  98.9 1.8 %stencil.1 = f32[8,5,8,512]{3,2,1,0:T(8,128)} custom-call(f32[2,15,8,512]{3,2,1,0:T(8,128)S(1)} %cotangent.4.refs_0_, f32[2,15,8,512]{3,2,1,0:T(8,128)S(1)} %cotangent.5.refs_1_, f32[2,15,8,512]{3,2,1,0:T(8,128)S(1)} %cotangent.6.refs_2_, f32[2,15,8,512]{3,2,1,0:T(8,128)S(1)} %cotangent.7.refs_3_), custom_call_target="tpu_custom_call" | custom-call | tf_op jit(solution)/shard_map/stencil/pallas_call | solution.py:411
  100.6 3.5 %all-to-all-start.1 = ((f32[8,5,8,512]{3,2,1,0:T(8,128)}), f32[8,5,8,512]{3,2,1,0:T(8,128)S(1)}, u32[]{:S(2)}, u32[]{:S(2)}) async-start(f32[8,5,8,512]{3,2,1,0:T(8,128)} %stencil.1), calls=%async_computation.1 | async-start | bytes 1310720 | tf_op jit(solution)/shard_map/all_to_all | solution.py:419
  104.2 1.1 copy-done.3
  105.3 1.6 %assemble.1 = (f32[5,2,6,4096]{3,2,1,0:T(8,128)S(1)}, f32[5,3,6,4096]{3,2,1,0:T(8,128)}) custom-call(f32[2,25,8,512]{3,2,1,0:T(8,128)S(1)} %get-tuple-element.38.refs_0_, f32[2,25,8,512]{3,2,1,0:T(8,128)S(1)} %copy-done.3, f32[2,25,8,512]{3,2,1,0:T(8,128)S(1)} %get-tuple-element.42.refs_2_, f32[2,25,8,512]{3,2,1,0:T(8,128)S(1)} %get-tuple-element.46.refs_3_), custom_call_target="tpu_custom_call" | custom-call | tf_op jit(solution)/shard_map/assemble/pallas_call | solution.py:420
  106.9 1.7 %copy.8 = f32[5,2,6,4096]{3,1,2,0:T(2,128)} copy(f32[5,2,6,4096]{3,2,1,0:T(8,128)S(1)} %get-tuple-element.65) | data formatting | bytes 1966080
  108.6 6.7 %all-to-all-done.1.in_ref = f32[8,5,8,512]{3,2,1,0:T(8,128)S(1)} async-done(((f32[8,5,8,512]{3,2,1,0:T(8,128)}), f32[8,5,8,512]{3,2,1,0:T(8,128)S(1)}, u32[]{:S(2)}, u32[]{:S(2)}) %all-to-all-start.1) | async-done | bytes 655392 | tf_op jit(solution)/shard_map/all_to_all | solution.py:419
  115.3 0.9 combine.1
  (37 shorter events, 0.8 us)
Async XLA Ops:
  0.6 40.6 %copy-start = (f32[5,3,6,4096]{3,2,1,0:T(8,128)S(1)}, f32[5,3,6,4096]{3,2,1,0:T(8,128)}, u32[]{:S(2)}) copy-start(f32[5,3,6,4096]{3,2,1,0:T(8,128)} %refs_6_.7) | copy-start | bytes 4423684
  0.6 40.6 %copy-start.1 = (f32[5,6,4096]{2,1,0:T(8,128)S(1)}, f32[5,6,4096]{2,1,0:T(8,128)}, u32[]{:S(2)}) copy-start(f32[5,6,4096]{2,1,0:T(8,128)} %refs_7_.7) | copy-start | bytes 1474564
  1.5 1.0 copy-start.4
  20.0 12.4 %collective-permute-start = (f32[9,5,8,128]{3,2,1,0:T(8,128)S(1)}, f32[9,5,8,128]{3,2,1,0:T(8,128)S(1)}, u32[]{:S(2)}, u32[]{:S(2)}) collective-permute-start(f32[9,5,8,128]{3,2,1,0:T(8,128)S(1)} %get-tuple-element.35.refs_3_), channel_id=1, source_target_pairs={{0,8},{8,16},{16,24},{1,9},{9,17},{17,25},{2,10},{10,18},{18,26},{... | collective-permute-start | bytes 552968 | tf_op jit(solution)/shard_map/ppermute | solution.py:325
  23.5 9.6 %collective-permute-start.9 = (f32[8,5,8,128]{3,2,1,0:T(8,128)S(1)}, f32[8,5,8,128]{3,2,1,0:T(8,128)S(1)}, u32[]{:S(2)}, u32[]{:S(2)}) collective-permute-start(f32[8,5,8,128]{3,2,1,0:T(8,128)S(1)} %get-tuple-element.43.refs_3_), channel_id=1, source_target_pairs={{0,8},{8,16},{16,24},{1,9},{9,17},{17,25},{2,10},{10,18},{18,26},{... | collective-permute-start | bytes 491528 | tf_op jit(solution)/shard_map/ppermute | solution.py:325
  27.0 8.1 %collective-permute-start.6 = (f32[8,5,8,128]{3,2,1,0:T(8,128)S(1)}, f32[8,5,8,128]{3,2,1,0:T(8,128)S(1)}, u32[]{:S(2)}, u32[]{:S(2)}) collective-permute-start(f32[8,5,8,128]{3,2,1,0:T(8,128)S(1)} %get-tuple-element.41.refs_3_), channel_id=1, source_target_pairs={{0,8},{8,16},{16,24},{1,9},{9,17},{17,25},{2,10},{10,18},{18,26},{... | collective-permute-start | bytes 491528 | tf_op jit(solution)/shard_map/ppermute | solution.py:325
  30.5 7.2 %collective-permute-start.3 = (f32[8,5,8,128]{3,2,1,0:T(8,128)S(1)}, f32[8,5,8,128]{3,2,1,0:T(8,128)S(1)}, u32[]{:S(2)}, u32[]{:S(2)}) collective-permute-start(f32[8,5,8,128]{3,2,1,0:T(8,128)S(1)} %get-tuple-element.39.refs_3_), channel_id=1, source_target_pairs={{0,8},{8,16},{16,24},{1,9},{9,17},{17,25},{2,10},{10,18},{18,26},{... | collective-permute-start | bytes 491528 | tf_op jit(solution)/shard_map/ppermute | solution.py:325
  32.4 6.0 %collective-permute-start.1 = (f32[9,5,8,128]{3,2,1,0:T(8,128)S(1)}, f32[9,5,8,128]{3,2,1,0:T(8,128)S(1)}, u32[]{:S(2)}, u32[]{:S(2)}) collective-permute-start(f32[9,5,8,128]{3,2,1,0:T(8,128)S(1)} %collective-permute-done.refs_2_), channel_id=1, source_target_pairs={{8,16},{16,24},{9,17},{17,25},{10,18},{18,26},{11,19},{19,27},{12,... | collective-permute-start | bytes 552968 | tf_op jit(solution)/shard_map/ppermute | solution.py:325
  33.1 6.0 %collective-permute-start.10 = (f32[8,5,8,128]{3,2,1,0:T(8,128)S(1)}, f32[8,5,8,128]{3,2,1,0:T(8,128)S(1)}, u32[]{:S(2)}, u32[]{:S(2)}) collective-permute-start(f32[8,5,8,128]{3,2,1,0:T(8,128)S(1)} %collective-permute-done.9.refs_2_), channel_id=1, source_target_pairs={{8,16},{16,24},{9,17},{17,25},{10,18},{18,26},{11,19},{19,27},{12,... | collective-permute-start | bytes 491528 | tf_op jit(solution)/shard_map/ppermute | solution.py:325
  35.1 4.6 %collective-permute-start.7 = (f32[8,5,8,128]{3,2,1,0:T(8,128)S(1)}, f32[8,5,8,128]{3,2,1,0:T(8,128)S(1)}, u32[]{:S(2)}, u32[]{:S(2)}) collective-permute-start(f32[8,5,8,128]{3,2,1,0:T(8,128)S(1)} %collective-permute-done.6.refs_2_), channel_id=1, source_target_pairs={{8,16},{16,24},{9,17},{17,25},{10,18},{18,26},{11,19},{19,27},{12,... | collective-permute-start | bytes 491528 | tf_op jit(solution)/shard_map/ppermute | solution.py:325
  37.7 2.7 %collective-permute-start.4 = (f32[8,5,8,128]{3,2,1,0:T(8,128)S(1)}, f32[8,5,8,128]{3,2,1,0:T(8,128)S(1)}, u32[]{:S(2)}, u32[]{:S(2)}) collective-permute-start(f32[8,5,8,128]{3,2,1,0:T(8,128)S(1)} %collective-permute-done.3.refs_2_), channel_id=1, source_target_pairs={{8,16},{16,24},{9,17},{17,25},{10,18},{18,26},{11,19},{19,27},{12,... | collective-permute-start | bytes 491528 | tf_op jit(solution)/shard_map/ppermute | solution.py:325
  38.4 2.8 %collective-permute-start.2 = (f32[9,5,8,128]{3,2,1,0:T(8,128)S(1)}, f32[9,5,8,128]{3,2,1,0:T(8,128)S(1)}, u32[]{:S(2)}, u32[]{:S(2)}) collective-permute-start(f32[9,5,8,128]{3,2,1,0:T(8,128)S(1)} %collective-permute-done.1.refs_1_), channel_id=1, source_target_pairs={{16,24},{17,25},{18,26},{19,27},{20,28},{21,29},{22,30},{23,31}} | collective-permute-start | bytes 552968 | tf_op jit(solution)/shard_map/ppermute | solution.py:325
  39.1 3.6 %collective-permute-start.11 = (f32[8,5,8,128]{3,2,1,0:T(8,128)S(1)}, f32[8,5,8,128]{3,2,1,0:T(8,128)S(1)}, u32[]{:S(2)}, u32[]{:S(2)}) collective-permute-start(f32[8,5,8,128]{3,2,1,0:T(8,128)S(1)} %collective-permute-done.10.refs_1_), channel_id=1, source_target_pairs={{16,24},{17,25},{18,26},{19,27},{20,28},{21,29},{22,30},{23,31}} | collective-permute-start | bytes 491528 | tf_op jit(solution)/shard_map/ppermute | solution.py:325
  39.7 5.0 %collective-permute-start.8 = (f32[8,5,8,128]{3,2,1,0:T(8,128)S(1)}, f32[8,5,8,128]{3,2,1,0:T(8,128)S(1)}, u32[]{:S(2)}, u32[]{:S(2)}) collective-permute-start(f32[8,5,8,128]{3,2,1,0:T(8,128)S(1)} %collective-permute-done.7.refs_1_), channel_id=1, source_target_pairs={{16,24},{17,25},{18,26},{19,27},{20,28},{21,29},{22,30},{23,31}} | collective-permute-start | bytes 491528 | tf_op jit(solution)/shard_map/ppermute | solution.py:325
  40.4 6.4 %collective-permute-start.5 = (f32[8,5,8,128]{3,2,1,0:T(8,128)S(1)}, f32[8,5,8,128]{3,2,1,0:T(8,128)S(1)}, u32[]{:S(2)}, u32[]{:S(2)}) collective-permute-start(f32[8,5,8,128]{3,2,1,0:T(8,128)S(1)} %collective-permute-done.4.refs_1_), channel_id=1, source_target_pairs={{16,24},{17,25},{18,26},{19,27},{20,28},{21,29},{22,30},{23,31}} | collective-permute-start | bytes 491528 | tf_op jit(solution)/shard_map/ppermute | solution.py:325
  44.1 5.5 %collective-permute-start.21 = (f32[2,6,8,512]{3,2,1,0:T(8,128)S(1)}, f32[2,6,8,512]{3,2,1,0:T(8,128)S(1)}, u32[]{:S(2)}, u32[]{:S(2)}) collective-permute-start(f32[2,6,8,512]{3,2,1,0:T(8,128)S(1)} %get-tuple-element.64.b_ref), channel_id=1, source_target_pairs={{24,16},{25,17},{26,18},{27,19},{28,20},{29,21},{30,22},{31,23}} | collective-permute-start | bytes 589832 | tf_op jit(solution)/shard_map/ppermute | solution.py:328
  46.2 4.2 %collective-permute-start.18 = (f32[2,6,8,512]{3,2,1,0:T(8,128)S(1)}, f32[2,6,8,512]{3,2,1,0:T(8,128)S(1)}, u32[]{:S(2)}, u32[]{:S(2)}) collective-permute-start(f32[2,6,8,512]{3,2,1,0:T(8,128)S(1)} %get-tuple-element.60.b_ref), channel_id=1, source_target_pairs={{24,16},{25,17},{26,18},{27,19},{28,20},{29,21},{30,22},{31,23}} | collective-permute-start | bytes 589832 | tf_op jit(solution)/shard_map/ppermute | solution.py:328
  48.3 3.6 %copy-start.2 = (f32[2,25,8,512]{3,2,1,0:T(8,128)}, f32[2,25,8,512]{3,2,1,0:T(8,128)S(1)}, u32[]{:S(2)}) copy-start(f32[2,25,8,512]{3,2,1,0:T(8,128)S(1)} %get-tuple-element.40.refs_1_) | copy-start | bytes 2457604
  48.3 2.8 %collective-permute-start.15 = (f32[2,6,8,512]{3,2,1,0:T(8,128)S(1)}, f32[2,6,8,512]{3,2,1,0:T(8,128)S(1)}, u32[]{:S(2)}, u32[]{:S(2)}) collective-permute-start(f32[2,6,8,512]{3,2,1,0:T(8,128)S(1)} %get-tuple-element.56.b_ref), channel_id=1, source_target_pairs={{24,16},{25,17},{26,18},{27,19},{28,20},{29,21},{30,22},{31,23}} | collective-permute-start | bytes 589832 | tf_op jit(solution)/shard_map/ppermute | solution.py:328
  49.0 2.8 %collective-permute-start.12 = (f32[2,6,8,512]{3,2,1,0:T(8,128)S(1)}, f32[2,6,8,512]{3,2,1,0:T(8,128)S(1)}, u32[]{:S(2)}, u32[]{:S(2)}) collective-permute-start(f32[2,6,8,512]{3,2,1,0:T(8,128)S(1)} %get-tuple-element.44.b_ref), channel_id=1, source_target_pairs={{24,16},{25,17},{26,18},{27,19},{28,20},{29,21},{30,22},{31,23}} | collective-permute-start | bytes 589832 | tf_op jit(solution)/shard_map/ppermute | solution.py:328
  49.7 2.8 %collective-permute-start.22 = (f32[2,6,8,512]{3,2,1,0:T(8,128)S(1)}, f32[2,6,8,512]{3,2,1,0:T(8,128)S(1)}, u32[]{:S(2)}, u32[]{:S(2)}) collective-permute-start(f32[2,6,8,512]{3,2,1,0:T(8,128)S(1)} %carry.14), channel_id=1, source_target_pairs={{16,8},{17,9},{18,10},{19,11},{20,12},{21,13},{22,14},{23,15}} | collective-permute-start | bytes 589832 | tf_op jit(solution)/shard_map/ppermute | solution.py:328
  50.4 3.5 %collective-permute-start.19 = (f32[2,6,8,512]{3,2,1,0:T(8,128)S(1)}, f32[2,6,8,512]{3,2,1,0:T(8,128)S(1)}, u32[]{:S(2)}, u32[]{:S(2)}) collective-permute-start(f32[2,6,8,512]{3,2,1,0:T(8,128)S(1)} %carry.12), channel_id=1, source_target_pairs={{16,8},{17,9},{18,10},{19,11},{20,12},{21,13},{22,14},{23,15}} | collective-permute-start | bytes 589832 | tf_op jit(solution)/shard_map/ppermute | solution.py:328
  51.1 4.1 %collective-permute-start.16 = (f32[2,6,8,512]{3,2,1,0:T(8,128)S(1)}, f32[2,6,8,512]{3,2,1,0:T(8,128)S(1)}, u32[]{:S(2)}, u32[]{:S(2)}) collective-permute-start(f32[2,6,8,512]{3,2,1,0:T(8,128)S(1)} %carry.10), channel_id=1, source_target_pairs={{16,8},{17,9},{18,10},{19,11},{20,12},{21,13},{22,14},{23,15}} | collective-permute-start | bytes 589832 | tf_op jit(solution)/shard_map/ppermute | solution.py:328
  51.8 4.7 %collective-permute-start.13 = (f32[2,6,8,512]{3,2,1,0:T(8,128)S(1)}, f32[2,6,8,512]{3,2,1,0:T(8,128)S(1)}, u32[]{:S(2)}, u32[]{:S(2)}) collective-permute-start(f32[2,6,8,512]{3,2,1,0:T(8,128)S(1)} %carry.8), channel_id=1, source_target_pairs={{16,8},{17,9},{18,10},{19,11},{20,12},{21,13},{22,14},{23,15}} | collective-permute-start | bytes 589832 | tf_op jit(solution)/shard_map/ppermute | solution.py:328
  52.6 35.5 %collective-permute-start.23 = (f32[2,6,8,512]{3,2,1,0:T(8,128)S(1)}, f32[2,6,8,512]{3,2,1,0:T(8,128)S(1)}, u32[]{:S(2)}, u32[]{:S(2)}) collective-permute-start(f32[2,6,8,512]{3,2,1,0:T(8,128)S(1)} %carry.15), channel_id=1, source_target_pairs={{8,0},{9,1},{10,2},{11,3},{12,4},{13,5},{14,6},{15,7}} | collective-permute-start | bytes 589832 | tf_op jit(solution)/shard_map/ppermute | solution.py:328
  53.9 38.4 %collective-permute-start.20 = (f32[2,6,8,512]{3,2,1,0:T(8,128)S(1)}, f32[2,6,8,512]{3,2,1,0:T(8,128)S(1)}, u32[]{:S(2)}, u32[]{:S(2)}) collective-permute-start(f32[2,6,8,512]{3,2,1,0:T(8,128)S(1)} %carry.13), channel_id=1, source_target_pairs={{8,0},{9,1},{10,2},{11,3},{12,4},{13,5},{14,6},{15,7}} | collective-permute-start | bytes 589832 | tf_op jit(solution)/shard_map/ppermute | solution.py:328
  55.2 41.3 %collective-permute-start.17 = (f32[2,6,8,512]{3,2,1,0:T(8,128)S(1)}, f32[2,6,8,512]{3,2,1,0:T(8,128)S(1)}, u32[]{:S(2)}, u32[]{:S(2)}) collective-permute-start(f32[2,6,8,512]{3,2,1,0:T(8,128)S(1)} %carry.11), channel_id=1, source_target_pairs={{8,0},{9,1},{10,2},{11,3},{12,4},{13,5},{14,6},{15,7}} | collective-permute-start | bytes 589832 | tf_op jit(solution)/shard_map/ppermute | solution.py:328
  56.6 42.0 %collective-permute-start.14 = (f32[2,6,8,512]{3,2,1,0:T(8,128)S(1)}, f32[2,6,8,512]{3,2,1,0:T(8,128)S(1)}, u32[]{:S(2)}, u32[]{:S(2)}) collective-permute-start(f32[2,6,8,512]{3,2,1,0:T(8,128)S(1)} %carry.9), channel_id=1, source_target_pairs={{8,0},{9,1},{10,2},{11,3},{12,4},{13,5},{14,6},{15,7}} | collective-permute-start | bytes 589832 | tf_op jit(solution)/shard_map/ppermute | solution.py:328
  100.6 14.6 %all-to-all-start.1 = ((f32[8,5,8,512]{3,2,1,0:T(8,128)}), f32[8,5,8,512]{3,2,1,0:T(8,128)S(1)}, u32[]{:S(2)}, u32[]{:S(2)}) async-start(f32[8,5,8,512]{3,2,1,0:T(8,128)} %stencil.1), calls=%async_computation.1 | async-start | bytes 1310720 | tf_op jit(solution)/shard_map/all_to_all | solution.py:419
  104.2 1.1 copy-start.3

commit v12 on v11

--- a/solution.py
+++ b/solution.py
@@ -386,7 +386,7 @@
         )(*strips[c], beside, excess, observed, noise_weight)
 
     cots = [None] * CHUNKS
-    for c in range(CHUNKS):
+    for c in list(range(1, CHUNKS)) + [0]:
         matrices, states, sources, b = work[c]
         arrived = [descend(b, 0)]
         for hop in range(1, groups - 1):

time: 117 us -> 117 us (level)
  no operation moved by 1% of the time
where the time goes in v12:
time: 117 us; the launch traced here: 116 us
  waiting for transfers between devices  49.9 us (43%)
  starting transfers between devices  31.8 us (27%)
  blocking collectives  16.1 us (14%)
  Pallas kernels  12.5 us (11%)
  local copies, waits for them, and re-layouts  3.89 us (3%)
    ppermute x12, waiting for transfers between devices, descend(): return lax.ppermute(x, 'plane', [(groups - 1 - hop, groups - 2 - hop)])  40 us
    ppermute x12, starting transfers between devices, climb(): lax.ppermute(x, 'plane', [(i, i + 1) for i in range(hop, groups - 1)])  17.7 us
    all_to_all x1, blocking collectives, on_device(): lax.all_to_all(packed, 'slab', split_axis=0, concat_axis=0, tiled=True)  16.1 us
    ppermute x12, starting transfers between devices, descend(): return lax.ppermute(x, 'plane', [(groups - 1 - hop, groups - 2 - hop)])  10.6 us
    all_to_all x1, waiting for transfers between devices, on_device(): lax.all_to_all(partial, 'slab', split_axis=0, concat_axis=0, tiled=True)  6.68 us
    pallas_call x4, Pallas kernels, on_device(): pl.pallas_call(functools.partial(forward_kernel, groups, planes, c, lengt...  5.56 us
    unnamed x11, local copies, waits for them, and re-layouts  3.89 us
    all_to_all x1, starting transfers between devices, on_device(): lax.all_to_all(partial, 'slab', split_axis=0, concat_axis=0, tiled=True)  3.54 us
  transfers between devices with their start and end apart: 25, of which 7 were waited for; matrix products, arithmetic and copies ran while one was open for 1% of the time, Pallas kernels for 7%

profile of v12, /device:TPU:0, one launch (start us, length us, event | category | flops | bytes accessed | tf_op | source)
XLA Modules:
  0.0 116.2 jit_solution(15203956441672838508)
XLA Ops:
  0.7 0.8 pad_maximum_fusion.coef_ref
  1.5 1.0 copy-done.4
  2.5 0.7 pack.1
  3.2 16.1 %all_to_all.10 = f32[8,4,5,8,128]{4,3,2,1,0:T(8,128)S(1)} all-to-all(f32[8,4,5,8,128]{4,3,2,1,0:T(8,128)S(1)} %get-tuple-element.34), channel_id=1, replica_groups=mesh['plane'=4,'slab'=8] {'slab'}, dimensions={0} | all-to-all | bytes 1310720 | tf_op jit(solution)/shard_map/all_to_all | solution.py:339
  19.3 0.7 split.1
  20.0 3.5 %collective-permute-start = (f32[9,5,8,128]{3,2,1,0:T(8,128)S(1)}, f32[9,5,8,128]{3,2,1,0:T(8,128)S(1)}, u32[]{:S(2)}, u32[]{:S(2)}) collective-permute-start(f32[9,5,8,128]{3,2,1,0:T(8,128)S(1)} %get-tuple-element.35.refs_3_), channel_id=1, source_target_pairs={{0,8},{8,16},{16,24},{1,9},{9,17},{17,25},{2,10},{10,18},{18,26},{... | collective-permute-start | bytes 552968 | tf_op jit(solution)/shard_map/ppermute | solution.py:325
  23.5 3.5 %collective-permute-start.9 = (f32[8,5,8,128]{3,2,1,0:T(8,128)S(1)}, f32[8,5,8,128]{3,2,1,0:T(8,128)S(1)}, u32[]{:S(2)}, u32[]{:S(2)}) collective-permute-start(f32[8,5,8,128]{3,2,1,0:T(8,128)S(1)} %get-tuple-element.43.refs_3_), channel_id=1, source_target_pairs={{0,8},{8,16},{16,24},{1,9},{9,17},{17,25},{2,10},{10,18},{18,26},{... | collective-permute-start | bytes 491528 | tf_op jit(solution)/shard_map/ppermute | solution.py:325
  27.0 3.5 %collective-permute-start.6 = (f32[8,5,8,128]{3,2,1,0:T(8,128)S(1)}, f32[8,5,8,128]{3,2,1,0:T(8,128)S(1)}, u32[]{:S(2)}, u32[]{:S(2)}) collective-permute-start(f32[8,5,8,128]{3,2,1,0:T(8,128)S(1)} %get-tuple-element.41.refs_3_), channel_id=1, source_target_pairs={{0,8},{8,16},{16,24},{1,9},{9,17},{17,25},{2,10},{10,18},{18,26},{... | collective-permute-start | bytes 491528 | tf_op jit(solution)/shard_map/ppermute | solution.py:325
  30.5 1.9 %collective-permute-start.3 = (f32[8,5,8,128]{3,2,1,0:T(8,128)S(1)}, f32[8,5,8,128]{3,2,1,0:T(8,128)S(1)}, u32[]{:S(2)}, u32[]{:S(2)}) collective-permute-start(f32[8,5,8,128]{3,2,1,0:T(8,128)S(1)} %get-tuple-element.39.refs_3_), channel_id=1, source_target_pairs={{0,8},{8,16},{16,24},{1,9},{9,17},{17,25},{2,10},{10,18},{18,26},{... | collective-permute-start | bytes 491528 | tf_op jit(solution)/shard_map/ppermute | solution.py:325
  32.4 0.7 collective-permute-start.1
  33.1 0.7 collective-permute-start.10
  33.8 1.3 %collective-permute-done.6.refs_2_ = f32[8,5,8,128]{3,2,1,0:T(8,128)S(1)} collective-permute-done((f32[8,5,8,128]{3,2,1,0:T(8,128)S(1)}, f32[8,5,8,128]{3,2,1,0:T(8,128)S(1)}, u32[]{:S(2)}, u32[]{:S(2)}) %collective-permute-start.6) | collective-permute-done | bytes 163872 | tf_op jit(solution)/shard_map/ppermute | solution.py:325
  35.1 0.7 collective-permute-start.7
  35.8 1.9 %collective-permute-done.3.refs_2_ = f32[8,5,8,128]{3,2,1,0:T(8,128)S(1)} collective-permute-done((f32[8,5,8,128]{3,2,1,0:T(8,128)S(1)}, f32[8,5,8,128]{3,2,1,0:T(8,128)S(1)}, u32[]{:S(2)}, u32[]{:S(2)}) %collective-permute-start.3) | collective-permute-done | bytes 163872 | tf_op jit(solution)/shard_map/ppermute | solution.py:325
  37.7 0.7 collective-permute-start.4
  38.4 0.7 collective-permute-start.2
  39.1 0.7 collective-permute-start.11
  39.7 0.7 collective-permute-start.8
  40.4 0.7 collective-permute-start.5
  41.3 1.4 %forward.4 = (f32[2,25,8,512]{3,2,1,0:T(8,128)S(1)}, f32[2,15,8,512]{3,2,1,0:T(8,128)S(1)}, f32[2,20,8,512]{3,2,1,0:T(8,128)S(1)}, f32[2,15,8,512]{3,2,1,0:T(8,128)S(1)}, f32[2,6,8,512]{3,2,1,0:T(8,128)S(1)}) custom-call(f32[9,5,8,128]{3,2,1,0:T(8,128)S(1)} %collective-permute-done.2.refs_0_, f32[9,5,8,128]{3,2,1,0:T(8,128)S(1)} %collective-permute-done.1.refs_1_, ...), custom_call_target="tpu_custom_call" | custom-call | tf_op jit(solution)/shard_map/forward/pallas_call | solution.py:373
  42.7 1.4 %forward.7 = (f32[2,25,8,512]{3,2,1,0:T(8,128)S(1)}, f32[2,15,8,512]{3,2,1,0:T(8,128)S(1)}, f32[2,20,8,512]{3,2,1,0:T(8,128)S(1)}, f32[2,15,8,512]{3,2,1,0:T(8,128)S(1)}, f32[2,6,8,512]{3,2,1,0:T(8,128)S(1)}) custom-call(f32[8,5,8,128]{3,2,1,0:T(8,128)S(1)} %collective-permute-done.11.refs_0_, f32[8,5,8,128]{3,2,1,0:T(8,128)S(1)} %collective-permute-done.10.refs_1_, ...), custom_call_target="tpu_custom_call" | custom-call | tf_op jit(solution)/shard_map/forward/pallas_call | solution.py:373
  44.1 0.7 collective-permute-start.21
  44.8 1.4 %forward.6 = (f32[2,25,8,512]{3,2,1,0:T(8,128)S(1)}, f32[2,15,8,512]{3,2,1,0:T(8,128)S(1)}, f32[2,20,8,512]{3,2,1,0:T(8,128)S(1)}, f32[2,15,8,512]{3,2,1,0:T(8,128)S(1)}, f32[2,6,8,512]{3,2,1,0:T(8,128)S(1)}) custom-call(f32[8,5,8,128]{3,2,1,0:T(8,128)S(1)} %collective-permute-done.8.refs_0_, f32[8,5,8,128]{3,2,1,0:T(8,128)S(1)} %collective-permute-done.7.refs_1_, ...), custom_call_target="tpu_custom_call" | custom-call | tf_op jit(solution)/shard_map/forward/pallas_call | solution.py:373
  46.2 0.7 collective-permute-start.18
  46.9 1.4 %forward.5 = (f32[2,25,8,512]{3,2,1,0:T(8,128)S(1)}, f32[2,15,8,512]{3,2,1,0:T(8,128)S(1)}, f32[2,20,8,512]{3,2,1,0:T(8,128)S(1)}, f32[2,15,8,512]{3,2,1,0:T(8,128)S(1)}, f32[2,6,8,512]{3,2,1,0:T(8,128)S(1)}) custom-call(f32[8,5,8,128]{3,2,1,0:T(8,128)S(1)} %collective-permute-done.5.refs_0_, f32[8,5,8,128]{3,2,1,0:T(8,128)S(1)} %collective-permute-done.4.refs_1_, ...), custom_call_target="tpu_custom_call" | custom-call | tf_op jit(solution)/shard_map/forward/pallas_call | solution.py:373
  48.3 0.7 collective-permute-start.15
  49.0 0.7 collective-permute-start.12
  49.7 0.7 collective-permute-start.22
  50.4 0.7 collective-permute-start.19
  51.1 0.7 collective-permute-start.16
  51.8 0.7 collective-permute-start.13
  52.6 1.3 %collective-permute-start.23 = (f32[2,6,8,512]{3,2,1,0:T(8,128)S(1)}, f32[2,6,8,512]{3,2,1,0:T(8,128)S(1)}, u32[]{:S(2)}, u32[]{:S(2)}) collective-permute-start(f32[2,6,8,512]{3,2,1,0:T(8,128)S(1)} %carry.15), channel_id=1, source_target_pairs={{8,0},{9,1},{10,2},{11,3},{12,4},{13,5},{14,6},{15,7}} | collective-permute-start | bytes 589832 | tf_op jit(solution)/shard_map/ppermute | solution.py:328
  53.9 1.3 %collective-permute-start.20 = (f32[2,6,8,512]{3,2,1,0:T(8,128)S(1)}, f32[2,6,8,512]{3,2,1,0:T(8,128)S(1)}, u32[]{:S(2)}, u32[]{:S(2)}) collective-permute-start(f32[2,6,8,512]{3,2,1,0:T(8,128)S(1)} %carry.13), channel_id=1, source_target_pairs={{8,0},{9,1},{10,2},{11,3},{12,4},{13,5},{14,6},{15,7}} | collective-permute-start | bytes 589832 | tf_op jit(solution)/shard_map/ppermute | solution.py:328
  55.2 1.3 %collective-permute-start.17 = (f32[2,6,8,512]{3,2,1,0:T(8,128)S(1)}, f32[2,6,8,512]{3,2,1,0:T(8,128)S(1)}, u32[]{:S(2)}, u32[]{:S(2)}) collective-permute-start(f32[2,6,8,512]{3,2,1,0:T(8,128)S(1)} %carry.11), channel_id=1, source_target_pairs={{8,0},{9,1},{10,2},{11,3},{12,4},{13,5},{14,6},{15,7}} | collective-permute-start | bytes 589832 | tf_op jit(solution)/shard_map/ppermute | solution.py:328
  56.6 1.3 %collective-permute-start.14 = (f32[2,6,8,512]{3,2,1,0:T(8,128)S(1)}, f32[2,6,8,512]{3,2,1,0:T(8,128)S(1)}, u32[]{:S(2)}, u32[]{:S(2)}) collective-permute-start(f32[2,6,8,512]{3,2,1,0:T(8,128)S(1)} %carry.9), channel_id=1, source_target_pairs={{8,0},{9,1},{10,2},{11,3},{12,4},{13,5},{14,6},{15,7}} | collective-permute-start | bytes 589832 | tf_op jit(solution)/shard_map/ppermute | solution.py:328
  57.9 30.2 %collective-permute-done.23.refs_2_ = f32[2,6,8,512]{3,2,1,0:T(8,128)S(1)} collective-permute-done((f32[2,6,8,512]{3,2,1,0:T(8,128)S(1)}, f32[2,6,8,512]{3,2,1,0:T(8,128)S(1)}, u32[]{:S(2)}, u32[]{:S(2)}) %collective-permute-start.23) | collective-permute-done | bytes 196640 | tf_op jit(solution)/shard_map/ppermute | solution.py:328
  88.3 4.0 %collective-permute-done.20.refs_2_ = f32[2,6,8,512]{3,2,1,0:T(8,128)S(1)} collective-permute-done((f32[2,6,8,512]{3,2,1,0:T(8,128)S(1)}, f32[2,6,8,512]{3,2,1,0:T(8,128)S(1)}, u32[]{:S(2)}, u32[]{:S(2)}) %collective-permute-start.20) | collective-permute-done | bytes 196640 | tf_op jit(solution)/shard_map/ppermute | solution.py:328
  92.5 4.0 %collective-permute-done.17.refs_2_ = f32[2,6,8,512]{3,2,1,0:T(8,128)S(1)} collective-permute-done((f32[2,6,8,512]{3,2,1,0:T(8,128)S(1)}, f32[2,6,8,512]{3,2,1,0:T(8,128)S(1)}, u32[]{:S(2)}, u32[]{:S(2)}) %collective-permute-start.17) | collective-permute-done | bytes 196640 | tf_op jit(solution)/shard_map/ppermute | solution.py:328
  96.5 0.3 cotangent.5.refs_1_
  96.8 1.8 %collective-permute-done.14.refs_2_ = f32[2,6,8,512]{3,2,1,0:T(8,128)S(1)} collective-permute-done((f32[2,6,8,512]{3,2,1,0:T(8,128)S(1)}, f32[2,6,8,512]{3,2,1,0:T(8,128)S(1)}, u32[]{:S(2)}, u32[]{:S(2)}) %collective-permute-start.14) | collective-permute-done | bytes 196640 | tf_op jit(solution)/shard_map/ppermute | solution.py:328
  98.6 0.3 cotangent.4.refs_0_
  98.9 1.8 %stencil.1 = f32[8,5,8,512]{3,2,1,0:T(8,128)} custom-call(f32[2,15,8,512]{3,2,1,0:T(8,128)S(1)} %cotangent.4.refs_0_, f32[2,15,8,512]{3,2,1,0:T(8,128)S(1)} %cotangent.5.refs_1_, f32[2,15,8,512]{3,2,1,0:T(8,128)S(1)} %cotangent.6.refs_2_, f32[2,15,8,512]{3,2,1,0:T(8,128)S(1)} %cotangent.7.refs_3_), custom_call_target="tpu_custom_call" | custom-call | tf_op jit(solution)/shard_map/stencil/pallas_call | solution.py:411
  100.6 3.5 %all-to-all-start.1 = ((f32[8,5,8,512]{3,2,1,0:T(8,128)}), f32[8,5,8,512]{3,2,1,0:T(8,128)S(1)}, u32[]{:S(2)}, u32[]{:S(2)}) async-start(f32[8,5,8,512]{3,2,1,0:T(8,128)} %stencil.1), calls=%async_computation.1 | async-start | bytes 1310720 | tf_op jit(solution)/shard_map/all_to_all | solution.py:419
  104.2 1.1 copy-done.3
  105.3 1.6 %assemble.1 = (f32[5,2,6,4096]{3,2,1,0:T(8,128)S(1)}, f32[5,3,6,4096]{3,2,1,0:T(8,128)}) custom-call(f32[2,25,8,512]{3,2,1,0:T(8,128)S(1)} %get-tuple-element.38.refs_0_, f32[2,25,8,512]{3,2,1,0:T(8,128)S(1)} %copy-done.3, f32[2,25,8,512]{3,2,1,0:T(8,128)S(1)} %get-tuple-element.42.refs_2_, f32[2,25,8,512]{3,2,1,0:T(8,128)S(1)} %get-tuple-element.46.refs_3_), custom_call_target="tpu_custom_call" | custom-call | tf_op jit(solution)/shard_map/assemble/pallas_call | solution.py:420
  106.9 1.7 %copy.8 = f32[5,2,6,4096]{3,1,2,0:T(2,128)} copy(f32[5,2,6,4096]{3,2,1,0:T(8,128)S(1)} %get-tuple-element.65) | data formatting | bytes 1966080
  108.6 6.7 %all-to-all-done.1.in_ref = f32[8,5,8,512]{3,2,1,0:T(8,128)S(1)} async-done(((f32[8,5,8,512]{3,2,1,0:T(8,128)}), f32[8,5,8,512]{3,2,1,0:T(8,128)S(1)}, u32[]{:S(2)}, u32[]{:S(2)}) %all-to-all-start.1) | async-done | bytes 655392 | tf_op jit(solution)/shard_map/all_to_all | solution.py:419
  115.3 0.9 combine.1
  (37 shorter events, 0.8 us)
Async XLA Ops:
  0.6 40.6 %copy-start = (f32[5,3,6,4096]{3,2,1,0:T(8,128)S(1)}, f32[5,3,6,4096]{3,2,1,0:T(8,128)}, u32[]{:S(2)}) copy-start(f32[5,3,6,4096]{3,2,1,0:T(8,128)} %refs_6_.7) | copy-start | bytes 4423684
  0.6 40.6 %copy-start.1 = (f32[5,6,4096]{2,1,0:T(8,128)S(1)}, f32[5,6,4096]{2,1,0:T(8,128)}, u32[]{:S(2)}) copy-start(f32[5,6,4096]{2,1,0:T(8,128)} %refs_7_.7) | copy-start | bytes 1474564
  1.5 1.0 copy-start.4
  20.0 12.4 %collective-permute-start = (f32[9,5,8,128]{3,2,1,0:T(8,128)S(1)}, f32[9,5,8,128]{3,2,1,0:T(8,128)S(1)}, u32[]{:S(2)}, u32[]{:S(2)}) collective-permute-start(f32[9,5,8,128]{3,2,1,0:T(8,128)S(1)} %get-tuple-element.35.refs_3_), channel_id=1, source_target_pairs={{0,8},{8,16},{16,24},{1,9},{9,17},{17,25},{2,10},{10,18},{18,26},{... | collective-permute-start | bytes 552968 | tf_op jit(solution)/shard_map/ppermute | solution.py:325
  23.5 9.6 %collective-permute-start.9 = (f32[8,5,8,128]{3,2,1,0:T(8,128)S(1)}, f32[8,5,8,128]{3,2,1,0:T(8,128)S(1)}, u32[]{:S(2)}, u32[]{:S(2)}) collective-permute-start(f32[8,5,8,128]{3,2,1,0:T(8,128)S(1)} %get-tuple-element.43.refs_3_), channel_id=1, source_target_pairs={{0,8},{8,16},{16,24},{1,9},{9,17},{17,25},{2,10},{10,18},{18,26},{... | collective-permute-start | bytes 491528 | tf_op jit(solution)/shard_map/ppermute | solution.py:325
  27.0 8.1 %collective-permute-start.6 = (f32[8,5,8,128]{3,2,1,0:T(8,128)S(1)}, f32[8,5,8,128]{3,2,1,0:T(8,128)S(1)}, u32[]{:S(2)}, u32[]{:S(2)}) collective-permute-start(f32[8,5,8,128]{3,2,1,0:T(8,128)S(1)} %get-tuple-element.41.refs_3_), channel_id=1, source_target_pairs={{0,8},{8,16},{16,24},{1,9},{9,17},{17,25},{2,10},{10,18},{18,26},{... | collective-permute-start | bytes 491528 | tf_op jit(solution)/shard_map/ppermute | solution.py:325
  30.5 7.2 %collective-permute-start.3 = (f32[8,5,8,128]{3,2,1,0:T(8,128)S(1)}, f32[8,5,8,128]{3,2,1,0:T(8,128)S(1)}, u32[]{:S(2)}, u32[]{:S(2)}) collective-permute-start(f32[8,5,8,128]{3,2,1,0:T(8,128)S(1)} %get-tuple-element.39.refs_3_), channel_id=1, source_target_pairs={{0,8},{8,16},{16,24},{1,9},{9,17},{17,25},{2,10},{10,18},{18,26},{... | collective-permute-start | bytes 491528 | tf_op jit(solution)/shard_map/ppermute | solution.py:325
  32.4 6.0 %collective-permute-start.1 = (f32[9,5,8,128]{3,2,1,0:T(8,128)S(1)}, f32[9,5,8,128]{3,2,1,0:T(8,128)S(1)}, u32[]{:S(2)}, u32[]{:S(2)}) collective-permute-start(f32[9,5,8,128]{3,2,1,0:T(8,128)S(1)} %collective-permute-done.refs_2_), channel_id=1, source_target_pairs={{8,16},{16,24},{9,17},{17,25},{10,18},{18,26},{11,19},{19,27},{12,... | collective-permute-start | bytes 552968 | tf_op jit(solution)/shard_map/ppermute | solution.py:325
  33.1 6.0 %collective-permute-start.10 = (f32[8,5,8,128]{3,2,1,0:T(8,128)S(1)}, f32[8,5,8,128]{3,2,1,0:T(8,128)S(1)}, u32[]{:S(2)}, u32[]{:S(2)}) collective-permute-start(f32[8,5,8,128]{3,2,1,0:T(8,128)S(1)} %collective-permute-done.9.refs_2_), channel_id=1, source_target_pairs={{8,16},{16,24},{9,17},{17,25},{10,18},{18,26},{11,19},{19,27},{12,... | collective-permute-start | bytes 491528 | tf_op jit(solution)/shard_map/ppermute | solution.py:325
  35.1 4.6 %collective-permute-start.7 = (f32[8,5,8,128]{3,2,1,0:T(8,128)S(1)}, f32[8,5,8,128]{3,2,1,0:T(8,128)S(1)}, u32[]{:S(2)}, u32[]{:S(2)}) collective-permute-start(f32[8,5,8,128]{3,2,1,0:T(8,128)S(1)} %collective-permute-done.6.refs_2_), channel_id=1, source_target_pairs={{8,16},{16,24},{9,17},{17,25},{10,18},{18,26},{11,19},{19,27},{12,... | collective-permute-start | bytes 491528 | tf_op jit(solution)/shard_map/ppermute | solution.py:325
  37.7 2.7 %collective-permute-start.4 = (f32[8,5,8,128]{3,2,1,0:T(8,128)S(1)}, f32[8,5,8,128]{3,2,1,0:T(8,128)S(1)}, u32[]{:S(2)}, u32[]{:S(2)}) collective-permute-start(f32[8,5,8,128]{3,2,1,0:T(8,128)S(1)} %collective-permute-done.3.refs_2_), channel_id=1, source_target_pairs={{8,16},{16,24},{9,17},{17,25},{10,18},{18,26},{11,19},{19,27},{12,... | collective-permute-start | bytes 491528 | tf_op jit(solution)/shard_map/ppermute | solution.py:325
  38.4 2.8 %collective-permute-start.2 = (f32[9,5,8,128]{3,2,1,0:T(8,128)S(1)}, f32[9,5,8,128]{3,2,1,0:T(8,128)S(1)}, u32[]{:S(2)}, u32[]{:S(2)}) collective-permute-start(f32[9,5,8,128]{3,2,1,0:T(8,128)S(1)} %collective-permute-done.1.refs_1_), channel_id=1, source_target_pairs={{16,24},{17,25},{18,26},{19,27},{20,28},{21,29},{22,30},{23,31}} | collective-permute-start | bytes 552968 | tf_op jit(solution)/shard_map/ppermute | solution.py:325
  39.1 3.6 %collective-permute-start.11 = (f32[8,5,8,128]{3,2,1,0:T(8,128)S(1)}, f32[8,5,8,128]{3,2,1,0:T(8,128)S(1)}, u32[]{:S(2)}, u32[]{:S(2)}) collective-permute-start(f32[8,5,8,128]{3,2,1,0:T(8,128)S(1)} %collective-permute-done.10.refs_1_), channel_id=1, source_target_pairs={{16,24},{17,25},{18,26},{19,27},{20,28},{21,29},{22,30},{23,31}} | collective-permute-start | bytes 491528 | tf_op jit(solution)/shard_map/ppermute | solution.py:325
  39.7 5.0 %collective-permute-start.8 = (f32[8,5,8,128]{3,2,1,0:T(8,128)S(1)}, f32[8,5,8,128]{3,2,1,0:T(8,128)S(1)}, u32[]{:S(2)}, u32[]{:S(2)}) collective-permute-start(f32[8,5,8,128]{3,2,1,0:T(8,128)S(1)} %collective-permute-done.7.refs_1_), channel_id=1, source_target_pairs={{16,24},{17,25},{18,26},{19,27},{20,28},{21,29},{22,30},{23,31}} | collective-permute-start | bytes 491528 | tf_op jit(solution)/shard_map/ppermute | solution.py:325
  40.4 6.4 %collective-permute-start.5 = (f32[8,5,8,128]{3,2,1,0:T(8,128)S(1)}, f32[8,5,8,128]{3,2,1,0:T(8,128)S(1)}, u32[]{:S(2)}, u32[]{:S(2)}) collective-permute-start(f32[8,5,8,128]{3,2,1,0:T(8,128)S(1)} %collective-permute-done.4.refs_1_), channel_id=1, source_target_pairs={{16,24},{17,25},{18,26},{19,27},{20,28},{21,29},{22,30},{23,31}} | collective-permute-start | bytes 491528 | tf_op jit(solution)/shard_map/ppermute | solution.py:325
  44.1 5.5 %collective-permute-start.21 = (f32[2,6,8,512]{3,2,1,0:T(8,128)S(1)}, f32[2,6,8,512]{3,2,1,0:T(8,128)S(1)}, u32[]{:S(2)}, u32[]{:S(2)}) collective-permute-start(f32[2,6,8,512]{3,2,1,0:T(8,128)S(1)} %get-tuple-element.64.b_ref), channel_id=1, source_target_pairs={{24,16},{25,17},{26,18},{27,19},{28,20},{29,21},{30,22},{31,23}} | collective-permute-start | bytes 589832 | tf_op jit(solution)/shard_map/ppermute | solution.py:328
  46.2 4.2 %collective-permute-start.18 = (f32[2,6,8,512]{3,2,1,0:T(8,128)S(1)}, f32[2,6,8,512]{3,2,1,0:T(8,128)S(1)}, u32[]{:S(2)}, u32[]{:S(2)}) collective-permute-start(f32[2,6,8,512]{3,2,1,0:T(8,128)S(1)} %get-tuple-element.60.b_ref), channel_id=1, source_target_pairs={{24,16},{25,17},{26,18},{27,19},{28,20},{29,21},{30,22},{31,23}} | collective-permute-start | bytes 589832 | tf_op jit(solution)/shard_map/ppermute | solution.py:328
  48.3 3.6 %copy-start.2 = (f32[2,25,8,512]{3,2,1,0:T(8,128)}, f32[2,25,8,512]{3,2,1,0:T(8,128)S(1)}, u32[]{:S(2)}) copy-start(f32[2,25,8,512]{3,2,1,0:T(8,128)S(1)} %get-tuple-element.40.refs_1_) | copy-start | bytes 2457604
  48.3 2.8 %collective-permute-start.15 = (f32[2,6,8,512]{3,2,1,0:T(8,128)S(1)}, f32[2,6,8,512]{3,2,1,0:T(8,128)S(1)}, u32[]{:S(2)}, u32[]{:S(2)}) collective-permute-start(f32[2,6,8,512]{3,2,1,0:T(8,128)S(1)} %get-tuple-element.56.b_ref), channel_id=1, source_target_pairs={{24,16},{25,17},{26,18},{27,19},{28,20},{29,21},{30,22},{31,23}} | collective-permute-start | bytes 589832 | tf_op jit(solution)/shard_map/ppermute | solution.py:328
  49.0 2.8 %collective-permute-start.12 = (f32[2,6,8,512]{3,2,1,0:T(8,128)S(1)}, f32[2,6,8,512]{3,2,1,0:T(8,128)S(1)}, u32[]{:S(2)}, u32[]{:S(2)}) collective-permute-start(f32[2,6,8,512]{3,2,1,0:T(8,128)S(1)} %get-tuple-element.44.b_ref), channel_id=1, source_target_pairs={{24,16},{25,17},{26,18},{27,19},{28,20},{29,21},{30,22},{31,23}} | collective-permute-start | bytes 589832 | tf_op jit(solution)/shard_map/ppermute | solution.py:328
  49.7 2.8 %collective-permute-start.22 = (f32[2,6,8,512]{3,2,1,0:T(8,128)S(1)}, f32[2,6,8,512]{3,2,1,0:T(8,128)S(1)}, u32[]{:S(2)}, u32[]{:S(2)}) collective-permute-start(f32[2,6,8,512]{3,2,1,0:T(8,128)S(1)} %carry.14), channel_id=1, source_target_pairs={{16,8},{17,9},{18,10},{19,11},{20,12},{21,13},{22,14},{23,15}} | collective-permute-start | bytes 589832 | tf_op jit(solution)/shard_map/ppermute | solution.py:328
  50.4 3.5 %collective-permute-start.19 = (f32[2,6,8,512]{3,2,1,0:T(8,128)S(1)}, f32[2,6,8,512]{3,2,1,0:T(8,128)S(1)}, u32[]{:S(2)}, u32[]{:S(2)}) collective-permute-start(f32[2,6,8,512]{3,2,1,0:T(8,128)S(1)} %carry.12), channel_id=1, source_target_pairs={{16,8},{17,9},{18,10},{19,11},{20,12},{21,13},{22,14},{23,15}} | collective-permute-start | bytes 589832 | tf_op jit(solution)/shard_map/ppermute | solution.py:328
  51.1 4.1 %collective-permute-start.16 = (f32[2,6,8,512]{3,2,1,0:T(8,128)S(1)}, f32[2,6,8,512]{3,2,1,0:T(8,128)S(1)}, u32[]{:S(2)}, u32[]{:S(2)}) collective-permute-start(f32[2,6,8,512]{3,2,1,0:T(8,128)S(1)} %carry.10), channel_id=1, source_target_pairs={{16,8},{17,9},{18,10},{19,11},{20,12},{21,13},{22,14},{23,15}} | collective-permute-start | bytes 589832 | tf_op jit(solution)/shard_map/ppermute | solution.py:328
  51.8 4.7 %collective-permute-start.13 = (f32[2,6,8,512]{3,2,1,0:T(8,128)S(1)}, f32[2,6,8,512]{3,2,1,0:T(8,128)S(1)}, u32[]{:S(2)}, u32[]{:S(2)}) collective-permute-start(f32[2,6,8,512]{3,2,1,0:T(8,128)S(1)} %carry.8), channel_id=1, source_target_pairs={{16,8},{17,9},{18,10},{19,11},{20,12},{21,13},{22,14},{23,15}} | collective-permute-start | bytes 589832 | tf_op jit(solution)/shard_map/ppermute | solution.py:328
  52.6 35.5 %collective-permute-start.23 = (f32[2,6,8,512]{3,2,1,0:T(8,128)S(1)}, f32[2,6,8,512]{3,2,1,0:T(8,128)S(1)}, u32[]{:S(2)}, u32[]{:S(2)}) collective-permute-start(f32[2,6,8,512]{3,2,1,0:T(8,128)S(1)} %carry.15), channel_id=1, source_target_pairs={{8,0},{9,1},{10,2},{11,3},{12,4},{13,5},{14,6},{15,7}} | collective-permute-start | bytes 589832 | tf_op jit(solution)/shard_map/ppermute | solution.py:328
  53.9 38.4 %collective-permute-start.20 = (f32[2,6,8,512]{3,2,1,0:T(8,128)S(1)}, f32[2,6,8,512]{3,2,1,0:T(8,128)S(1)}, u32[]{:S(2)}, u32[]{:S(2)}) collective-permute-start(f32[2,6,8,512]{3,2,1,0:T(8,128)S(1)} %carry.13), channel_id=1, source_target_pairs={{8,0},{9,1},{10,2},{11,3},{12,4},{13,5},{14,6},{15,7}} | collective-permute-start | bytes 589832 | tf_op jit(solution)/shard_map/ppermute | solution.py:328
  55.2 41.3 %collective-permute-start.17 = (f32[2,6,8,512]{3,2,1,0:T(8,128)S(1)}, f32[2,6,8,512]{3,2,1,0:T(8,128)S(1)}, u32[]{:S(2)}, u32[]{:S(2)}) collective-permute-start(f32[2,6,8,512]{3,2,1,0:T(8,128)S(1)} %carry.11), channel_id=1, source_target_pairs={{8,0},{9,1},{10,2},{11,3},{12,4},{13,5},{14,6},{15,7}} | collective-permute-start | bytes 589832 | tf_op jit(solution)/shard_map/ppermute | solution.py:328
  56.6 42.0 %collective-permute-start.14 = (f32[2,6,8,512]{3,2,1,0:T(8,128)S(1)}, f32[2,6,8,512]{3,2,1,0:T(8,128)S(1)}, u32[]{:S(2)}, u32[]{:S(2)}) collective-permute-start(f32[2,6,8,512]{3,2,1,0:T(8,128)S(1)} %carry.9), channel_id=1, source_target_pairs={{8,0},{9,1},{10,2},{11,3},{12,4},{13,5},{14,6},{15,7}} | collective-permute-start | bytes 589832 | tf_op jit(solution)/shard_map/ppermute | solution.py:328
  100.6 14.6 %all-to-all-start.1 = ((f32[8,5,8,512]{3,2,1,0:T(8,128)}), f32[8,5,8,512]{3,2,1,0:T(8,128)S(1)}, u32[]{:S(2)}, u32[]{:S(2)}) async-start(f32[8,5,8,512]{3,2,1,0:T(8,128)} %stencil.1), calls=%async_computation.1 | async-start | bytes 1310720 | tf_op jit(solution)/shard_map/all_to_all | solution.py:419
  104.2 1.1 copy-start.3
